TPU v7x, 256 devices: a whole 4x4x8 slice. The times are simulated.
256 devices in a mesh: row: 32 (over x, y, core), col: 8 (over z).
Axes of the slice: x: 4, y: 4, z: 8, core: 2. Of those that a mesh axis runs over, the one named last changes fastest.
Arguments:
- hidden_in: bfloat16 [1152, 2048], P('col', 'row'), may hold values from -21 to 21
- state: float32 [128, 2048, 1152], P('col', 'row'), may hold values from -4 to 4
- attn_norm_gain: bfloat16 [2048], replicated, may hold values from 0.099609375 to 1.8984375
- w_query: bfloat16 [2048, 2048], P(None, 'row'), may hold values from -0.125 to 0.125
- w_key: bfloat16 [2048, 2048], P(None, 'row'), may hold values from -0.125 to 0.125
- w_value: bfloat16 [2048, 2048], P(None, 'row'), may hold values from -0.125 to 0.125
- w_gate: bfloat16 [2048, 2048], P(None, 'row'), may hold values from -0.125 to 0.125
- w_decay: bfloat16 [2048, 16], replicated, may hold values from -0.125 to 0.125
- w_beta: bfloat16 [2048, 16], replicated, may hold values from -0.125 to 0.125
- decay_log: float32 [16], replicated, may hold values from -3 to 1.5
- decay_bias: float32 [16], replicated, may hold values from -2 to 1
- head_gain: float32 [128], replicated, may hold values from 0.1 to 1.9
- w_out: bfloat16 [2048, 2048], P('row'), may hold values from -0.125 to 0.125
- final_gain: bfloat16 [2048], P('row'), may hold values from 0.099609375 to 1.8984375
- lm_weight: bfloat16 [2048, 163840], P(None, ('row', 'col')), may hold values from -0.28726213 to 0.28726213
- token_ids: int32 [1152], replicated, may hold values from 0 to 163839
- ref_logprob: float32 [1152], replicated, may hold values from -16 to -6
Outputs:
- new_state: float32 [128, 2048, 1152], P('col', 'row')
- logprob: float32 [1152], replicated
- entropy: float32 [1152], replicated
- kl: float32 [1152], replicated
All inputs are finite; a program needn't handle non-finite values.
Results may differ from a plain program's by a relative error of at most 0.0014.
The roundings to bfloat16 on the way count: a program that leaves them out, or rounds other values in their place, can miss the bound.
Values may be sent and summed in bfloat16 or wider, within the bound.
No kernel may reach another device: no remote copies, remote signals or barrier semaphores. Data moves between devices by JAX's collectives and lax.ppermute only.
A program may use at most 64 MiB of HBM per device.

v0:
```python
import jax
import jax.numpy as jnp
from jax import lax
from jax.sharding import Mesh
from jax.sharding import PartitionSpec as P

D = 2048
HEADS = 16
DK = 128
DV = 128
ROW = ("row_0", "row_1", "row_2")
ROW_COL = ("row_0", "row_1", "row_2", "col")


def in_order(pieces, dim):
    dims = list(pieces.shape[1:])
    dims[dim] *= pieces.shape[0]
    return jnp.moveaxis(pieces, 0, dim).reshape(dims)


def sent_to_all(array, axis):
    copies = jnp.broadcast_to(array, (lax.axis_size(axis), *array.shape))
    return lax.all_to_all(copies, axis, split_axis=0, concat_axis=0, tiled=True)


def collect(array, axis, dim):
    return in_order(sent_to_all(array, axis), dim)


def partner_2(block, axis, apart):
    count = lax.axis_size(axis)
    route = []
    for low in range(count):
        high = low | 1 << apart
        if high != low and high < count:
            route += [(low, high), (high, low)]
    return lax.ppermute(block, axis, route)


def turned_gather(arrays, axis, dims):
    turned = [jnp.moveaxis(a, dim, 0) for a, dim in zip(arrays, dims)]
    widths = [t[0].size for t in turned]
    both = jnp.concatenate([t.reshape(-1, w) for t, w in zip(turned, widths)], axis=1)
    out = lax.all_gather(both, axis, axis=0, tiled=True)
    pieces = jnp.split(out, [sum(widths[:k]) for k in range(1, len(widths))], axis=1)
    return tuple(
        (
            jnp.moveaxis(b.reshape(-1, *t.shape[1:]), 0, dim)
            for b, t, dim in zip(pieces, turned, dims)
        )
    )


def in_one(arrays, axis):
    flat, at, outs = (jnp.concatenate([a.reshape(-1) for a in arrays]), 0, [])
    running = lax.psum(flat, axis)
    for a in arrays:
        outs.append(running[at : at + a.size].reshape(a.shape))
        at += a.size
    return tuple(outs)


def in_blocks(array, dim, size):
    dims = array.shape
    pieces = array.reshape(*dims[:dim], size, dims[dim] // size, *dims[dim + 1 :])
    return jnp.moveaxis(pieces, dim, 0)


def sent_and_summed(array, axis, dim):
    size = lax.axis_size(axis)
    pieces = lax.all_to_all(in_blocks(array, dim, size), axis, 0, 0, tiled=True)
    return jnp.sum(pieces, axis=0)


def taken_together(array, axis):
    everything = sent_to_all(array, axis)
    return jnp.sum(everything, axis=0)


def gathered_once(array, axis):
    leaves = jax.tree.leaves(array)
    turns = sorted(range(len(leaves)), key=lambda k: -leaves[k].size)
    width = (1, *leaves[turns[0]].shape)[-1]
    lines = [
        jnp.pad(leaves[k].reshape(-1), (0, -leaves[k].size % width)).reshape(-1, width)
        for k in turns
    ]
    both, at, found = (lax.all_gather(jnp.concatenate(lines), axis), 0, {})
    for k, line in zip(turns, lines):
        slab = both[:, at : at + len(line)].reshape(len(both), -1)
        found[k] = slab[:, : leaves[k].size].reshape(-1, *leaves[k].shape)
        at += len(line)
    numbers = iter(range(len(leaves)))
    return jax.tree.map(lambda _: found[next(numbers)], array)


def joined_all(array, axes, combine):
    for axis in axes:
        pieces = gathered_once(array, axis)
        array = jax.tree.map(lambda part: part[0], pieces)
        for k in range(1, lax.axis_size(axis)):
            array = combine(array, jax.tree.map(lambda part: part[k], pieces))
    return array


def project(weight, normed):
    return lax.dot_general(
        weight, normed, (((0,), (1,)), ((), ())), preferred_element_type=jnp.float32
    )


def per_device(
    hidden_in,
    state,
    attn_norm_gain,
    w_query,
    w_key,
    w_value,
    w_gate,
    w_decay,
    w_beta,
    decay_log,
    decay_bias,
    head_gain,
    w_out,
    final_gain,
    lm_weight,
    token_ids,
    ref_logprob,
):
    highest = lax.Precision.HIGHEST
    row_count = lax.axis_size(ROW)
    col_count = lax.axis_size("col")
    row_index = lax.axis_index(ROW)
    col_index = lax.axis_index("col")
    group = max(1, row_count // HEADS)
    local_heads = max(1, HEADS // row_count)
    first_head = row_index // group * local_heads
    value_cols = w_value.shape[1]
    value_part = value_cols // local_heads
    block_rows = hidden_in.shape[0]
    key_rows = state.shape[0]
    batch = state.shape[2]
    vocab_dev = lm_weight.shape[1]
    whole_rows = collect(hidden_in, ROW, 1)
    xfull = whole_rows.astype(jnp.float32)
    normed = (
        xfull
        * lax.rsqrt(jnp.mean(xfull * xfull, axis=1, keepdims=True) + 1e-06)
        * attn_norm_gain.astype(jnp.float32)
    ).astype(jnp.bfloat16)
    raw_pair = jnp.stack([project(w_query, normed), project(w_key, normed)]).astype(jnp.bfloat16)
    raw_pair = lax.optimization_barrier(raw_pair)
    level = 0
    partner = partner_2(raw_pair, ROW, level)
    upper = row_index >> level & 1 == 1
    raw_pair = jnp.where(
        upper,
        jnp.concatenate([partner, raw_pair], axis=1),
        jnp.concatenate([raw_pair, partner], axis=1),
    )
    pair_f = raw_pair.astype(jnp.float32).reshape(2, local_heads, DK, block_rows)
    unit_pair = (
        pair_f * lax.rsqrt(jnp.sum(pair_f * pair_f, axis=2, keepdims=True) + 1e-06)
    ).astype(jnp.bfloat16)
    tiles_qk = lax.all_to_all(unit_pair, "col", split_axis=2, concat_axis=3, tiled=True)
    query = tiles_qk[0].astype(jnp.float32)
    key = tiles_qk[1].astype(jnp.float32)
    value_t = project(w_value, normed)
    gate_t = project(w_gate, normed)
    decay_in = lax.dynamic_slice_in_dim(project(w_decay, normed), first_head, local_heads, 0)
    beta_in = lax.dynamic_slice_in_dim(project(w_beta, normed), first_head, local_heads, 0)
    rate = jnp.exp(lax.dynamic_slice_in_dim(decay_log, first_head, local_heads, 0))
    bias = lax.dynamic_slice_in_dim(decay_bias, first_head, local_heads, 0)
    alpha_t = jnp.exp(-rate[:, None] * jax.nn.softplus(decay_in + bias[:, None]))
    beta_t = jax.nn.sigmoid(beta_in)
    value_all, gate_all, alpha, beta = turned_gather(
        (value_t, gate_t, alpha_t, beta_t), "col", (1, 1, 1, 1)
    )
    tiles = state.reshape(key_rows, local_heads, value_part, batch)
    value4 = value_all.reshape(local_heads, value_part, batch)
    key_major = jnp.transpose(key, (1, 0, 2))
    recall, answer, intersection = in_one(
        (
            jnp.einsum("khvb,hkb->hvb", tiles, key, precision=highest),
            jnp.einsum("khvb,hkb->hvb", tiles, query, precision=highest),
            jnp.sum(key * query, axis=1),
        ),
        "col",
    )
    write = beta[:, None, :] * (value4 - alpha[:, None, :] * recall)
    updated = alpha[None, :, None, :] * tiles + key_major[:, :, None, :] * write[None]
    readout = alpha[:, None, :] * answer + intersection[:, None, :] * write
    power = jnp.sum(readout * readout, axis=1)
    level = 0
    power = power + partner_2(power, ROW, level)
    gain_part = lax.dynamic_slice_in_dim(head_gain, row_index % group * value_part, value_part, 0)
    gate4 = gate_all.reshape(local_heads, value_part, batch)
    mixed = (
        readout
        * lax.rsqrt(power / DV + 1e-05)[:, None, :]
        * gain_part[None, :, None]
        * jax.nn.silu(gate4)
    )
    mixed_heads = mixed.reshape(value_cols, batch).astype(jnp.bfloat16)
    mine = lax.dynamic_slice_in_dim(mixed_heads, col_index * block_rows, block_rows, 1)
    branch = sent_and_summed(
        lax.dot_general(w_out, mine, (((0,), (0,)), ((), ())), preferred_element_type=jnp.float32),
        ROW,
        0,
    )
    hidden = hidden_in.astype(jnp.float32) + branch.T
    energy = taken_together(jnp.sum(hidden * hidden, axis=1), ROW)
    final = (
        hidden * lax.rsqrt(energy / D + 1e-06)[:, None] * final_gain.astype(jnp.float32)[None, :]
    ).astype(jnp.bfloat16)
    tall = collect(final, "col", 0)
    logits = jnp.dot(
        lax.all_gather(tall, ROW, axis=1, tiled=True), lm_weight, preferred_element_type=jnp.float32
    )
    vocab_start = (row_index * col_count + col_index) * vocab_dev
    hits = jnp.arange(vocab_dev, dtype=jnp.int32)[None, :] + vocab_start == token_ids[:, None]
    local_pick = jnp.sum(jnp.where(hits, logits, jnp.zeros_like(logits)), axis=1)
    local_top = jnp.max(logits, axis=1)
    expo = jnp.exp(logits - local_top[:, None])
    local_total = jnp.sum(expo, axis=1)
    local_weighted = jnp.sum(expo * logits, axis=1)

    def combine(first, second):
        peak = jnp.maximum(first[0], second[0])
        left = jnp.exp(first[0] - peak)
        right = jnp.exp(second[0] - peak)
        return (
            peak,
            first[1] * left + second[1] * right,
            first[2] * left + second[2] * right,
            first[3] + second[3],
        )

    top, total, weighted, picked = joined_all(
        (local_top, local_total, local_weighted, local_pick), ROW_COL, combine
    )
    lse = top + jnp.log(total)
    logprob = picked - lse
    entropy = lse - weighted / total
    gap = jnp.clip(ref_logprob - logprob, -20.0, 20.0)
    kl = jnp.minimum(jnp.exp(gap) - gap - 1.0, 10.0)
    new_state = updated.reshape(key_rows, value_cols, batch)
    return (new_state, logprob, entropy, kl)


def solution(mesh):
    split = Mesh(
        mesh.devices.reshape(4, 4, 2, mesh.shape["col"]), ("row_0", "row_1", "row_2", "col")
    )
    in_specs = (
        P("col", ROW),
        P("col", ROW, None),
        P(),
        P(None, ROW),
        P(None, ROW),
        P(None, ROW),
        P(None, ROW),
        P(),
        P(),
        P(),
        P(),
        P(),
        P(ROW, None),
        P(ROW),
        P(None, ROW_COL),
        P(),
        P(),
    )
    out_specs = (P("col", ROW, None), P(), P(), P())
    return jax.shard_map(
        per_device, mesh=split, in_specs=in_specs, out_specs=out_specs, check_vma=False
    )
```

profile of v0, /device:TPU:1, one launch (start us, length us, event | category | flops | bytes accessed | tf_op | source)
XLA Modules:
  0.0 324.7 jit_solution(17454968034841087661)
XLA Ops:
  7.2 2.0 broadcast_in_dim.8
  9.2 8.6 %all-to-all-start = ((bf16[32,144,64]{1,2,0:T(8,128)(2,1)}), bf16[32,144,64]{1,2,0:T(8,128)(2,1)}, u32[]{:S(2)}, u32[]{:S(2)}) async-start(bf16[32,144,64]{1,2,0:T(8,128)(2,1)} %broadcast_in_dim.8), calls=%async_computation | async-start | bytes 2097152 | tf_op jit(solution)/shard_map/all_to_all | solution.py:23
  20.4 14.5 %all-to-all-done = bf16[32,144,64]{1,2,0:T(8,128)(2,1)} async-done(((bf16[32,144,64]{1,2,0:T(8,128)(2,1)}), bf16[32,144,64]{1,2,0:T(8,128)(2,1)}, u32[]{:S(2)}, u32[]{:S(2)}) %all-to-all-start) | async-done | bytes 589856 | tf_op jit(solution)/shard_map/all_to_all | solution.py:23
  34.8 2.8 convert_element_type.92
  37.6 2.7 copy.84
  40.4 1.6 multiply_reduce_fusion.3
  42.0 1.5 multiply_convert_fusion
  43.5 0.9 fusion.93
  44.4 0.9 fusion.94
  46.5 0.9 collective-permute-done
  47.5 0.8 copy.65
  48.3 8.2 %all-to-all-start.1 = ((bf16[2,1,128,144]{3,0,1,2:T(2,128)(2,1)}), bf16[2,1,128,144]{3,0,1,2:T(2,128)(2,1)S(1)}, u32[]{:S(2)}, u32[]{:S(2)}) async-start(bf16[2,1,128,144]{3,0,1,2:T(2,128)(2,1)} %copy.65), calls=%async_computation.1 | async-start | bytes 262144 | tf_op jit(solution)/shard_map/all_to_all | solution.py:166
  56.5 0.9 fusion.96
  57.4 7.4 %all-to-all-done.1 = bf16[2,1,128,144]{3,0,1,2:T(2,128)(2,1)S(1)} async-done(((bf16[2,1,128,144]{3,0,1,2:T(2,128)(2,1)}), bf16[2,1,128,144]{3,0,1,2:T(2,128)(2,1)S(1)}, u32[]{:S(2)}, u32[]{:S(2)}) %all-to-all-start.1) | async-done | bytes 73760 | tf_op jit(solution)/shard_map/all_to_all | solution.py:166
  65.2 0.7 fusion.91
  65.9 3.1 multiply_reduce_fusion.1
  69.1 0.9 pad_maximum_fusion
  70.0 1.4 add_divide_fusion
  71.4 0.9 maximum_bitcast_fusion
  72.2 23.7 %all-gather.4 = f32[8,144,130]{1,2,0:T(8,128)S(1)} all-gather(f32[1,144,130]{1,2,0:T(8,128)S(1)} %maximum_bitcast_fusion), channel_id=1, replica_groups=mesh['row_0'=4,'row_1'=4,'row_2'=2,'col'=8] {'col'}, dimensions={0}, use_global_device_ids=true | all-gather | bytes 673920 | tf_op jit(solution)/shard_map/all_gather | solution.py:44
  96.0 1.3 copy.64
  97.3 1.7 reshape.1197
  99.6 34.8 %all-reduce.2.cloned.1.call-done = f32[148608]{0:T(1024)} async-done(((f32[148608]{0:T(1024)}), f32[148608]{0:T(1024)}) %all-reduce.2.cloned.1.call-update) | async-done | bytes 594448 | tf_op jit(solution)/shard_map/psum | solution.py:56
  134.4 1.8 fusion.89
  136.2 1.7 slice.416
  137.9 0.8 slice.418
  138.7 0.7 slice.496
  139.4 1.2 multiply_reduce_fusion.4
  140.6 5.6 %collective-permute-start.1 = (f32[1,1152]{1,0:T(1,128)S(1)}, f32[1,1152]{1,0:T(1,128)S(1)}, u32[]{:S(2)}, u32[]{:S(2)}) collective-permute-start(f32[1,1152]{1,0:T(1,128)S(1)} %reduce_sum.96), channel_id=1, source_target_pairs={{0,8},{8,0},{16,24},{24,16},{32,40},{40,32},{48,56},{56,48},{64,72... | collective-permute-start | bytes 13832 | tf_op jit(solution)/shard_map/ppermute | solution.py:37
  146.2 0.8 collective-permute-done.1
  147.1 2.4 convolution_bitcast_fusion
  149.5 2.7 copy.85
  152.3 35.6 %all_to_all.36 = f32[32,64,144]{2,1,0:T(8,128)} all-to-all(f32[32,64,144]{2,1,0:T(8,128)} %bitcast.390), channel_id=1, replica_groups=mesh['row_0'=4,'row_1'=4,'row_2'=2,'col'=8] {'row_0','row_1','row_2'}, dimensions={0} | all-to-all | bytes 2359296 | tf_op jit(solution)/shard_map/all_to_all | solution.py:71
  187.8 1.8 reduce_sum.97
  190.3 4.0 %all-to-all-start.3 = ((f32[32,1,144]{2,1,0:T(1,128)}), f32[32,1,144]{2,1,0:T(1,128)S(1)}, u32[]{:S(2)}, u32[]{:S(2)}) async-start(f32[32,1,144]{2,1,0:T(1,128)} %broadcast_in_dim.9), calls=%async_computation.3 | async-start | bytes 65536 | tf_op jit(solution)/shard_map/all_to_all | solution.py:23
  194.3 7.2 %all-to-all-done.3 = f32[32,1,144]{2,1,0:T(1,128)S(1)} async-done(((f32[32,1,144]{2,1,0:T(1,128)}), f32[32,1,144]{2,1,0:T(1,128)S(1)}, u32[]{:S(2)}, u32[]{:S(2)}) %all-to-all-start.3) | async-done | bytes 18464 | tf_op jit(solution)/shard_map/all_to_all | solution.py:23
  201.7 14.5 %all_to_all.37 = bf16[8,144,64]{1,2,0:T(8,128)(2,1)S(1)} all-to-all(bf16[8,144,64]{1,2,0:T(8,128)(2,1)S(1)} %broadcast_in_dim.10), channel_id=1, replica_groups=mesh['row_0'=4,'row_1'=4,'row_2'=2,'col'=8] {'col'}, dimensions={0} | all-to-all | bytes 294912 | tf_op jit(solution)/shard_map/all_to_all | solution.py:23
  216.4 0.9 reshape.1183
  217.4 5.1 %multiply_add_fusion = f32[16,64,1152]{2,1,0:T(8,128)} fusion(f32[16,64,1152]{2,1,0:T(8,128)} %param.18, f32[64,1152]{1,0:T(8,128)S(1)} %get-tuple-element.46, f32[16,1152]{1,0:T(8,128)S(1)} %copy-done.1, f32[1152]{0:T(1024)S(1)} %get-tuple-element.10), kind=kLoop, calls=%fused_computation.2 | loop fusion | flops 3538944 | bytes 9810432 | tf_op jit(solution)/shard_map/add | solution.py:192
  222.5 40.9 %all-gather.11.cloned.1.call-done = bf16[1152,2048]{0,1:T(8,128)(2,1)} async-done(((bf16[1152,64]{0,1:T(8,128)(2,1)}), bf16[1152,2048]{0,1:T(8,128)(2,1)}) %all-gather.11.cloned.1.call-update) | async-done | bytes 4718608 | tf_op jit(solution)/shard_map/all_gather | solution.py:219
  263.4 5.9 %fusion.92 = (f32[1152]{0:T(1024)S(1)}, f32[1152,640]{0,1:T(8,128)S(1)}) fusion(bf16[1152,2048]{0,1:T(8,128)(2,1)} %all-gather.11.cloned.1.call-done, bf16[2048,640]{1,0:T(8,128)(2,1)S(1)} %copy-done), kind=kOutput, calls=%fused_computation.234 | convolution fusion | flops 3020635136 | bytes 10293760 | tf_op jit(solution)/shard_map/dot_general | solution.py:218
  269.4 0.9 fusion
  270.4 9.4 %all-gather.5 = f32[4,4,1152]{2,1,0:T(4,128)S(1)} all-gather(f32[1,4,1152]{2,1,0:T(4,128)S(1)} %maximum_bitcast_fusion.1), channel_id=2, replica_groups=mesh['row_0'=4,'row_1'=4,'row_2'=2,'col'=8] {'row_0'}, dimensions={0}, use_global_device_ids=true | all-gather | bytes 92160 | tf_op jit(solution)/shard_map/all_gather | solution.py:88
  280.0 9.0 %all-gather.6 = f32[4,4,1152]{2,1,0:T(4,128)S(1)} all-gather(f32[1,4,1152]{2,1,0:T(4,128)S(1)} %maximum_bitcast_fusion.2), channel_id=3, replica_groups=mesh['row_0'=4,'row_1'=4,'row_2'=2,'col'=8] {'row_1'}, dimensions={0}, use_global_device_ids=true | all-gather | bytes 92160 | tf_op jit(solution)/shard_map/all_gather | solution.py:88
  289.1 7.1 %all-gather.7 = f32[2,4,1152]{2,1,0:T(4,128)S(1)} all-gather(f32[1,4,1152]{2,1,0:T(4,128)S(1)} %maximum_bitcast_fusion.3), channel_id=4, replica_groups=mesh['row_0'=4,'row_1'=4,'row_2'=2,'col'=8] {'row_2'}, dimensions={0}, use_global_device_ids=true | all-gather | bytes 55296 | tf_op jit(solution)/shard_map/all_gather | solution.py:88
  296.4 19.9 %all-gather.8 = f32[8,4,1152]{2,1,0:T(4,128)S(1)} all-gather(f32[1,4,1152]{2,1,0:T(4,128)S(1)} %maximum_bitcast_fusion.4), channel_id=5, replica_groups=mesh['row_0'=4,'row_1'=4,'row_2'=2,'col'=8] {'col'}, dimensions={0}, use_global_device_ids=true | all-gather | bytes 165888 | tf_op jit(solution)/shard_map/all_gather | solution.py:88
  316.6 0.7 fusion.17
  317.2 0.6 divide_subtract_fusion
  (92 shorter events, 6.2 us)
Async XLA Ops:
  7.2 256.3 %copy-start = (bf16[2048,640]{1,0:T(8,128)(2,1)S(1)}, bf16[2048,640]{1,0:T(8,128)(2,1)}, u32[]{:S(2)}) copy-start(bf16[2048,640]{1,0:T(8,128)(2,1)} %param.31) | copy-start | bytes 7864324
  7.2 10.7 %copy-start.13 = (f32[16]{0:T(128)S(1)}, f32[16]{0:T(128)}, u32[]{:S(2)}) copy-start(f32[16]{0:T(128)} %param.26) | copy-start | bytes 196
  7.2 12.0 %copy-start.14 = (f32[16]{0:T(128)S(1)}, f32[16]{0:T(128)}, u32[]{:S(2)}) copy-start(f32[16]{0:T(128)} %param.27) | copy-start | bytes 196
  7.2 12.6 %copy-start.11 = (bf16[2048]{0:T(1024)(128)(2,1)S(1)}, bf16[2048]{0:T(1024)(128)(2,1)}, u32[]{:S(2)}) copy-start(bf16[2048]{0:T(1024)(128)(2,1)} %param.19) | copy-start | bytes 12292
  7.2 12.6 %copy-start.15 = (f32[128]{0:T(128)S(1)}, f32[128]{0:T(128)}, u32[]{:S(2)}) copy-start(f32[128]{0:T(128)} %param.28) | copy-start | bytes 1540
  9.2 25.6 %all-to-all-start = ((bf16[32,144,64]{1,2,0:T(8,128)(2,1)}), bf16[32,144,64]{1,2,0:T(8,128)(2,1)}, u32[]{:S(2)}, u32[]{:S(2)}) async-start(bf16[32,144,64]{1,2,0:T(8,128)(2,1)} %broadcast_in_dim.8), calls=%async_computation | async-start | bytes 2097152 | tf_op jit(solution)/shard_map/all_to_all | solution.py:23
  37.6 5.8 %copy-start.3 = (bf16[2048,64]{0,1:T(8,128)(2,1)S(1)}, bf16[2048,64]{0,1:T(8,128)(2,1)}, u32[]{:S(2)}) copy-start(bf16[2048,64]{0,1:T(8,128)(2,1)} %param.22) | copy-start | bytes 786436
  40.3 4.1 %copy-start.4 = (bf16[2048,64]{0,1:T(8,128)(2,1)S(1)}, bf16[2048,64]{0,1:T(8,128)(2,1)}, u32[]{:S(2)}) copy-start(bf16[2048,64]{0,1:T(8,128)(2,1)} %param.23) | copy-start | bytes 786436
  40.3 5.0 %copy-start.5 = (bf16[2048,64]{0,1:T(8,128)(2,1)S(1)}, bf16[2048,64]{0,1:T(8,128)(2,1)}, u32[]{:S(2)}) copy-start(bf16[2048,64]{0,1:T(8,128)(2,1)} %param.20) | copy-start | bytes 786436
  40.4 5.3 %copy-start.6 = (bf16[2048,64]{0,1:T(8,128)(2,1)S(1)}, bf16[2048,64]{0,1:T(8,128)(2,1)}, u32[]{:S(2)}) copy-start(bf16[2048,64]{0,1:T(8,128)(2,1)} %param.21) | copy-start | bytes 786436
  42.0 4.3 %copy-start.7 = (bf16[2048,16]{0,1:T(8,128)(2,1)S(1)}, bf16[2048,16]{0,1:T(8,128)(2,1)}, u32[]{:S(2)}) copy-start(bf16[2048,16]{0,1:T(8,128)(2,1)} %param.24) | copy-start | bytes 196612
  43.5 13.1 %copy-start.8 = (bf16[2048,16]{0,1:T(8,128)(2,1)S(1)}, bf16[2048,16]{0,1:T(8,128)(2,1)}, u32[]{:S(2)}) copy-start(bf16[2048,16]{0,1:T(8,128)(2,1)} %param.25) | copy-start | bytes 196612
  46.0 1.3 collective-permute-start
  48.3 16.5 %all-to-all-start.1 = ((bf16[2,1,128,144]{3,0,1,2:T(2,128)(2,1)}), bf16[2,1,128,144]{3,0,1,2:T(2,128)(2,1)S(1)}, u32[]{:S(2)}, u32[]{:S(2)}) async-start(bf16[2,1,128,144]{3,0,1,2:T(2,128)(2,1)} %copy.65), calls=%async_computation.1 | async-start | bytes 262144 | tf_op jit(solution)/shard_map/all_to_all | solution.py:166
  56.5 77.9 %all-reduce.2.cloned.1.call-start = ((), (), s32[]{:S(2)}) async-start(), calls=%async_computation.5 | async-start | bytes 1196032 | tf_op jit(solution)/shard_map/psum | solution.py:56
  98.9 48.2 %copy-start.12 = (f32[64]{0:T(128)S(1)}, f32[64]{0:T(128)}, u32[]{:S(2)}) copy-start(f32[64]{0:T(128)} %dynamic_slice.16) | copy-start | bytes 772
  140.6 6.5 %collective-permute-start.1 = (f32[1,1152]{1,0:T(1,128)S(1)}, f32[1,1152]{1,0:T(1,128)S(1)}, u32[]{:S(2)}, u32[]{:S(2)}) collective-permute-start(f32[1,1152]{1,0:T(1,128)S(1)} %reduce_sum.96), channel_id=1, source_target_pairs={{0,8},{8,0},{16,24},{24,16},{32,40},{40,32},{48,56},{56,48},{64,72... | collective-permute-start | bytes 13832 | tf_op jit(solution)/shard_map/ppermute | solution.py:37
  152.2 37.4 %copy-start.2 = (bf16[144,64]{0,1:T(8,128)(2,1)S(1)}, bf16[144,64]{0,1:T(8,128)(2,1)}, u32[]{:S(2)}) copy-start(bf16[144,64]{0,1:T(8,128)(2,1)} %param.17) | copy-start | bytes 55300
  152.3 42.0 %copy-start.16 = (bf16[64]{0:T(256)(128)(2,1)S(1)}, bf16[64]{0:T(256)(128)(2,1)}, u32[]{:S(2)}) copy-start(bf16[64]{0:T(256)(128)(2,1)} %param.30) | copy-start | bytes 388
  187.8 29.5 %copy-start.1 = (f32[16,1152]{1,0:T(8,128)S(1)}, f32[16,1152]{1,0:T(8,128)}, u32[]{:S(2)}) copy-start(f32[16,1152]{1,0:T(8,128)} %get-tuple-element.52) | copy-start | bytes 221188
  190.3 11.2 %all-to-all-start.3 = ((f32[32,1,144]{2,1,0:T(1,128)}), f32[32,1,144]{2,1,0:T(1,128)S(1)}, u32[]{:S(2)}, u32[]{:S(2)}) async-start(f32[32,1,144]{2,1,0:T(1,128)} %broadcast_in_dim.9), calls=%async_computation.3 | async-start | bytes 65536 | tf_op jit(solution)/shard_map/all_to_all | solution.py:23
  194.2 69.2 %all-gather.11.cloned.1.call-start = ((), (), s32[]{:S(2)}) async-start(), calls=%async_computation.6 | async-start | bytes 4866048 | tf_op jit(solution)/shard_map/all_gather | solution.py:219
  222.5 46.9 %copy-start.9 = (s32[1152]{0:T(1024)S(1)}, s32[1152]{0:T(1024)}, u32[]{:S(2)}) copy-start(s32[1152]{0:T(1024)} %param.32) | copy-start | bytes 13828
  269.4 47.2 %copy-start.10 = (f32[1152]{0:T(1024)S(1)}, f32[1152]{0:T(1024)}, u32[]{:S(2)}) copy-start(f32[1152]{0:T(1024)} %param.33) | copy-start | bytes 13828
Sparse Core Ops, SparseCore 0:
  70.1 64.2 all-reduce.1
  217.5 45.9 all-gather.10
where the time goes:
time: 331 us; the launch traced here: 325 us
  blocking collectives  119 us (36%)
  waiting for transfers between devices  107 us (32%)
  starting transfers between devices  26.7 us (8%)
  other arithmetic  23.9 us (7%)
  local copies, waits for them, and re-layouts  21.2 us (6%)
  between operations  15.2 us (5%)
  matrix products  12 us (4%)
    all_gather x4, blocking collectives, gathered_once(): both, at, found = (lax.all_gather(jnp.concatenate(lines), axis), 0, {})  45.4 us
    all_gather x1, waiting for transfers between devices, per_device(): lax.all_gather(tall, ROW, axis=1, tiled=True)  40.9 us
    all_to_all x1, blocking collectives, sent_and_summed(): pieces = lax.all_to_all(in_blocks(array, dim, size), axis, 0, 0, tiled=True)  35.6 us
    psum x1, waiting for transfers between devices, in_one(): running = lax.psum(flat, axis)  34.8 us
    all_gather x1, blocking collectives, turned_gather(): out = lax.all_gather(both, axis, axis=0, tiled=True)  23.7 us
    all_to_all x2, waiting for transfers between devices, sent_to_all(): return lax.all_to_all(copies, axis, split_axis=0, concat_axis=0, tiled=True)  21.7 us
    all_to_all x1, blocking collectives, sent_to_all(): return lax.all_to_all(copies, axis, split_axis=0, concat_axis=0, tiled=True)  14.5 us
    all_to_all x2, starting transfers between devices, sent_to_all(): return lax.all_to_all(copies, axis, split_axis=0, concat_axis=0, tiled=True)  12.6 us
  transfers between devices with their start and end apart: 7, of which 7 were waited for; matrix products, arithmetic and copies ran while one was open for 4% of the time, Pallas kernels for 0%

commit v1 on v0

v1 whole, which is shorter than its diff:
```python
import jax
import jax.numpy as jnp
from jax import lax
from jax.sharding import Mesh
from jax.sharding import PartitionSpec as P

D = 2048
HEADS = 16
DK = 128
DV = 128
X = "row_0"
Y = "row_1"
CORE = "row_2"
Z = "col"
XY = (X, Y)
ZC = (Z, CORE)
ROW = (X, Y, CORE)
ROW_COL = (X, Y, CORE, Z)


def swapped(array):
    return lax.ppermute(array, CORE, [(0, 1), (1, 0)])


def exchange(blocks, axes):
    return lax.all_to_all(blocks, axes, split_axis=0, concat_axis=0, tiled=True)


def to_all(array, axes):
    return exchange(jnp.broadcast_to(array, (lax.axis_size(axes), *array.shape)), axes)


def in_core_order(core, own, other, dim):
    first = jnp.where(core == 0, own, other)
    second = jnp.where(core == 0, other, own)
    return jnp.concatenate([first, second], axis=dim)


def merged(stats, dim):
    top_n, total_n, weighted_n, picked_n = stats
    top = jnp.max(top_n, axis=dim, keepdims=True)
    scale = jnp.exp(top_n - top)
    return (
        jnp.squeeze(top, dim),
        jnp.sum(total_n * scale, axis=dim),
        jnp.sum(weighted_n * scale, axis=dim),
        jnp.sum(picked_n, axis=dim),
    )


def per_device(
    hidden_in,
    state,
    attn_norm_gain,
    w_query,
    w_key,
    w_value,
    w_gate,
    w_decay,
    w_beta,
    decay_log,
    decay_bias,
    head_gain,
    w_out,
    final_gain,
    lm_weight,
    token_ids,
    ref_logprob,
):
    core = lax.axis_index(CORE)
    zed = lax.axis_index(Z)
    head = lax.axis_index(XY)
    n_xy = lax.axis_size(XY)
    n_z = lax.axis_size(Z)
    key_rows, half, batch = state.shape
    rows = hidden_in.shape[0] // 2
    vocab_dev = lm_weight.shape[1]

    kept = lax.dynamic_slice_in_dim(hidden_in, core * rows, rows, 0)
    given = lax.dynamic_slice_in_dim(hidden_in, (1 - core) * rows, rows, 0)
    x_block = in_core_order(core, kept, swapped(given), 1)
    pieces = to_all(x_block, XY)

    w_own = jnp.concatenate([w_query, w_key, w_value, w_gate], axis=1)
    w_other = swapped(w_own)
    out_other = swapped(w_out)
    lm_other = swapped(lm_weight)
    gain_block = in_core_order(core, final_gain, swapped(final_gain), 0).astype(jnp.float32)

    x_full = jnp.moveaxis(pieces, 0, 1).reshape(rows, D).astype(jnp.float32)
    normed = (
        x_full
        * lax.rsqrt(jnp.mean(x_full * x_full, axis=1, keepdims=True) + 1e-06)
        * attn_norm_gain.astype(jnp.float32)
    ).astype(jnp.bfloat16)

    def project(weight):
        return lax.dot_general(
            weight, normed, (((0,), (1,)), ((), ())), preferred_element_type=jnp.float32
        )

    own = project(w_own).reshape(4, half, rows)
    other = project(w_other).reshape(4, half, rows)
    qkvg = in_core_order(core, own, other, 1)
    small = project(jnp.concatenate([w_decay, w_beta], axis=1))
    decay_in = lax.dynamic_slice_in_dim(small, head, 1, 0)
    beta_in = lax.dynamic_slice_in_dim(small, HEADS + head, 1, 0)
    rate = jnp.exp(lax.dynamic_slice_in_dim(decay_log, head, 1, 0))[:, None]
    bias = lax.dynamic_slice_in_dim(decay_bias, head, 1, 0)[:, None]
    alpha = jnp.exp(-rate * jax.nn.softplus(decay_in + bias))
    beta = jax.nn.sigmoid(beta_in)

    raw = lax.optimization_barrier(qkvg[:2].astype(jnp.bfloat16)).astype(jnp.float32)
    unit = (raw * lax.rsqrt(jnp.sum(raw * raw, axis=1, keepdims=True) + 1e-06)).astype(
        jnp.bfloat16
    )
    unit_f = unit.astype(jnp.float32)
    meet = jnp.sum(unit_f[0] * unit_f[1], axis=0, keepdims=True)

    parts = jnp.moveaxis(unit.reshape(2, n_z, key_rows, rows), 1, 0)
    parts = jnp.broadcast_to(parts[:, None], (n_z, 2, 2, key_rows, rows))
    landed = exchange(parts.reshape(2 * n_z, 2, key_rows, rows), ZC)
    qk = jnp.moveaxis(landed, 0, 2).reshape(2, key_rows, batch).astype(jnp.float32)
    query_k, key_k = qk[0], qk[1]

    recall_p = jnp.sum(state * key_k[:, None, :], axis=0)
    answer_p = jnp.sum(state * query_k[:, None, :], axis=0)
    both = jnp.stack([recall_p, answer_p]).reshape(2, half, 2 * n_z, rows)
    both = exchange(jnp.moveaxis(both, 2, 0).astype(jnp.bfloat16), ZC)
    both = jnp.sum(both.reshape(n_z, 2, 2, half, rows).astype(jnp.float32), axis=0)
    both = jnp.moveaxis(both, 0, 1).reshape(2, DV, rows)
    recall, answer = both[0], both[1]
    value, gate = qkvg[2], qkvg[3]
    write = beta * (value - alpha * recall)
    readout = alpha * answer + meet * write
    power = jnp.mean(readout * readout, axis=0, keepdims=True)
    mixed = (
        readout * lax.rsqrt(power + 1e-05) * head_gain[:, None] * jax.nn.silu(gate)
    ).astype(jnp.bfloat16)

    first = jnp.where(core == 0, mixed[:half], mixed[half:])
    second = jnp.where(core == 0, mixed[half:], mixed[:half])

    def projected(m, w):
        return lax.dot_general(
            m, w, (((0,), (0,)), ((), ())), preferred_element_type=jnp.float32
        )

    branch = projected(first, w_out) + projected(second, out_other)
    branch = jnp.moveaxis(branch.reshape(rows, n_xy, 2 * final_gain.shape[0]), 1, 0)
    branch = jnp.sum(exchange(branch, XY), axis=0)
    hidden = x_block.astype(jnp.float32) + branch
    energy = jnp.sum(to_all(jnp.sum(hidden * hidden, axis=1), XY), axis=0)
    final = (
        hidden * lax.rsqrt(energy / D + 1e-06)[:, None] * gain_block[None, :]
    ).astype(jnp.bfloat16)

    tall = to_all(final, Z).reshape(n_z * rows, final.shape[1])
    wide = lax.all_gather(tall, XY, axis=1, tiled=True)

    sent = jnp.concatenate(
        [write.reshape(2, half, rows), jnp.broadcast_to(alpha, (2, 1, rows))], axis=1
    )
    sent = jnp.broadcast_to(sent, (n_z, 2, half + 1, rows)).reshape(2 * n_z, half + 1, rows)
    back = jnp.moveaxis(exchange(sent, ZC), 0, 1).reshape(half + 1, batch)
    new_state = back[half] * state + key_k[:, None, :] * back[None, :half]

    ids = lax.dynamic_index_in_dim(token_ids.reshape(n_z, 2, rows), core, 1, False).reshape(-1)

    def statistics(weight, owner):
        logits = jnp.dot(wide, weight, preferred_element_type=jnp.float32)
        start = ((head * 2 + owner) * n_z + zed) * vocab_dev
        hits = jnp.arange(vocab_dev, dtype=jnp.int32)[None, :] + start == ids[:, None]
        picked = jnp.sum(jnp.where(hits, logits, jnp.zeros_like(logits)), axis=1)
        top = jnp.max(logits, axis=1)
        expo = jnp.exp(logits - top[:, None])
        return top, jnp.sum(expo, axis=1), jnp.sum(expo * logits, axis=1), picked

    pair = [jnp.stack(s) for s in zip(statistics(lm_weight, core), statistics(lm_other, 1 - core))]
    stats = jnp.stack(merged(pair, 0))
    stats = jnp.stack(merged(jnp.moveaxis(to_all(stats, XY), 1, 0), 0))
    stats = to_all(stats, ZC).reshape(n_z, 2, 4, n_z * rows)
    top, total, weighted, picked = merged(jnp.moveaxis(stats, 2, 0), 0)
    lse = top + jnp.log(total)
    logprob = picked - lse
    entropy = lse - weighted / total

    def in_order(two):
        return jnp.moveaxis(two.reshape(2, n_z, rows), 0, 1).reshape(batch)

    logprob = in_order(logprob)
    entropy = in_order(entropy)
    gap = jnp.clip(ref_logprob - logprob, -20.0, 20.0)
    kl = jnp.minimum(jnp.exp(gap) - gap - 1.0, 10.0)
    return (new_state, logprob, entropy, kl)


def solution(mesh):
    split = Mesh(mesh.devices.reshape(4, 4, 2, mesh.shape["col"]), (X, Y, CORE, Z))
    in_specs = (
        P(Z, ROW),
        P(Z, ROW, None),
        P(),
        P(None, ROW),
        P(None, ROW),
        P(None, ROW),
        P(None, ROW),
        P(),
        P(),
        P(),
        P(),
        P(),
        P(ROW, None),
        P(ROW),
        P(None, ROW_COL),
        P(),
        P(),
    )
    out_specs = (P(Z, ROW, None), P(), P(), P())
    return jax.shard_map(
        per_device, mesh=split, in_specs=in_specs, out_specs=out_specs, check_vma=False
    )
```

time: 331 us -> 214 us (0.65); the launches traced: 325 us -> 213 us
  blocking collectives: 119 us -> 11.2 us
  starting transfers between devices: 26.7 us -> 50.8 us
  other arithmetic: 23.9 us -> 12.8 us
  waiting for transfers between devices: 107 us -> 99.4 us
  local copies, waits for them, and re-layouts: 21.2 us -> 14.7 us
  matrix products: 12 us -> 8.47 us
    all_gather x5 -> x0, blocking collectives: 69.1 us -> none  [the longest x4 45.4 us: gathered_once(): both, at, found = (lax.all_gather(jnp.concatenate(lines), axis), 0, {})]
    all_to_all x2 -> x1, blocking collectives: 50.1 us -> 11.2 us  [exchange(): return lax.all_to_all(blocks, axes, split_axis=0, concat_axis=0, tiled=True)]
    psum x1 -> x0, waiting for transfers between devices: 34.8 us -> none  [in_one(): running = lax.psum(flat, axis)]
    all_to_all x3 -> x8, waiting for transfers between devices: 29.1 us -> 58.2 us  [exchange(): return lax.all_to_all(blocks, axes, split_axis=0, concat_axis=0, tiled=True)]
    all_to_all x3 -> x8, starting transfers between devices: 20.8 us -> 44 us  [exchange(): return lax.all_to_all(blocks, axes, split_axis=0, concat_axis=0, tiled=True)]
    slice x6, local copies, waits for them, and re-layouts: 5.25 us -> 0.49 us  [the longest x3 0.38 us: per_device(): new_state = back[half] * state + key_k[:, None, :] * back[None, :half]]
    convert_element_type x7 -> x6, other arithmetic: 5.06 us -> 0.42 us  [the longest x1 0.12 us: per_device(): both = exchange(jnp.moveaxis(both, 2, 0).astype(jnp.bfloat16), ZC)]
    dot_general x2 -> x4, matrix products: 8.33 us -> 7.34 us  [the longest x2 6.83 us: statistics(): logits = jnp.dot(wide, weight, preferred_element_type=jnp.float32)]
  transfers between devices with their start and end apart: 7 -> 14, of which waited for: 7 -> 10; matrix products, arithmetic and copies ran while one was open for 4% -> 13% of each run, Pallas kernels for 0% -> 0%
where the time goes in v1:
time: 214 us; the launch traced here: 213 us
  waiting for transfers between devices  99.4 us (46%)
  starting transfers between devices  50.8 us (24%)
  between operations  15.5 us (7%)
  local copies, waits for them, and re-layouts  14.7 us (7%)
  other arithmetic  12.8 us (6%)
  blocking collectives  11.2 us (5%)
  matrix products  8.47 us (4%)
    all_to_all x8, waiting for transfers between devices, exchange(): return lax.all_to_all(blocks, axes, split_axis=0, concat_axis=0, tiled=True)  58.2 us
    all_to_all x8, starting transfers between devices, exchange(): return lax.all_to_all(blocks, axes, split_axis=0, concat_axis=0, tiled=True)  44 us
    all_gather x1, waiting for transfers between devices, per_device(): wide = lax.all_gather(tall, XY, axis=1, tiled=True)  40 us
    all_to_all x1, blocking collectives, exchange(): return lax.all_to_all(blocks, axes, split_axis=0, concat_axis=0, tiled=True)  11.2 us
    ppermute x5, starting transfers between devices, swapped(): return lax.ppermute(array, CORE, [(0, 1), (1, 0)])  6.84 us
    dot_general x2, matrix products, statistics(): logits = jnp.dot(wide, weight, preferred_element_type=jnp.float32)  6.83 us
    add x1, other arithmetic, per_device(): new_state = back[half] * state + key_k[:, None, :] * back[None, :half]  5.17 us
  transfers between devices with their start and end apart: 14, of which 10 were waited for; matrix products, arithmetic and copies ran while one was open for 13% of the time, Pallas kernels for 0%

profile of v1, /device:TPU:1, one launch (start us, length us, event | category | flops | bytes accessed | tf_op | source)
XLA Modules:
  0.0 212.9 jit_solution(12076017366194941060)
XLA Ops:
  7.2 0.9 constant_dynamic-slice_fusion.3
  8.2 3.3 %collective-permute-start = (bf16[72,64]{1,0:T(8,128)(2,1)S(1)}, bf16[72,64]{1,0:T(8,128)(2,1)S(1)}, u32[]{:S(2)}, u32[]{:S(2)}) collective-permute-start(bf16[72,64]{1,0:T(8,128)(2,1)S(1)} %copy.160), channel_id=1, source_target_pairs={{0,8},{8,0},{1,9},{9,1},{2,10},{10,2},{3,11},{11,3},{4,12},{12,4},... | collective-permute-start | bytes 27656 | tf_op jit(solution)/shard_map/ppermute | solution.py:22
  11.5 1.0 constant_dynamic-update-slice_fusion.3
  12.5 1.0 constant_dynamic-update-slice_fusion.2
  13.5 1.0 constant_dynamic-update-slice_fusion.1
  14.7 0.8 broadcast_in_dim.18
  15.4 5.0 %all-to-all-start = ((bf16[16,72,128]{2,1,0:T(8,128)(2,1)}), bf16[16,72,128]{2,1,0:T(8,128)(2,1)S(1)}, u32[]{:S(2)}, u32[]{:S(2)}) async-start(bf16[16,72,128]{2,1,0:T(8,128)(2,1)} %broadcast_in_dim.18), calls=%async_computation | async-start | bytes 589824 | tf_op jit(solution)/shard_map/all_to_all | solution.py:26
  20.5 0.4 collective-permute-start.1
  20.9 7.7 %all-to-all-done = bf16[16,72,128]{2,1,0:T(8,128)(2,1)S(1)} async-done(((bf16[16,72,128]{2,1,0:T(8,128)(2,1)}), bf16[16,72,128]{2,1,0:T(8,128)(2,1)S(1)}, u32[]{:S(2)}, u32[]{:S(2)}) %all-to-all-start) | async-done | bytes 294944 | tf_op jit(solution)/shard_map/all_to_all | solution.py:26
  29.1 0.4 fusion.70
  29.5 0.4 broadcast_select_fusion
  30.1 0.7 broadcast_in_dim.19
  30.8 10.2 %all-to-all-start.1 = ((bf16[16,2,16,72]{3,2,1,0:T(8,128)(2,1)}), bf16[16,2,16,72]{3,2,1,0:T(8,128)(2,1)S(1)}, u32[]{:S(2)}, u32[]{:S(2)}) async-start(bf16[16,2,16,72]{3,2,1,0:T(8,128)(2,1)} %bitcast.14), calls=%async_computation.1 | async-start | bytes 262144 | tf_op jit(solution)/shard_map/all_to_all | solution.py:26
  41.1 0.6 dynamic_slice.25
  42.4 0.6 dynamic_slice.27
  43.0 7.1 %all-to-all-done.1 = bf16[16,2,16,72]{3,2,1,0:T(8,128)(2,1)S(1)} async-done(((bf16[16,2,16,72]{3,2,1,0:T(8,128)(2,1)}), bf16[16,2,16,72]{3,2,1,0:T(8,128)(2,1)S(1)}, u32[]{:S(2)}, u32[]{:S(2)}) %all-to-all-start.1) | async-done | bytes 73760 | tf_op jit(solution)/shard_map/all_to_all | solution.py:26
  50.5 3.0 %multiply_reduce_fusion.1 = (bf16[64,1152]{1,0:T(8,128)(2,1)S(1)}, bf16[64,1152]{1,0:T(8,128)(2,1)S(1)}) fusion(f32[16,64,1152]{2,1,0:T(8,128)} %param.18, f32[16,1152]{1,0:T(8,128)S(1)} %mul.288, f32[16,1152]{1,0:T(8,128)S(1)} %mul.291), kind=kLoop, calls=%fused_computation.2 | loop fusion | flops 4571136 | bytes 5160960 | tf_op jit(solution)/shard_map/reduce_sum | solution.py:126
  53.5 0.5 stack.57
  54.0 0.5 stack.58
  54.6 0.9 copy.134
  55.5 3.5 %all-to-all-start.2 = ((bf16[16,2,64,72]{3,2,1,0:T(8,128)(2,1)}), bf16[16,2,64,72]{3,2,1,0:T(8,128)(2,1)S(1)}, u32[]{:S(2)}, u32[]{:S(2)}) async-start(bf16[16,2,64,72]{3,2,1,0:T(8,128)(2,1)} %copy.134), calls=%async_computation.2 | async-start | bytes 1048576 | tf_op jit(solution)/shard_map/all_to_all | solution.py:26
  59.3 0.7 divide_bitcast_fusion
  60.1 15.8 %all-to-all-done.2 = bf16[16,2,64,72]{3,2,1,0:T(8,128)(2,1)S(1)} async-done(((bf16[16,2,64,72]{3,2,1,0:T(8,128)(2,1)}), bf16[16,2,64,72]{3,2,1,0:T(8,128)(2,1)S(1)}, u32[]{:S(2)}, u32[]{:S(2)}) %all-to-all-start.2) | async-done | bytes 294944 | tf_op jit(solution)/shard_map/all_to_all | solution.py:26
  76.7 0.9 copy.203
  77.6 3.6 %all-to-all-start.4 = ((f32[16,72,128]{2,1,0:T(8,128)}), f32[16,72,128]{2,1,0:T(8,128)S(1)}, u32[]{:S(2)}, u32[]{:S(2)}) async-start(f32[16,72,128]{2,1,0:T(8,128)} %bitcast.148), calls=%async_computation.4 | async-start | bytes 1179648 | tf_op jit(solution)/shard_map/all_to_all | solution.py:26
  81.3 1.1 collective-permute-done.3
  82.4 10.8 %all-to-all-done.4 = f32[16,72,128]{2,1,0:T(8,128)S(1)} async-done(((f32[16,72,128]{2,1,0:T(8,128)}), f32[16,72,128]{2,1,0:T(8,128)S(1)}, u32[]{:S(2)}, u32[]{:S(2)}) %all-to-all-start.4) | async-done | bytes 589856 | tf_op jit(solution)/shard_map/all_to_all | solution.py:26
  93.4 0.6 broadcast_in_dim.22
  94.1 3.5 %all-to-all-start.5 = ((f32[16,1,72]{2,1,0:T(1,128)}), f32[16,1,72]{2,1,0:T(1,128)S(1)}, u32[]{:S(2)}, u32[]{:S(2)}) async-start(f32[16,1,72]{2,1,0:T(1,128)} %broadcast_in_dim.22), calls=%async_computation.5 | async-start | bytes 16384 | tf_op jit(solution)/shard_map/all_to_all | solution.py:26
  97.7 6.1 %all-to-all-done.5 = f32[16,1,72]{2,1,0:T(1,128)S(1)} async-done(((f32[16,1,72]{2,1,0:T(1,128)}), f32[16,1,72]{2,1,0:T(1,128)S(1)}, u32[]{:S(2)}, u32[]{:S(2)}) %all-to-all-start.5) | async-done | bytes 4640 | tf_op jit(solution)/shard_map/all_to_all | solution.py:26
  104.0 11.2 %all_to_all.46 = bf16[8,72,128]{2,1,0:T(8,128)(2,1)} all-to-all(bf16[8,72,128]{2,1,0:T(8,128)(2,1)S(1)} %broadcast_in_dim.23), channel_id=1, replica_groups=mesh['row_0'=4,'row_1'=4,'row_2'=2,'col'=8] {'col'}, dimensions={0} | all-to-all | bytes 294912 | tf_op jit(solution)/shard_map/all_to_all | solution.py:26
  115.2 2.8 %collective-permute-start.4 = (bf16[2048,640]{1,0:T(8,128)(2,1)}, bf16[2048,640]{1,0:T(8,128)(2,1)}, u32[]{:S(2)}, u32[]{:S(2)}) collective-permute-start(bf16[2048,640]{1,0:T(8,128)(2,1)} %param.31), channel_id=1, source_target_pairs={{0,8},{8,0},{1,9},{9,1},{2,10},{10,2},{3,11},{11,3},{4,12},{12,4},... | collective-permute-start | bytes 7864328 | tf_op jit(solution)/shard_map/ppermute | solution.py:22
  118.3 0.9 broadcast_in_dim.21
  119.1 3.7 %all-to-all-start.3 = ((f32[16,65,72]{2,1,0:T(8,128)}), f32[16,65,72]{2,1,0:T(8,128)S(1)}, u32[]{:S(2)}, u32[]{:S(2)}) async-start(f32[16,65,72]{2,1,0:T(8,128)} %bitcast.20), calls=%async_computation.3 | async-start | bytes 1179648 | tf_op jit(solution)/shard_map/all_to_all | solution.py:26
  122.9 40.0 %all-gather.2.cloned.1.call-done = bf16[576,2048]{1,0:T(8,128)(2,1)} async-done(((bf16[576,128]{1,0:T(8,128)(2,1)}), bf16[576,2048]{1,0:T(8,128)(2,1)}) %all-gather.2.cloned.1.call-update) | async-done | bytes 2359312 | tf_op jit(solution)/shard_map/all_gather | solution.py:159
  162.9 4.7 %fusion.68 = (f32[576]{0:T(1024)S(1)}, f32[576,640]{1,0:T(8,128)S(1)}) fusion(bf16[576,2048]{1,0:T(8,128)(2,1)} %all-gather.2.cloned.1.call-done, bf16[2048,640]{1,0:T(8,128)(2,1)} %collective-permute-done.4), kind=kOutput, calls=%fused_computation.146 | convolution fusion | flops 1510317568 | bytes 6457600 | tf_op jit(solution)/shard_map/dot_general | solution.py:171
  167.7 2.1 fusion.69
  169.8 1.5 fusion
  171.5 0.7 broadcast_in_dim.24
  172.2 4.7 %all-to-all-start.7 = ((f32[16,4,576]{2,1,0:T(4,128)}), f32[16,4,576]{2,1,0:T(4,128)S(1)}, u32[]{:S(2)}, u32[]{:S(2)}) async-start(f32[16,4,576]{2,1,0:T(4,128)} %broadcast_in_dim.24), calls=%async_computation.7 | async-start | bytes 327680 | tf_op jit(solution)/shard_map/all_to_all | solution.py:26
  176.9 0.3 copy.135
  177.6 6.2 %all-to-all-done.7 = f32[16,4,576]{2,1,0:T(4,128)S(1)} async-done(((f32[16,4,576]{2,1,0:T(4,128)}), f32[16,4,576]{2,1,0:T(4,128)S(1)}, u32[]{:S(2)}, u32[]{:S(2)}) %all-to-all-start.7) | async-done | bytes 147488 | tf_op jit(solution)/shard_map/all_to_all | solution.py:26
  184.0 0.7 broadcast_in_dim.26
  184.7 9.9 %all-to-all-start.8 = ((f32[16,4,576]{2,1,0:T(4,128)}), f32[16,4,576]{2,1,0:T(4,128)S(1)}, u32[]{:S(2)}, u32[]{:S(2)}) async-start(f32[16,4,576]{2,1,0:T(4,128)} %broadcast_in_dim.26), calls=%async_computation.8 | async-start | bytes 327680 | tf_op jit(solution)/shard_map/all_to_all | solution.py:26
  194.6 5.2 %multiply_add_fusion = f32[16,64,1152]{2,1,0:T(8,128)} fusion(f32[16,64,1152]{2,1,0:T(8,128)} %param.18, f32[64,1152]{1,0:T(8,128)S(1)} %mul.299, f32[1152]{0:T(1024)S(1)} %mul.296, f32[16,1152]{1,0:T(8,128)S(1)} %mul.288), kind=kLoop, calls=%fused_computation | loop fusion | flops 3538944 | bytes 9810432 | tf_op jit(solution)/shard_map/add | solution.py:166
  199.7 4.5 %all-to-all-done.8 = f32[16,4,576]{2,1,0:T(4,128)S(1)} async-done(((f32[16,4,576]{2,1,0:T(4,128)}), f32[16,4,576]{2,1,0:T(4,128)S(1)}, u32[]{:S(2)}, u32[]{:S(2)}) %all-to-all-start.8) | async-done | bytes 147488 | tf_op jit(solution)/shard_map/all_to_all | solution.py:26
  204.8 0.7 reshape.250
  205.5 0.6 fusion.53
  (117 shorter events, 4.8 us)
Async XLA Ops:
  7.2 13.3 %copy-start.1 = (bf16[2048,64]{0,1:T(8,128)(2,1)S(1)}, bf16[2048,64]{0,1:T(8,128)(2,1)}, u32[]{:S(2)}) copy-start(bf16[2048,64]{0,1:T(8,128)(2,1)} %param.23) | copy-start | bytes 786436
  7.2 13.7 %copy-start.5 = (bf16[2048]{0:T(1024)(128)(2,1)S(1)}, bf16[2048]{0:T(1024)(128)(2,1)}, u32[]{:S(2)}) copy-start(bf16[2048]{0:T(1024)(128)(2,1)} %param.19) | copy-start | bytes 12292
  8.2 6.4 %collective-permute-start = (bf16[72,64]{1,0:T(8,128)(2,1)S(1)}, bf16[72,64]{1,0:T(8,128)(2,1)S(1)}, u32[]{:S(2)}, u32[]{:S(2)}) collective-permute-start(bf16[72,64]{1,0:T(8,128)(2,1)S(1)} %copy.160), channel_id=1, source_target_pairs={{0,8},{8,0},{1,9},{9,1},{2,10},{10,2},{3,11},{11,3},{4,12},{12,4},... | collective-permute-start | bytes 27656 | tf_op jit(solution)/shard_map/ppermute | solution.py:22
  15.4 13.1 %all-to-all-start = ((bf16[16,72,128]{2,1,0:T(8,128)(2,1)}), bf16[16,72,128]{2,1,0:T(8,128)(2,1)S(1)}, u32[]{:S(2)}, u32[]{:S(2)}) async-start(bf16[16,72,128]{2,1,0:T(8,128)(2,1)} %broadcast_in_dim.18), calls=%async_computation | async-start | bytes 589824 | tf_op jit(solution)/shard_map/all_to_all | solution.py:26
  20.5 9.0 %collective-permute-start.1 = (bf16[2048,256]{0,1:T(8,128)(2,1)S(1)}, bf16[2048,256]{0,1:T(8,128)(2,1)S(1)}, u32[]{:S(2)}, u32[]{:S(2)}) collective-permute-start(bf16[2048,256]{0,1:T(8,128)(2,1)S(1)} %constant_dynamic-update-slice_fusion), channel_id=1, source_target_pairs={{0,8},{8,0},{1,9},{9,1},{2,10},{10,2},{3,11},{11,3},{4,12},{12,4},... | collective-permute-start | bytes 3145736 | tf_op jit(solution)/shard_map/ppermute | solution.py:22
  29.1 11.9 %copy-start = (bf16[64,2048]{1,0:T(8,128)(2,1)S(1)}, bf16[64,2048]{1,0:T(8,128)(2,1)}, u32[]{:S(2)}) copy-start(bf16[64,2048]{1,0:T(8,128)(2,1)} %param.29) | copy-start | bytes 786436
  29.1 12.1 %copy-start.12 = (f32[16]{0:T(128)S(1)}, f32[16]{0:T(128)}, u32[]{:S(2)}) copy-start(f32[16]{0:T(128)} %param.26) | copy-start | bytes 196
  29.1 13.3 %copy-start.13 = (f32[16]{0:T(128)S(1)}, f32[16]{0:T(128)}, u32[]{:S(2)}) copy-start(f32[16]{0:T(128)} %param.27) | copy-start | bytes 196
  30.8 19.4 %all-to-all-start.1 = ((bf16[16,2,16,72]{3,2,1,0:T(8,128)(2,1)}), bf16[16,2,16,72]{3,2,1,0:T(8,128)(2,1)S(1)}, u32[]{:S(2)}, u32[]{:S(2)}) async-start(bf16[16,2,16,72]{3,2,1,0:T(8,128)(2,1)} %bitcast.14), calls=%async_computation.1 | async-start | bytes 262144 | tf_op jit(solution)/shard_map/all_to_all | solution.py:26
  40.9 35.5 %collective-permute-start.2 = (bf16[64,2048]{1,0:T(8,128)(2,1)S(1)}, bf16[64,2048]{1,0:T(8,128)(2,1)S(1)}, u32[]{:S(2)}, u32[]{:S(2)}) collective-permute-start(bf16[64,2048]{1,0:T(8,128)(2,1)S(1)} %copy-done), channel_id=1, source_target_pairs={{0,8},{8,0},{1,9},{9,1},{2,10},{10,2},{3,11},{11,3},{4,12},{12,4},... | collective-permute-start | bytes 786440 | tf_op jit(solution)/shard_map/ppermute | solution.py:22
  53.5 5.5 %copy-start.10 = (bf16[2048,16]{0,1:T(8,128)(2,1)S(1)}, bf16[2048,16]{0,1:T(8,128)(2,1)}, u32[]{:S(2)}) copy-start(bf16[2048,16]{0,1:T(8,128)(2,1)} %param.25) | copy-start | bytes 196612
  53.5 5.5 %copy-start.11 = (bf16[2048,16]{0,1:T(8,128)(2,1)S(1)}, bf16[2048,16]{0,1:T(8,128)(2,1)}, u32[]{:S(2)}) copy-start(bf16[2048,16]{0,1:T(8,128)(2,1)} %param.24) | copy-start | bytes 196612
  54.6 21.5 %copy-start.6 = (f32[128]{0:T(128)S(1)}, f32[128]{0:T(128)}, u32[]{:S(2)}) copy-start(f32[128]{0:T(128)} %param.28) | copy-start | bytes 1540
  55.5 20.3 %all-to-all-start.2 = ((bf16[16,2,64,72]{3,2,1,0:T(8,128)(2,1)}), bf16[16,2,64,72]{3,2,1,0:T(8,128)(2,1)S(1)}, u32[]{:S(2)}, u32[]{:S(2)}) async-start(bf16[16,2,64,72]{3,2,1,0:T(8,128)(2,1)} %copy.134), calls=%async_computation.2 | async-start | bytes 1048576 | tf_op jit(solution)/shard_map/all_to_all | solution.py:26
  76.2 5.0 %copy-start.7 = (bf16[64]{0:T(256)(128)(2,1)S(1)}, bf16[64]{0:T(256)(128)(2,1)}, u32[]{:S(2)}) copy-start(bf16[64]{0:T(256)(128)(2,1)} %param.30) | copy-start | bytes 388
  76.4 41.6 %copy-start.4 = (s32[1152]{0:T(1024)S(1)}, s32[1152]{0:T(1024)}, u32[]{:S(2)}) copy-start(s32[1152]{0:T(1024)} %param.32) | copy-start | bytes 13828
  77.6 15.6 %all-to-all-start.4 = ((f32[16,72,128]{2,1,0:T(8,128)}), f32[16,72,128]{2,1,0:T(8,128)S(1)}, u32[]{:S(2)}, u32[]{:S(2)}) async-start(f32[16,72,128]{2,1,0:T(8,128)} %bitcast.148), calls=%async_computation.4 | async-start | bytes 1179648 | tf_op jit(solution)/shard_map/all_to_all | solution.py:26
  81.2 1.2 collective-permute-start.3
  94.1 9.8 %all-to-all-start.5 = ((f32[16,1,72]{2,1,0:T(1,128)}), f32[16,1,72]{2,1,0:T(1,128)S(1)}, u32[]{:S(2)}, u32[]{:S(2)}) async-start(f32[16,1,72]{2,1,0:T(1,128)} %broadcast_in_dim.22), calls=%async_computation.5 | async-start | bytes 16384 | tf_op jit(solution)/shard_map/all_to_all | solution.py:26
  97.5 65.4 %all-gather.2.cloned.1.call-start = ((), (), s32[]{:S(2)}) async-start(), calls=%async_computation.9 | async-start | bytes 2506752 | tf_op jit(solution)/shard_map/all_gather | solution.py:159
  115.2 7.7 %collective-permute-start.4 = (bf16[2048,640]{1,0:T(8,128)(2,1)}, bf16[2048,640]{1,0:T(8,128)(2,1)}, u32[]{:S(2)}, u32[]{:S(2)}) collective-permute-start(bf16[2048,640]{1,0:T(8,128)(2,1)} %param.31), channel_id=1, source_target_pairs={{0,8},{8,0},{1,9},{9,1},{2,10},{10,2},{3,11},{11,3},{4,12},{12,4},... | collective-permute-start | bytes 7864328 | tf_op jit(solution)/shard_map/ppermute | solution.py:22
  119.1 52.3 %all-to-all-start.3 = ((f32[16,65,72]{2,1,0:T(8,128)}), f32[16,65,72]{2,1,0:T(8,128)S(1)}, u32[]{:S(2)}, u32[]{:S(2)}) async-start(f32[16,65,72]{2,1,0:T(8,128)} %bitcast.20), calls=%async_computation.3 | async-start | bytes 1179648 | tf_op jit(solution)/shard_map/all_to_all | solution.py:26
  122.8 44.8 %copy-start.8 = (bf16[2048,640]{1,0:T(8,128)(2,1)S(1)}, bf16[2048,640]{1,0:T(8,128)(2,1)}, u32[]{:S(2)}) copy-start(bf16[2048,640]{1,0:T(8,128)(2,1)} %param.31) | copy-start | bytes 7864324
  162.9 4.7 %copy-start.9 = (bf16[576,2048]{1,0:T(8,128)(2,1)S(1)}, bf16[576,2048]{1,0:T(8,128)(2,1)}, u32[]{:S(2)}) copy-start(bf16[576,2048]{1,0:T(8,128)(2,1)} %all-gather.2.cloned.1.call-done) | copy-start | bytes 7077892
  172.2 11.6 %all-to-all-start.7 = ((f32[16,4,576]{2,1,0:T(4,128)}), f32[16,4,576]{2,1,0:T(4,128)S(1)}, u32[]{:S(2)}, u32[]{:S(2)}) async-start(f32[16,4,576]{2,1,0:T(4,128)} %broadcast_in_dim.24), calls=%async_computation.7 | async-start | bytes 327680 | tf_op jit(solution)/shard_map/all_to_all | solution.py:26
  184.7 19.5 %all-to-all-start.8 = ((f32[16,4,576]{2,1,0:T(4,128)}), f32[16,4,576]{2,1,0:T(4,128)S(1)}, u32[]{:S(2)}, u32[]{:S(2)}) async-start(f32[16,4,576]{2,1,0:T(4,128)} %broadcast_in_dim.26), calls=%async_computation.8 | async-start | bytes 327680 | tf_op jit(solution)/shard_map/all_to_all | solution.py:26
  194.6 10.9 %copy-start.3 = (f32[1152]{0:T(1024)S(1)}, f32[1152]{0:T(1024)}, u32[]{:S(2)}) copy-start(f32[1152]{0:T(1024)} %param.33) | copy-start | bytes 13828
  204.7 1.4 copy-start.2
Sparse Core Ops, SparseCore 0:
  115.3 47.5 all-gather.1

commit v2 on v1

v2 whole, which is shorter than its diff:
```python
import jax
import jax.numpy as jnp
from jax import lax
from jax.sharding import Mesh
from jax.sharding import PartitionSpec as P

D = 2048
HEADS = 16
DK = 128
DV = 128
X = "row_0"
Y = "row_1"
CORE = "row_2"
Z = "col"
XY = (X, Y)
ZC = (Z, CORE)
ROW = (X, Y, CORE)
ROW_COL = (X, Y, CORE, Z)


def swapped(array):
    return lax.ppermute(array, CORE, [(0, 1), (1, 0)])


def exchange(blocks, axes):
    return lax.all_to_all(blocks, axes, split_axis=0, concat_axis=0, tiled=True)


def to_all(array, axes):
    return exchange(jnp.broadcast_to(array, (lax.axis_size(axes), *array.shape)), axes)


def in_core_order(core, own, other, dim):
    first = jnp.where(core == 0, own, other)
    second = jnp.where(core == 0, other, own)
    return jnp.concatenate([first, second], axis=dim)


def merged(stats, dim):
    top_n, total_n, weighted_n, picked_n = stats
    top = jnp.max(top_n, axis=dim, keepdims=True)
    scale = jnp.exp(top_n - top)
    return (
        jnp.squeeze(top, dim),
        jnp.sum(total_n * scale, axis=dim),
        jnp.sum(weighted_n * scale, axis=dim),
        jnp.sum(picked_n, axis=dim),
    )


def per_device(
    hidden_in,
    state,
    attn_norm_gain,
    w_query,
    w_key,
    w_value,
    w_gate,
    w_decay,
    w_beta,
    decay_log,
    decay_bias,
    head_gain,
    w_out,
    final_gain,
    lm_weight,
    token_ids,
    ref_logprob,
):
    core = lax.axis_index(CORE)
    zed = lax.axis_index(Z)
    head = lax.axis_index(XY)
    n_xy = lax.axis_size(XY)
    n_z = lax.axis_size(Z)
    key_rows, half, batch = state.shape
    rows = hidden_in.shape[0] // 2
    vocab_dev = lm_weight.shape[1]

    kept = lax.dynamic_slice_in_dim(hidden_in, core * rows, rows, 0)
    given = lax.dynamic_slice_in_dim(hidden_in, (1 - core) * rows, rows, 0)
    gain_row = final_gain[None, :]
    given = jnp.concatenate([given, gain_row])
    x_block = in_core_order(core, jnp.concatenate([kept, gain_row]), swapped(given), 1)
    pieces = to_all(x_block, XY)
    gain_full = pieces[:, rows].reshape(D).astype(jnp.float32)

    weights = (w_query, w_key, w_value, w_gate)
    w_own = jnp.concatenate(weights, axis=1)
    w_other = jnp.concatenate([swapped(w) for w in weights], axis=1)
    out_full = lax.all_gather(w_out, ROW, axis=0, tiled=True)
    lm_other = swapped(lm_weight)

    x_full = jnp.moveaxis(pieces[:, :rows], 0, 1).reshape(rows, D).astype(jnp.float32)
    normed = (
        x_full
        * lax.rsqrt(jnp.mean(x_full * x_full, axis=1, keepdims=True) + 1e-06)
        * attn_norm_gain.astype(jnp.float32)
    ).astype(jnp.bfloat16)

    def project(weight):
        return jnp.dot(normed, weight, preferred_element_type=jnp.float32)

    own = project(w_own).reshape(rows, 4, half)
    other = project(w_other).reshape(rows, 4, half)
    qkvg = in_core_order(core, own, other, 2)
    small = project(jnp.concatenate([w_decay, w_beta], axis=1))
    decay_in = lax.dynamic_slice_in_dim(small, head, 1, 1)
    beta_in = lax.dynamic_slice_in_dim(small, HEADS + head, 1, 1)
    rate = jnp.exp(lax.dynamic_slice_in_dim(decay_log, head, 1, 0))
    bias = lax.dynamic_slice_in_dim(decay_bias, head, 1, 0)
    alpha = jnp.exp(-rate * jax.nn.softplus(decay_in + bias))
    beta = jax.nn.sigmoid(beta_in)

    raw = lax.optimization_barrier(qkvg[:, :2].astype(jnp.bfloat16)).astype(jnp.float32)
    unit = (raw * lax.rsqrt(jnp.sum(raw * raw, axis=2, keepdims=True) + 1e-06)).astype(
        jnp.bfloat16
    )
    unit_f = unit.astype(jnp.float32)
    meet = jnp.sum(unit_f[:, 0] * unit_f[:, 1], axis=1, keepdims=True)

    parts = unit.reshape(rows, 2, n_z, key_rows).transpose(2, 1, 3, 0)
    landed = exchange(parts.reshape(n_z, 2 * key_rows, rows), Z)
    landed = in_core_order(core, landed, swapped(landed), 2)
    qk = jnp.moveaxis(landed, 0, 1).reshape(2, key_rows, batch).astype(jnp.float32)
    query_k, key_k = qk[0], qk[1]

    recall_p = jnp.sum(state * key_k[:, None, :], axis=0)
    answer_p = jnp.sum(state * query_k[:, None, :], axis=0)
    both = jnp.concatenate([recall_p, answer_p]).T.astype(jnp.bfloat16)
    both = exchange(both.reshape(n_z, 2 * rows, 2 * half), Z)
    both = jnp.sum(both.astype(jnp.float32), axis=0)
    kept = lax.dynamic_slice_in_dim(both, core * rows, rows, 0)
    given = lax.dynamic_slice_in_dim(both, (1 - core) * rows, rows, 0)
    both = in_core_order(
        core, kept.reshape(rows, 2, half), swapped(given).reshape(rows, 2, half), 2
    )
    recall, answer = both[:, 0], both[:, 1]
    value, gate = qkvg[:, 2], qkvg[:, 3]
    write = beta * (value - alpha * recall)
    readout = alpha * answer + meet * write
    power = jnp.mean(readout * readout, axis=1, keepdims=True)
    mixed = (
        readout * lax.rsqrt(power + 1e-05) * head_gain[None, :] * jax.nn.silu(gate)
    ).astype(jnp.bfloat16)

    mixed_full = jnp.moveaxis(to_all(mixed, XY), 0, 1).reshape(rows, D)
    hidden = x_full + jnp.dot(mixed_full, out_full, preferred_element_type=jnp.float32)
    energy = jnp.mean(hidden * hidden, axis=1, keepdims=True)
    final = (hidden * lax.rsqrt(energy + 1e-06) * gain_full[None, :]).astype(jnp.bfloat16)

    ids = lax.dynamic_index_in_dim(token_ids.reshape(n_z, 2, rows), core, 1, False)
    ids = lax.dynamic_slice_in_dim(jnp.concatenate([ids, ids]), zed, n_z, 0)

    def statistics(block, ids):
        found = []
        for weight, owner in ((lm_weight, core), (lm_other, 1 - core)):
            logits = jnp.dot(block, weight, preferred_element_type=jnp.float32)
            start = ((head * 2 + owner) * n_z + zed) * vocab_dev
            hits = jnp.arange(vocab_dev, dtype=jnp.int32)[None, :] + start == ids[:, None]
            picked = jnp.sum(jnp.where(hits, logits, jnp.zeros_like(logits)), axis=1)
            top = jnp.max(logits, axis=1)
            expo = jnp.exp(logits - top[:, None])
            found.append((top, jnp.sum(expo, axis=1), jnp.sum(expo * logits, axis=1), picked))
        return jnp.stack(merged([jnp.stack(s) for s in zip(*found)], 0))

    def along_z(block, step):
        return lax.ppermute(block, Z, [(k, (k + step) % n_z) for k in range(n_z)])

    by_distance = [None] * n_z
    by_distance[0] = statistics(final, ids[0])
    up = down = final
    cut = rows // 2
    for step in range(1, n_z // 2):
        up, down = along_z(up, 1), along_z(down, -1)
        two = statistics(
            jnp.concatenate([up, down]), jnp.concatenate([ids[n_z - step], ids[step]])
        )
        by_distance[n_z - step], by_distance[step] = two[:, :rows], two[:, rows:]
    up, down = along_z(up[:cut], 1), along_z(down[cut:], -1)
    by_distance[n_z // 2] = statistics(jnp.concatenate([up, down]), ids[n_z // 2])
    stats = jnp.stack(by_distance)
    stats = lax.dynamic_slice_in_dim(jnp.concatenate([stats, stats]), n_z - zed, n_z, 0)
    stats = jnp.moveaxis(stats, 1, 0).reshape(4, n_z * rows)

    sent = jnp.concatenate(
        [write.reshape(rows, 2, half), jnp.broadcast_to(alpha[:, :, None], (rows, 2, 1))],
        axis=2,
    )
    kept = lax.dynamic_index_in_dim(sent, core, 1, False)
    given = lax.dynamic_index_in_dim(sent, 1 - core, 1, False)
    back = to_all(in_core_order(core, kept, swapped(given), 0), Z).reshape(batch, half + 1).T
    new_state = back[half] * state + key_k[:, None, :] * back[None, :half]

    stats = jnp.stack(merged(jnp.moveaxis(to_all(stats, Z), 1, 0), 0))
    top, total, weighted, picked = merged(jnp.moveaxis(to_all(stats, XY), 1, 0), 0)
    lse = top + jnp.log(total)
    mine = jnp.stack([picked - lse, lse - weighted / total])
    logprob, entropy = in_core_order(core, mine[:, None], swapped(mine)[:, None], 1)

    def in_order(two):
        return jnp.moveaxis(two.reshape(2, n_z, rows), 0, 1).reshape(batch)

    logprob = in_order(logprob)
    entropy = in_order(entropy)
    gap = jnp.clip(ref_logprob - logprob, -20.0, 20.0)
    kl = jnp.minimum(jnp.exp(gap) - gap - 1.0, 10.0)
    return (new_state, logprob, entropy, kl)


def solution(mesh):
    split = Mesh(mesh.devices.reshape(4, 4, 2, mesh.shape["col"]), (X, Y, CORE, Z))
    in_specs = (
        P(Z, ROW),
        P(Z, ROW, None),
        P(),
        P(None, ROW),
        P(None, ROW),
        P(None, ROW),
        P(None, ROW),
        P(),
        P(),
        P(),
        P(),
        P(),
        P(ROW, None),
        P(ROW),
        P(None, ROW_COL),
        P(),
        P(),
    )
    out_specs = (P(Z, ROW, None), P(), P(), P())
    return jax.shard_map(
        per_device, mesh=split, in_specs=in_specs, out_specs=out_specs, check_vma=False
    )
```

time: 214 us -> 208 us (0.972)
  waiting for transfers between devices: 99.4 us -> 61.5 us
  matrix products: 8.47 us -> 26 us
  starting transfers between devices: 50.8 us -> 63.3 us
  blocking collectives: 11.2 us -> 0 us
  other arithmetic: 12.8 us -> 23.2 us
    all_gather x1, waiting for transfers between devices: 40 us -> 0.01 us  [per_device(): out_full = lax.all_gather(w_out, ROW, axis=0, tiled=True)]
    dot_general x7 -> x14, matrix products: 8.47 us -> 26 us  [the longest x10 15.8 us: statistics(): logits = jnp.dot(block, weight, preferred_element_type=jnp.float32)]
    ppermute x0 -> x8, starting transfers between devices: none -> 11.3 us  [along_z(): return lax.ppermute(block, Z, [(k, (k + step) % n_z) for k in range(n_z)])]
    all_to_all x1 -> x0, blocking collectives: 11.2 us -> none  [exchange(): return lax.all_to_all(blocks, axes, split_axis=0, concat_axis=0, tiled=True)]
    ppermute x5 -> x10, starting transfers between devices: 6.84 us -> 17.6 us  [swapped(): return lax.ppermute(array, CORE, [(0, 1), (1, 0)])]
    all_to_all x8 -> x7, starting transfers between devices: 44 us -> 34.3 us  [exchange(): return lax.all_to_all(blocks, axes, split_axis=0, concat_axis=0, tiled=True)]
    concatenate x1 -> x6, other arithmetic: 0.01 us -> 5.74 us  [the longest x1 2.27 us: per_device(): w_own = jnp.concatenate(weights, axis=1)]
    ppermute x0 -> x8, waiting for transfers between devices: none -> 5.33 us  [along_z(): return lax.ppermute(block, Z, [(k, (k + step) % n_z) for k in range(n_z)])]
  transfers between devices with their start and end apart: 14 -> 26, of which waited for: 10 -> 10; matrix products, arithmetic and copies ran while one was open for 13% -> 30% of each run, Pallas kernels for 0% -> 0%
where the time goes in v2:
time: 208 us; the launch traced here: 206 us
  starting transfers between devices  63.3 us (30%)
  waiting for transfers between devices  61.5 us (30%)
  matrix products  26 us (12%)
  other arithmetic  23.2 us (11%)
  local copies, waits for them, and re-layouts  16.4 us (8%)
  between operations  15.8 us (8%)
    all_to_all x7, waiting for transfers between devices, exchange(): return lax.all_to_all(blocks, axes, split_axis=0, concat_axis=0, tiled=True)  55.5 us
    all_to_all x7, starting transfers between devices, exchange(): return lax.all_to_all(blocks, axes, split_axis=0, concat_axis=0, tiled=True)  34.3 us
    ppermute x10, starting transfers between devices, swapped(): return lax.ppermute(array, CORE, [(0, 1), (1, 0)])  17.6 us
    dot_general x10, matrix products, statistics(): logits = jnp.dot(block, weight, preferred_element_type=jnp.float32)  15.8 us
    ppermute x8, starting transfers between devices, along_z(): return lax.ppermute(block, Z, [(k, (k + step) % n_z) for k in range(n_z)])  11.3 us
    ppermute x8, waiting for transfers between devices, along_z(): return lax.ppermute(block, Z, [(k, (k + step) % n_z) for k in range(n_z)])  5.33 us
    add x1, other arithmetic, per_device(): new_state = back[half] * state + key_k[:, None, :] * back[None, :half]  5.16 us
    dot_general x3, matrix products, project(): return jnp.dot(normed, weight, preferred_element_type=jnp.float32)  5.11 us
  transfers between devices with their start and end apart: 26, of which 10 were waited for; matrix products, arithmetic and copies ran while one was open for 30% of the time, Pallas kernels for 0%

profile of v2, /device:TPU:1, one launch (start us, length us, event | category | flops | bytes accessed | tf_op | source)
XLA Modules:
  0.0 206.0 jit_solution(3890587223689940912)
XLA Ops:
  7.9 0.8 copy.114
  8.7 0.9 constant_dynamic-slice_fusion.5
  9.7 3.3 %collective-permute-start = (bf16[73,64]{0,1:T(8,128)(2,1)S(1)}, bf16[73,64]{0,1:T(8,128)(2,1)S(1)}, u32[]{:S(2)}, u32[]{:S(2)}) collective-permute-start(bf16[73,64]{0,1:T(8,128)(2,1)S(1)} %pad_maximum_fusion.10), channel_id=1, source_target_pairs={{0,8},{8,0},{1,9},{9,1},{2,10},{10,2},{3,11},{11,3},{4,12},{12,4},... | collective-permute-start | bytes 28040 | tf_op jit(solution)/shard_map/ppermute | solution.py:22
  16.2 2.3 %pad_maximum_fusion = bf16[2048,256]{0,1:T(8,128)(2,1)} fusion(bf16[2048,64]{0,1:T(8,128)(2,1)} %param.23, bf16[2048,64]{0,1:T(8,128)(2,1)} %param.22, bf16[2048,64]{0,1:T(8,128)(2,1)} %param.21, bf16[2048,64]{0,1:T(8,128)(2,1)} %param.20), kind=kLoop, calls=%fused_computation.4 | loop fusion | flops 4194304 | bytes 2097152 | tf_op jit(solution)/shard_map/concatenate | solution.py:88
  19.6 5.0 %all-to-all-start = ((bf16[16,73,128]{2,1,0:T(8,128)(2,1)}), bf16[16,73,128]{2,1,0:T(8,128)(2,1)S(1)}, u32[]{:S(2)}, u32[]{:S(2)}) async-start(bf16[16,73,128]{2,1,0:T(8,128)(2,1)} %broadcast_in_dim.17), calls=%async_computation | async-start | bytes 655360 | tf_op jit(solution)/shard_map/all_to_all | solution.py:26
  24.7 2.1 %pad_maximum_fusion.1 = bf16[2048,256]{0,1:T(8,128)(2,1)} fusion(bf16[2048,64]{0,1:T(8,128)(2,1)} %collective-permute-done.4, bf16[2048,64]{0,1:T(8,128)(2,1)} %collective-permute-done.3, bf16[2048,64]{0,1:T(8,128)(2,1)S(1)} %collective-permute-done.2, bf16[2048,64]{0,1:T(8,128)(2,1)S(1)} %collective-permute-done.1), kind=kLoop, calls=%fused_computation.5 | loop fusion | flops 4194304 | bytes 2097152 | tf_op jit(solution)/shard_map/concatenate | solution.py:89
  26.8 5.8 %all-to-all-done = bf16[16,73,128]{2,1,0:T(8,128)(2,1)S(1)} async-done(((bf16[16,73,128]{2,1,0:T(8,128)(2,1)}), bf16[16,73,128]{2,1,0:T(8,128)(2,1)S(1)}, u32[]{:S(2)}, u32[]{:S(2)}) %all-to-all-start) | async-done | bytes 299040 | tf_op jit(solution)/shard_map/all_to_all | solution.py:26
  33.8 1.7 fusion.102
  35.4 1.7 broadcast_select_fusion.2
  38.5 9.8 %all-to-all-start.1 = ((bf16[8,32,72]{2,1,0:T(8,128)(2,1)}), bf16[8,32,72]{2,1,0:T(8,128)(2,1)S(1)}, u32[]{:S(2)}, u32[]{:S(2)}) async-start(bf16[8,32,72]{2,1,0:T(8,128)(2,1)} %bitcast.15), calls=%async_computation.1 | async-start | bytes 131072 | tf_op jit(solution)/shard_map/all_to_all | solution.py:26
  49.0 6.6 %all-to-all-done.1 = bf16[8,32,72]{2,1,0:T(8,128)(2,1)S(1)} async-done(((bf16[8,32,72]{2,1,0:T(8,128)(2,1)}), bf16[8,32,72]{2,1,0:T(8,128)(2,1)S(1)}, u32[]{:S(2)}, u32[]{:S(2)}) %all-to-all-start.1) | async-done | bytes 36896 | tf_op jit(solution)/shard_map/all_to_all | solution.py:26
  55.5 3.6 %collective-permute-start.5 = (bf16[8,32,72]{2,1,0:T(8,128)(2,1)S(1)}, bf16[8,32,72]{2,1,0:T(8,128)(2,1)S(1)}, u32[]{:S(2)}, u32[]{:S(2)}) collective-permute-start(bf16[8,32,72]{2,1,0:T(8,128)(2,1)S(1)} %all-to-all-done.1), channel_id=1, source_target_pairs={{0,8},{8,0},{1,9},{9,1},{2,10},{10,2},{3,11},{11,3},{4,12},{12,4},... | collective-permute-start | bytes 110600 | tf_op jit(solution)/shard_map/ppermute | solution.py:22
  59.7 1.2 dynamic_slice.44
  61.7 1.3 dynamic_slice.46
  63.9 1.0 copy.121
  65.1 3.2 %multiply_reduce_fusion.1 = (bf16[64,1152]{1,0:T(8,128)(2,1)S(1)}, bf16[64,1152]{1,0:T(8,128)(2,1)S(1)}) fusion(f32[16,64,1152]{2,1,0:T(8,128)} %param.18, f32[16,1152]{1,0:T(8,128)S(1)} %mul.341, f32[16,1152]{1,0:T(8,128)S(1)} %mul.344), kind=kLoop, calls=%fused_computation.2 | loop fusion | flops 4571136 | bytes 5160960 | tf_op jit(solution)/shard_map/reduce_sum | solution.py:127
  68.3 0.9 copy.122
  69.2 3.4 %all-to-all-start.2 = ((bf16[8,144,128]{2,1,0:T(8,128)(2,1)}), bf16[8,144,128]{2,1,0:T(8,128)(2,1)S(1)}, u32[]{:S(2)}, u32[]{:S(2)}) async-start(bf16[8,144,128]{2,1,0:T(8,128)(2,1)} %bitcast.282), calls=%async_computation.2 | async-start | bytes 589824 | tf_op jit(solution)/shard_map/all_to_all | solution.py:26
  72.6 0.9 fusion.34
  73.6 1.8 fusion.11
  75.4 10.3 %all-to-all-done.2 = bf16[8,144,128]{2,1,0:T(8,128)(2,1)S(1)} async-done(((bf16[8,144,128]{2,1,0:T(8,128)(2,1)}), bf16[8,144,128]{2,1,0:T(8,128)(2,1)S(1)}, u32[]{:S(2)}, u32[]{:S(2)}) %all-to-all-start.2) | async-done | bytes 294944 | tf_op jit(solution)/shard_map/all_to_all | solution.py:26
  86.2 1.3 exponential_bitcast_fusion
  89.5 3.7 %all-to-all-start.4 = ((bf16[16,72,128]{2,1,0:T(8,128)(2,1)}), bf16[16,72,128]{2,1,0:T(8,128)(2,1)S(1)}, u32[]{:S(2)}, u32[]{:S(2)}) async-start(bf16[16,72,128]{2,1,0:T(8,128)(2,1)} %broadcast_in_dim.20), calls=%async_computation.4 | async-start | bytes 589824 | tf_op jit(solution)/shard_map/all_to_all | solution.py:26
  93.2 0.9 subtract_multiply_fusion
  94.5 6.7 %all-to-all-done.4 = bf16[16,72,128]{2,1,0:T(8,128)(2,1)S(1)} async-done(((bf16[16,72,128]{2,1,0:T(8,128)(2,1)}), bf16[16,72,128]{2,1,0:T(8,128)(2,1)S(1)}, u32[]{:S(2)}, u32[]{:S(2)}) %all-to-all-start.4) | async-done | bytes 294944 | tf_op jit(solution)/shard_map/all_to_all | solution.py:26
  101.2 5.1 %multiply_reduce_fusion.2 = (f32[72]{0:T(128)S(1)}, f32[72,2048]{1,0:T(8,128)S(1)}) fusion(bf16[2048,2048]{1,0:T(8,128)(2,1)} %all-gather.2.cloned.1.call-done, bf16[16,73,128]{2,1,0:T(8,128)(2,1)S(1)} %all-to-all-done, bf16[16,72,128]{2,1,0:T(8,128)(2,1)S(1)} %all-to-all-done.4), kind=kOutput, calls=%fused_computation.16 | convolution fusion | flops 604569536 | bytes 9568544 | tf_op jit(solution)/shard_map/dot_general | solution.py:147
  106.9 2.3 %collective-permute-start.10 = (bf16[72,2048]{1,0:T(8,128)(2,1)S(1)}, bf16[72,2048]{1,0:T(8,128)(2,1)S(1)}, u32[]{:S(2)}, u32[]{:S(2)}) collective-permute-start(bf16[72,2048]{1,0:T(8,128)(2,1)S(1)} %multiply_convert_fusion), channel_id=1, source_target_pairs={{0,7},{1,0},{2,1},{3,2},{4,3},{5,4},{6,5},{7,6},{8,15},{9,8},{10,9... | collective-permute-start | bytes 884744 | tf_op jit(solution)/shard_map/ppermute | solution.py:167
  109.9 2.4 %fusion.94 = (f32[72]{0:T(128)S(1)}, f32[72,640]{1,0:T(8,128)S(1)}) fusion(bf16[72,2048]{1,0:T(8,128)(2,1)S(1)} %multiply_convert_fusion, bf16[2048,640]{1,0:T(8,128)(2,1)} %collective-permute-done.8), kind=kOutput, calls=%fused_computation.270 | convolution fusion | flops 188789696 | bytes 3100960 | tf_op jit(solution)/shard_map/dot_general | solution.py:157
  112.3 2.2 %collective-permute-done.9 = bf16[72,2048]{1,0:T(8,128)(2,1)S(1)} collective-permute-done((bf16[72,2048]{1,0:T(8,128)(2,1)S(1)}, bf16[72,2048]{1,0:T(8,128)(2,1)S(1)}, u32[]{:S(2)}, u32[]{:S(2)}) %collective-permute-start.9) | collective-permute-done | bytes 294944 | tf_op jit(solution)/shard_map/ppermute | solution.py:167
  115.4 2.7 %collective-permute-start.12 = (bf16[72,2048]{1,0:T(8,128)(2,1)S(1)}, bf16[72,2048]{1,0:T(8,128)(2,1)S(1)}, u32[]{:S(2)}, u32[]{:S(2)}) collective-permute-start(bf16[72,2048]{1,0:T(8,128)(2,1)S(1)} %collective-permute-done.10), channel_id=1, source_target_pairs={{0,7},{1,0},{2,1},{3,2},{4,3},{5,4},{6,5},{7,6},{8,15},{9,8},{10,9... | collective-permute-start | bytes 884744 | tf_op jit(solution)/shard_map/ppermute | solution.py:167
  118.0 2.5 %fusion.99 = (f32[144]{0:T(256)S(1)}, f32[144,640]{1,0:T(8,128)S(1)}) fusion(bf16[144,2048]{1,0:T(8,128)(2,1)S(1)} %constant_dynamic-update-slice_fusion, bf16[2048,640]{1,0:T(8,128)(2,1)} %collective-permute-done.8), kind=kOutput, calls=%fused_computation.275 | convolution fusion | flops 377579392 | bytes 3580480 | tf_op jit(solution)/shard_map/dot_general | solution.py:157
  120.5 1.6 collective-permute-done.11
  123.0 2.7 %collective-permute-start.14 = (bf16[72,2048]{1,0:T(8,128)(2,1)S(1)}, bf16[72,2048]{1,0:T(8,128)(2,1)S(1)}, u32[]{:S(2)}, u32[]{:S(2)}) collective-permute-start(bf16[72,2048]{1,0:T(8,128)(2,1)S(1)} %collective-permute-done.12), channel_id=1, source_target_pairs={{0,7},{1,0},{2,1},{3,2},{4,3},{5,4},{6,5},{7,6},{8,15},{9,8},{10,9... | collective-permute-start | bytes 884744 | tf_op jit(solution)/shard_map/ppermute | solution.py:167
  125.7 2.5 %fusion.100 = (f32[144]{0:T(256)S(1)}, f32[144,640]{1,0:T(8,128)S(1)}) fusion(bf16[144,2048]{1,0:T(8,128)(2,1)S(1)} %constant_dynamic-update-slice_fusion.2, bf16[2048,640]{1,0:T(8,128)(2,1)} %collective-permute-done.8), kind=kOutput, calls=%fused_computation.276 | convolution fusion | flops 377579392 | bytes 3580480 | tf_op jit(solution)/shard_map/dot_general | solution.py:157
  128.3 1.5 collective-permute-done.13
  130.0 2.9 %collective-permute-start.16 = (bf16[36,2048]{1,0:T(8,128)(2,1)S(1)}, bf16[36,2048]{1,0:T(8,128)(2,1)S(1)}, u32[]{:S(2)}, u32[]{:S(2)}) collective-permute-start(bf16[36,2048]{1,0:T(8,128)(2,1)S(1)} %slice.137), channel_id=1, source_target_pairs={{0,7},{1,0},{2,1},{3,2},{4,3},{5,4},{6,5},{7,6},{8,15},{9,8},{10,9... | collective-permute-start | bytes 442376 | tf_op jit(solution)/shard_map/ppermute | solution.py:167
  133.8 2.5 %fusion.101 = (f32[144]{0:T(256)S(1)}, f32[144,640]{1,0:T(8,128)S(1)}) fusion(bf16[144,2048]{1,0:T(8,128)(2,1)S(1)} %constant_dynamic-update-slice_fusion.4, bf16[2048,640]{1,0:T(8,128)(2,1)} %collective-permute-done.8), kind=kOutput, calls=%fused_computation.277 | convolution fusion | flops 377579392 | bytes 3580480 | tf_op jit(solution)/shard_map/dot_general | solution.py:157
  136.3 1.1 fusion.6
  137.7 2.4 %fusion.95 = (f32[72]{0:T(128)S(1)}, f32[72,640]{1,0:T(8,128)S(1)}) fusion(bf16[2048,640]{1,0:T(8,128)(2,1)} %collective-permute-done.8, bf16[36,2048]{1,0:T(8,128)(2,1)S(1)} %collective-permute-done.16, bf16[36,2048]{1,0:T(8,128)(2,1)S(1)} %collective-permute-done.15), kind=kOutput, calls=%fused_computation.271 | convolution fusion | flops 189379520 | bytes 3100960 | tf_op jit(solution)/shard_map/dot_general | solution.py:157
  142.6 3.4 %all-to-all-start.5 = ((f32[8,4,576]{2,1,0:T(4,128)}), f32[8,4,576]{2,1,0:T(4,128)S(1)}, u32[]{:S(2)}, u32[]{:S(2)}) async-start(f32[8,4,576]{2,1,0:T(4,128)} %broadcast_in_dim.21), calls=%async_computation.5 | async-start | bytes 163840 | tf_op jit(solution)/shard_map/all_to_all | solution.py:26
  146.1 7.2 %all-to-all-done.5 = f32[8,4,576]{2,1,0:T(4,128)S(1)} async-done(((f32[8,4,576]{2,1,0:T(4,128)}), f32[8,4,576]{2,1,0:T(4,128)S(1)}, u32[]{:S(2)}, u32[]{:S(2)}) %all-to-all-start.5) | async-done | bytes 73760 | tf_op jit(solution)/shard_map/all_to_all | solution.py:26
  153.3 0.9 broadcast_in_dim.19
  154.2 3.7 %all-to-all-start.3 = ((f32[8,144,65]{1,2,0:T(8,128)}), f32[8,144,65]{1,2,0:T(8,128)S(1)}, u32[]{:S(2)}, u32[]{:S(2)}) async-start(f32[8,144,65]{1,2,0:T(8,128)} %broadcast_in_dim.19), calls=%async_computation.3 | async-start | bytes 1179648 | tf_op jit(solution)/shard_map/all_to_all | solution.py:26
  158.1 12.7 %all-to-all-done.3 = f32[8,144,65]{1,2,0:T(8,128)S(1)} async-done(((f32[8,144,65]{1,2,0:T(8,128)}), f32[8,144,65]{1,2,0:T(8,128)S(1)}, u32[]{:S(2)}, u32[]{:S(2)}) %all-to-all-start.3) | async-done | bytes 299552 | tf_op jit(solution)/shard_map/all_to_all | solution.py:26
  171.4 5.3 %all-to-all-start.6 = ((f32[16,4,576]{2,1,0:T(4,128)}), f32[16,4,576]{2,1,0:T(4,128)S(1)}, u32[]{:S(2)}, u32[]{:S(2)}) async-start(f32[16,4,576]{2,1,0:T(4,128)} %broadcast_in_dim.23), calls=%async_computation.6 | async-start | bytes 327680 | tf_op jit(solution)/shard_map/all_to_all | solution.py:26
  177.2 6.3 %all-to-all-done.6 = f32[16,4,576]{2,1,0:T(4,128)S(1)} async-done(((f32[16,4,576]{2,1,0:T(4,128)}), f32[16,4,576]{2,1,0:T(4,128)S(1)}, u32[]{:S(2)}, u32[]{:S(2)}) %all-to-all-start.6) | async-done | bytes 147488 | tf_op jit(solution)/shard_map/all_to_all | solution.py:26
  183.8 8.6 %collective-permute-start.17 = (f32[2,576]{1,0:T(2,128)S(1)}, f32[2,576]{1,0:T(2,128)S(1)}, u32[]{:S(2)}, u32[]{:S(2)}) collective-permute-start(f32[2,576]{1,0:T(2,128)S(1)} %pad_maximum_fusion.13), channel_id=1, source_target_pairs={{0,8},{8,0},{1,9},{9,1},{2,10},{10,2},{3,11},{11,3},{4,12},{12,4},... | collective-permute-start | bytes 13832 | tf_op jit(solution)/shard_map/ppermute | solution.py:22
  192.4 5.2 %multiply_add_fusion = f32[16,64,1152]{2,1,0:T(8,128)} fusion(f32[16,64,1152]{2,1,0:T(8,128)} %param.18, f32[64,1152]{1,0:T(8,128)S(1)} %slice.129, f32[1152]{0:T(1024)S(1)} %slice_reduce_fusion.2, f32[16,1152]{1,0:T(8,128)S(1)} %copy-done.2), kind=kLoop, calls=%fused_computation | loop fusion | flops 3538944 | bytes 9810432 | tf_op jit(solution)/shard_map/add | solution.py:192
  (200 shorter events, 22.8 us)
Async XLA Ops:
  7.2 11.3 %copy-start = (bf16[2048,640]{1,0:T(8,128)(2,1)S(1)}, bf16[2048,640]{1,0:T(8,128)(2,1)}, u32[]{:S(2)}) copy-start(bf16[2048,640]{1,0:T(8,128)(2,1)} %param.31) | copy-start | bytes 7864324
  7.2 94.0 %all-gather.2.cloned.1.call-start = ((), (), s32[]{:S(2)}) async-start(), calls=%async_computation.7 | async-start | bytes 8650752 | tf_op jit(solution)/shard_map/all_gather | solution.py:90
  9.7 8.7 %collective-permute-start = (bf16[73,64]{0,1:T(8,128)(2,1)S(1)}, bf16[73,64]{0,1:T(8,128)(2,1)S(1)}, u32[]{:S(2)}, u32[]{:S(2)}) collective-permute-start(bf16[73,64]{0,1:T(8,128)(2,1)S(1)} %pad_maximum_fusion.10), channel_id=1, source_target_pairs={{0,8},{8,0},{1,9},{9,1},{2,10},{10,2},{3,11},{11,3},{4,12},{12,4},... | collective-permute-start | bytes 28040 | tf_op jit(solution)/shard_map/ppermute | solution.py:22
  13.0 11.7 %collective-permute-start.1 = (bf16[2048,64]{0,1:T(8,128)(2,1)}, bf16[2048,64]{0,1:T(8,128)(2,1)S(1)}, u32[]{:S(2)}, u32[]{:S(2)}) collective-permute-start(bf16[2048,64]{0,1:T(8,128)(2,1)} %param.20), channel_id=1, source_target_pairs={{0,8},{8,0},{1,9},{9,1},{2,10},{10,2},{3,11},{11,3},{4,12},{12,4},... | collective-permute-start | bytes 786440 | tf_op jit(solution)/shard_map/ppermute | solution.py:22
  13.1 11.6 %collective-permute-start.2 = (bf16[2048,64]{0,1:T(8,128)(2,1)}, bf16[2048,64]{0,1:T(8,128)(2,1)S(1)}, u32[]{:S(2)}, u32[]{:S(2)}) collective-permute-start(bf16[2048,64]{0,1:T(8,128)(2,1)} %param.21), channel_id=1, source_target_pairs={{0,8},{8,0},{1,9},{9,1},{2,10},{10,2},{3,11},{11,3},{4,12},{12,4},... | collective-permute-start | bytes 786440 | tf_op jit(solution)/shard_map/ppermute | solution.py:22
  13.5 11.2 %collective-permute-start.3 = (bf16[2048,64]{0,1:T(8,128)(2,1)}, bf16[2048,64]{0,1:T(8,128)(2,1)}, u32[]{:S(2)}, u32[]{:S(2)}) collective-permute-start(bf16[2048,64]{0,1:T(8,128)(2,1)} %param.22), channel_id=1, source_target_pairs={{0,8},{8,0},{1,9},{9,1},{2,10},{10,2},{3,11},{11,3},{4,12},{12,4},... | collective-permute-start | bytes 786440 | tf_op jit(solution)/shard_map/ppermute | solution.py:22
  13.6 11.1 %collective-permute-start.4 = (bf16[2048,64]{0,1:T(8,128)(2,1)}, bf16[2048,64]{0,1:T(8,128)(2,1)}, u32[]{:S(2)}, u32[]{:S(2)}) collective-permute-start(bf16[2048,64]{0,1:T(8,128)(2,1)} %param.23), channel_id=1, source_target_pairs={{0,8},{8,0},{1,9},{9,1},{2,10},{10,2},{3,11},{11,3},{4,12},{12,4},... | collective-permute-start | bytes 786440 | tf_op jit(solution)/shard_map/ppermute | solution.py:22
  18.4 91.4 %collective-permute-start.8 = (bf16[2048,640]{1,0:T(8,128)(2,1)S(1)}, bf16[2048,640]{1,0:T(8,128)(2,1)}, u32[]{:S(2)}, u32[]{:S(2)}) collective-permute-start(bf16[2048,640]{1,0:T(8,128)(2,1)S(1)} %copy-done), channel_id=1, source_target_pairs={{0,8},{8,0},{1,9},{9,1},{2,10},{10,2},{3,11},{11,3},{4,12},{12,4},... | collective-permute-start | bytes 7864328 | tf_op jit(solution)/shard_map/ppermute | solution.py:22
  19.6 13.0 %all-to-all-start = ((bf16[16,73,128]{2,1,0:T(8,128)(2,1)}), bf16[16,73,128]{2,1,0:T(8,128)(2,1)S(1)}, u32[]{:S(2)}, u32[]{:S(2)}) async-start(bf16[16,73,128]{2,1,0:T(8,128)(2,1)} %broadcast_in_dim.17), calls=%async_computation | async-start | bytes 655360 | tf_op jit(solution)/shard_map/all_to_all | solution.py:26
  32.8 0.6 copy-start.17
  33.7 14.6 %copy-start.10 = (s32[72]{0:T(128)S(1)}, s32[72]{0:T(128)}, u32[]{:S(2)}) copy-start(s32[72]{0:T(128)} %get-tuple-element.101) | copy-start | bytes 868
  33.7 14.6 %copy-start.11 = (s32[72]{0:T(128)S(1)}, s32[72]{0:T(128)}, u32[]{:S(2)}) copy-start(s32[72]{0:T(128)} %get-tuple-element.102) | copy-start | bytes 868
  33.7 14.6 %copy-start.12 = (s32[72]{0:T(128)S(1)}, s32[72]{0:T(128)}, u32[]{:S(2)}) copy-start(s32[72]{0:T(128)} %get-tuple-element.103) | copy-start | bytes 868
  33.7 14.6 %copy-start.13 = (s32[72]{0:T(128)S(1)}, s32[72]{0:T(128)}, u32[]{:S(2)}) copy-start(s32[72]{0:T(128)} %get-tuple-element.104) | copy-start | bytes 868
  33.7 25.4 %copy-start.8 = (s32[72]{0:T(128)S(1)}, s32[72]{0:T(128)}, u32[]{:S(2)}) copy-start(s32[72]{0:T(128)} %get-tuple-element.99) | copy-start | bytes 868
  33.7 25.4 %copy-start.9 = (s32[72]{0:T(128)S(1)}, s32[72]{0:T(128)}, u32[]{:S(2)}) copy-start(s32[72]{0:T(128)} %get-tuple-element.100) | copy-start | bytes 868
  38.5 17.0 %all-to-all-start.1 = ((bf16[8,32,72]{2,1,0:T(8,128)(2,1)}), bf16[8,32,72]{2,1,0:T(8,128)(2,1)S(1)}, u32[]{:S(2)}, u32[]{:S(2)}) async-start(bf16[8,32,72]{2,1,0:T(8,128)(2,1)} %bitcast.15), calls=%async_computation.1 | async-start | bytes 131072 | tf_op jit(solution)/shard_map/all_to_all | solution.py:26
  55.5 7.4 %collective-permute-start.5 = (bf16[8,32,72]{2,1,0:T(8,128)(2,1)S(1)}, bf16[8,32,72]{2,1,0:T(8,128)(2,1)S(1)}, u32[]{:S(2)}, u32[]{:S(2)}) collective-permute-start(bf16[8,32,72]{2,1,0:T(8,128)(2,1)S(1)} %all-to-all-done.1), channel_id=1, source_target_pairs={{0,8},{8,0},{1,9},{9,1},{2,10},{10,2},{3,11},{11,3},{4,12},{12,4},... | collective-permute-start | bytes 110600 | tf_op jit(solution)/shard_map/ppermute | solution.py:22
  63.9 4.3 %copy-start.1 = (f32[16,1152]{1,0:T(8,128)}, f32[16,1152]{1,0:T(8,128)S(1)}, u32[]{:S(2)}) copy-start(f32[16,1152]{1,0:T(8,128)S(1)} %mul.341) | copy-start | bytes 221188
  65.1 8.5 %copy-start.18 = (f32[72]{0:T(128)S(1)}, f32[72]{0:T(128)}, u32[]{:S(2)}) copy-start(f32[72]{0:T(128)} %copy-done.17) | copy-start | bytes 868
  68.3 20.2 %copy-start.16 = (f32[128]{0:T(128)S(1)}, f32[128]{0:T(128)}, u32[]{:S(2)}) copy-start(f32[128]{0:T(128)} %param.28) | copy-start | bytes 1540
  69.2 16.4 %all-to-all-start.2 = ((bf16[8,144,128]{2,1,0:T(8,128)(2,1)}), bf16[8,144,128]{2,1,0:T(8,128)(2,1)S(1)}, u32[]{:S(2)}, u32[]{:S(2)}) async-start(bf16[8,144,128]{2,1,0:T(8,128)(2,1)} %bitcast.282), calls=%async_computation.2 | async-start | bytes 589824 | tf_op jit(solution)/shard_map/all_to_all | solution.py:26
  85.7 1.9 collective-permute-start.6
  89.5 11.7 %all-to-all-start.4 = ((bf16[16,72,128]{2,1,0:T(8,128)(2,1)}), bf16[16,72,128]{2,1,0:T(8,128)(2,1)S(1)}, u32[]{:S(2)}, u32[]{:S(2)}) async-start(bf16[16,72,128]{2,1,0:T(8,128)(2,1)} %broadcast_in_dim.20), calls=%async_computation.4 | async-start | bytes 589824 | tf_op jit(solution)/shard_map/all_to_all | solution.py:26
  94.1 51.9 %collective-permute-start.7 = (f32[72,65]{0,1:T(8,128)S(1)}, f32[72,65]{0,1:T(8,128)S(1)}, u32[]{:S(2)}, u32[]{:S(2)}) collective-permute-start(f32[72,65]{0,1:T(8,128)S(1)} %fusion.47), channel_id=1, source_target_pairs={{0,8},{8,0},{1,9},{9,1},{2,10},{10,2},{3,11},{11,3},{4,12},{12,4},... | collective-permute-start | bytes 56168 | tf_op jit(solution)/shard_map/ppermute | solution.py:22
  106.4 8.0 %collective-permute-start.9 = (bf16[72,2048]{1,0:T(8,128)(2,1)S(1)}, bf16[72,2048]{1,0:T(8,128)(2,1)S(1)}, u32[]{:S(2)}, u32[]{:S(2)}) collective-permute-start(bf16[72,2048]{1,0:T(8,128)(2,1)S(1)} %multiply_convert_fusion), channel_id=1, source_target_pairs={{0,1},{1,2},{2,3},{3,4},{4,5},{5,6},{6,7},{7,0},{8,9},{9,10},{10,1... | collective-permute-start | bytes 884744 | tf_op jit(solution)/shard_map/ppermute | solution.py:167
  106.9 7.6 %collective-permute-start.10 = (bf16[72,2048]{1,0:T(8,128)(2,1)S(1)}, bf16[72,2048]{1,0:T(8,128)(2,1)S(1)}, u32[]{:S(2)}, u32[]{:S(2)}) collective-permute-start(bf16[72,2048]{1,0:T(8,128)(2,1)S(1)} %multiply_convert_fusion), channel_id=1, source_target_pairs={{0,7},{1,0},{2,1},{3,2},{4,3},{5,4},{6,5},{7,6},{8,15},{9,8},{10,9... | collective-permute-start | bytes 884744 | tf_op jit(solution)/shard_map/ppermute | solution.py:167
  115.3 6.9 %collective-permute-start.11 = (bf16[72,2048]{1,0:T(8,128)(2,1)S(1)}, bf16[72,2048]{1,0:T(8,128)(2,1)S(1)}, u32[]{:S(2)}, u32[]{:S(2)}) collective-permute-start(bf16[72,2048]{1,0:T(8,128)(2,1)S(1)} %collective-permute-done.9), channel_id=1, source_target_pairs={{0,1},{1,2},{2,3},{3,4},{4,5},{5,6},{6,7},{7,0},{8,9},{9,10},{10,1... | collective-permute-start | bytes 884744 | tf_op jit(solution)/shard_map/ppermute | solution.py:167
  115.4 6.8 %collective-permute-start.12 = (bf16[72,2048]{1,0:T(8,128)(2,1)S(1)}, bf16[72,2048]{1,0:T(8,128)(2,1)S(1)}, u32[]{:S(2)}, u32[]{:S(2)}) collective-permute-start(bf16[72,2048]{1,0:T(8,128)(2,1)S(1)} %collective-permute-done.10), channel_id=1, source_target_pairs={{0,7},{1,0},{2,1},{3,2},{4,3},{5,4},{6,5},{7,6},{8,15},{9,8},{10,9... | collective-permute-start | bytes 884744 | tf_op jit(solution)/shard_map/ppermute | solution.py:167
  122.9 6.9 %collective-permute-start.13 = (bf16[72,2048]{1,0:T(8,128)(2,1)S(1)}, bf16[72,2048]{1,0:T(8,128)(2,1)S(1)}, u32[]{:S(2)}, u32[]{:S(2)}) collective-permute-start(bf16[72,2048]{1,0:T(8,128)(2,1)S(1)} %collective-permute-done.11), channel_id=1, source_target_pairs={{0,1},{1,2},{2,3},{3,4},{4,5},{5,6},{6,7},{7,0},{8,9},{9,10},{10,1... | collective-permute-start | bytes 884744 | tf_op jit(solution)/shard_map/ppermute | solution.py:167
  123.0 6.9 %collective-permute-start.14 = (bf16[72,2048]{1,0:T(8,128)(2,1)S(1)}, bf16[72,2048]{1,0:T(8,128)(2,1)S(1)}, u32[]{:S(2)}, u32[]{:S(2)}) collective-permute-start(bf16[72,2048]{1,0:T(8,128)(2,1)S(1)} %collective-permute-done.12), channel_id=1, source_target_pairs={{0,7},{1,0},{2,1},{3,2},{4,3},{5,4},{6,5},{7,6},{8,15},{9,8},{10,9... | collective-permute-start | bytes 884744 | tf_op jit(solution)/shard_map/ppermute | solution.py:167
  129.8 7.8 %collective-permute-start.15 = (bf16[36,2048]{1,0:T(8,128)(2,1)S(1)}, bf16[36,2048]{1,0:T(8,128)(2,1)S(1)}, u32[]{:S(2)}, u32[]{:S(2)}) collective-permute-start(bf16[36,2048]{1,0:T(8,128)(2,1)S(1)} %slice.136), channel_id=1, source_target_pairs={{0,1},{1,2},{2,3},{3,4},{4,5},{5,6},{6,7},{7,0},{8,9},{9,10},{10,1... | collective-permute-start | bytes 442376 | tf_op jit(solution)/shard_map/ppermute | solution.py:167
  130.0 7.7 %collective-permute-start.16 = (bf16[36,2048]{1,0:T(8,128)(2,1)S(1)}, bf16[36,2048]{1,0:T(8,128)(2,1)S(1)}, u32[]{:S(2)}, u32[]{:S(2)}) collective-permute-start(bf16[36,2048]{1,0:T(8,128)(2,1)S(1)} %slice.137), channel_id=1, source_target_pairs={{0,7},{1,0},{2,1},{3,2},{4,3},{5,4},{6,5},{7,6},{8,15},{9,8},{10,9... | collective-permute-start | bytes 442376 | tf_op jit(solution)/shard_map/ppermute | solution.py:167
  133.7 2.6 %copy-start.5 = (s32[144]{0:T(256)S(1)}, s32[144]{0:T(256)}, u32[]{:S(2)}) copy-start(s32[144]{0:T(256)} %pad_add_fusion.2) | copy-start | bytes 1732
  133.7 2.6 %copy-start.6 = (s32[144]{0:T(256)S(1)}, s32[144]{0:T(256)}, u32[]{:S(2)}) copy-start(s32[144]{0:T(256)} %get-tuple-element.157) | copy-start | bytes 1732
  133.7 2.6 %copy-start.7 = (s32[144]{0:T(256)S(1)}, s32[144]{0:T(256)}, u32[]{:S(2)}) copy-start(s32[144]{0:T(256)} %get-tuple-element.158) | copy-start | bytes 1732
  137.6 3.1 %copy-start.14 = (s32[72]{0:T(128)S(1)}, s32[72]{0:T(128)}, u32[]{:S(2)}) copy-start(s32[72]{0:T(128)} %get-tuple-element.98) | copy-start | bytes 868
  137.6 3.1 %copy-start.15 = (s32[72]{0:T(128)S(1)}, s32[72]{0:T(128)}, u32[]{:S(2)}) copy-start(s32[72]{0:T(128)} %get-tuple-element.105) | copy-start | bytes 868
  142.6 10.7 %all-to-all-start.5 = ((f32[8,4,576]{2,1,0:T(4,128)}), f32[8,4,576]{2,1,0:T(4,128)S(1)}, u32[]{:S(2)}, u32[]{:S(2)}) async-start(f32[8,4,576]{2,1,0:T(4,128)} %broadcast_in_dim.21), calls=%async_computation.5 | async-start | bytes 163840 | tf_op jit(solution)/shard_map/all_to_all | solution.py:26
  154.2 38.2 %copy-start.2 = (f32[16,1152]{1,0:T(8,128)S(1)}, f32[16,1152]{1,0:T(8,128)}, u32[]{:S(2)}) copy-start(f32[16,1152]{1,0:T(8,128)} %copy-done.1) | copy-start | bytes 221188
  154.2 16.5 %all-to-all-start.3 = ((f32[8,144,65]{1,2,0:T(8,128)}), f32[8,144,65]{1,2,0:T(8,128)S(1)}, u32[]{:S(2)}, u32[]{:S(2)}) async-start(f32[8,144,65]{1,2,0:T(8,128)} %broadcast_in_dim.19), calls=%async_computation.3 | async-start | bytes 1179648 | tf_op jit(solution)/shard_map/all_to_all | solution.py:26
  171.4 12.1 %all-to-all-start.6 = ((f32[16,4,576]{2,1,0:T(4,128)}), f32[16,4,576]{2,1,0:T(4,128)S(1)}, u32[]{:S(2)}, u32[]{:S(2)}) async-start(f32[16,4,576]{2,1,0:T(4,128)} %broadcast_in_dim.23), calls=%async_computation.6 | async-start | bytes 327680 | tf_op jit(solution)/shard_map/all_to_all | solution.py:26
  183.8 14.8 %copy-start.4 = (f32[1152]{0:T(1024)S(1)}, f32[1152]{0:T(1024)}, u32[]{:S(2)}) copy-start(f32[1152]{0:T(1024)} %param.33) | copy-start | bytes 13828
  183.8 13.7 %collective-permute-start.17 = (f32[2,576]{1,0:T(2,128)S(1)}, f32[2,576]{1,0:T(2,128)S(1)}, u32[]{:S(2)}, u32[]{:S(2)}) collective-permute-start(f32[2,576]{1,0:T(2,128)S(1)} %pad_maximum_fusion.13), channel_id=1, source_target_pairs={{0,8},{8,0},{1,9},{9,1},{2,10},{10,2},{3,11},{11,3},{4,12},{12,4},... | collective-permute-start | bytes 13832 | tf_op jit(solution)/shard_map/ppermute | solution.py:22
  197.8 1.4 copy-start.3
Sparse Core Ops, SparseCore 0:
  10.6 64.3 all-gather.1

commit v3 on v2

v3 whole, which is shorter than its diff:
```python
import jax
import jax.numpy as jnp
from jax import lax
from jax.experimental import pallas as pl
from jax.experimental.pallas import tpu as pltpu
from jax.sharding import Mesh
from jax.sharding import PartitionSpec as P

D = 2048
HEADS = 16
DK = 128
DV = 128
X = "row_0"
Y = "row_1"
CORE = "row_2"
Z = "col"
XY = (X, Y)
ZC = (Z, CORE)
ROW = (X, Y, CORE)
ROW_COL = (X, Y, CORE, Z)


def swapped(array):
    return lax.ppermute(array, CORE, [(0, 1), (1, 0)])


def exchange(blocks, axes):
    return lax.all_to_all(blocks, axes, split_axis=0, concat_axis=0, tiled=True)


def to_all(array, axes):
    return exchange(jnp.broadcast_to(array, (lax.axis_size(axes), *array.shape)), axes)


def in_core_order(core, own, other, dim):
    first = jnp.where(core == 0, own, other)
    second = jnp.where(core == 0, other, own)
    return jnp.concatenate([first, second], axis=dim)


def merged(stats, dim):
    top_n, total_n, weighted_n, picked_n = stats
    top = jnp.max(top_n, axis=dim, keepdims=True)
    scale = jnp.exp(top_n - top)
    return (
        jnp.squeeze(top, dim),
        jnp.sum(total_n * scale, axis=dim),
        jnp.sum(weighted_n * scale, axis=dim),
        jnp.sum(picked_n, axis=dim),
    )


def state_sums_kernel(landed_ref, state_ref, out_ref, qk_ref):
    pieces, both, width = landed_ref.shape
    key_rows, half, lanes = state_ref.shape
    step = pl.program_id(0)

    @pl.when(step == 0)
    def _():
        for k in range(pieces):
            qk_ref[:, k * width : (k + 1) * width] = landed_ref[k].astype(jnp.float32)

    for part in range(lanes // 128):
        at = pl.ds(pl.multiple_of(step * lanes + part * 128, 128), 128)
        chunk = qk_ref[:, at]
        answer = jnp.zeros((half, 128), jnp.float32)
        recall = jnp.zeros((half, 128), jnp.float32)
        for k in range(key_rows):
            tile = state_ref[k, :, part * 128 : (part + 1) * 128]
            answer += tile * chunk[k : k + 1]
            recall += tile * chunk[key_rows + k : key_rows + k + 1]
        pair = jnp.concatenate([recall, answer], axis=0).T
        out_ref[part * 128 : (part + 1) * 128, :] = pair.astype(jnp.bfloat16)


def state_sums(landed, state):
    key_rows, half, batch = state.shape
    lanes = 384
    return pl.pallas_call(
        state_sums_kernel,
        grid=(batch // lanes,),
        in_specs=[
            pl.BlockSpec(landed.shape, lambda i: (0, 0, 0)),
            pl.BlockSpec((key_rows, half, lanes), lambda i: (0, 0, i)),
        ],
        out_specs=pl.BlockSpec((lanes, 2 * half), lambda i: (i, 0)),
        out_shape=jax.ShapeDtypeStruct((batch, 2 * half), jnp.bfloat16),
        scratch_shapes=[pltpu.VMEM((2 * key_rows, batch), jnp.float32)],
        compiler_params=pltpu.CompilerParams(vmem_limit_bytes=24 * 1024 * 1024),
        cost_estimate=pl.CostEstimate(
            flops=4 * state.size, bytes_accessed=4 * state.size, transcendentals=0
        ),
    )(landed, state)


def per_device(
    hidden_in,
    state,
    attn_norm_gain,
    w_query,
    w_key,
    w_value,
    w_gate,
    w_decay,
    w_beta,
    decay_log,
    decay_bias,
    head_gain,
    w_out,
    final_gain,
    lm_weight,
    token_ids,
    ref_logprob,
):
    core = lax.axis_index(CORE)
    zed = lax.axis_index(Z)
    head = lax.axis_index(XY)
    n_xy = lax.axis_size(XY)
    n_z = lax.axis_size(Z)
    key_rows, half, batch = state.shape
    rows = hidden_in.shape[0] // 2
    vocab_dev = lm_weight.shape[1]

    x_chip = in_core_order(core, hidden_in, swapped(hidden_in), 1)
    gain_chip = in_core_order(core, final_gain, swapped(final_gain), 0)
    x_block = lax.dynamic_slice_in_dim(x_chip, core * rows, rows, 0)
    x_block = jnp.concatenate([x_block, gain_chip[None, :]])

    weights = (w_query, w_key, w_value, w_gate)
    w_other = [swapped(w) for w in weights]
    out_full = lax.all_gather(w_out, ROW, axis=0, tiled=True)
    lm_other = swapped(lm_weight)
    x_block, *weights = lax.optimization_barrier((x_block, *weights, w_decay, w_beta))
    pieces = to_all(x_block, XY)
    w_own = jnp.concatenate(weights[:4], axis=1)
    w_small = jnp.concatenate(weights[4:], axis=1)
    w_other = jnp.concatenate(w_other, axis=1)

    gain_full = pieces[:, rows].reshape(D).astype(jnp.float32)
    x_full = jnp.moveaxis(pieces[:, :rows], 0, 1).reshape(rows, D).astype(jnp.float32)
    normed = (
        x_full
        * lax.rsqrt(jnp.mean(x_full * x_full, axis=1, keepdims=True) + 1e-06)
        * attn_norm_gain.astype(jnp.float32)
    ).astype(jnp.bfloat16)

    def project(weight):
        return lax.dot_general(
            weight, normed, (((0,), (1,)), ((), ())), preferred_element_type=jnp.float32
        )

    own = project(w_own).reshape(4, half, rows)
    other = project(w_other).reshape(4, half, rows)
    qkvg = in_core_order(core, own, other, 1)
    raw = lax.optimization_barrier(qkvg[:2].astype(jnp.bfloat16)).astype(jnp.float32)
    unit = (raw * lax.rsqrt(jnp.sum(raw * raw, axis=1, keepdims=True) + 1e-06)).astype(
        jnp.bfloat16
    )

    unit_pair = in_core_order(core, unit, swapped(unit), 2)
    parts = jnp.moveaxis(unit_pair.reshape(2, n_z, key_rows, 2 * rows), 1, 0)
    landed = exchange(parts.reshape(n_z, 2 * key_rows, 2 * rows), Z)

    both = state_sums(landed, state)
    both = exchange(both.reshape(n_z, 2 * rows, 2 * half), Z)
    both = jnp.sum(both.astype(jnp.float32), axis=0)

    small = project(w_small)
    alpha = jnp.exp(
        -jnp.exp(decay_log)[:, None] * jax.nn.softplus(small[:HEADS] + decay_bias[:, None])
    )
    alpha = lax.dynamic_slice_in_dim(alpha, head, 1, 0)
    beta = lax.dynamic_slice_in_dim(jax.nn.sigmoid(small[HEADS:]), head, 1, 0)
    unit_f = unit.astype(jnp.float32)
    meet = jnp.sum(unit_f[0] * unit_f[1], axis=0, keepdims=True)
    value, gate = qkvg[2].T, qkvg[3].T
    columns = jnp.concatenate([alpha, beta, meet]).T
    alpha_c, beta_c, meet_c = columns[:, :1], columns[:, 1:2], columns[:, 2:]

    kept = lax.dynamic_slice_in_dim(both, core * rows, rows, 0)
    given = lax.dynamic_slice_in_dim(both, (1 - core) * rows, rows, 0)
    given = swapped(given)
    recall = in_core_order(core, kept[:, :half], given[:, :half], 1)
    answer = in_core_order(core, kept[:, half:], given[:, half:], 1)
    write = beta_c * (value - alpha_c * recall)
    readout = alpha_c * answer + meet_c * write
    power = jnp.mean(readout * readout, axis=1, keepdims=True)
    mixed = (
        readout * lax.rsqrt(power + 1e-05) * head_gain[None, :] * jax.nn.silu(gate)
    ).astype(jnp.bfloat16)

    mixed_full = jnp.moveaxis(to_all(mixed, XY), 0, 1).reshape(rows, D)
    hidden = x_full + jnp.dot(mixed_full, out_full, preferred_element_type=jnp.float32)
    energy = jnp.mean(hidden * hidden, axis=1, keepdims=True)
    final = (hidden * lax.rsqrt(energy + 1e-06) * gain_full[None, :]).astype(jnp.bfloat16)

    ids = lax.dynamic_index_in_dim(token_ids.reshape(n_z, 2, rows), core, 1, False)
    ids = lax.dynamic_slice_in_dim(jnp.concatenate([ids, ids]), zed, n_z, 0).T

    def statistics(block, ids):
        found = []
        for weight, owner in ((lm_weight, core), (lm_other, 1 - core)):
            logits = jnp.dot(block, weight, preferred_element_type=jnp.float32)
            start = ((head * 2 + owner) * n_z + zed) * vocab_dev
            hits = lax.broadcasted_iota(jnp.int32, logits.shape, 1) + start == ids
            picked = jnp.sum(jnp.where(hits, logits, jnp.zeros_like(logits)), axis=1)
            top = jnp.max(logits, axis=1)
            expo = jnp.exp(logits - top[:, None])
            found.append((top, jnp.sum(expo, axis=1), jnp.sum(expo * logits, axis=1), picked))
        return jnp.stack(merged([jnp.stack(s) for s in zip(*found)], 0))

    def along_z(block, step):
        return lax.ppermute(block, Z, [(k, (k + step) % n_z) for k in range(n_z)])

    by_distance = [None] * n_z
    by_distance[0] = statistics(final, ids[:, :1])
    up = down = (final[:, : D // 2], final[:, D // 2 :])
    for step in range(1, n_z // 2):
        pairs = [(along_z(u, 1), along_z(d, -1)) for u, d in zip(up, down)]
        up, down = zip(*pairs)
        block = jnp.concatenate([jnp.concatenate(p) for p in pairs], axis=1)
        back = n_z - step
        two = statistics(
            block, jnp.concatenate([ids[:, back : back + 1], ids[:, step : step + 1]])
        )
        by_distance[back], by_distance[step] = two[:, :rows], two[:, rows:]
    middle = n_z // 2
    block = jnp.concatenate([along_z(up[0], 1), along_z(down[1], -1)], axis=1)
    by_distance[middle] = statistics(block, ids[:, middle : middle + 1])
    stats = jnp.stack(by_distance)
    stats = lax.dynamic_slice_in_dim(jnp.concatenate([stats, stats]), n_z - zed, n_z, 0)
    stats = jnp.moveaxis(stats, 1, 0).reshape(4, n_z * rows)

    kept = lax.dynamic_slice_in_dim(write, core * half, half, 1)
    given = lax.dynamic_slice_in_dim(write, (1 - core) * half, half, 1)
    w_block = in_core_order(core, kept, swapped(given), 1)
    a_block = in_core_order(core, alpha, swapped(alpha), 0)
    lanes = 2 * half
    n_stats = 4 * n_z * rows // lanes
    tail = jnp.concatenate([stats.reshape(n_stats, lanes), jnp.pad(a_block, ((0, 0), (0, lanes - rows)))])
    tail = jnp.pad(tail, ((0, -tail.shape[0] % 8), (0, 0)))
    sent = to_all(jnp.concatenate([w_block, tail]), Z)
    stats = sent[:, rows : rows + n_stats].reshape(n_z, 4, n_z * rows)
    stats = jnp.stack(merged(jnp.moveaxis(stats, 1, 0), 0))
    shared = to_all(stats, XY)

    back = jnp.transpose(sent[:, :rows].reshape(n_z, rows, 2, half), (3, 0, 2, 1))
    back = back.reshape(half, batch)
    decay = sent[:, rows + n_stats : rows + n_stats + 2, :rows].reshape(batch)
    key_k = jnp.moveaxis(landed[:, key_rows:], 0, 1).reshape(key_rows, batch)
    new_state = decay * state + key_k.astype(jnp.float32)[:, None, :] * back[None]

    top, total, weighted, picked = merged(jnp.moveaxis(shared, 1, 0), 0)
    lse = top + jnp.log(total)
    mine = jnp.stack([picked - lse, lse - weighted / total])
    logprob, entropy = in_core_order(core, mine[:, None], swapped(mine)[:, None], 1)

    def in_order(two):
        return jnp.moveaxis(two.reshape(2, n_z, rows), 0, 1).reshape(batch)

    logprob = in_order(logprob)
    entropy = in_order(entropy)
    gap = jnp.clip(ref_logprob - logprob, -20.0, 20.0)
    kl = jnp.minimum(jnp.exp(gap) - gap - 1.0, 10.0)
    return (new_state, logprob, entropy, kl)


def solution(mesh):
    split = Mesh(mesh.devices.reshape(4, 4, 2, mesh.shape["col"]), (X, Y, CORE, Z))
    in_specs = (
        P(Z, ROW),
        P(Z, ROW, None),
        P(),
        P(None, ROW),
        P(None, ROW),
        P(None, ROW),
        P(None, ROW),
        P(),
        P(),
        P(),
        P(),
        P(),
        P(ROW, None),
        P(ROW),
        P(None, ROW_COL),
        P(),
        P(),
    )
    out_specs = (P(Z, ROW, None), P(), P(), P())
    return jax.shard_map(
        per_device, mesh=split, in_specs=in_specs, out_specs=out_specs, check_vma=False
    )
```

time: 208 us -> 185 us (0.89)
  waiting for transfers between devices: 61.5 us -> 41.1 us
  blocking collectives: 0 us -> 14.1 us
  other arithmetic: 23.2 us -> 15.4 us
  local copies, waits for them, and re-layouts: 16.4 us -> 11.4 us
  matrix products: 26 us -> 22.1 us
  Pallas kernels: 0 us -> 2.28 us
    all_to_all x7 -> x5, waiting for transfers between devices: 55.5 us -> 34.4 us  [exchange(): return lax.all_to_all(blocks, axes, split_axis=0, concat_axis=0, tiled=True)]
    all_to_all x0 -> x1, blocking collectives: none -> 14.1 us  [exchange(): return lax.all_to_all(blocks, axes, split_axis=0, concat_axis=0, tiled=True)]
    all_to_all x7 -> x5, starting transfers between devices: 34.3 us -> 27.6 us  [exchange(): return lax.all_to_all(blocks, axes, split_axis=0, concat_axis=0, tiled=True)]
    reduce_sum x3 -> x2, other arithmetic: 4.12 us -> 0.07 us  [the longest x1 0.03 us: per_device(): jnp.sum(raw * raw, axis=1, keepdims=True) + 1e-06]
    dot_general x3, matrix products: 5.11 us -> 1.12 us  [project(): lax.dot_general(weight, normed, (((0,), (1,)), ((), ())), preferred_eleme...]
    ppermute x8 -> x14, starting transfers between devices: 11.3 us -> 14.8 us  [along_z(): return lax.ppermute(block, Z, [(k, (k + step) % n_z) for k in range(n_z)])]
    concatenate x6 -> x7, other arithmetic: 5.74 us -> 2.62 us  [the longest x1 1.26 us: per_device(): w_own = jnp.concatenate(weights[:4], axis=1)]
    dynamic_slice x3 -> x2, local copies, waits for them, and re-layouts: 3.41 us -> 0.6 us  [the longest x1 0.59 us: per_device(): alpha = lax.dynamic_slice_in_dim(alpha, head, 1, 0)]
  transfers between devices with their start and end apart: 26 -> 32, of which waited for: 10 -> 11; matrix products, arithmetic and copies ran while one was open for 30% -> 19% of each run, Pallas kernels for 0% -> 1%
where the time goes in v3:
time: 185 us; the launch traced here: 184 us
  starting transfers between devices  62.5 us (34%)
  waiting for transfers between devices  41.1 us (22%)
  matrix products  22.1 us (12%)
  other arithmetic  15.4 us (8%)
  between operations  14.9 us (8%)
  blocking collectives  14.1 us (8%)
  local copies, waits for them, and re-layouts  11.4 us (6%)
  Pallas kernels  2.28 us (1%)
    all_to_all x5, waiting for transfers between devices, exchange(): return lax.all_to_all(blocks, axes, split_axis=0, concat_axis=0, tiled=True)  34.4 us
    all_to_all x5, starting transfers between devices, exchange(): return lax.all_to_all(blocks, axes, split_axis=0, concat_axis=0, tiled=True)  27.6 us
    ppermute x12, starting transfers between devices, swapped(): return lax.ppermute(array, CORE, [(0, 1), (1, 0)])  20 us
    dot_general x10, matrix products, statistics(): logits = jnp.dot(block, weight, preferred_element_type=jnp.float32)  15.9 us
    ppermute x14, starting transfers between devices, along_z(): return lax.ppermute(block, Z, [(k, (k + step) % n_z) for k in range(n_z)])  14.8 us
    all_to_all x1, blocking collectives, exchange(): return lax.all_to_all(blocks, axes, split_axis=0, concat_axis=0, tiled=True)  14.1 us
    add x1, other arithmetic, per_device(): decay * state + key_k.astype(jnp.float32)[:, None, :] * back[None]  5.13 us
    dot_general x1, matrix products, per_device(): jnp.dot(mixed_full, out_full, preferred_element_type=jnp.float32)  5.09 us
  transfers between devices with their start and end apart: 32, of which 11 were waited for; matrix products, arithmetic and copies ran while one was open for 19% of the time, Pallas kernels for 1%

profile of v3, /device:TPU:1, one launch (start us, length us, event | category | flops | bytes accessed | tf_op | source)
XLA Modules:
  0.0 183.8 jit_solution(12042087961568729479)
XLA Ops:
  7.9 3.3 %collective-permute-start = (bf16[144,64]{0,1:T(8,128)(2,1)}, bf16[144,64]{0,1:T(8,128)(2,1)S(1)}, u32[]{:S(2)}, u32[]{:S(2)}) collective-permute-start(bf16[144,64]{0,1:T(8,128)(2,1)} %param.17), channel_id=1, source_target_pairs={{0,8},{8,0},{1,9},{9,1},{2,10},{10,2},{3,11},{11,3},{4,12},{12,4},... | collective-permute-start | bytes 55304 | tf_op jit(solution)/shard_map/ppermute | solution.py:24
  12.2 0.8 reshape.322
  16.7 0.8 broadcast_select_fusion.4
  17.8 0.8 broadcast_in_dim.15
  18.6 5.0 %all-to-all-start = ((bf16[16,73,128]{2,1,0:T(8,128)(2,1)}), bf16[16,73,128]{2,1,0:T(8,128)(2,1)S(1)}, u32[]{:S(2)}, u32[]{:S(2)}) async-start(bf16[16,73,128]{2,1,0:T(8,128)(2,1)} %broadcast_in_dim.15), calls=%async_computation | async-start | bytes 655360 | tf_op jit(solution)/shard_map/all_to_all | solution.py:28
  23.6 1.3 pad_maximum_fusion
  24.9 1.0 pad_maximum_fusion.1
  26.0 5.9 %all-to-all-done = bf16[16,73,128]{2,1,0:T(8,128)(2,1)S(1)} async-done(((bf16[16,73,128]{2,1,0:T(8,128)(2,1)}), bf16[16,73,128]{2,1,0:T(8,128)(2,1)S(1)}, u32[]{:S(2)}, u32[]{:S(2)}) %all-to-all-start) | async-done | bytes 299040 | tf_op jit(solution)/shard_map/all_to_all | solution.py:28
  33.4 1.9 %collective-permute-start.6 = (bf16[2,128,72]{2,1,0:T(8,128)(2,1)S(1)}, bf16[2,128,72]{2,1,0:T(8,128)(2,1)S(1)}, u32[]{:S(2)}, u32[]{:S(2)}) collective-permute-start(bf16[2,128,72]{2,1,0:T(8,128)(2,1)S(1)} %get-tuple-element.69), channel_id=1, source_target_pairs={{0,8},{8,0},{1,9},{9,1},{2,10},{10,2},{3,11},{11,3},{4,12},{12,4},... | collective-permute-start | bytes 110600 | tf_op jit(solution)/shard_map/ppermute | solution.py:24
  37.3 9.3 %all-to-all-start.1 = ((bf16[8,32,144]{2,1,0:T(8,128)(2,1)}), bf16[8,32,144]{2,1,0:T(8,128)(2,1)S(1)}, u32[]{:S(2)}, u32[]{:S(2)}) async-start(bf16[8,32,144]{2,1,0:T(8,128)(2,1)} %bitcast.16), calls=%async_computation.1 | async-start | bytes 262144 | tf_op jit(solution)/shard_map/all_to_all | solution.py:28
  46.7 7.7 %all-to-all-done.1.landed_ref = bf16[8,32,144]{2,1,0:T(8,128)(2,1)S(1)} async-done(((bf16[8,32,144]{2,1,0:T(8,128)(2,1)}), bf16[8,32,144]{2,1,0:T(8,128)(2,1)S(1)}, u32[]{:S(2)}, u32[]{:S(2)}) %all-to-all-start.1) | async-done | bytes 73760 | tf_op jit(solution)/shard_map/all_to_all | solution.py:28
  54.4 2.3 %copy-done = f32[16,64,1152]{2,1,0:T(8,128)S(1)} copy-done((f32[16,64,1152]{2,1,0:T(8,128)S(1)}, f32[16,64,1152]{2,1,0:T(8,128)}, u32[]{:S(2)}) %copy-start) | copy-done | bytes 4718616
  56.8 2.3 %shard_map.192 = bf16[1152,128]{1,0:T(8,128)(2,1)} custom-call(bf16[8,32,144]{2,1,0:T(8,128)(2,1)S(1)} %all-to-all-done.1.landed_ref, f32[16,64,1152]{2,1,0:T(8,128)S(1)} %copy-done), custom_call_target="tpu_custom_call" | custom-call | flops 4718592 | bytes 4718592 | tf_op jit(solution)/shard_map/pallas_call | solution.py:79
  59.0 3.6 %all-to-all-start.2 = ((bf16[8,144,128]{2,1,0:T(8,128)(2,1)}), bf16[8,144,128]{2,1,0:T(8,128)(2,1)S(1)}, u32[]{:S(2)}, u32[]{:S(2)}) async-start(bf16[8,144,128]{2,1,0:T(8,128)(2,1)} %bitcast.17), calls=%async_computation.2 | async-start | bytes 589824 | tf_op jit(solution)/shard_map/all_to_all | solution.py:28
  62.7 9.8 %all-to-all-done.2 = bf16[8,144,128]{2,1,0:T(8,128)(2,1)S(1)} async-done(((bf16[8,144,128]{2,1,0:T(8,128)(2,1)}), bf16[8,144,128]{2,1,0:T(8,128)(2,1)S(1)}, u32[]{:S(2)}, u32[]{:S(2)}) %all-to-all-start.2) | async-done | bytes 294944 | tf_op jit(solution)/shard_map/all_to_all | solution.py:28
  72.6 3.7 %collective-permute-start.7 = (f32[72,128]{0,1:T(8,128)S(1)}, f32[72,128]{0,1:T(8,128)S(1)}, u32[]{:S(2)}, u32[]{:S(2)}) collective-permute-start(f32[72,128]{0,1:T(8,128)S(1)} %copy.148), channel_id=1, source_target_pairs={{0,8},{8,0},{1,9},{9,1},{2,10},{10,2},{3,11},{11,3},{4,12},{12,4},... | collective-permute-start | bytes 110600 | tf_op jit(solution)/shard_map/ppermute | solution.py:24
  77.5 0.8 broadcast_in_dim.17
  78.3 4.3 %all-to-all-start.3 = ((bf16[16,72,128]{2,1,0:T(8,128)(2,1)}), bf16[16,72,128]{2,1,0:T(8,128)(2,1)S(1)}, u32[]{:S(2)}, u32[]{:S(2)}) async-start(bf16[16,72,128]{2,1,0:T(8,128)(2,1)} %broadcast_in_dim.17), calls=%async_computation.3 | async-start | bytes 589824 | tf_op jit(solution)/shard_map/all_to_all | solution.py:28
  82.5 0.7 collective-permute-start.8
  83.3 0.9 collective-permute-done.8
  84.1 6.1 %all-to-all-done.3 = bf16[16,72,128]{2,1,0:T(8,128)(2,1)S(1)} async-done(((bf16[16,72,128]{2,1,0:T(8,128)(2,1)}), bf16[16,72,128]{2,1,0:T(8,128)(2,1)S(1)}, u32[]{:S(2)}, u32[]{:S(2)}) %all-to-all-start.3) | async-done | bytes 294944 | tf_op jit(solution)/shard_map/all_to_all | solution.py:28
  90.3 5.1 %multiply_reduce_fusion = (f32[72]{0:T(128)S(1)}, f32[72,2048]{1,0:T(8,128)S(1)}) fusion(bf16[2048,2048]{1,0:T(8,128)(2,1)} %all-gather.2.cloned.1.call-done, bf16[16,73,128]{2,1,0:T(8,128)(2,1)S(1)} %all-to-all-done, bf16[16,72,128]{2,1,0:T(8,128)(2,1)S(1)} %all-to-all-done.3), kind=kOutput, calls=%fused_computation.17 | convolution fusion | flops 604569536 | bytes 9568544 | tf_op jit(solution)/shard_map/dot_general | solution.py:193
  96.1 2.4 %collective-permute-start.11 = (bf16[72,1024]{1,0:T(8,128)(2,1)S(1)}, bf16[72,1024]{1,0:T(8,128)(2,1)S(1)}, u32[]{:S(2)}, u32[]{:S(2)}) collective-permute-start(bf16[72,1024]{1,0:T(8,128)(2,1)S(1)} %get-tuple-element.72), channel_id=1, source_target_pairs={{0,7},{1,0},{2,1},{3,2},{4,3},{5,4},{6,5},{7,6},{8,15},{9,8},{10,9... | collective-permute-start | bytes 442376 | tf_op jit(solution)/shard_map/ppermute | solution.py:213
  98.5 1.4 collective-permute-start.12
  100.6 2.4 %fusion.96 = (f32[72]{0:T(128)S(1)}, f32[72,640]{1,0:T(8,128)S(1)}) fusion(bf16[72,2048]{1,0:T(8,128)(2,1)S(1)} %multiply_convert_fusion, bf16[2048,640]{1,0:T(8,128)(2,1)} %collective-permute-done.9), kind=kOutput, calls=%fused_computation.275 | convolution fusion | flops 188789696 | bytes 3100960 | tf_op jit(solution)/shard_map/dot_general | solution.py:203
  103.2 0.9 collective-permute-done.13
  104.0 1.8 collective-permute-start.17
  105.9 1.4 collective-permute-start.16
  107.3 2.5 %fusion.101 = (f32[144]{0:T(256)S(1)}, f32[144,640]{1,0:T(8,128)S(1)}) fusion(bf16[2048,640]{1,0:T(8,128)(2,1)} %collective-permute-done.9, bf16[72,1024]{1,0:T(8,128)(2,1)S(1)} %collective-permute-done.13, bf16[72,1024]{1,0:T(8,128)(2,1)S(1)} %collective-permute-done.12, bf16[72,1024]{1,0:T(8,128)(2,1)S(1)} %collective-permute-done.11, ...), kind=kOutput, calls=%fused_computation.280 | convolution fusion | flops 379938688 | bytes 3580480 | tf_op jit(solution)/shard_map/dot_general | solution.py:203
  109.8 0.8 fusion.100
  110.7 2.7 %collective-permute-start.21 = (bf16[72,1024]{1,0:T(8,128)(2,1)S(1)}, bf16[72,1024]{1,0:T(8,128)(2,1)S(1)}, u32[]{:S(2)}, u32[]{:S(2)}) collective-permute-start(bf16[72,1024]{1,0:T(8,128)(2,1)S(1)} %collective-permute-done.17), channel_id=1, source_target_pairs={{0,7},{1,0},{2,1},{3,2},{4,3},{5,4},{6,5},{7,6},{8,15},{9,8},{10,9... | collective-permute-start | bytes 442376 | tf_op jit(solution)/shard_map/ppermute | solution.py:213
  113.5 1.4 collective-permute-start.20
  114.9 2.5 %fusion.102 = (f32[144]{0:T(256)S(1)}, f32[144,640]{1,0:T(8,128)S(1)}) fusion(bf16[2048,640]{1,0:T(8,128)(2,1)} %collective-permute-done.9, bf16[72,1024]{1,0:T(8,128)(2,1)S(1)} %collective-permute-done.17, bf16[72,1024]{1,0:T(8,128)(2,1)S(1)} %collective-permute-done.16, bf16[72,1024]{1,0:T(8,128)(2,1)S(1)} %collective-permute-done.15, ...), kind=kOutput, calls=%fused_computation.281 | convolution fusion | flops 379938688 | bytes 3580480 | tf_op jit(solution)/shard_map/dot_general | solution.py:203
  117.4 0.8 fusion.99
  118.2 0.7 collective-permute-done.20
  118.9 2.5 %fusion.103 = (f32[144]{0:T(256)S(1)}, f32[144,640]{1,0:T(8,128)S(1)}) fusion(bf16[2048,640]{1,0:T(8,128)(2,1)} %collective-permute-done.9, bf16[72,1024]{1,0:T(8,128)(2,1)S(1)} %collective-permute-done.21, bf16[72,1024]{1,0:T(8,128)(2,1)S(1)} %collective-permute-done.20, bf16[72,1024]{1,0:T(8,128)(2,1)S(1)} %collective-permute-done.19, ...), kind=kOutput, calls=%fused_computation.282 | convolution fusion | flops 379938688 | bytes 3580480 | tf_op jit(solution)/shard_map/dot_general | solution.py:203
  121.4 0.8 fusion.98
  122.2 1.1 fusion.6
  123.5 1.6 collective-permute-start.22
  125.1 1.2 collective-permute-start.23
  126.3 2.4 %collective-permute-done.22 = bf16[72,1024]{1,0:T(8,128)(2,1)S(1)} collective-permute-done((bf16[72,1024]{1,0:T(8,128)(2,1)S(1)}, bf16[72,1024]{1,0:T(8,128)(2,1)S(1)}, u32[]{:S(2)}, u32[]{:S(2)}) %collective-permute-start.22) | collective-permute-done | bytes 147488 | tf_op jit(solution)/shard_map/ppermute | solution.py:213
  129.9 2.4 %fusion.97 = (f32[72]{0:T(128)S(1)}, f32[72,640]{1,0:T(8,128)S(1)}) fusion(bf16[72,2048]{1,0:T(8,128)(2,1)S(1)} %constant_dynamic-update-slice_fusion, bf16[2048,640]{1,0:T(8,128)(2,1)} %collective-permute-done.9), kind=kOutput, calls=%fused_computation.276 | convolution fusion | flops 188789696 | bytes 3100960 | tf_op jit(solution)/shard_map/dot_general | solution.py:203
  133.9 14.1 %all_to_all.30 = f32[8,96,128]{2,1,0:T(8,128)S(1)} all-to-all(f32[8,96,128]{2,1,0:T(8,128)S(1)} %broadcast_in_dim.18), channel_id=1, replica_groups=mesh['row_0'=4,'row_1'=4,'row_2'=2,'col'=8] {'col'}, dimensions={0} | all-to-all | bytes 786432 | tf_op jit(solution)/shard_map/all_to_all | solution.py:28
  149.0 5.4 %all-to-all-start.5 = ((f32[16,4,576]{2,1,0:T(4,128)}), f32[16,4,576]{2,1,0:T(4,128)S(1)}, u32[]{:S(2)}, u32[]{:S(2)}) async-start(f32[16,4,576]{2,1,0:T(4,128)} %broadcast_in_dim.20), calls=%async_computation.5 | async-start | bytes 327680 | tf_op jit(solution)/shard_map/all_to_all | solution.py:28
  155.6 0.7 mul.369
  156.4 4.8 %all-to-all-done.5 = f32[16,4,576]{2,1,0:T(4,128)S(1)} async-done(((f32[16,4,576]{2,1,0:T(4,128)}), f32[16,4,576]{2,1,0:T(4,128)S(1)}, u32[]{:S(2)}, u32[]{:S(2)}) %all-to-all-start.5) | async-done | bytes 147488 | tf_op jit(solution)/shard_map/all_to_all | solution.py:28
  161.5 8.6 %collective-permute-start.25 = (f32[2,576]{1,0:T(2,128)S(1)}, f32[2,576]{1,0:T(2,128)S(1)}, u32[]{:S(2)}, u32[]{:S(2)}) collective-permute-start(f32[2,576]{1,0:T(2,128)S(1)} %pad_maximum_fusion.8), channel_id=1, source_target_pairs={{0,8},{8,0},{1,9},{9,1},{2,10},{10,2},{3,11},{11,3},{4,12},{12,4},... | collective-permute-start | bytes 13832 | tf_op jit(solution)/shard_map/ppermute | solution.py:24
  170.1 5.1 %multiply_add_fusion = f32[16,64,1152]{2,1,0:T(8,128)} fusion(f32[16,64,1152]{2,1,0:T(8,128)} %state_ref.1, f32[64,1152]{1,0:T(8,128)S(1)} %mul.369, f32[16,1152]{1,0:T(8,128)S(1)} %reshape.329, f32[1152]{0:T(1024)S(1)} %mul.365), kind=kLoop, calls=%fused_computation | loop fusion | flops 3538944 | bytes 9810432 | tf_op jit(solution)/shard_map/add | solution.py:251
  (195 shorter events, 19.0 us)
Async XLA Ops:
  7.2 83.1 %all-gather.2.cloned.1.call-start = ((), (), s32[]{:S(2)}) async-start(), calls=%async_computation.6 | async-start | bytes 8650752 | tf_op jit(solution)/shard_map/all_gather | solution.py:131
  7.9 8.3 %collective-permute-start = (bf16[144,64]{0,1:T(8,128)(2,1)}, bf16[144,64]{0,1:T(8,128)(2,1)S(1)}, u32[]{:S(2)}, u32[]{:S(2)}) collective-permute-start(bf16[144,64]{0,1:T(8,128)(2,1)} %param.17), channel_id=1, source_target_pairs={{0,8},{8,0},{1,9},{9,1},{2,10},{10,2},{3,11},{11,3},{4,12},{12,4},... | collective-permute-start | bytes 55304 | tf_op jit(solution)/shard_map/ppermute | solution.py:24
  11.2 4.0 %collective-permute-start.1 = (bf16[64]{0:T(256)(128)(2,1)}, bf16[64]{0:T(256)(128)(2,1)S(1)}, u32[]{:S(2)}, u32[]{:S(2)}) collective-permute-start(bf16[64]{0:T(256)(128)(2,1)} %param.30), channel_id=1, source_target_pairs={{0,8},{8,0},{1,9},{9,1},{2,10},{10,2},{3,11},{11,3},{4,12},{12,4},... | collective-permute-start | bytes 392 | tf_op jit(solution)/shard_map/ppermute | solution.py:24
  11.3 13.5 %collective-permute-start.2 = (bf16[2048,64]{0,1:T(8,128)(2,1)}, bf16[2048,64]{0,1:T(8,128)(2,1)S(1)}, u32[]{:S(2)}, u32[]{:S(2)}) collective-permute-start(bf16[2048,64]{0,1:T(8,128)(2,1)} %param.20), channel_id=1, source_target_pairs={{0,8},{8,0},{1,9},{9,1},{2,10},{10,2},{3,11},{11,3},{4,12},{12,4},... | collective-permute-start | bytes 786440 | tf_op jit(solution)/shard_map/ppermute | solution.py:24
  11.7 13.1 %collective-permute-start.3 = (bf16[2048,64]{0,1:T(8,128)(2,1)}, bf16[2048,64]{0,1:T(8,128)(2,1)S(1)}, u32[]{:S(2)}, u32[]{:S(2)}) collective-permute-start(bf16[2048,64]{0,1:T(8,128)(2,1)} %param.21), channel_id=1, source_target_pairs={{0,8},{8,0},{1,9},{9,1},{2,10},{10,2},{3,11},{11,3},{4,12},{12,4},... | collective-permute-start | bytes 786440 | tf_op jit(solution)/shard_map/ppermute | solution.py:24
  11.8 13.1 %collective-permute-start.4 = (bf16[2048,64]{0,1:T(8,128)(2,1)}, bf16[2048,64]{0,1:T(8,128)(2,1)S(1)}, u32[]{:S(2)}, u32[]{:S(2)}) collective-permute-start(bf16[2048,64]{0,1:T(8,128)(2,1)} %param.22), channel_id=1, source_target_pairs={{0,8},{8,0},{1,9},{9,1},{2,10},{10,2},{3,11},{11,3},{4,12},{12,4},... | collective-permute-start | bytes 786440 | tf_op jit(solution)/shard_map/ppermute | solution.py:24
  15.2 9.7 %collective-permute-start.5 = (bf16[2048,64]{0,1:T(8,128)(2,1)}, bf16[2048,64]{0,1:T(8,128)(2,1)}, u32[]{:S(2)}, u32[]{:S(2)}) collective-permute-start(bf16[2048,64]{0,1:T(8,128)(2,1)} %param.23), channel_id=1, source_target_pairs={{0,8},{8,0},{1,9},{9,1},{2,10},{10,2},{3,11},{11,3},{4,12},{12,4},... | collective-permute-start | bytes 786440 | tf_op jit(solution)/shard_map/ppermute | solution.py:24
  16.2 84.4 %collective-permute-start.9 = (bf16[2048,640]{1,0:T(8,128)(2,1)}, bf16[2048,640]{1,0:T(8,128)(2,1)}, u32[]{:S(2)}, u32[]{:S(2)}) collective-permute-start(bf16[2048,640]{1,0:T(8,128)(2,1)} %param.31), channel_id=1, source_target_pairs={{0,8},{8,0},{1,9},{9,1},{2,10},{10,2},{3,11},{11,3},{4,12},{12,4},... | collective-permute-start | bytes 7864328 | tf_op jit(solution)/shard_map/ppermute | solution.py:24
  18.6 13.3 %all-to-all-start = ((bf16[16,73,128]{2,1,0:T(8,128)(2,1)}), bf16[16,73,128]{2,1,0:T(8,128)(2,1)S(1)}, u32[]{:S(2)}, u32[]{:S(2)}) async-start(bf16[16,73,128]{2,1,0:T(8,128)(2,1)} %broadcast_in_dim.15), calls=%async_computation | async-start | bytes 655360 | tf_op jit(solution)/shard_map/all_to_all | solution.py:28
  32.3 3.1 %copy-start.6 = (bf16[2048,16]{0,1:T(8,128)(2,1)S(1)}, bf16[2048,16]{0,1:T(8,128)(2,1)}, u32[]{:S(2)}) copy-start(bf16[2048,16]{0,1:T(8,128)(2,1)} %param.25) | copy-start | bytes 196612
  32.4 2.9 %copy-start.7 = (bf16[2048,16]{0,1:T(8,128)(2,1)S(1)}, bf16[2048,16]{0,1:T(8,128)(2,1)}, u32[]{:S(2)}) copy-start(bf16[2048,16]{0,1:T(8,128)(2,1)} %param.24) | copy-start | bytes 196612
  32.4 3.2 %copy-start.5 = (f32[16]{0:T(128)S(1)}, f32[16]{0:T(128)}, u32[]{:S(2)}) copy-start(f32[16]{0:T(128)} %param.27) | copy-start | bytes 196
  33.4 3.1 %collective-permute-start.6 = (bf16[2,128,72]{2,1,0:T(8,128)(2,1)S(1)}, bf16[2,128,72]{2,1,0:T(8,128)(2,1)S(1)}, u32[]{:S(2)}, u32[]{:S(2)}) collective-permute-start(bf16[2,128,72]{2,1,0:T(8,128)(2,1)S(1)} %get-tuple-element.69), channel_id=1, source_target_pairs={{0,8},{8,0},{1,9},{9,1},{2,10},{10,2},{3,11},{11,3},{4,12},{12,4},... | collective-permute-start | bytes 110600 | tf_op jit(solution)/shard_map/ppermute | solution.py:24
  36.4 26.3 %collective-permute-start.24 = (f32[1,72]{1,0:T(1,128)S(1)}, f32[1,72]{1,0:T(1,128)S(1)}, u32[]{:S(2)}, u32[]{:S(2)}) collective-permute-start(f32[1,72]{1,0:T(1,128)S(1)} %fusion.80), channel_id=1, source_target_pairs={{0,8},{8,0},{1,9},{9,1},{2,10},{10,2},{3,11},{11,3},{4,12},{12,4},... | collective-permute-start | bytes 872 | tf_op jit(solution)/shard_map/ppermute | solution.py:24
  37.3 17.1 %all-to-all-start.1 = ((bf16[8,32,144]{2,1,0:T(8,128)(2,1)}), bf16[8,32,144]{2,1,0:T(8,128)(2,1)S(1)}, u32[]{:S(2)}, u32[]{:S(2)}) async-start(bf16[8,32,144]{2,1,0:T(8,128)(2,1)} %bitcast.16), calls=%async_computation.1 | async-start | bytes 262144 | tf_op jit(solution)/shard_map/all_to_all | solution.py:28
  54.4 2.3 %copy-start = (f32[16,64,1152]{2,1,0:T(8,128)S(1)}, f32[16,64,1152]{2,1,0:T(8,128)}, u32[]{:S(2)}) copy-start(f32[16,64,1152]{2,1,0:T(8,128)} %state_ref.1) | copy-start | bytes 14155780
  59.0 18.3 %copy-start.4 = (f32[128]{0:T(128)S(1)}, f32[128]{0:T(128)}, u32[]{:S(2)}) copy-start(f32[128]{0:T(128)} %param.28) | copy-start | bytes 1540
  59.0 13.4 %all-to-all-start.2 = ((bf16[8,144,128]{2,1,0:T(8,128)(2,1)}), bf16[8,144,128]{2,1,0:T(8,128)(2,1)S(1)}, u32[]{:S(2)}, u32[]{:S(2)}) async-start(bf16[8,144,128]{2,1,0:T(8,128)(2,1)} %bitcast.17), calls=%async_computation.2 | async-start | bytes 589824 | tf_op jit(solution)/shard_map/all_to_all | solution.py:28
  72.6 4.6 %collective-permute-start.7 = (f32[72,128]{0,1:T(8,128)S(1)}, f32[72,128]{0,1:T(8,128)S(1)}, u32[]{:S(2)}, u32[]{:S(2)}) collective-permute-start(f32[72,128]{0,1:T(8,128)S(1)} %copy.148), channel_id=1, source_target_pairs={{0,8},{8,0},{1,9},{9,1},{2,10},{10,2},{3,11},{11,3},{4,12},{12,4},... | collective-permute-start | bytes 110600 | tf_op jit(solution)/shard_map/ppermute | solution.py:24
  78.3 12.0 %all-to-all-start.3 = ((bf16[16,72,128]{2,1,0:T(8,128)(2,1)}), bf16[16,72,128]{2,1,0:T(8,128)(2,1)S(1)}, u32[]{:S(2)}, u32[]{:S(2)}) async-start(bf16[16,72,128]{2,1,0:T(8,128)(2,1)} %broadcast_in_dim.17), calls=%async_computation.3 | async-start | bytes 589824 | tf_op jit(solution)/shard_map/all_to_all | solution.py:28
  82.5 1.6 collective-permute-start.8
  84.1 15.8 %copy-start.1 = (bf16[2048,640]{1,0:T(8,128)(2,1)S(1)}, bf16[2048,640]{1,0:T(8,128)(2,1)}, u32[]{:S(2)}) copy-start(bf16[2048,640]{1,0:T(8,128)(2,1)} %param.31) | copy-start | bytes 7864324
  95.5 7.5 %collective-permute-start.10 = (bf16[72,1024]{1,0:T(8,128)(2,1)S(1)}, bf16[72,1024]{1,0:T(8,128)(2,1)S(1)}, u32[]{:S(2)}, u32[]{:S(2)}) collective-permute-start(bf16[72,1024]{1,0:T(8,128)(2,1)S(1)} %get-tuple-element.72), channel_id=1, source_target_pairs={{0,1},{1,2},{2,3},{3,4},{4,5},{5,6},{6,7},{7,0},{8,9},{9,10},{10,1... | collective-permute-start | bytes 442376 | tf_op jit(solution)/shard_map/ppermute | solution.py:213
  96.1 9.8 %collective-permute-start.11 = (bf16[72,1024]{1,0:T(8,128)(2,1)S(1)}, bf16[72,1024]{1,0:T(8,128)(2,1)S(1)}, u32[]{:S(2)}, u32[]{:S(2)}) collective-permute-start(bf16[72,1024]{1,0:T(8,128)(2,1)S(1)} %get-tuple-element.72), channel_id=1, source_target_pairs={{0,7},{1,0},{2,1},{3,2},{4,3},{5,4},{6,5},{7,6},{8,15},{9,8},{10,9... | collective-permute-start | bytes 442376 | tf_op jit(solution)/shard_map/ppermute | solution.py:213
  98.5 5.6 %collective-permute-start.13 = (bf16[72,1024]{1,0:T(8,128)(2,1)S(1)}, bf16[72,1024]{1,0:T(8,128)(2,1)S(1)}, u32[]{:S(2)}, u32[]{:S(2)}) collective-permute-start(bf16[72,1024]{1,0:T(8,128)(2,1)S(1)} %get-tuple-element.73), channel_id=1, source_target_pairs={{0,7},{1,0},{2,1},{3,2},{4,3},{5,4},{6,5},{7,6},{8,15},{9,8},{10,9... | collective-permute-start | bytes 442376 | tf_op jit(solution)/shard_map/ppermute | solution.py:213
  98.5 7.4 %collective-permute-start.12 = (bf16[72,1024]{1,0:T(8,128)(2,1)S(1)}, bf16[72,1024]{1,0:T(8,128)(2,1)S(1)}, u32[]{:S(2)}, u32[]{:S(2)}) collective-permute-start(bf16[72,1024]{1,0:T(8,128)(2,1)S(1)} %get-tuple-element.73), channel_id=1, source_target_pairs={{0,1},{1,2},{2,3},{3,4},{4,5},{5,6},{6,7},{7,0},{8,9},{9,10},{10,1... | collective-permute-start | bytes 442376 | tf_op jit(solution)/shard_map/ppermute | solution.py:213
  103.1 7.6 %collective-permute-start.14 = (bf16[72,1024]{1,0:T(8,128)(2,1)S(1)}, bf16[72,1024]{1,0:T(8,128)(2,1)S(1)}, u32[]{:S(2)}, u32[]{:S(2)}) collective-permute-start(bf16[72,1024]{1,0:T(8,128)(2,1)S(1)} %collective-permute-done.10), channel_id=1, source_target_pairs={{0,1},{1,2},{2,3},{3,4},{4,5},{5,6},{6,7},{7,0},{8,9},{9,10},{10,1... | collective-permute-start | bytes 442376 | tf_op jit(solution)/shard_map/ppermute | solution.py:213
  104.0 6.7 %collective-permute-start.17 = (bf16[72,1024]{1,0:T(8,128)(2,1)S(1)}, bf16[72,1024]{1,0:T(8,128)(2,1)S(1)}, u32[]{:S(2)}, u32[]{:S(2)}) collective-permute-start(bf16[72,1024]{1,0:T(8,128)(2,1)S(1)} %collective-permute-done.13), channel_id=1, source_target_pairs={{0,7},{1,0},{2,1},{3,2},{4,3},{5,4},{6,5},{7,6},{8,15},{9,8},{10,9... | collective-permute-start | bytes 442376 | tf_op jit(solution)/shard_map/ppermute | solution.py:213
  105.9 7.5 %collective-permute-start.15 = (bf16[72,1024]{1,0:T(8,128)(2,1)S(1)}, bf16[72,1024]{1,0:T(8,128)(2,1)S(1)}, u32[]{:S(2)}, u32[]{:S(2)}) collective-permute-start(bf16[72,1024]{1,0:T(8,128)(2,1)S(1)} %collective-permute-done.11), channel_id=1, source_target_pairs={{0,7},{1,0},{2,1},{3,2},{4,3},{5,4},{6,5},{7,6},{8,15},{9,8},{10,9... | collective-permute-start | bytes 442376 | tf_op jit(solution)/shard_map/ppermute | solution.py:213
  105.9 7.6 %collective-permute-start.16 = (bf16[72,1024]{1,0:T(8,128)(2,1)S(1)}, bf16[72,1024]{1,0:T(8,128)(2,1)S(1)}, u32[]{:S(2)}, u32[]{:S(2)}) collective-permute-start(bf16[72,1024]{1,0:T(8,128)(2,1)S(1)} %collective-permute-done.12), channel_id=1, source_target_pairs={{0,1},{1,2},{2,3},{3,4},{4,5},{5,6},{6,7},{7,0},{8,9},{9,10},{10,1... | collective-permute-start | bytes 442376 | tf_op jit(solution)/shard_map/ppermute | solution.py:213
  110.6 7.5 %collective-permute-start.18 = (bf16[72,1024]{1,0:T(8,128)(2,1)S(1)}, bf16[72,1024]{1,0:T(8,128)(2,1)S(1)}, u32[]{:S(2)}, u32[]{:S(2)}) collective-permute-start(bf16[72,1024]{1,0:T(8,128)(2,1)S(1)} %collective-permute-done.14), channel_id=1, source_target_pairs={{0,1},{1,2},{2,3},{3,4},{4,5},{5,6},{6,7},{7,0},{8,9},{9,10},{10,1... | collective-permute-start | bytes 442376 | tf_op jit(solution)/shard_map/ppermute | solution.py:213
  110.7 7.4 %collective-permute-start.21 = (bf16[72,1024]{1,0:T(8,128)(2,1)S(1)}, bf16[72,1024]{1,0:T(8,128)(2,1)S(1)}, u32[]{:S(2)}, u32[]{:S(2)}) collective-permute-start(bf16[72,1024]{1,0:T(8,128)(2,1)S(1)} %collective-permute-done.17), channel_id=1, source_target_pairs={{0,7},{1,0},{2,1},{3,2},{4,3},{5,4},{6,5},{7,6},{8,15},{9,8},{10,9... | collective-permute-start | bytes 442376 | tf_op jit(solution)/shard_map/ppermute | solution.py:213
  113.4 4.8 %collective-permute-start.19 = (bf16[72,1024]{1,0:T(8,128)(2,1)S(1)}, bf16[72,1024]{1,0:T(8,128)(2,1)S(1)}, u32[]{:S(2)}, u32[]{:S(2)}) collective-permute-start(bf16[72,1024]{1,0:T(8,128)(2,1)S(1)} %collective-permute-done.15), channel_id=1, source_target_pairs={{0,7},{1,0},{2,1},{3,2},{4,3},{5,4},{6,5},{7,6},{8,15},{9,8},{10,9... | collective-permute-start | bytes 442376 | tf_op jit(solution)/shard_map/ppermute | solution.py:213
  113.5 5.4 %collective-permute-start.20 = (bf16[72,1024]{1,0:T(8,128)(2,1)S(1)}, bf16[72,1024]{1,0:T(8,128)(2,1)S(1)}, u32[]{:S(2)}, u32[]{:S(2)}) collective-permute-start(bf16[72,1024]{1,0:T(8,128)(2,1)S(1)} %collective-permute-done.16), channel_id=1, source_target_pairs={{0,1},{1,2},{2,3},{3,4},{4,5},{5,6},{6,7},{7,0},{8,9},{9,10},{10,1... | collective-permute-start | bytes 442376 | tf_op jit(solution)/shard_map/ppermute | solution.py:213
  123.5 5.3 %collective-permute-start.22 = (bf16[72,1024]{1,0:T(8,128)(2,1)S(1)}, bf16[72,1024]{1,0:T(8,128)(2,1)S(1)}, u32[]{:S(2)}, u32[]{:S(2)}) collective-permute-start(bf16[72,1024]{1,0:T(8,128)(2,1)S(1)} %collective-permute-done.18), channel_id=1, source_target_pairs={{0,1},{1,2},{2,3},{3,4},{4,5},{5,6},{6,7},{7,0},{8,9},{9,10},{10,1... | collective-permute-start | bytes 442376 | tf_op jit(solution)/shard_map/ppermute | solution.py:213
  125.1 4.1 %collective-permute-start.23 = (bf16[72,1024]{1,0:T(8,128)(2,1)S(1)}, bf16[72,1024]{1,0:T(8,128)(2,1)S(1)}, u32[]{:S(2)}, u32[]{:S(2)}) collective-permute-start(bf16[72,1024]{1,0:T(8,128)(2,1)S(1)} %collective-permute-done.21), channel_id=1, source_target_pairs={{0,7},{1,0},{2,1},{3,2},{4,3},{5,4},{6,5},{7,6},{8,15},{9,8},{10,9... | collective-permute-start | bytes 442376 | tf_op jit(solution)/shard_map/ppermute | solution.py:213
  149.0 12.2 %all-to-all-start.5 = ((f32[16,4,576]{2,1,0:T(4,128)}), f32[16,4,576]{2,1,0:T(4,128)S(1)}, u32[]{:S(2)}, u32[]{:S(2)}) async-start(f32[16,4,576]{2,1,0:T(4,128)} %broadcast_in_dim.20), calls=%async_computation.5 | async-start | bytes 327680 | tf_op jit(solution)/shard_map/all_to_all | solution.py:28
  161.5 14.8 %copy-start.3 = (f32[1152]{0:T(1024)S(1)}, f32[1152]{0:T(1024)}, u32[]{:S(2)}) copy-start(f32[1152]{0:T(1024)} %param.33) | copy-start | bytes 13828
  161.5 13.8 %collective-permute-start.25 = (f32[2,576]{1,0:T(2,128)S(1)}, f32[2,576]{1,0:T(2,128)S(1)}, u32[]{:S(2)}, u32[]{:S(2)}) collective-permute-start(f32[2,576]{1,0:T(2,128)S(1)} %pad_maximum_fusion.8), channel_id=1, source_target_pairs={{0,8},{8,0},{1,9},{9,1},{2,10},{10,2},{3,11},{11,3},{4,12},{12,4},... | collective-permute-start | bytes 13832 | tf_op jit(solution)/shard_map/ppermute | solution.py:24
  175.5 1.4 copy-start.2
Sparse Core Ops, SparseCore 0:
  10.6 63.4 all-gather.1

commit v4 on v3

--- a/solution.py
+++ b/solution.py
@@ -86,7 +86,7 @@
         out_specs=pl.BlockSpec((lanes, 2 * half), lambda i: (i, 0)),
         out_shape=jax.ShapeDtypeStruct((batch, 2 * half), jnp.bfloat16),
         scratch_shapes=[pltpu.VMEM((2 * key_rows, batch), jnp.float32)],
-        compiler_params=pltpu.CompilerParams(vmem_limit_bytes=24 * 1024 * 1024),
+        compiler_params=pltpu.CompilerParams(vmem_limit_bytes=60 * 1024 * 1024),
         cost_estimate=pl.CostEstimate(
             flops=4 * state.size, bytes_accessed=4 * state.size, transcendentals=0
         ),
@@ -126,15 +126,15 @@
     x_block = lax.dynamic_slice_in_dim(x_chip, core * rows, rows, 0)
     x_block = jnp.concatenate([x_block, gain_chip[None, :]])
 
-    weights = (w_query, w_key, w_value, w_gate)
-    w_other = [swapped(w) for w in weights]
     out_full = lax.all_gather(w_out, ROW, axis=0, tiled=True)
-    lm_other = swapped(lm_weight)
-    x_block, *weights = lax.optimization_barrier((x_block, *weights, w_decay, w_beta))
+    weights = (w_query, w_key, w_value, w_gate, w_decay, w_beta)
+    x_block, weights, attn_norm_gain, decay_log, decay_bias, token_ids = lax.optimization_barrier(
+        (x_block, weights, attn_norm_gain, decay_log, decay_bias, token_ids)
+    )
     pieces = to_all(x_block, XY)
     w_own = jnp.concatenate(weights[:4], axis=1)
+    w_other = jnp.concatenate([swapped(w) for w in weights[:4]], axis=1)
     w_small = jnp.concatenate(weights[4:], axis=1)
-    w_other = jnp.concatenate(w_other, axis=1)
 
     gain_full = pieces[:, rows].reshape(D).astype(jnp.float32)
     x_full = jnp.moveaxis(pieces[:, :rows], 0, 1).reshape(rows, D).astype(jnp.float32)
@@ -159,9 +159,14 @@
 
     unit_pair = in_core_order(core, unit, swapped(unit), 2)
     parts = jnp.moveaxis(unit_pair.reshape(2, n_z, key_rows, 2 * rows), 1, 0)
-    landed = exchange(parts.reshape(n_z, 2 * key_rows, 2 * rows), Z)
+    parts = parts.reshape(n_z, 2 * key_rows, 2 * rows)
+    parts, lm_weight = lax.optimization_barrier((parts, lm_weight))
+    lm_other = swapped(lm_weight)
+    landed = exchange(parts, Z)
 
     both = state_sums(landed, state)
+    both, lm_weight, lm_other = lax.optimization_barrier((both, lm_weight, lm_other))
+    lm_both = jnp.concatenate([lm_weight, lm_other], axis=1)
     both = exchange(both.reshape(n_z, 2 * rows, 2 * half), Z)
     both = jnp.sum(both.astype(jnp.float32), axis=0)
 
@@ -197,17 +202,17 @@
     ids = lax.dynamic_index_in_dim(token_ids.reshape(n_z, 2, rows), core, 1, False)
     ids = lax.dynamic_slice_in_dim(jnp.concatenate([ids, ids]), zed, n_z, 0).T
 
+    own_start = ((head * 2 + core) * n_z + zed) * vocab_dev
+    other_start = ((head * 2 + 1 - core) * n_z + zed) * vocab_dev
+
     def statistics(block, ids):
-        found = []
-        for weight, owner in ((lm_weight, core), (lm_other, 1 - core)):
-            logits = jnp.dot(block, weight, preferred_element_type=jnp.float32)
-            start = ((head * 2 + owner) * n_z + zed) * vocab_dev
-            hits = lax.broadcasted_iota(jnp.int32, logits.shape, 1) + start == ids
-            picked = jnp.sum(jnp.where(hits, logits, jnp.zeros_like(logits)), axis=1)
-            top = jnp.max(logits, axis=1)
-            expo = jnp.exp(logits - top[:, None])
-            found.append((top, jnp.sum(expo, axis=1), jnp.sum(expo * logits, axis=1), picked))
-        return jnp.stack(merged([jnp.stack(s) for s in zip(*found)], 0))
+        logits = jnp.dot(block, lm_both, preferred_element_type=jnp.float32)
+        at = lax.broadcasted_iota(jnp.int32, logits.shape, 1)
+        at = at + jnp.where(at < vocab_dev, own_start, other_start - vocab_dev)
+        picked = jnp.sum(jnp.where(at == ids, logits, jnp.zeros_like(logits)), axis=1)
+        top = jnp.max(logits, axis=1)
+        expo = jnp.exp(logits - top[:, None])
+        return jnp.stack([top, jnp.sum(expo, axis=1), jnp.sum(expo * logits, axis=1), picked])
 
     def along_z(block, step):
         return lax.ppermute(block, Z, [(k, (k + step) % n_z) for k in range(n_z)])
@@ -250,6 +255,7 @@
     key_k = jnp.moveaxis(landed[:, key_rows:], 0, 1).reshape(key_rows, batch)
     new_state = decay * state + key_k.astype(jnp.float32)[:, None, :] * back[None]
 
+    shared, new_state = lax.optimization_barrier((shared, new_state))
     top, total, weighted, picked = merged(jnp.moveaxis(shared, 1, 0), 0)
     lse = top + jnp.log(total)
     mine = jnp.stack([picked - lse, lse - weighted / total])

time: 185 us -> 185 us (level)
  blocking collectives: 14.1 us -> 0 us
  matrix products: 22.1 us -> 15 us
  starting transfers between devices: 62.5 us -> 68.7 us
  local copies, waits for them, and re-layouts: 11.4 us -> 17.5 us
  waiting for transfers between devices: 41.1 us -> 47.1 us
  Pallas kernels: 2.28 us -> 4.51 us
    all_to_all x1 -> x0, blocking collectives: 14.1 us -> none  [exchange(): return lax.all_to_all(blocks, axes, split_axis=0, concat_axis=0, tiled=True)]
    dot_general x10 -> x5, matrix products: 15.9 us -> 7.94 us  [statistics(): logits = jnp.dot(block, lm_both, preferred_element_type=jnp.float32)]
    ppermute x14, starting transfers between devices: 14.8 us -> 19.2 us  [along_z(): return lax.ppermute(block, Z, [(k, (k + step) % n_z) for k in range(n_z)])]
    all_to_all x5 -> x6, waiting for transfers between devices: 34.4 us -> 38.7 us  [exchange(): return lax.all_to_all(blocks, axes, split_axis=0, concat_axis=0, tiled=True)]
    unnamed x31 -> x57, local copies, waits for them, and re-layouts: 3.14 us -> 6.08 us
    pallas_call x1, Pallas kernels: 2.28 us -> 4.51 us  [state_sums(): pl.pallas_call(state_sums_kernel, grid=(batch // lanes,), in_specs=[pl.Bl...]
    all_to_all x5 -> x6, starting transfers between devices: 27.6 us -> 29.3 us  [exchange(): return lax.all_to_all(blocks, axes, split_axis=0, concat_axis=0, tiled=True)]
  transfers between devices with their start and end apart: 32 -> 33, of which waited for: 11 -> 12; matrix products, arithmetic and copies ran while one was open for 19% -> 17% of each run, Pallas kernels for 1% -> 2%
where the time goes in v4:
time: 185 us; the launch traced here: 184 us
  starting transfers between devices  68.7 us (37%)
  waiting for transfers between devices  47.1 us (25%)
  local copies, waits for them, and re-layouts  17.5 us (9%)
  other arithmetic  15.8 us (9%)
  matrix products  15 us (8%)
  between operations  14.9 us (8%)
  Pallas kernels  4.51 us (2%)
    all_to_all x6, waiting for transfers between devices, exchange(): return lax.all_to_all(blocks, axes, split_axis=0, concat_axis=0, tiled=True)  38.7 us
    all_to_all x6, starting transfers between devices, exchange(): return lax.all_to_all(blocks, axes, split_axis=0, concat_axis=0, tiled=True)  29.3 us
    ppermute x12, starting transfers between devices, swapped(): return lax.ppermute(array, CORE, [(0, 1), (1, 0)])  20.1 us
    ppermute x14, starting transfers between devices, along_z(): return lax.ppermute(block, Z, [(k, (k + step) % n_z) for k in range(n_z)])  19.2 us
    dot_general x5, matrix products, statistics(): logits = jnp.dot(block, lm_both, preferred_element_type=jnp.float32)  7.94 us
    unnamed x57, local copies, waits for them, and re-layouts  6.08 us
    add x1, other arithmetic, per_device(): decay * state + key_k.astype(jnp.float32)[:, None, :] * back[None]  5.14 us
    dot_general x1, matrix products, per_device(): jnp.dot(mixed_full, out_full, preferred_element_type=jnp.float32)  5.09 us
  transfers between devices with their start and end apart: 33, of which 12 were waited for; matrix products, arithmetic and copies ran while one was open for 17% of the time, Pallas kernels for 2%

profile of v4, /device:TPU:1, one launch (start us, length us, event | category | flops | bytes accessed | tf_op | source)
XLA Modules:
  0.0 183.5 jit_solution(14662659382627487294)
XLA Ops:
  7.9 3.3 %collective-permute-start = (bf16[144,64]{0,1:T(8,128)(2,1)}, bf16[144,64]{0,1:T(8,128)(2,1)S(1)}, u32[]{:S(2)}, u32[]{:S(2)}) collective-permute-start(bf16[144,64]{0,1:T(8,128)(2,1)} %param.17), channel_id=1, source_target_pairs={{0,8},{8,0},{1,9},{9,1},{2,10},{10,2},{3,11},{11,3},{4,12},{12,4},... | collective-permute-start | bytes 55304 | tf_op jit(solution)/shard_map/ppermute | solution.py:24
  11.3 1.2 collective-permute-done.1
  13.4 0.8 broadcast_select_fusion.4
  15.5 1.3 pad_maximum_fusion
  16.8 0.8 broadcast_in_dim.58
  17.6 5.0 %all-to-all-start = ((bf16[16,73,128]{2,1,0:T(8,128)(2,1)}), bf16[16,73,128]{2,1,0:T(8,128)(2,1)S(1)}, u32[]{:S(2)}, u32[]{:S(2)}) async-start(bf16[16,73,128]{2,1,0:T(8,128)(2,1)} %broadcast_in_dim.58), calls=%async_computation | async-start | bytes 655360 | tf_op jit(solution)/shard_map/all_to_all | solution.py:28
  22.8 8.0 %all-to-all-done = bf16[16,73,128]{2,1,0:T(8,128)(2,1)S(1)} async-done(((bf16[16,73,128]{2,1,0:T(8,128)(2,1)}), bf16[16,73,128]{2,1,0:T(8,128)(2,1)S(1)}, u32[]{:S(2)}, u32[]{:S(2)}) %all-to-all-start) | async-done | bytes 299040 | tf_op jit(solution)/shard_map/all_to_all | solution.py:28
  32.3 2.1 %collective-permute-start.6 = (bf16[2,128,72]{2,1,0:T(8,128)(2,1)S(1)}, bf16[2,128,72]{2,1,0:T(8,128)(2,1)S(1)}, u32[]{:S(2)}, u32[]{:S(2)}) collective-permute-start(bf16[2,128,72]{2,1,0:T(8,128)(2,1)S(1)} %get-tuple-element.66), channel_id=1, source_target_pairs={{0,8},{8,0},{1,9},{9,1},{2,10},{10,2},{3,11},{11,3},{4,12},{12,4},... | collective-permute-start | bytes 110600 | tf_op jit(solution)/shard_map/ppermute | solution.py:24
  34.4 0.9 collective-permute-done.6
  39.1 1.1 fusion.34
  41.3 8.6 %all-to-all-start.1 = ((bf16[8,32,144]{2,1,0:T(8,128)(2,1)}), bf16[8,32,144]{2,1,0:T(8,128)(2,1)S(1)}, u32[]{:S(2)}, u32[]{:S(2)}) async-start(bf16[8,32,144]{2,1,0:T(8,128)(2,1)} %bitcast.16), calls=%async_computation.1 | async-start | bytes 262144 | tf_op jit(solution)/shard_map/all_to_all | solution.py:28
  50.0 7.9 %all-to-all-done.1.landed_ref = bf16[8,32,144]{2,1,0:T(8,128)(2,1)S(1)} async-done(((bf16[8,32,144]{2,1,0:T(8,128)(2,1)}), bf16[8,32,144]{2,1,0:T(8,128)(2,1)S(1)}, u32[]{:S(2)}, u32[]{:S(2)}) %all-to-all-start.1) | async-done | bytes 73760 | tf_op jit(solution)/shard_map/all_to_all | solution.py:28
  58.5 4.5 %shard_map.192 = bf16[1152,128]{1,0:T(8,128)(2,1)} custom-call(bf16[8,32,144]{2,1,0:T(8,128)(2,1)} %copy-done.1, f32[16,64,1152]{2,1,0:T(8,128)} %state_ref.1), custom_call_target="tpu_custom_call" | custom-call | flops 4718592 | bytes 4718592 | tf_op jit(solution)/shard_map/pallas_call | solution.py:79
  63.0 3.4 %all-to-all-start.2 = ((bf16[8,144,128]{2,1,0:T(8,128)(2,1)}), bf16[8,144,128]{2,1,0:T(8,128)(2,1)S(1)}, u32[]{:S(2)}, u32[]{:S(2)}) async-start(bf16[8,144,128]{2,1,0:T(8,128)(2,1)} %bitcast.209), calls=%async_computation.2 | async-start | bytes 589824 | tf_op jit(solution)/shard_map/all_to_all | solution.py:28
  67.1 3.6 %constant_dynamic-update-slice_fusion.1 = bf16[2048,1280]{1,0:T(8,128)(2,1)} fusion(bf16[2048,640]{1,0:T(8,128)(2,1)} %param.31), kind=kLoop, calls=%fused_computation.116 | loop fusion | bytes 5242880
  70.7 5.3 %all-to-all-done.2 = bf16[8,144,128]{2,1,0:T(8,128)(2,1)S(1)} async-done(((bf16[8,144,128]{2,1,0:T(8,128)(2,1)}), bf16[8,144,128]{2,1,0:T(8,128)(2,1)S(1)}, u32[]{:S(2)}, u32[]{:S(2)}) %all-to-all-start.2) | async-done | bytes 294944 | tf_op jit(solution)/shard_map/all_to_all | solution.py:28
  76.8 4.0 %collective-permute-start.8 = (f32[72,128]{0,1:T(8,128)S(1)}, f32[72,128]{0,1:T(8,128)S(1)}, u32[]{:S(2)}, u32[]{:S(2)}) collective-permute-start(f32[72,128]{0,1:T(8,128)S(1)} %copy.148), channel_id=1, source_target_pairs={{0,8},{8,0},{1,9},{9,1},{2,10},{10,2},{3,11},{11,3},{4,12},{12,4},... | collective-permute-start | bytes 110600 | tf_op jit(solution)/shard_map/ppermute | solution.py:24
  80.8 0.9 constant_dynamic-slice_fusion
  82.6 0.8 multiply_convert_fusion.1
  83.5 0.8 broadcast_in_dim.60
  84.2 3.9 %all-to-all-start.3 = ((bf16[16,72,128]{2,1,0:T(8,128)(2,1)}), bf16[16,72,128]{2,1,0:T(8,128)(2,1)S(1)}, u32[]{:S(2)}, u32[]{:S(2)}) async-start(bf16[16,72,128]{2,1,0:T(8,128)(2,1)} %broadcast_in_dim.60), calls=%async_computation.3 | async-start | bytes 589824 | tf_op jit(solution)/shard_map/all_to_all | solution.py:28
  88.1 1.8 constant_dynamic-update-slice_fusion
  89.9 0.8 dynamic-slice_select_fusion.1
  90.7 5.4 %all-to-all-done.3 = bf16[16,72,128]{2,1,0:T(8,128)(2,1)S(1)} async-done(((bf16[16,72,128]{2,1,0:T(8,128)(2,1)}), bf16[16,72,128]{2,1,0:T(8,128)(2,1)S(1)}, u32[]{:S(2)}, u32[]{:S(2)}) %all-to-all-start.3) | async-done | bytes 294944 | tf_op jit(solution)/shard_map/all_to_all | solution.py:28
  96.0 5.1 %multiply_reduce_fusion.3 = (f32[72]{0:T(128)S(1)}, f32[72,2048]{1,0:T(8,128)S(1)}) fusion(bf16[2048,2048]{1,0:T(8,128)(2,1)} %all-gather.2.cloned.1.call-done, bf16[16,73,128]{2,1,0:T(8,128)(2,1)S(1)} %all-to-all-done, bf16[16,72,128]{2,1,0:T(8,128)(2,1)S(1)} %all-to-all-done.3), kind=kOutput, calls=%fused_computation.50 | convolution fusion | flops 604569536 | bytes 9568544 | tf_op jit(solution)/shard_map/dot_general | solution.py:198
  101.9 2.4 %collective-permute-start.11 = (bf16[72,1024]{1,0:T(8,128)(2,1)S(1)}, bf16[72,1024]{1,0:T(8,128)(2,1)S(1)}, u32[]{:S(2)}, u32[]{:S(2)}) collective-permute-start(bf16[72,1024]{1,0:T(8,128)(2,1)S(1)} %get-tuple-element.69), channel_id=1, source_target_pairs={{0,7},{1,0},{2,1},{3,2},{4,3},{5,4},{6,5},{7,6},{8,15},{9,8},{10,9... | collective-permute-start | bytes 442376 | tf_op jit(solution)/shard_map/ppermute | solution.py:218
  104.2 2.7 %collective-permute-start.13 = (bf16[72,1024]{1,0:T(8,128)(2,1)S(1)}, bf16[72,1024]{1,0:T(8,128)(2,1)S(1)}, u32[]{:S(2)}, u32[]{:S(2)}) collective-permute-start(bf16[72,1024]{1,0:T(8,128)(2,1)S(1)} %get-tuple-element.70), channel_id=1, source_target_pairs={{0,7},{1,0},{2,1},{3,2},{4,3},{5,4},{6,5},{7,6},{8,15},{9,8},{10,9... | collective-permute-start | bytes 442376 | tf_op jit(solution)/shard_map/ppermute | solution.py:218
  106.9 3.6 %fusion.95 = (f32[72]{0:T(128)S(1)}, f32[72,1280]{1,0:T(8,128)S(1)}) fusion(bf16[72,2048]{1,0:T(8,128)(2,1)S(1)} %multiply_convert_fusion, bf16[2048,1280]{1,0:T(8,128)(2,1)} %constant_dynamic-update-slice_fusion), kind=kOutput, calls=%fused_computation.237 | convolution fusion | flops 377579456 | bytes 5906720 | tf_op jit(solution)/shard_map/dot_general | solution.py:209
  110.7 2.7 %collective-permute-start.15 = (bf16[72,1024]{1,0:T(8,128)(2,1)S(1)}, bf16[72,1024]{1,0:T(8,128)(2,1)S(1)}, u32[]{:S(2)}, u32[]{:S(2)}) collective-permute-start(bf16[72,1024]{1,0:T(8,128)(2,1)S(1)} %collective-permute-done.11), channel_id=1, source_target_pairs={{0,7},{1,0},{2,1},{3,2},{4,3},{5,4},{6,5},{7,6},{8,15},{9,8},{10,9... | collective-permute-start | bytes 442376 | tf_op jit(solution)/shard_map/ppermute | solution.py:218
  113.3 2.7 %collective-permute-start.17 = (bf16[72,1024]{1,0:T(8,128)(2,1)S(1)}, bf16[72,1024]{1,0:T(8,128)(2,1)S(1)}, u32[]{:S(2)}, u32[]{:S(2)}) collective-permute-start(bf16[72,1024]{1,0:T(8,128)(2,1)S(1)} %collective-permute-done.13), channel_id=1, source_target_pairs={{0,7},{1,0},{2,1},{3,2},{4,3},{5,4},{6,5},{7,6},{8,15},{9,8},{10,9... | collective-permute-start | bytes 442376 | tf_op jit(solution)/shard_map/ppermute | solution.py:218
  116.0 1.1 fusion.98
  117.2 2.7 %collective-permute-start.19 = (bf16[72,1024]{1,0:T(8,128)(2,1)S(1)}, bf16[72,1024]{1,0:T(8,128)(2,1)S(1)}, u32[]{:S(2)}, u32[]{:S(2)}) collective-permute-start(bf16[72,1024]{1,0:T(8,128)(2,1)S(1)} %collective-permute-done.15), channel_id=1, source_target_pairs={{0,7},{1,0},{2,1},{3,2},{4,3},{5,4},{6,5},{7,6},{8,15},{9,8},{10,9... | collective-permute-start | bytes 442376 | tf_op jit(solution)/shard_map/ppermute | solution.py:218
  119.8 2.7 %collective-permute-start.21 = (bf16[72,1024]{1,0:T(8,128)(2,1)S(1)}, bf16[72,1024]{1,0:T(8,128)(2,1)S(1)}, u32[]{:S(2)}, u32[]{:S(2)}) collective-permute-start(bf16[72,1024]{1,0:T(8,128)(2,1)S(1)} %collective-permute-done.17), channel_id=1, source_target_pairs={{0,7},{1,0},{2,1},{3,2},{4,3},{5,4},{6,5},{7,6},{8,15},{9,8},{10,9... | collective-permute-start | bytes 442376 | tf_op jit(solution)/shard_map/ppermute | solution.py:218
  122.5 1.1 fusion.97
  124.1 1.9 %collective-permute-done.20 = bf16[72,1024]{1,0:T(8,128)(2,1)S(1)} collective-permute-done((bf16[72,1024]{1,0:T(8,128)(2,1)S(1)}, bf16[72,1024]{1,0:T(8,128)(2,1)S(1)}, u32[]{:S(2)}, u32[]{:S(2)}) %collective-permute-start.20) | collective-permute-done | bytes 147488 | tf_op jit(solution)/shard_map/ppermute | solution.py:218
  125.9 1.1 fusion.96
  127.0 0.9 fusion
  128.1 2.7 %collective-permute-start.23 = (bf16[72,1024]{1,0:T(8,128)(2,1)S(1)}, bf16[72,1024]{1,0:T(8,128)(2,1)S(1)}, u32[]{:S(2)}, u32[]{:S(2)}) collective-permute-start(bf16[72,1024]{1,0:T(8,128)(2,1)S(1)} %collective-permute-done.21), channel_id=1, source_target_pairs={{0,7},{1,0},{2,1},{3,2},{4,3},{5,4},{6,5},{7,6},{8,15},{9,8},{10,9... | collective-permute-start | bytes 442376 | tf_op jit(solution)/shard_map/ppermute | solution.py:218
  130.8 2.5 %collective-permute-done.22 = bf16[72,1024]{1,0:T(8,128)(2,1)S(1)} collective-permute-done((bf16[72,1024]{1,0:T(8,128)(2,1)S(1)}, bf16[72,1024]{1,0:T(8,128)(2,1)S(1)}, u32[]{:S(2)}, u32[]{:S(2)}) %collective-permute-start.22) | collective-permute-done | bytes 147488 | tf_op jit(solution)/shard_map/ppermute | solution.py:218
  133.3 1.1 fusion.94
  135.9 0.8 broadcast_in_dim.63
  136.6 3.9 %all-to-all-start.4 = ((f32[8,96,128]{2,1,0:T(8,128)}), f32[8,96,128]{2,1,0:T(8,128)S(1)}, u32[]{:S(2)}, u32[]{:S(2)}) async-start(f32[8,96,128]{2,1,0:T(8,128)} %broadcast_in_dim.63), calls=%async_computation.4 | async-start | bytes 786432 | tf_op jit(solution)/shard_map/all_to_all | solution.py:28
  140.8 10.5 %all-to-all-done.4 = f32[8,96,128]{2,1,0:T(8,128)S(1)} async-done(((f32[8,96,128]{2,1,0:T(8,128)}), f32[8,96,128]{2,1,0:T(8,128)S(1)}, u32[]{:S(2)}, u32[]{:S(2)}) %all-to-all-start.4) | async-done | bytes 393248 | tf_op jit(solution)/shard_map/all_to_all | solution.py:28
  154.0 4.4 %all-to-all-start.5 = ((f32[16,4,576]{2,1,0:T(4,128)}), f32[16,4,576]{2,1,0:T(4,128)S(1)}, u32[]{:S(2)}, u32[]{:S(2)}) async-start(f32[16,4,576]{2,1,0:T(4,128)} %broadcast_in_dim.65), calls=%async_computation.5 | async-start | bytes 327680 | tf_op jit(solution)/shard_map/all_to_all | solution.py:28
  158.5 5.1 %multiply_add_fusion = f32[16,64,1152]{2,1,0:T(8,128)} fusion(f32[16,64,1152]{2,1,0:T(8,128)} %state_ref.1, f32[64,1152]{1,0:T(8,128)S(1)} %mul.287, f32[16,1152]{1,0:T(8,128)S(1)} %reshape.179, f32[1152]{0:T(1024)S(1)} %mul.283), kind=kLoop, calls=%fused_computation | loop fusion | flops 3538944 | bytes 9810432 | tf_op jit(solution)/shard_map/add | solution.py:256
  163.6 1.6 all-to-all-done.5
  165.5 8.7 %collective-permute-start.25 = (f32[2,576]{1,0:T(2,128)S(1)}, f32[2,576]{1,0:T(2,128)S(1)}, u32[]{:S(2)}, u32[]{:S(2)}) collective-permute-start(f32[2,576]{1,0:T(2,128)S(1)} %pad_maximum_fusion.8), channel_id=1, source_target_pairs={{0,8},{8,0},{1,9},{9,1},{2,10},{10,2},{3,11},{11,3},{4,12},{12,4},... | collective-permute-start | bytes 13832 | tf_op jit(solution)/shard_map/ppermute | solution.py:24
  174.2 0.8 collective-permute-done.25
  (197 shorter events, 20.0 us)
Async XLA Ops:
  7.2 15.5 %copy-start.14 = (bf16[2048]{0:T(1024)(128)(2,1)S(1)}, bf16[2048]{0:T(1024)(128)(2,1)}, u32[]{:S(2)}) copy-start(bf16[2048]{0:T(1024)(128)(2,1)} %param.19) | copy-start | bytes 12292
  7.2 88.9 %all-gather.2.cloned.1.call-start = ((), (), s32[]{:S(2)}) async-start(), calls=%async_computation.6 | async-start | bytes 8650752 | tf_op jit(solution)/shard_map/all_gather | solution.py:129
  7.9 5.5 %collective-permute-start = (bf16[144,64]{0,1:T(8,128)(2,1)}, bf16[144,64]{0,1:T(8,128)(2,1)S(1)}, u32[]{:S(2)}, u32[]{:S(2)}) collective-permute-start(bf16[144,64]{0,1:T(8,128)(2,1)} %param.17), channel_id=1, source_target_pairs={{0,8},{8,0},{1,9},{9,1},{2,10},{10,2},{3,11},{11,3},{4,12},{12,4},... | collective-permute-start | bytes 55304 | tf_op jit(solution)/shard_map/ppermute | solution.py:24
  11.2 1.3 collective-permute-start.1
  14.4 8.3 %collective-permute-start.2 = (bf16[2048,64]{0,1:T(8,128)(2,1)}, bf16[2048,64]{0,1:T(8,128)(2,1)S(1)}, u32[]{:S(2)}, u32[]{:S(2)}) collective-permute-start(bf16[2048,64]{0,1:T(8,128)(2,1)} %param.20), channel_id=1, source_target_pairs={{0,8},{8,0},{1,9},{9,1},{2,10},{10,2},{3,11},{11,3},{4,12},{12,4},... | collective-permute-start | bytes 786440 | tf_op jit(solution)/shard_map/ppermute | solution.py:24
  14.7 8.0 %collective-permute-start.3 = (bf16[2048,64]{0,1:T(8,128)(2,1)}, bf16[2048,64]{0,1:T(8,128)(2,1)S(1)}, u32[]{:S(2)}, u32[]{:S(2)}) collective-permute-start(bf16[2048,64]{0,1:T(8,128)(2,1)} %param.21), channel_id=1, source_target_pairs={{0,8},{8,0},{1,9},{9,1},{2,10},{10,2},{3,11},{11,3},{4,12},{12,4},... | collective-permute-start | bytes 786440 | tf_op jit(solution)/shard_map/ppermute | solution.py:24
  15.0 7.7 %collective-permute-start.4 = (bf16[2048,64]{0,1:T(8,128)(2,1)}, bf16[2048,64]{0,1:T(8,128)(2,1)S(1)}, u32[]{:S(2)}, u32[]{:S(2)}) collective-permute-start(bf16[2048,64]{0,1:T(8,128)(2,1)} %param.22), channel_id=1, source_target_pairs={{0,8},{8,0},{1,9},{9,1},{2,10},{10,2},{3,11},{11,3},{4,12},{12,4},... | collective-permute-start | bytes 786440 | tf_op jit(solution)/shard_map/ppermute | solution.py:24
  15.2 7.5 %collective-permute-start.5 = (bf16[2048,64]{0,1:T(8,128)(2,1)}, bf16[2048,64]{0,1:T(8,128)(2,1)S(1)}, u32[]{:S(2)}, u32[]{:S(2)}) collective-permute-start(bf16[2048,64]{0,1:T(8,128)(2,1)} %param.23), channel_id=1, source_target_pairs={{0,8},{8,0},{1,9},{9,1},{2,10},{10,2},{3,11},{11,3},{4,12},{12,4},... | collective-permute-start | bytes 786440 | tf_op jit(solution)/shard_map/ppermute | solution.py:24
  17.6 13.2 %all-to-all-start = ((bf16[16,73,128]{2,1,0:T(8,128)(2,1)}), bf16[16,73,128]{2,1,0:T(8,128)(2,1)S(1)}, u32[]{:S(2)}, u32[]{:S(2)}) async-start(bf16[16,73,128]{2,1,0:T(8,128)(2,1)} %broadcast_in_dim.58), calls=%async_computation | async-start | bytes 655360 | tf_op jit(solution)/shard_map/all_to_all | solution.py:28
  31.2 5.3 %copy-start.8 = (s32[1152]{0:T(1024)S(1)}, s32[1152]{0:T(1024)}, u32[]{:S(2)}) copy-start(s32[1152]{0:T(1024)} %param.32) | copy-start | bytes 13828
  31.2 5.4 %copy-start.20 = (f32[16]{0:T(128)S(1)}, f32[16]{0:T(128)}, u32[]{:S(2)}) copy-start(f32[16]{0:T(128)} %param.26) | copy-start | bytes 196
  31.2 7.9 %copy-start.19 = (bf16[2048,16]{0,1:T(8,128)(2,1)S(1)}, bf16[2048,16]{0,1:T(8,128)(2,1)}, u32[]{:S(2)}) copy-start(bf16[2048,16]{0,1:T(8,128)(2,1)} %param.25) | copy-start | bytes 196612
  31.3 8.9 %copy-start.18 = (f32[16]{0:T(128)S(1)}, f32[16]{0:T(128)}, u32[]{:S(2)}) copy-start(f32[16]{0:T(128)} %param.27) | copy-start | bytes 196
  32.3 3.0 %collective-permute-start.6 = (bf16[2,128,72]{2,1,0:T(8,128)(2,1)S(1)}, bf16[2,128,72]{2,1,0:T(8,128)(2,1)S(1)}, u32[]{:S(2)}, u32[]{:S(2)}) collective-permute-start(bf16[2,128,72]{2,1,0:T(8,128)(2,1)S(1)} %get-tuple-element.66), channel_id=1, source_target_pairs={{0,8},{8,0},{1,9},{9,1},{2,10},{10,2},{3,11},{11,3},{4,12},{12,4},... | collective-permute-start | bytes 110600 | tf_op jit(solution)/shard_map/ppermute | solution.py:24
  36.1 26.9 %collective-permute-start.7 = (bf16[2048,640]{1,0:T(8,128)(2,1)}, bf16[2048,640]{1,0:T(8,128)(2,1)S(1)}, u32[]{:S(2)}, u32[]{:S(2)}) collective-permute-start(bf16[2048,640]{1,0:T(8,128)(2,1)} %param.31), channel_id=1, source_target_pairs={{0,8},{8,0},{1,9},{9,1},{2,10},{10,2},{3,11},{11,3},{4,12},{12,4},... | collective-permute-start | bytes 7864328 | tf_op jit(solution)/shard_map/ppermute | solution.py:24
  41.0 25.5 %collective-permute-start.24 = (f32[1,72]{1,0:T(1,128)S(1)}, f32[1,72]{1,0:T(1,128)S(1)}, u32[]{:S(2)}, u32[]{:S(2)}) collective-permute-start(f32[1,72]{1,0:T(1,128)S(1)} %fusion.82), channel_id=1, source_target_pairs={{0,8},{8,0},{1,9},{9,1},{2,10},{10,2},{3,11},{11,3},{4,12},{12,4},... | collective-permute-start | bytes 872 | tf_op jit(solution)/shard_map/ppermute | solution.py:24
  41.3 16.6 %all-to-all-start.1 = ((bf16[8,32,144]{2,1,0:T(8,128)(2,1)}), bf16[8,32,144]{2,1,0:T(8,128)(2,1)S(1)}, u32[]{:S(2)}, u32[]{:S(2)}) async-start(bf16[8,32,144]{2,1,0:T(8,128)(2,1)} %bitcast.16), calls=%async_computation.1 | async-start | bytes 262144 | tf_op jit(solution)/shard_map/all_to_all | solution.py:28
  50.0 32.0 %copy-start.9 = (f32[72]{0:T(128)}, f32[72]{0:T(128)S(1)}, u32[]{:S(2)}) copy-start(f32[72]{0:T(128)S(1)} %get-tuple-element.124) | copy-start | bytes 868
  50.0 32.0 %copy-start.10 = (f32[72]{0:T(128)}, f32[72]{0:T(128)S(1)}, u32[]{:S(2)}) copy-start(f32[72]{0:T(128)S(1)} %get-tuple-element.125) | copy-start | bytes 868
  63.0 13.0 %all-to-all-start.2 = ((bf16[8,144,128]{2,1,0:T(8,128)(2,1)}), bf16[8,144,128]{2,1,0:T(8,128)(2,1)S(1)}, u32[]{:S(2)}, u32[]{:S(2)}) async-start(bf16[8,144,128]{2,1,0:T(8,128)(2,1)} %bitcast.209), calls=%async_computation.2 | async-start | bytes 589824 | tf_op jit(solution)/shard_map/all_to_all | solution.py:28
  76.8 5.1 %collective-permute-start.8 = (f32[72,128]{0,1:T(8,128)S(1)}, f32[72,128]{0,1:T(8,128)S(1)}, u32[]{:S(2)}, u32[]{:S(2)}) collective-permute-start(f32[72,128]{0,1:T(8,128)S(1)} %copy.148), channel_id=1, source_target_pairs={{0,8},{8,0},{1,9},{9,1},{2,10},{10,2},{3,11},{11,3},{4,12},{12,4},... | collective-permute-start | bytes 110600 | tf_op jit(solution)/shard_map/ppermute | solution.py:24
  82.0 7.9 %collective-permute-start.9 = (f32[72,64]{0,1:T(8,128)S(1)}, f32[72,64]{0,1:T(8,128)}, u32[]{:S(2)}, u32[]{:S(2)}) collective-permute-start(f32[72,64]{0,1:T(8,128)S(1)} %constant_dynamic-slice_fusion.3), channel_id=1, source_target_pairs={{0,8},{8,0},{1,9},{9,1},{2,10},{10,2},{3,11},{11,3},{4,12},{12,4},... | collective-permute-start | bytes 55304 | tf_op jit(solution)/shard_map/ppermute | solution.py:24
  84.2 11.8 %all-to-all-start.3 = ((bf16[16,72,128]{2,1,0:T(8,128)(2,1)}), bf16[16,72,128]{2,1,0:T(8,128)(2,1)S(1)}, u32[]{:S(2)}, u32[]{:S(2)}) async-start(bf16[16,72,128]{2,1,0:T(8,128)(2,1)} %broadcast_in_dim.60), calls=%async_computation.3 | async-start | bytes 589824 | tf_op jit(solution)/shard_map/all_to_all | solution.py:28
  101.3 9.2 %collective-permute-start.10 = (bf16[72,1024]{1,0:T(8,128)(2,1)S(1)}, bf16[72,1024]{1,0:T(8,128)(2,1)S(1)}, u32[]{:S(2)}, u32[]{:S(2)}) collective-permute-start(bf16[72,1024]{1,0:T(8,128)(2,1)S(1)} %get-tuple-element.69), channel_id=1, source_target_pairs={{0,1},{1,2},{2,3},{3,4},{4,5},{5,6},{6,7},{7,0},{8,9},{9,10},{10,1... | collective-permute-start | bytes 442376 | tf_op jit(solution)/shard_map/ppermute | solution.py:218
  101.9 8.8 %collective-permute-start.11 = (bf16[72,1024]{1,0:T(8,128)(2,1)S(1)}, bf16[72,1024]{1,0:T(8,128)(2,1)S(1)}, u32[]{:S(2)}, u32[]{:S(2)}) collective-permute-start(bf16[72,1024]{1,0:T(8,128)(2,1)S(1)} %get-tuple-element.69), channel_id=1, source_target_pairs={{0,7},{1,0},{2,1},{3,2},{4,3},{5,4},{6,5},{7,6},{8,15},{9,8},{10,9... | collective-permute-start | bytes 442376 | tf_op jit(solution)/shard_map/ppermute | solution.py:218
  104.2 11.8 %copy-start = (bf16[2048,1280]{1,0:T(8,128)(2,1)S(1)}, bf16[2048,1280]{1,0:T(8,128)(2,1)}, u32[]{:S(2)}) copy-start(bf16[2048,1280]{1,0:T(8,128)(2,1)} %constant_dynamic-update-slice_fusion) | copy-start | bytes 15728644
  104.2 9.1 %collective-permute-start.12 = (bf16[72,1024]{1,0:T(8,128)(2,1)S(1)}, bf16[72,1024]{1,0:T(8,128)(2,1)S(1)}, u32[]{:S(2)}, u32[]{:S(2)}) collective-permute-start(bf16[72,1024]{1,0:T(8,128)(2,1)S(1)} %get-tuple-element.70), channel_id=1, source_target_pairs={{0,1},{1,2},{2,3},{3,4},{4,5},{5,6},{6,7},{7,0},{8,9},{9,10},{10,1... | collective-permute-start | bytes 442376 | tf_op jit(solution)/shard_map/ppermute | solution.py:218
  104.2 9.1 %collective-permute-start.13 = (bf16[72,1024]{1,0:T(8,128)(2,1)S(1)}, bf16[72,1024]{1,0:T(8,128)(2,1)S(1)}, u32[]{:S(2)}, u32[]{:S(2)}) collective-permute-start(bf16[72,1024]{1,0:T(8,128)(2,1)S(1)} %get-tuple-element.70), channel_id=1, source_target_pairs={{0,7},{1,0},{2,1},{3,2},{4,3},{5,4},{6,5},{7,6},{8,15},{9,8},{10,9... | collective-permute-start | bytes 442376 | tf_op jit(solution)/shard_map/ppermute | solution.py:218
  110.6 6.5 %collective-permute-start.14 = (bf16[72,1024]{1,0:T(8,128)(2,1)S(1)}, bf16[72,1024]{1,0:T(8,128)(2,1)S(1)}, u32[]{:S(2)}, u32[]{:S(2)}) collective-permute-start(bf16[72,1024]{1,0:T(8,128)(2,1)S(1)} %collective-permute-done.10), channel_id=1, source_target_pairs={{0,1},{1,2},{2,3},{3,4},{4,5},{5,6},{6,7},{7,0},{8,9},{9,10},{10,1... | collective-permute-start | bytes 442376 | tf_op jit(solution)/shard_map/ppermute | solution.py:218
  110.7 6.5 %collective-permute-start.15 = (bf16[72,1024]{1,0:T(8,128)(2,1)S(1)}, bf16[72,1024]{1,0:T(8,128)(2,1)S(1)}, u32[]{:S(2)}, u32[]{:S(2)}) collective-permute-start(bf16[72,1024]{1,0:T(8,128)(2,1)S(1)} %collective-permute-done.11), channel_id=1, source_target_pairs={{0,7},{1,0},{2,1},{3,2},{4,3},{5,4},{6,5},{7,6},{8,15},{9,8},{10,9... | collective-permute-start | bytes 442376 | tf_op jit(solution)/shard_map/ppermute | solution.py:218
  113.3 6.5 %collective-permute-start.16 = (bf16[72,1024]{1,0:T(8,128)(2,1)S(1)}, bf16[72,1024]{1,0:T(8,128)(2,1)S(1)}, u32[]{:S(2)}, u32[]{:S(2)}) collective-permute-start(bf16[72,1024]{1,0:T(8,128)(2,1)S(1)} %collective-permute-done.12), channel_id=1, source_target_pairs={{0,1},{1,2},{2,3},{3,4},{4,5},{5,6},{6,7},{7,0},{8,9},{9,10},{10,1... | collective-permute-start | bytes 442376 | tf_op jit(solution)/shard_map/ppermute | solution.py:218
  113.3 6.5 %collective-permute-start.17 = (bf16[72,1024]{1,0:T(8,128)(2,1)S(1)}, bf16[72,1024]{1,0:T(8,128)(2,1)S(1)}, u32[]{:S(2)}, u32[]{:S(2)}) collective-permute-start(bf16[72,1024]{1,0:T(8,128)(2,1)S(1)} %collective-permute-done.13), channel_id=1, source_target_pairs={{0,7},{1,0},{2,1},{3,2},{4,3},{5,4},{6,5},{7,6},{8,15},{9,8},{10,9... | collective-permute-start | bytes 442376 | tf_op jit(solution)/shard_map/ppermute | solution.py:218
  117.1 7.0 %collective-permute-start.18 = (bf16[72,1024]{1,0:T(8,128)(2,1)S(1)}, bf16[72,1024]{1,0:T(8,128)(2,1)S(1)}, u32[]{:S(2)}, u32[]{:S(2)}) collective-permute-start(bf16[72,1024]{1,0:T(8,128)(2,1)S(1)} %collective-permute-done.14), channel_id=1, source_target_pairs={{0,1},{1,2},{2,3},{3,4},{4,5},{5,6},{6,7},{7,0},{8,9},{9,10},{10,1... | collective-permute-start | bytes 442376 | tf_op jit(solution)/shard_map/ppermute | solution.py:218
  117.2 6.9 %collective-permute-start.19 = (bf16[72,1024]{1,0:T(8,128)(2,1)S(1)}, bf16[72,1024]{1,0:T(8,128)(2,1)S(1)}, u32[]{:S(2)}, u32[]{:S(2)}) collective-permute-start(bf16[72,1024]{1,0:T(8,128)(2,1)S(1)} %collective-permute-done.15), channel_id=1, source_target_pairs={{0,7},{1,0},{2,1},{3,2},{4,3},{5,4},{6,5},{7,6},{8,15},{9,8},{10,9... | collective-permute-start | bytes 442376 | tf_op jit(solution)/shard_map/ppermute | solution.py:218
  119.8 6.1 %collective-permute-start.20 = (bf16[72,1024]{1,0:T(8,128)(2,1)S(1)}, bf16[72,1024]{1,0:T(8,128)(2,1)S(1)}, u32[]{:S(2)}, u32[]{:S(2)}) collective-permute-start(bf16[72,1024]{1,0:T(8,128)(2,1)S(1)} %collective-permute-done.16), channel_id=1, source_target_pairs={{0,1},{1,2},{2,3},{3,4},{4,5},{5,6},{6,7},{7,0},{8,9},{9,10},{10,1... | collective-permute-start | bytes 442376 | tf_op jit(solution)/shard_map/ppermute | solution.py:218
  119.8 6.1 %collective-permute-start.21 = (bf16[72,1024]{1,0:T(8,128)(2,1)S(1)}, bf16[72,1024]{1,0:T(8,128)(2,1)S(1)}, u32[]{:S(2)}, u32[]{:S(2)}) collective-permute-start(bf16[72,1024]{1,0:T(8,128)(2,1)S(1)} %collective-permute-done.17), channel_id=1, source_target_pairs={{0,7},{1,0},{2,1},{3,2},{4,3},{5,4},{6,5},{7,6},{8,15},{9,8},{10,9... | collective-permute-start | bytes 442376 | tf_op jit(solution)/shard_map/ppermute | solution.py:218
  123.6 3.4 %copy-start.11 = (s32[144,1]{0,1:T(1,128)S(1)}, s32[144,1]{0,1:T(1,128)}, u32[]{:S(2)}) copy-start(s32[144,1]{0,1:T(1,128)} %pad_add_fusion.2) | copy-start | bytes 1732
  123.6 3.4 %copy-start.12 = (s32[144,1]{0,1:T(1,128)S(1)}, s32[144,1]{0,1:T(1,128)}, u32[]{:S(2)}) copy-start(s32[144,1]{0,1:T(1,128)} %get-tuple-element.142) | copy-start | bytes 1732
  128.0 5.3 %collective-permute-start.22 = (bf16[72,1024]{1,0:T(8,128)(2,1)S(1)}, bf16[72,1024]{1,0:T(8,128)(2,1)S(1)}, u32[]{:S(2)}, u32[]{:S(2)}) collective-permute-start(bf16[72,1024]{1,0:T(8,128)(2,1)S(1)} %collective-permute-done.18), channel_id=1, source_target_pairs={{0,1},{1,2},{2,3},{3,4},{4,5},{5,6},{6,7},{7,0},{8,9},{9,10},{10,1... | collective-permute-start | bytes 442376 | tf_op jit(solution)/shard_map/ppermute | solution.py:218
  128.1 5.2 %collective-permute-start.23 = (bf16[72,1024]{1,0:T(8,128)(2,1)S(1)}, bf16[72,1024]{1,0:T(8,128)(2,1)S(1)}, u32[]{:S(2)}, u32[]{:S(2)}) collective-permute-start(bf16[72,1024]{1,0:T(8,128)(2,1)S(1)} %collective-permute-done.21), channel_id=1, source_target_pairs={{0,7},{1,0},{2,1},{3,2},{4,3},{5,4},{6,5},{7,6},{8,15},{9,8},{10,9... | collective-permute-start | bytes 442376 | tf_op jit(solution)/shard_map/ppermute | solution.py:218
  130.8 3.6 %copy-start.16 = (s32[72]{0:T(128)S(1)}, s32[72]{0:T(128)}, u32[]{:S(2)}) copy-start(s32[72]{0:T(128)} %get-tuple-element.113) | copy-start | bytes 868
  130.8 3.6 %copy-start.17 = (s32[72]{0:T(128)S(1)}, s32[72]{0:T(128)}, u32[]{:S(2)}) copy-start(s32[72]{0:T(128)} %get-tuple-element.120) | copy-start | bytes 868
  130.8 4.8 %copy-start.15 = (f32[2,128]{1,0:T(2,128)S(1)}, f32[2,128]{1,0:T(2,128)}, u32[]{:S(2)}) copy-start(f32[2,128]{1,0:T(2,128)} %select_maximum_fusion.1) | copy-start | bytes 3076
  134.4 6.2 %copy-start.2 = (bf16[8,32,144]{2,1,0:T(8,128)(2,1)S(1)}, bf16[8,32,144]{2,1,0:T(8,128)(2,1)}, u32[]{:S(2)}) copy-start(bf16[8,32,144]{2,1,0:T(8,128)(2,1)} %copy-done.1) | copy-start | bytes 221188
  136.6 14.7 %all-to-all-start.4 = ((f32[8,96,128]{2,1,0:T(8,128)}), f32[8,96,128]{2,1,0:T(8,128)S(1)}, u32[]{:S(2)}, u32[]{:S(2)}) async-start(f32[8,96,128]{2,1,0:T(8,128)} %broadcast_in_dim.63), calls=%async_computation.4 | async-start | bytes 786432 | tf_op jit(solution)/shard_map/all_to_all | solution.py:28
  154.0 11.2 %all-to-all-start.5 = ((f32[16,4,576]{2,1,0:T(4,128)}), f32[16,4,576]{2,1,0:T(4,128)S(1)}, u32[]{:S(2)}, u32[]{:S(2)}) async-start(f32[16,4,576]{2,1,0:T(4,128)} %broadcast_in_dim.65), calls=%async_computation.5 | async-start | bytes 327680 | tf_op jit(solution)/shard_map/all_to_all | solution.py:28
  158.5 17.6 %copy-start.7 = (f32[1152]{0:T(1024)S(1)}, f32[1152]{0:T(1024)}, u32[]{:S(2)}) copy-start(f32[1152]{0:T(1024)} %param.33) | copy-start | bytes 13828
  165.5 9.5 %collective-permute-start.25 = (f32[2,576]{1,0:T(2,128)S(1)}, f32[2,576]{1,0:T(2,128)S(1)}, u32[]{:S(2)}, u32[]{:S(2)}) collective-permute-start(f32[2,576]{1,0:T(2,128)S(1)} %pad_maximum_fusion.8), channel_id=1, source_target_pairs={{0,8},{8,0},{1,9},{9,1},{2,10},{10,2},{3,11},{11,3},{4,12},{12,4},... | collective-permute-start | bytes 13832 | tf_op jit(solution)/shard_map/ppermute | solution.py:24
  (6 other events, 8.5 us)
Sparse Core Ops, SparseCore 0:
  10.6 62.7 all-gather.1

commit v5 on v4

--- a/solution.py
+++ b/solution.py
@@ -50,42 +50,46 @@
     )
 
 
-def state_sums_kernel(landed_ref, state_ref, out_ref, qk_ref):
+def state_sums_kernel(landed_ref, state_ref, out_ref, qk_ref, held_ref, sems):
     pieces, both, width = landed_ref.shape
-    key_rows, half, lanes = state_ref.shape
-    step = pl.program_id(0)
-
-    @pl.when(step == 0)
-    def _():
-        for k in range(pieces):
-            qk_ref[:, k * width : (k + 1) * width] = landed_ref[k].astype(jnp.float32)
-
-    for part in range(lanes // 128):
-        at = pl.ds(pl.multiple_of(step * lanes + part * 128, 128), 128)
-        chunk = qk_ref[:, at]
-        answer = jnp.zeros((half, 128), jnp.float32)
-        recall = jnp.zeros((half, 128), jnp.float32)
-        for k in range(key_rows):
-            tile = state_ref[k, :, part * 128 : (part + 1) * 128]
-            answer += tile * chunk[k : k + 1]
-            recall += tile * chunk[key_rows + k : key_rows + k + 1]
-        pair = jnp.concatenate([recall, answer], axis=0).T
-        out_ref[part * 128 : (part + 1) * 128, :] = pair.astype(jnp.bfloat16)
+    chunks, key_rows, half, lanes = held_ref.shape
+    copies = []
+    for c in range(chunks):
+        copies.append(
+            pltpu.make_async_copy(
+                state_ref.at[:, :, pl.ds(c * lanes, lanes)], held_ref.at[c], sems.at[c]
+            )
+        )
+        copies[c].start()
+    for k in range(pieces):
+        qk_ref[:, k * width : (k + 1) * width] = landed_ref[k].astype(jnp.float32)
+    for c in range(chunks):
+        copies[c].wait()
+        for at in range(0, lanes, 128):
+            chunk = qk_ref[:, c * lanes + at : c * lanes + at + 128]
+            answer = jnp.zeros((half, 128), jnp.float32)
+            recall = jnp.zeros((half, 128), jnp.float32)
+            for k in range(key_rows):
+                tile = held_ref[c, k, :, at : at + 128]
+                answer += tile * chunk[k : k + 1]
+                recall += tile * chunk[key_rows + k : key_rows + k + 1]
+            pair = jnp.concatenate([recall, answer], axis=0).T
+            out_ref[c * lanes + at : c * lanes + at + 128, :] = pair.astype(jnp.bfloat16)
 
 
 def state_sums(landed, state):
     key_rows, half, batch = state.shape
-    lanes = 384
+    chunks = 3
     return pl.pallas_call(
         state_sums_kernel,
-        grid=(batch // lanes,),
-        in_specs=[
-            pl.BlockSpec(landed.shape, lambda i: (0, 0, 0)),
-            pl.BlockSpec((key_rows, half, lanes), lambda i: (0, 0, i)),
+        in_specs=[pl.BlockSpec(memory_space=pltpu.VMEM), pl.BlockSpec(memory_space=pl.ANY)],
+        out_specs=pl.BlockSpec(memory_space=pltpu.VMEM),
+        out_shape=jax.ShapeDtypeStruct((batch, 2 * half), jnp.bfloat16),
+        scratch_shapes=[
+            pltpu.VMEM((2 * key_rows, batch), jnp.float32),
+            pltpu.VMEM((chunks, key_rows, half, batch // chunks), jnp.float32),
+            pltpu.SemaphoreType.DMA((chunks,)),
         ],
-        out_specs=pl.BlockSpec((lanes, 2 * half), lambda i: (i, 0)),
-        out_shape=jax.ShapeDtypeStruct((batch, 2 * half), jnp.bfloat16),
-        scratch_shapes=[pltpu.VMEM((2 * key_rows, batch), jnp.float32)],
         compiler_params=pltpu.CompilerParams(vmem_limit_bytes=60 * 1024 * 1024),
         cost_estimate=pl.CostEstimate(
             flops=4 * state.size, bytes_accessed=4 * state.size, transcendentals=0
@@ -127,16 +131,13 @@
     x_block = jnp.concatenate([x_block, gain_chip[None, :]])
 
     out_full = lax.all_gather(w_out, ROW, axis=0, tiled=True)
-    weights = (w_query, w_key, w_value, w_gate, w_decay, w_beta)
-    x_block, weights, attn_norm_gain, decay_log, decay_bias, token_ids = lax.optimization_barrier(
-        (x_block, weights, attn_norm_gain, decay_log, decay_bias, token_ids)
-    )
-    pieces = to_all(x_block, XY)
-    w_own = jnp.concatenate(weights[:4], axis=1)
-    w_other = jnp.concatenate([swapped(w) for w in weights[:4]], axis=1)
-    w_small = jnp.concatenate(weights[4:], axis=1)
-
-    gain_full = pieces[:, rows].reshape(D).astype(jnp.float32)
+    weights = (w_query, w_key, w_value, w_gate)
+    copies = jnp.broadcast_to(x_block, (lax.axis_size(XY), *x_block.shape))
+    copies, weights, attn_norm_gain = lax.optimization_barrier((copies, weights, attn_norm_gain))
+    pieces = exchange(copies, XY)
+    w_own = jnp.concatenate(weights, axis=1)
+    w_other = jnp.concatenate([swapped(w) for w in weights], axis=1)
+
     x_full = jnp.moveaxis(pieces[:, :rows], 0, 1).reshape(rows, D).astype(jnp.float32)
     normed = (
         x_full
@@ -165,12 +166,17 @@
     landed = exchange(parts, Z)
 
     both = state_sums(landed, state)
-    both, lm_weight, lm_other = lax.optimization_barrier((both, lm_weight, lm_other))
+    small_in = (w_decay, w_beta, decay_log, decay_bias, token_ids, pieces, head_gain)
+    both, lm_weight, lm_other, small_in = lax.optimization_barrier(
+        (both, lm_weight, lm_other, small_in)
+    )
+    w_decay, w_beta, decay_log, decay_bias, token_ids, pieces, head_gain = small_in
     lm_both = jnp.concatenate([lm_weight, lm_other], axis=1)
+    gain_full = pieces[:, rows].reshape(D).astype(jnp.float32)
     both = exchange(both.reshape(n_z, 2 * rows, 2 * half), Z)
     both = jnp.sum(both.astype(jnp.float32), axis=0)
 
-    small = project(w_small)
+    small = project(jnp.concatenate([w_decay, w_beta], axis=1))
     alpha = jnp.exp(
         -jnp.exp(decay_log)[:, None] * jax.nn.softplus(small[:HEADS] + decay_bias[:, None])
     )
@@ -218,7 +224,6 @@
         return lax.ppermute(block, Z, [(k, (k + step) % n_z) for k in range(n_z)])
 
     by_distance = [None] * n_z
-    by_distance[0] = statistics(final, ids[:, :1])
     up = down = (final[:, : D // 2], final[:, D // 2 :])
     for step in range(1, n_z // 2):
         pairs = [(along_z(u, 1), along_z(d, -1)) for u, d in zip(up, down)]
@@ -231,7 +236,10 @@
         by_distance[back], by_distance[step] = two[:, :rows], two[:, rows:]
     middle = n_z // 2
     block = jnp.concatenate([along_z(up[0], 1), along_z(down[1], -1)], axis=1)
-    by_distance[middle] = statistics(block, ids[:, middle : middle + 1])
+    two = statistics(
+        jnp.concatenate([final, block]), jnp.concatenate([ids[:, :1], ids[:, middle : middle + 1]])
+    )
+    by_distance[0], by_distance[middle] = two[:, :rows], two[:, rows:]
     stats = jnp.stack(by_distance)
     stats = lax.dynamic_slice_in_dim(jnp.concatenate([stats, stats]), n_z - zed, n_z, 0)
     stats = jnp.moveaxis(stats, 1, 0).reshape(4, n_z * rows)

time: 185 us -> 180 us (0.973)
  starting transfers between devices: 68.7 us -> 62.6 us
  matrix products: 15 us -> 20.4 us
  local copies, waits for them, and re-layouts: 17.5 us -> 14.9 us
  other arithmetic: 15.8 us -> 13.7 us
    dot_general x5 -> x4, matrix products: 7.94 us -> 14.2 us  [statistics(): logits = jnp.dot(block, lm_both, preferred_element_type=jnp.float32)]
    ppermute x14, starting transfers between devices: 19.2 us -> 15.7 us  [along_z(): return lax.ppermute(block, Z, [(k, (k + step) % n_z) for k in range(n_z)])]
    all_to_all x6, starting transfers between devices: 29.3 us -> 27.5 us  [exchange(): return lax.all_to_all(blocks, axes, split_axis=0, concat_axis=0, tiled=True)]
    unnamed x57 -> x24, local copies, waits for them, and re-layouts: 6.08 us -> 4.52 us
  transfers between devices with their start and end apart: 33 -> 33, of which waited for: 12 -> 13; matrix products, arithmetic and copies ran while one was open for 17% -> 22% of each run, Pallas kernels for 2% -> 2%
where the time goes in v5:
time: 180 us; the launch traced here: 179 us
  starting transfers between devices  62.6 us (35%)
  waiting for transfers between devices  48.4 us (27%)
  matrix products  20.4 us (11%)
  local copies, waits for them, and re-layouts  14.9 us (8%)
  between operations  14.8 us (8%)
  other arithmetic  13.7 us (8%)
  Pallas kernels  4.36 us (2%)
    all_to_all x6, waiting for transfers between devices, exchange(): return lax.all_to_all(blocks, axes, split_axis=0, concat_axis=0, tiled=True)  40.1 us
    all_to_all x6, starting transfers between devices, exchange(): return lax.all_to_all(blocks, axes, split_axis=0, concat_axis=0, tiled=True)  27.5 us
    ppermute x12, starting transfers between devices, swapped(): return lax.ppermute(array, CORE, [(0, 1), (1, 0)])  19.3 us
    ppermute x14, starting transfers between devices, along_z(): return lax.ppermute(block, Z, [(k, (k + step) % n_z) for k in range(n_z)])  15.7 us
    dot_general x4, matrix products, statistics(): logits = jnp.dot(block, lm_both, preferred_element_type=jnp.float32)  14.2 us
    add x1, other arithmetic, per_device(): decay * state + key_k.astype(jnp.float32)[:, None, :] * back[None]  5.14 us
    dot_general x1, matrix products, per_device(): jnp.dot(mixed_full, out_full, preferred_element_type=jnp.float32)  5.08 us
    unnamed x24, local copies, waits for them, and re-layouts  4.52 us
  transfers between devices with their start and end apart: 33, of which 13 were waited for; matrix products, arithmetic and copies ran while one was open for 22% of the time, Pallas kernels for 2%

profile of v5, /device:TPU:1, one launch (start us, length us, event | category | flops | bytes accessed | tf_op | source)
XLA Modules:
  0.0 179.0 jit_solution(403527050948128243)
XLA Ops:
  7.2 0.7 all-gather.2.cloned.1.call-update
  7.9 3.3 %collective-permute-start.1 = (bf16[64]{0:T(256)(128)(2,1)}, bf16[64]{0:T(256)(128)(2,1)S(1)}, u32[]{:S(2)}, u32[]{:S(2)}) collective-permute-start(bf16[64]{0:T(256)(128)(2,1)} %param.30), channel_id=1, source_target_pairs={{0,8},{8,0},{1,9},{9,1},{2,10},{10,2},{3,11},{11,3},{4,12},{12,4},... | collective-permute-start | bytes 392 | tf_op jit(solution)/shard_map/ppermute | solution.py:24
  11.3 0.9 collective-permute-done.1
  13.1 0.8 broadcast_select_fusion.4
  14.2 0.8 broadcast_in_dim.53
  16.0 1.3 pad_maximum_fusion
  17.2 5.0 %all-to-all-start = ((bf16[16,73,128]{2,1,0:T(8,128)(2,1)}), bf16[16,73,128]{2,1,0:T(8,128)(2,1)S(1)}, u32[]{:S(2)}, u32[]{:S(2)}) async-start(bf16[16,73,128]{2,1,0:T(8,128)(2,1)} %broadcast_in_dim.53), calls=%async_computation | async-start | bytes 655360 | tf_op jit(solution)/shard_map/all_to_all | solution.py:28
  22.4 7.8 %all-to-all-done = bf16[16,73,128]{2,1,0:T(8,128)(2,1)S(1)} async-done(((bf16[16,73,128]{2,1,0:T(8,128)(2,1)}), bf16[16,73,128]{2,1,0:T(8,128)(2,1)S(1)}, u32[]{:S(2)}, u32[]{:S(2)}) %all-to-all-start) | async-done | bytes 299040 | tf_op jit(solution)/shard_map/all_to_all | solution.py:28
  31.7 2.3 %collective-permute-start.6 = (bf16[2,128,72]{2,1,0:T(8,128)(2,1)S(1)}, bf16[2,128,72]{2,1,0:T(8,128)(2,1)S(1)}, u32[]{:S(2)}, u32[]{:S(2)}) collective-permute-start(bf16[2,128,72]{2,1,0:T(8,128)(2,1)S(1)} %get-tuple-element.67), channel_id=1, source_target_pairs={{0,8},{8,0},{1,9},{9,1},{2,10},{10,2},{3,11},{11,3},{4,12},{12,4},... | collective-permute-start | bytes 110600 | tf_op jit(solution)/shard_map/ppermute | solution.py:24
  34.1 0.9 collective-permute-done.6
  36.1 8.1 %all-to-all-start.1 = ((bf16[8,32,144]{2,1,0:T(8,128)(2,1)}), bf16[8,32,144]{2,1,0:T(8,128)(2,1)S(1)}, u32[]{:S(2)}, u32[]{:S(2)}) async-start(bf16[8,32,144]{2,1,0:T(8,128)(2,1)} %bitcast.174), calls=%async_computation.1 | async-start | bytes 262144 | tf_op jit(solution)/shard_map/all_to_all | solution.py:28
  44.3 8.3 %all-to-all-done.1.landed_ref = bf16[8,32,144]{2,1,0:T(8,128)(2,1)S(1)} async-done(((bf16[8,32,144]{2,1,0:T(8,128)(2,1)}), bf16[8,32,144]{2,1,0:T(8,128)(2,1)S(1)}, u32[]{:S(2)}, u32[]{:S(2)}) %all-to-all-start.1) | async-done | bytes 73760 | tf_op jit(solution)/shard_map/all_to_all | solution.py:28
  53.2 4.4 %shard_map.192 = bf16[1152,128]{1,0:T(8,128)(2,1)} custom-call(bf16[8,32,144]{2,1,0:T(8,128)(2,1)} %copy-done, f32[16,64,1152]{2,1,0:T(8,128)} %state_ref.1), custom_call_target="tpu_custom_call" | custom-call | flops 4718592 | bytes 4718592 | tf_op jit(solution)/shard_map/pallas_call | solution.py:83
  59.3 1.9 %collective-permute-start.24 = (f32[1,72]{1,0:T(1,128)S(1)}, f32[1,72]{1,0:T(1,128)}, u32[]{:S(2)}, u32[]{:S(2)}) collective-permute-start(f32[1,72]{1,0:T(1,128)S(1)} %fusion.83), channel_id=1, source_target_pairs={{0,8},{8,0},{1,9},{9,1},{2,10},{10,2},{3,11},{11,3},{4,12},{12,4},... | collective-permute-start | bytes 872 | tf_op jit(solution)/shard_map/ppermute | solution.py:24
  61.2 3.4 %all-to-all-start.2 = ((bf16[8,144,128]{2,1,0:T(8,128)(2,1)}), bf16[8,144,128]{2,1,0:T(8,128)(2,1)S(1)}, u32[]{:S(2)}, u32[]{:S(2)}) async-start(bf16[8,144,128]{2,1,0:T(8,128)(2,1)} %bitcast.172), calls=%async_computation.2 | async-start | bytes 589824 | tf_op jit(solution)/shard_map/all_to_all | solution.py:28
  64.9 3.6 %constant_dynamic-update-slice_fusion.1 = bf16[2048,1280]{1,0:T(8,128)(2,1)} fusion(bf16[2048,640]{1,0:T(8,128)(2,1)} %param.31), kind=kLoop, calls=%fused_computation.148 | loop fusion | bytes 5242880
  68.6 1.8 constant_dynamic-update-slice_fusion
  70.3 7.3 %all-to-all-done.2 = bf16[8,144,128]{2,1,0:T(8,128)(2,1)S(1)} async-done(((bf16[8,144,128]{2,1,0:T(8,128)(2,1)}), bf16[8,144,128]{2,1,0:T(8,128)(2,1)S(1)}, u32[]{:S(2)}, u32[]{:S(2)}) %all-to-all-start.2) | async-done | bytes 294944 | tf_op jit(solution)/shard_map/all_to_all | solution.py:28
  79.3 0.7 multiply_convert_fusion.1
  80.1 0.8 broadcast_in_dim.55
  80.9 3.7 %all-to-all-start.3 = ((bf16[16,72,128]{2,1,0:T(8,128)(2,1)}), bf16[16,72,128]{2,1,0:T(8,128)(2,1)S(1)}, u32[]{:S(2)}, u32[]{:S(2)}) async-start(bf16[16,72,128]{2,1,0:T(8,128)(2,1)} %broadcast_in_dim.55), calls=%async_computation.3 | async-start | bytes 589824 | tf_op jit(solution)/shard_map/all_to_all | solution.py:28
  85.3 0.9 collective-permute-start.9
  86.2 6.2 %all-to-all-done.3 = bf16[16,72,128]{2,1,0:T(8,128)(2,1)S(1)} async-done(((bf16[16,72,128]{2,1,0:T(8,128)(2,1)}), bf16[16,72,128]{2,1,0:T(8,128)(2,1)S(1)}, u32[]{:S(2)}, u32[]{:S(2)}) %all-to-all-start.3) | async-done | bytes 294944 | tf_op jit(solution)/shard_map/all_to_all | solution.py:28
  92.4 5.1 %multiply_reduce_fusion.4 = (f32[72]{0:T(128)S(1)}, f32[72,2048]{1,0:T(8,128)S(1)}) fusion(bf16[2048,2048]{1,0:T(8,128)(2,1)} %all-gather.2.cloned.1.call-done, bf16[16,73,128]{2,1,0:T(8,128)(2,1)S(1)} %all-to-all-done, bf16[16,72,128]{2,1,0:T(8,128)(2,1)S(1)} %all-to-all-done.3), kind=kOutput, calls=%fused_computation.60 | convolution fusion | flops 604569536 | bytes 9568544 | tf_op jit(solution)/shard_map/dot_general | solution.py:204
  97.8 1.5 collective-permute-start.19
  99.2 1.3 collective-permute-start.18
  100.7 1.0 collective-permute-done.14
  101.7 1.6 collective-permute-start.15
  103.5 0.7 collective-permute-done.18
  104.2 2.6 %collective-permute-start.20 = (bf16[72,1024]{1,0:T(8,128)(2,1)S(1)}, bf16[72,1024]{1,0:T(8,128)(2,1)S(1)}, u32[]{:S(2)}, u32[]{:S(2)}) collective-permute-start(bf16[72,1024]{1,0:T(8,128)(2,1)S(1)} %collective-permute-done.18), channel_id=1, source_target_pairs={{0,7},{1,0},{2,1},{3,2},{4,3},{5,4},{6,5},{7,6},{8,15},{9,8},{10,9... | collective-permute-start | bytes 442376 | tf_op jit(solution)/shard_map/ppermute | solution.py:224
  107.3 3.5 %fusion.102 = (f32[144]{0:T(256)S(1)}, f32[144,1280]{1,0:T(8,128)S(1)}) fusion(bf16[2048,1280]{1,0:T(8,128)(2,1)} %constant_dynamic-update-slice_fusion, bf16[72,1024]{1,0:T(8,128)(2,1)S(1)} %collective-permute-done.14, bf16[72,1024]{1,0:T(8,128)(2,1)S(1)} %collective-permute-done.19, bf16[72,1024]{1,0:T(8,128)(2,1)S(1)} %collective-permute-done.18, ...), kind=kOutput, calls=%fused_computation.217 | convolution fusion | flops 757518208 | bytes 6570560 | tf_op jit(solution)/shard_map/dot_general | solution.py:215
  110.8 2.8 %collective-permute-start.16 = (bf16[72,1024]{1,0:T(8,128)(2,1)S(1)}, bf16[72,1024]{1,0:T(8,128)(2,1)S(1)}, u32[]{:S(2)}, u32[]{:S(2)}) collective-permute-start(bf16[72,1024]{1,0:T(8,128)(2,1)S(1)} %collective-permute-done.15), channel_id=1, source_target_pairs={{0,7},{1,0},{2,1},{3,2},{4,3},{5,4},{6,5},{7,6},{8,15},{9,8},{10,9... | collective-permute-start | bytes 442376 | tf_op jit(solution)/shard_map/ppermute | solution.py:224
  113.6 2.7 %collective-permute-start.22 = (bf16[72,1024]{1,0:T(8,128)(2,1)S(1)}, bf16[72,1024]{1,0:T(8,128)(2,1)S(1)}, u32[]{:S(2)}, u32[]{:S(2)}) collective-permute-start(bf16[72,1024]{1,0:T(8,128)(2,1)S(1)} %collective-permute-done.20), channel_id=1, source_target_pairs={{0,7},{1,0},{2,1},{3,2},{4,3},{5,4},{6,5},{7,6},{8,15},{9,8},{10,9... | collective-permute-start | bytes 442376 | tf_op jit(solution)/shard_map/ppermute | solution.py:224
  116.2 3.5 %fusion.103 = (f32[144]{0:T(256)S(1)}, f32[144,1280]{1,0:T(8,128)S(1)}) fusion(bf16[2048,1280]{1,0:T(8,128)(2,1)} %constant_dynamic-update-slice_fusion, bf16[72,1024]{1,0:T(8,128)(2,1)S(1)} %collective-permute-done.15, bf16[72,1024]{1,0:T(8,128)(2,1)S(1)} %collective-permute-done.21, bf16[72,1024]{1,0:T(8,128)(2,1)S(1)} %collective-permute-done.20, ...), kind=kOutput, calls=%fused_computation.218 | convolution fusion | flops 757518208 | bytes 6570560 | tf_op jit(solution)/shard_map/dot_general | solution.py:215
  119.8 3.0 %collective-permute-start.17 = (bf16[72,1024]{1,0:T(8,128)(2,1)S(1)}, bf16[72,1024]{1,0:T(8,128)(2,1)S(1)}, u32[]{:S(2)}, u32[]{:S(2)}) collective-permute-start(bf16[72,1024]{1,0:T(8,128)(2,1)S(1)} %collective-permute-done.16), channel_id=1, source_target_pairs={{0,7},{1,0},{2,1},{3,2},{4,3},{5,4},{6,5},{7,6},{8,15},{9,8},{10,9... | collective-permute-start | bytes 442376 | tf_op jit(solution)/shard_map/ppermute | solution.py:224
  122.8 3.5 %fusion.101 = (f32[144]{0:T(256)S(1)}, f32[144,1280]{1,0:T(8,128)S(1)}) fusion(bf16[2048,1280]{1,0:T(8,128)(2,1)} %constant_dynamic-update-slice_fusion, bf16[72,1024]{1,0:T(8,128)(2,1)S(1)} %collective-permute-done.16, bf16[72,1024]{1,0:T(8,128)(2,1)S(1)} %collective-permute-done.23, bf16[72,1024]{1,0:T(8,128)(2,1)S(1)} %collective-permute-done.22, ...), kind=kOutput, calls=%fused_computation.216 | convolution fusion | flops 757518208 | bytes 6570560 | tf_op jit(solution)/shard_map/dot_general | solution.py:215
  126.3 2.1 %collective-permute-done.13 = bf16[72,1024]{1,0:T(8,128)(2,1)S(1)} collective-permute-done((bf16[72,1024]{1,0:T(8,128)(2,1)S(1)}, bf16[72,1024]{1,0:T(8,128)(2,1)S(1)}, u32[]{:S(2)}, u32[]{:S(2)}) %collective-permute-start.13) | collective-permute-done | bytes 147488 | tf_op jit(solution)/shard_map/ppermute | solution.py:224
  128.4 3.5 %fusion.104 = (f32[144]{0:T(256)S(1)}, f32[144,1280]{1,0:T(8,128)S(1)}) fusion(bf16[2048,1280]{1,0:T(8,128)(2,1)} %constant_dynamic-update-slice_fusion, bf16[72,1024]{1,0:T(8,128)(2,1)S(1)} %collective-permute-done.17, bf16[72,1024]{1,0:T(8,128)(2,1)S(1)} %collective-permute-done.13, bf16[72,2048]{1,0:T(8,128)(2,1)S(1)} %multiply_convert_fusion), kind=kOutput, calls=%fused_computation.219 | convolution fusion | flops 756928384 | bytes 6570560 | tf_op jit(solution)/shard_map/dot_general | solution.py:215
  132.0 1.2 fusion
  134.0 0.8 broadcast_in_dim.58
  134.8 3.6 %all-to-all-start.4 = ((f32[8,96,128]{2,1,0:T(8,128)}), f32[8,96,128]{2,1,0:T(8,128)S(1)}, u32[]{:S(2)}, u32[]{:S(2)}) async-start(f32[8,96,128]{2,1,0:T(8,128)} %broadcast_in_dim.58), calls=%async_computation.4 | async-start | bytes 786432 | tf_op jit(solution)/shard_map/all_to_all | solution.py:28
  138.6 10.5 %all-to-all-done.4 = f32[8,96,128]{2,1,0:T(8,128)S(1)} async-done(((f32[8,96,128]{2,1,0:T(8,128)}), f32[8,96,128]{2,1,0:T(8,128)S(1)}, u32[]{:S(2)}, u32[]{:S(2)}) %all-to-all-start.4) | async-done | bytes 393248 | tf_op jit(solution)/shard_map/all_to_all | solution.py:28
  150.1 3.5 %all-to-all-start.5 = ((f32[16,4,576]{2,1,0:T(4,128)}), f32[16,4,576]{2,1,0:T(4,128)S(1)}, u32[]{:S(2)}, u32[]{:S(2)}) async-start(f32[16,4,576]{2,1,0:T(4,128)} %broadcast_in_dim.60), calls=%async_computation.5 | async-start | bytes 327680 | tf_op jit(solution)/shard_map/all_to_all | solution.py:28
  154.6 0.7 mul.283
  155.4 5.1 %multiply_add_fusion = f32[16,64,1152]{2,1,0:T(8,128)} fusion(f32[16,64,1152]{2,1,0:T(8,128)} %state_ref.1, f32[64,1152]{1,0:T(8,128)S(1)} %mul.283, f32[16,1152]{1,0:T(8,128)S(1)} %reshape.179, f32[1152]{0:T(1024)S(1)} %mul.279), kind=kLoop, calls=%fused_computation | loop fusion | flops 3538944 | bytes 9810432 | tf_op jit(solution)/shard_map/add | solution.py:264
  160.8 8.9 %collective-permute-start.25 = (f32[2,576]{1,0:T(2,128)S(1)}, f32[2,576]{1,0:T(2,128)S(1)}, u32[]{:S(2)}, u32[]{:S(2)}) collective-permute-start(f32[2,576]{1,0:T(2,128)S(1)} %pad_maximum_fusion.8), channel_id=1, source_target_pairs={{0,8},{8,0},{1,9},{9,1},{2,10},{10,2},{3,11},{11,3},{4,12},{12,4},... | collective-permute-start | bytes 13832 | tf_op jit(solution)/shard_map/ppermute | solution.py:24
  169.7 0.8 collective-permute-done.25
  170.8 0.7 reshape.176
  (162 shorter events, 15.3 us)
Async XLA Ops:
  7.2 15.1 %copy-start.5 = (bf16[2048]{0:T(1024)(128)(2,1)S(1)}, bf16[2048]{0:T(1024)(128)(2,1)}, u32[]{:S(2)}) copy-start(bf16[2048]{0:T(1024)(128)(2,1)} %param.19) | copy-start | bytes 12292
  7.2 85.2 %all-gather.2.cloned.1.call-start = ((), (), s32[]{:S(2)}) async-start(), calls=%async_computation.6 | async-start | bytes 8650752 | tf_op jit(solution)/shard_map/all_gather | solution.py:133
  7.9 4.3 %collective-permute-start.1 = (bf16[64]{0:T(256)(128)(2,1)}, bf16[64]{0:T(256)(128)(2,1)S(1)}, u32[]{:S(2)}, u32[]{:S(2)}) collective-permute-start(bf16[64]{0:T(256)(128)(2,1)} %param.30), channel_id=1, source_target_pairs={{0,8},{8,0},{1,9},{9,1},{2,10},{10,2},{3,11},{11,3},{4,12},{12,4},... | collective-permute-start | bytes 392 | tf_op jit(solution)/shard_map/ppermute | solution.py:24
  11.2 1.8 %collective-permute-start = (bf16[144,64]{0,1:T(8,128)(2,1)}, bf16[144,64]{0,1:T(8,128)(2,1)S(1)}, u32[]{:S(2)}, u32[]{:S(2)}) collective-permute-start(bf16[144,64]{0,1:T(8,128)(2,1)} %param.17), channel_id=1, source_target_pairs={{0,8},{8,0},{1,9},{9,1},{2,10},{10,2},{3,11},{11,3},{4,12},{12,4},... | collective-permute-start | bytes 55304 | tf_op jit(solution)/shard_map/ppermute | solution.py:24
  15.0 7.3 %collective-permute-start.5 = (bf16[2048,64]{0,1:T(8,128)(2,1)}, bf16[2048,64]{0,1:T(8,128)(2,1)S(1)}, u32[]{:S(2)}, u32[]{:S(2)}) collective-permute-start(bf16[2048,64]{0,1:T(8,128)(2,1)} %param.23), channel_id=1, source_target_pairs={{0,8},{8,0},{1,9},{9,1},{2,10},{10,2},{3,11},{11,3},{4,12},{12,4},... | collective-permute-start | bytes 786440 | tf_op jit(solution)/shard_map/ppermute | solution.py:24
  15.3 7.1 %collective-permute-start.4 = (bf16[2048,64]{0,1:T(8,128)(2,1)}, bf16[2048,64]{0,1:T(8,128)(2,1)S(1)}, u32[]{:S(2)}, u32[]{:S(2)}) collective-permute-start(bf16[2048,64]{0,1:T(8,128)(2,1)} %param.22), channel_id=1, source_target_pairs={{0,8},{8,0},{1,9},{9,1},{2,10},{10,2},{3,11},{11,3},{4,12},{12,4},... | collective-permute-start | bytes 786440 | tf_op jit(solution)/shard_map/ppermute | solution.py:24
  15.5 6.9 %collective-permute-start.3 = (bf16[2048,64]{0,1:T(8,128)(2,1)}, bf16[2048,64]{0,1:T(8,128)(2,1)S(1)}, u32[]{:S(2)}, u32[]{:S(2)}) collective-permute-start(bf16[2048,64]{0,1:T(8,128)(2,1)} %param.21), channel_id=1, source_target_pairs={{0,8},{8,0},{1,9},{9,1},{2,10},{10,2},{3,11},{11,3},{4,12},{12,4},... | collective-permute-start | bytes 786440 | tf_op jit(solution)/shard_map/ppermute | solution.py:24
  15.8 6.6 %collective-permute-start.2 = (bf16[2048,64]{0,1:T(8,128)(2,1)}, bf16[2048,64]{0,1:T(8,128)(2,1)S(1)}, u32[]{:S(2)}, u32[]{:S(2)}) collective-permute-start(bf16[2048,64]{0,1:T(8,128)(2,1)} %param.20), channel_id=1, source_target_pairs={{0,8},{8,0},{1,9},{9,1},{2,10},{10,2},{3,11},{11,3},{4,12},{12,4},... | collective-permute-start | bytes 786440 | tf_op jit(solution)/shard_map/ppermute | solution.py:24
  17.2 13.0 %all-to-all-start = ((bf16[16,73,128]{2,1,0:T(8,128)(2,1)}), bf16[16,73,128]{2,1,0:T(8,128)(2,1)S(1)}, u32[]{:S(2)}, u32[]{:S(2)}) async-start(bf16[16,73,128]{2,1,0:T(8,128)(2,1)} %broadcast_in_dim.53), calls=%async_computation | async-start | bytes 655360 | tf_op jit(solution)/shard_map/all_to_all | solution.py:28
  31.7 3.2 %collective-permute-start.6 = (bf16[2,128,72]{2,1,0:T(8,128)(2,1)S(1)}, bf16[2,128,72]{2,1,0:T(8,128)(2,1)S(1)}, u32[]{:S(2)}, u32[]{:S(2)}) collective-permute-start(bf16[2,128,72]{2,1,0:T(8,128)(2,1)S(1)} %get-tuple-element.67), channel_id=1, source_target_pairs={{0,8},{8,0},{1,9},{9,1},{2,10},{10,2},{3,11},{11,3},{4,12},{12,4},... | collective-permute-start | bytes 110600 | tf_op jit(solution)/shard_map/ppermute | solution.py:24
  35.8 21.8 %collective-permute-start.7 = (bf16[2048,640]{1,0:T(8,128)(2,1)}, bf16[2048,640]{1,0:T(8,128)(2,1)S(1)}, u32[]{:S(2)}, u32[]{:S(2)}) collective-permute-start(bf16[2048,640]{1,0:T(8,128)(2,1)} %param.31), channel_id=1, source_target_pairs={{0,8},{8,0},{1,9},{9,1},{2,10},{10,2},{3,11},{11,3},{4,12},{12,4},... | collective-permute-start | bytes 7864328 | tf_op jit(solution)/shard_map/ppermute | solution.py:24
  36.1 16.5 %all-to-all-start.1 = ((bf16[8,32,144]{2,1,0:T(8,128)(2,1)}), bf16[8,32,144]{2,1,0:T(8,128)(2,1)S(1)}, u32[]{:S(2)}, u32[]{:S(2)}) async-start(bf16[8,32,144]{2,1,0:T(8,128)(2,1)} %bitcast.174), calls=%async_computation.1 | async-start | bytes 262144 | tf_op jit(solution)/shard_map/all_to_all | solution.py:28
  44.3 13.3 %copy-start.9 = (f32[16]{0:T(128)S(1)}, f32[16]{0:T(128)}, u32[]{:S(2)}) copy-start(f32[16]{0:T(128)} %param.26) | copy-start | bytes 196
  44.3 14.0 %copy-start.7 = (bf16[2048,16]{0,1:T(8,128)(2,1)S(1)}, bf16[2048,16]{0,1:T(8,128)(2,1)}, u32[]{:S(2)}) copy-start(bf16[2048,16]{0,1:T(8,128)(2,1)} %param.25) | copy-start | bytes 196612
  44.3 14.2 %copy-start.6 = (f32[16]{0:T(128)S(1)}, f32[16]{0:T(128)}, u32[]{:S(2)}) copy-start(f32[16]{0:T(128)} %param.27) | copy-start | bytes 196
  44.3 20.3 %copy-start.4 = (s32[1152]{0:T(1024)S(1)}, s32[1152]{0:T(1024)}, u32[]{:S(2)}) copy-start(s32[1152]{0:T(1024)} %param.32) | copy-start | bytes 13828
  52.6 0.7 copy-start
  53.2 5.0 %copy-start.8 = (bf16[2048,16]{0,1:T(8,128)(2,1)S(1)}, bf16[2048,16]{0,1:T(8,128)(2,1)}, u32[]{:S(2)}) copy-start(bf16[2048,16]{0,1:T(8,128)(2,1)} %param.24) | copy-start | bytes 196612
  59.3 25.4 %collective-permute-start.24 = (f32[1,72]{1,0:T(1,128)S(1)}, f32[1,72]{1,0:T(1,128)}, u32[]{:S(2)}, u32[]{:S(2)}) collective-permute-start(f32[1,72]{1,0:T(1,128)S(1)} %fusion.83), channel_id=1, source_target_pairs={{0,8},{8,0},{1,9},{9,1},{2,10},{10,2},{3,11},{11,3},{4,12},{12,4},... | collective-permute-start | bytes 872 | tf_op jit(solution)/shard_map/ppermute | solution.py:24
  61.2 16.4 %all-to-all-start.2 = ((bf16[8,144,128]{2,1,0:T(8,128)(2,1)}), bf16[8,144,128]{2,1,0:T(8,128)(2,1)S(1)}, u32[]{:S(2)}, u32[]{:S(2)}) async-start(bf16[8,144,128]{2,1,0:T(8,128)(2,1)} %bitcast.172), calls=%async_computation.2 | async-start | bytes 589824 | tf_op jit(solution)/shard_map/all_to_all | solution.py:28
  77.8 1.4 collective-permute-start.8
  80.9 11.5 %all-to-all-start.3 = ((bf16[16,72,128]{2,1,0:T(8,128)(2,1)}), bf16[16,72,128]{2,1,0:T(8,128)(2,1)S(1)}, u32[]{:S(2)}, u32[]{:S(2)}) async-start(bf16[16,72,128]{2,1,0:T(8,128)(2,1)} %broadcast_in_dim.55), calls=%async_computation.3 | async-start | bytes 589824 | tf_op jit(solution)/shard_map/all_to_all | solution.py:28
  85.3 15.4 %collective-permute-start.9 = (f32[72,64]{0,1:T(8,128)S(1)}, f32[72,64]{0,1:T(8,128)S(1)}, u32[]{:S(2)}, u32[]{:S(2)}) collective-permute-start(f32[72,64]{0,1:T(8,128)S(1)} %constant_dynamic-slice_fusion.3), channel_id=1, source_target_pairs={{0,8},{8,0},{1,9},{9,1},{2,10},{10,2},{3,11},{11,3},{4,12},{12,4},... | collective-permute-start | bytes 55304 | tf_op jit(solution)/shard_map/ppermute | solution.py:24
  97.7 4.1 %collective-permute-start.14 = (bf16[72,1024]{1,0:T(8,128)(2,1)S(1)}, bf16[72,1024]{1,0:T(8,128)(2,1)S(1)}, u32[]{:S(2)}, u32[]{:S(2)}) collective-permute-start(bf16[72,1024]{1,0:T(8,128)(2,1)S(1)} %get-tuple-element.71), channel_id=1, source_target_pairs={{0,7},{1,0},{2,1},{3,2},{4,3},{5,4},{6,5},{7,6},{8,15},{9,8},{10,9... | collective-permute-start | bytes 442376 | tf_op jit(solution)/shard_map/ppermute | solution.py:224
  97.8 5.5 %collective-permute-start.19 = (bf16[72,1024]{1,0:T(8,128)(2,1)S(1)}, bf16[72,1024]{1,0:T(8,128)(2,1)S(1)}, u32[]{:S(2)}, u32[]{:S(2)}) collective-permute-start(bf16[72,1024]{1,0:T(8,128)(2,1)S(1)} %get-tuple-element.71), channel_id=1, source_target_pairs={{0,1},{1,2},{2,3},{3,4},{4,5},{5,6},{6,7},{7,0},{8,9},{9,10},{10,1... | collective-permute-start | bytes 442376 | tf_op jit(solution)/shard_map/ppermute | solution.py:224
  99.2 5.0 %collective-permute-start.18 = (bf16[72,1024]{1,0:T(8,128)(2,1)S(1)}, bf16[72,1024]{1,0:T(8,128)(2,1)S(1)}, u32[]{:S(2)}, u32[]{:S(2)}) collective-permute-start(bf16[72,1024]{1,0:T(8,128)(2,1)S(1)} %get-tuple-element.70), channel_id=1, source_target_pairs={{0,7},{1,0},{2,1},{3,2},{4,3},{5,4},{6,5},{7,6},{8,15},{9,8},{10,9... | collective-permute-start | bytes 442376 | tf_op jit(solution)/shard_map/ppermute | solution.py:224
  100.5 6.7 %collective-permute-start.10 = (bf16[72,1024]{1,0:T(8,128)(2,1)S(1)}, bf16[72,1024]{1,0:T(8,128)(2,1)S(1)}, u32[]{:S(2)}, u32[]{:S(2)}) collective-permute-start(bf16[72,1024]{1,0:T(8,128)(2,1)S(1)} %get-tuple-element.70), channel_id=1, source_target_pairs={{0,1},{1,2},{2,3},{3,4},{4,5},{5,6},{6,7},{7,0},{8,9},{9,10},{10,1... | collective-permute-start | bytes 442376 | tf_op jit(solution)/shard_map/ppermute | solution.py:224
  101.7 9.1 %collective-permute-start.15 = (bf16[72,1024]{1,0:T(8,128)(2,1)S(1)}, bf16[72,1024]{1,0:T(8,128)(2,1)S(1)}, u32[]{:S(2)}, u32[]{:S(2)}) collective-permute-start(bf16[72,1024]{1,0:T(8,128)(2,1)S(1)} %collective-permute-done.14), channel_id=1, source_target_pairs={{0,7},{1,0},{2,1},{3,2},{4,3},{5,4},{6,5},{7,6},{8,15},{9,8},{10,9... | collective-permute-start | bytes 442376 | tf_op jit(solution)/shard_map/ppermute | solution.py:224
  103.3 10.3 %collective-permute-start.21 = (bf16[72,1024]{1,0:T(8,128)(2,1)S(1)}, bf16[72,1024]{1,0:T(8,128)(2,1)S(1)}, u32[]{:S(2)}, u32[]{:S(2)}) collective-permute-start(bf16[72,1024]{1,0:T(8,128)(2,1)S(1)} %collective-permute-done.19), channel_id=1, source_target_pairs={{0,1},{1,2},{2,3},{3,4},{4,5},{5,6},{6,7},{7,0},{8,9},{9,10},{10,1... | collective-permute-start | bytes 442376 | tf_op jit(solution)/shard_map/ppermute | solution.py:224
  104.2 9.4 %collective-permute-start.20 = (bf16[72,1024]{1,0:T(8,128)(2,1)S(1)}, bf16[72,1024]{1,0:T(8,128)(2,1)S(1)}, u32[]{:S(2)}, u32[]{:S(2)}) collective-permute-start(bf16[72,1024]{1,0:T(8,128)(2,1)S(1)} %collective-permute-done.18), channel_id=1, source_target_pairs={{0,7},{1,0},{2,1},{3,2},{4,3},{5,4},{6,5},{7,6},{8,15},{9,8},{10,9... | collective-permute-start | bytes 442376 | tf_op jit(solution)/shard_map/ppermute | solution.py:224
  107.2 9.0 %collective-permute-start.11 = (bf16[72,1024]{1,0:T(8,128)(2,1)S(1)}, bf16[72,1024]{1,0:T(8,128)(2,1)S(1)}, u32[]{:S(2)}, u32[]{:S(2)}) collective-permute-start(bf16[72,1024]{1,0:T(8,128)(2,1)S(1)} %collective-permute-done.10), channel_id=1, source_target_pairs={{0,1},{1,2},{2,3},{3,4},{4,5},{5,6},{6,7},{7,0},{8,9},{9,10},{10,1... | collective-permute-start | bytes 442376 | tf_op jit(solution)/shard_map/ppermute | solution.py:224
  110.8 9.0 %collective-permute-start.16 = (bf16[72,1024]{1,0:T(8,128)(2,1)S(1)}, bf16[72,1024]{1,0:T(8,128)(2,1)S(1)}, u32[]{:S(2)}, u32[]{:S(2)}) collective-permute-start(bf16[72,1024]{1,0:T(8,128)(2,1)S(1)} %collective-permute-done.15), channel_id=1, source_target_pairs={{0,7},{1,0},{2,1},{3,2},{4,3},{5,4},{6,5},{7,6},{8,15},{9,8},{10,9... | collective-permute-start | bytes 442376 | tf_op jit(solution)/shard_map/ppermute | solution.py:224
  113.6 9.2 %collective-permute-start.23 = (bf16[72,1024]{1,0:T(8,128)(2,1)S(1)}, bf16[72,1024]{1,0:T(8,128)(2,1)S(1)}, u32[]{:S(2)}, u32[]{:S(2)}) collective-permute-start(bf16[72,1024]{1,0:T(8,128)(2,1)S(1)} %collective-permute-done.21), channel_id=1, source_target_pairs={{0,1},{1,2},{2,3},{3,4},{4,5},{5,6},{6,7},{7,0},{8,9},{9,10},{10,1... | collective-permute-start | bytes 442376 | tf_op jit(solution)/shard_map/ppermute | solution.py:224
  113.6 9.2 %collective-permute-start.22 = (bf16[72,1024]{1,0:T(8,128)(2,1)S(1)}, bf16[72,1024]{1,0:T(8,128)(2,1)S(1)}, u32[]{:S(2)}, u32[]{:S(2)}) collective-permute-start(bf16[72,1024]{1,0:T(8,128)(2,1)S(1)} %collective-permute-done.20), channel_id=1, source_target_pairs={{0,7},{1,0},{2,1},{3,2},{4,3},{5,4},{6,5},{7,6},{8,15},{9,8},{10,9... | collective-permute-start | bytes 442376 | tf_op jit(solution)/shard_map/ppermute | solution.py:224
  116.2 6.5 %collective-permute-start.12 = (bf16[72,1024]{1,0:T(8,128)(2,1)S(1)}, bf16[72,1024]{1,0:T(8,128)(2,1)S(1)}, u32[]{:S(2)}, u32[]{:S(2)}) collective-permute-start(bf16[72,1024]{1,0:T(8,128)(2,1)S(1)} %collective-permute-done.11), channel_id=1, source_target_pairs={{0,1},{1,2},{2,3},{3,4},{4,5},{5,6},{6,7},{7,0},{8,9},{9,10},{10,1... | collective-permute-start | bytes 442376 | tf_op jit(solution)/shard_map/ppermute | solution.py:224
  119.8 6.5 %collective-permute-start.17 = (bf16[72,1024]{1,0:T(8,128)(2,1)S(1)}, bf16[72,1024]{1,0:T(8,128)(2,1)S(1)}, u32[]{:S(2)}, u32[]{:S(2)}) collective-permute-start(bf16[72,1024]{1,0:T(8,128)(2,1)S(1)} %collective-permute-done.16), channel_id=1, source_target_pairs={{0,7},{1,0},{2,1},{3,2},{4,3},{5,4},{6,5},{7,6},{8,15},{9,8},{10,9... | collective-permute-start | bytes 442376 | tf_op jit(solution)/shard_map/ppermute | solution.py:224
  122.8 5.6 %collective-permute-start.13 = (bf16[72,1024]{1,0:T(8,128)(2,1)S(1)}, bf16[72,1024]{1,0:T(8,128)(2,1)S(1)}, u32[]{:S(2)}, u32[]{:S(2)}) collective-permute-start(bf16[72,1024]{1,0:T(8,128)(2,1)S(1)} %collective-permute-done.12), channel_id=1, source_target_pairs={{0,1},{1,2},{2,3},{3,4},{4,5},{5,6},{6,7},{7,0},{8,9},{9,10},{10,1... | collective-permute-start | bytes 442376 | tf_op jit(solution)/shard_map/ppermute | solution.py:224
  132.0 6.4 %copy-start.1 = (bf16[8,32,144]{2,1,0:T(8,128)(2,1)S(1)}, bf16[8,32,144]{2,1,0:T(8,128)(2,1)}, u32[]{:S(2)}) copy-start(bf16[8,32,144]{2,1,0:T(8,128)(2,1)} %copy-done) | copy-start | bytes 221188
  134.8 14.4 %all-to-all-start.4 = ((f32[8,96,128]{2,1,0:T(8,128)}), f32[8,96,128]{2,1,0:T(8,128)S(1)}, u32[]{:S(2)}, u32[]{:S(2)}) async-start(f32[8,96,128]{2,1,0:T(8,128)} %broadcast_in_dim.58), calls=%async_computation.4 | async-start | bytes 786432 | tf_op jit(solution)/shard_map/all_to_all | solution.py:28
  150.1 10.4 %all-to-all-start.5 = ((f32[16,4,576]{2,1,0:T(4,128)}), f32[16,4,576]{2,1,0:T(4,128)S(1)}, u32[]{:S(2)}, u32[]{:S(2)}) async-start(f32[16,4,576]{2,1,0:T(4,128)} %broadcast_in_dim.60), calls=%async_computation.5 | async-start | bytes 327680 | tf_op jit(solution)/shard_map/all_to_all | solution.py:28
  155.4 16.1 %copy-start.3 = (f32[1152]{0:T(1024)S(1)}, f32[1152]{0:T(1024)}, u32[]{:S(2)}) copy-start(f32[1152]{0:T(1024)} %param.33) | copy-start | bytes 13828
  160.8 9.7 %collective-permute-start.25 = (f32[2,576]{1,0:T(2,128)S(1)}, f32[2,576]{1,0:T(2,128)S(1)}, u32[]{:S(2)}, u32[]{:S(2)}) collective-permute-start(f32[2,576]{1,0:T(2,128)S(1)} %pad_maximum_fusion.8), channel_id=1, source_target_pairs={{0,8},{8,0},{1,9},{9,1},{2,10},{10,2},{3,11},{11,3},{4,12},{12,4},... | collective-permute-start | bytes 13832 | tf_op jit(solution)/shard_map/ppermute | solution.py:24
  170.7 1.4 copy-start.2
Sparse Core Ops, SparseCore 0:
  10.6 62.5 all-gather.1

commit v6 on v5

--- a/solution.py
+++ b/solution.py
@@ -53,18 +53,21 @@
 def state_sums_kernel(landed_ref, state_ref, out_ref, qk_ref, held_ref, sems):
     pieces, both, width = landed_ref.shape
     chunks, key_rows, half, lanes = held_ref.shape
-    copies = []
-    for c in range(chunks):
-        copies.append(
-            pltpu.make_async_copy(
-                state_ref.at[:, :, pl.ds(c * lanes, lanes)], held_ref.at[c], sems.at[c]
-            )
+    ahead = 3
+    copies = [
+        pltpu.make_async_copy(
+            state_ref.at[:, :, pl.ds(c * lanes, lanes)], held_ref.at[c], sems.at[c]
         )
+        for c in range(chunks)
+    ]
+    for c in range(ahead):
         copies[c].start()
     for k in range(pieces):
         qk_ref[:, k * width : (k + 1) * width] = landed_ref[k].astype(jnp.float32)
     for c in range(chunks):
         copies[c].wait()
+        if c + ahead < chunks:
+            copies[c + ahead].start()
         for at in range(0, lanes, 128):
             chunk = qk_ref[:, c * lanes + at : c * lanes + at + 128]
             answer = jnp.zeros((half, 128), jnp.float32)
@@ -79,7 +82,7 @@
 
 def state_sums(landed, state):
     key_rows, half, batch = state.shape
-    chunks = 3
+    chunks = batch // 128
     return pl.pallas_call(
         state_sums_kernel,
         in_specs=[pl.BlockSpec(memory_space=pltpu.VMEM), pl.BlockSpec(memory_space=pl.ANY)],
@@ -95,6 +98,64 @@
             flops=4 * state.size, bytes_accessed=4 * state.size, transcendentals=0
         ),
     )(landed, state)
+
+
+def state_update_kernel(landed_ref, sent_ref, state_ref, out_ref, key_ref, write_ref, decay_ref):
+    pieces, both, width = landed_ref.shape
+    key_rows, half, lanes = state_ref.shape
+    rows = width // 2
+    at_decay = both_rows(rows, pieces)
+    step = pl.program_id(0)
+
+    @pl.when(step == 0)
+    def _():
+        for k in range(pieces):
+            key_ref[:, k * width : (k + 1) * width] = landed_ref[k].astype(jnp.float32)
+            turned = sent_ref[k, :rows, :].T
+            for c in range(2):
+                at = k * width + c * rows
+                write_ref[:, at : at + rows] = turned[c * half : (c + 1) * half]
+                decay_ref[:, at : at + rows] = sent_ref[k, at_decay + c : at_decay + c + 1, :rows]
+
+    for at in range(0, lanes, 128):
+        here = pl.ds(pl.multiple_of(step * lanes + at, 128), 128)
+        write = write_ref[:, here]
+        decay = decay_ref[:, here]
+        key = key_ref[:, here]
+        for k in range(key_rows):
+            tile = state_ref[k, :, at : at + 128]
+            row = key[key_rows + k : key_rows + k + 1]
+            out_ref[k, :, at : at + 128] = decay * tile + row * write
+
+
+def both_rows(rows, pieces):
+    return rows + 4 * pieces * rows // 128
+
+
+def state_update(landed, sent, state):
+    key_rows, half, batch = state.shape
+    lanes = 384
+    block = pl.BlockSpec((key_rows, half, lanes), lambda i: (0, 0, i))
+    return pl.pallas_call(
+        state_update_kernel,
+        grid=(batch // lanes,),
+        in_specs=[
+            pl.BlockSpec(landed.shape, lambda i: (0, 0, 0)),
+            pl.BlockSpec(sent.shape, lambda i: (0, 0, 0)),
+            block,
+        ],
+        out_specs=block,
+        out_shape=jax.ShapeDtypeStruct(state.shape, jnp.float32),
+        scratch_shapes=[
+            pltpu.VMEM((2 * key_rows, batch), jnp.float32),
+            pltpu.VMEM((half, batch), jnp.float32),
+            pltpu.VMEM((1, batch), jnp.float32),
+        ],
+        compiler_params=pltpu.CompilerParams(vmem_limit_bytes=60 * 1024 * 1024),
+        cost_estimate=pl.CostEstimate(
+            flops=3 * state.size, bytes_accessed=8 * state.size, transcendentals=0
+        ),
+    )(landed, sent, state)
 
 
 def per_device(
@@ -135,8 +196,9 @@
     copies = jnp.broadcast_to(x_block, (lax.axis_size(XY), *x_block.shape))
     copies, weights, attn_norm_gain = lax.optimization_barrier((copies, weights, attn_norm_gain))
     pieces = exchange(copies, XY)
+    w_other, weights = lax.optimization_barrier(([swapped(w) for w in weights], weights))
     w_own = jnp.concatenate(weights, axis=1)
-    w_other = jnp.concatenate([swapped(w) for w in weights], axis=1)
+    w_other = jnp.concatenate(w_other, axis=1)
 
     x_full = jnp.moveaxis(pieces[:, :rows], 0, 1).reshape(rows, D).astype(jnp.float32)
     normed = (
@@ -223,9 +285,11 @@
     def along_z(block, step):
         return lax.ppermute(block, Z, [(k, (k + step) % n_z) for k in range(n_z)])
 
+    middle = n_z // 2
     by_distance = [None] * n_z
+    by_distance[0] = statistics(final, ids[:, :1])
     up = down = (final[:, : D // 2], final[:, D // 2 :])
-    for step in range(1, n_z // 2):
+    for step in range(1, middle):
         pairs = [(along_z(u, 1), along_z(d, -1)) for u, d in zip(up, down)]
         up, down = zip(*pairs)
         block = jnp.concatenate([jnp.concatenate(p) for p in pairs], axis=1)
@@ -234,12 +298,8 @@
             block, jnp.concatenate([ids[:, back : back + 1], ids[:, step : step + 1]])
         )
         by_distance[back], by_distance[step] = two[:, :rows], two[:, rows:]
-    middle = n_z // 2
     block = jnp.concatenate([along_z(up[0], 1), along_z(down[1], -1)], axis=1)
-    two = statistics(
-        jnp.concatenate([final, block]), jnp.concatenate([ids[:, :1], ids[:, middle : middle + 1]])
-    )
-    by_distance[0], by_distance[middle] = two[:, :rows], two[:, rows:]
+    by_distance[middle] = statistics(block, ids[:, middle : middle + 1])
     stats = jnp.stack(by_distance)
     stats = lax.dynamic_slice_in_dim(jnp.concatenate([stats, stats]), n_z - zed, n_z, 0)
     stats = jnp.moveaxis(stats, 1, 0).reshape(4, n_z * rows)
@@ -250,19 +310,17 @@
     a_block = in_core_order(core, alpha, swapped(alpha), 0)
     lanes = 2 * half
     n_stats = 4 * n_z * rows // lanes
-    tail = jnp.concatenate([stats.reshape(n_stats, lanes), jnp.pad(a_block, ((0, 0), (0, lanes - rows)))])
+    a_block = jnp.pad(a_block, ((0, 0), (0, lanes - rows)))
+    tail = jnp.concatenate([stats.reshape(n_stats, lanes), a_block])
     tail = jnp.pad(tail, ((0, -tail.shape[0] % 8), (0, 0)))
     sent = to_all(jnp.concatenate([w_block, tail]), Z)
     stats = sent[:, rows : rows + n_stats].reshape(n_z, 4, n_z * rows)
     stats = jnp.stack(merged(jnp.moveaxis(stats, 1, 0), 0))
-    shared = to_all(stats, XY)
-
-    back = jnp.transpose(sent[:, :rows].reshape(n_z, rows, 2, half), (3, 0, 2, 1))
-    back = back.reshape(half, batch)
-    decay = sent[:, rows + n_stats : rows + n_stats + 2, :rows].reshape(batch)
-    key_k = jnp.moveaxis(landed[:, key_rows:], 0, 1).reshape(key_rows, batch)
-    new_state = decay * state + key_k.astype(jnp.float32)[:, None, :] * back[None]
-
+    copies = jnp.broadcast_to(stats, (lax.axis_size(XY), *stats.shape))
+    copies, sent = lax.optimization_barrier((copies, sent))
+    shared = exchange(copies, XY)
+
+    new_state = state_update(landed, sent, state)
     shared, new_state = lax.optimization_barrier((shared, new_state))
     top, total, weighted, picked = merged(jnp.moveaxis(shared, 1, 0), 0)
     lse = top + jnp.log(total)

time: 180 us -> 182 us (1.011)
  waiting for transfers between devices: 48.4 us -> 31.3 us
  blocking collectives: 0 us -> 14.5 us
  Pallas kernels: 4.36 us -> 11.6 us
  other arithmetic: 13.7 us -> 7.01 us
  matrix products: 20.4 us -> 25 us
  local copies, waits for them, and re-layouts: 14.9 us -> 12.4 us
    all_to_all x6 -> x5, waiting for transfers between devices: 40.1 us -> 24.6 us  [exchange(): return lax.all_to_all(blocks, axes, split_axis=0, concat_axis=0, tiled=True)]
    all_to_all x0 -> x1, blocking collectives: none -> 14.5 us  [exchange(): return lax.all_to_all(blocks, axes, split_axis=0, concat_axis=0, tiled=True)]
    pallas_call x0 -> x1, Pallas kernels: none -> 5.99 us  [state_update(): pl.pallas_call(state_update_kernel, grid=(batch // lanes,), in_specs=[pl....]
    add x1 -> x0, other arithmetic: 5.14 us -> none  [per_device(): decay * state + key_k.astype(jnp.float32)[:, None, :] * back[None]]
    dot_general x4 -> x5, matrix products: 14.2 us -> 17.9 us  [statistics(): logits = jnp.dot(block, lm_both, preferred_element_type=jnp.float32)]
    ppermute x14, starting transfers between devices: 15.7 us -> 19 us  [along_z(): return lax.ppermute(block, Z, [(k, (k + step) % n_z) for k in range(n_z)])]
    all_to_all x6 -> x5, starting transfers between devices: 27.5 us -> 24.4 us  [exchange(): return lax.all_to_all(blocks, axes, split_axis=0, concat_axis=0, tiled=True)]
    unnamed x24 -> x39, local copies, waits for them, and re-layouts: 4.52 us -> 5.02 us
  transfers between devices with their start and end apart: 33 -> 32, of which waited for: 13 -> 10; matrix products, arithmetic and copies ran while one was open for 22% -> 14% of each run, Pallas kernels for 2% -> 6%
where the time goes in v6:
time: 182 us; the launch traced here: 181 us
  starting transfers between devices  64.4 us (35%)
  waiting for transfers between devices  31.3 us (17%)
  matrix products  25 us (14%)
  between operations  14.8 us (8%)
  blocking collectives  14.5 us (8%)
  local copies, waits for them, and re-layouts  12.4 us (7%)
  Pallas kernels  11.6 us (6%)
  other arithmetic  7.01 us (4%)
    all_to_all x5, waiting for transfers between devices, exchange(): return lax.all_to_all(blocks, axes, split_axis=0, concat_axis=0, tiled=True)  24.6 us
    all_to_all x5, starting transfers between devices, exchange(): return lax.all_to_all(blocks, axes, split_axis=0, concat_axis=0, tiled=True)  24.4 us
    ppermute x12, starting transfers between devices, swapped(): return lax.ppermute(array, CORE, [(0, 1), (1, 0)])  21 us
    ppermute x14, starting transfers between devices, along_z(): return lax.ppermute(block, Z, [(k, (k + step) % n_z) for k in range(n_z)])  19 us
    dot_general x5, matrix products, statistics(): logits = jnp.dot(block, lm_both, preferred_element_type=jnp.float32)  17.9 us
    all_to_all x1, blocking collectives, exchange(): return lax.all_to_all(blocks, axes, split_axis=0, concat_axis=0, tiled=True)  14.5 us
    pallas_call x1, Pallas kernels, state_update(): pl.pallas_call(state_update_kernel, grid=(batch // lanes,), in_specs=[pl....  5.99 us
    pallas_call x1, Pallas kernels, state_sums(): pl.pallas_call(state_sums_kernel, in_specs=[pl.BlockSpec(memory_space=plt...  5.57 us
  transfers between devices with their start and end apart: 32, of which 10 were waited for; matrix products, arithmetic and copies ran while one was open for 14% of the time, Pallas kernels for 6%

profile of v6, /device:TPU:1, one launch (start us, length us, event | category | flops | bytes accessed | tf_op | source)
XLA Modules:
  0.0 181.1 jit_solution(11133519960862741020)
XLA Ops:
  7.3 0.7 all-gather.2.cloned.1.call-update
  7.9 3.3 %collective-permute-start = (bf16[144,64]{0,1:T(8,128)(2,1)}, bf16[144,64]{0,1:T(8,128)(2,1)S(1)}, u32[]{:S(2)}, u32[]{:S(2)}) collective-permute-start(bf16[144,64]{0,1:T(8,128)(2,1)} %param.17), channel_id=1, source_target_pairs={{0,8},{8,0},{1,9},{9,1},{2,10},{10,2},{3,11},{11,3},{4,12},{12,4},... | collective-permute-start | bytes 55304 | tf_op jit(solution)/shard_map/ppermute | solution.py:24
  11.4 1.2 collective-permute-done.1
  13.4 0.8 broadcast_select_fusion.4
  14.5 0.8 broadcast_in_dim.57
  16.3 5.0 %all-to-all-start = ((bf16[16,73,128]{2,1,0:T(8,128)(2,1)}), bf16[16,73,128]{2,1,0:T(8,128)(2,1)S(1)}, u32[]{:S(2)}, u32[]{:S(2)}) async-start(bf16[16,73,128]{2,1,0:T(8,128)(2,1)} %broadcast_in_dim.57), calls=%async_computation | async-start | bytes 655360 | tf_op jit(solution)/shard_map/all_to_all | solution.py:28
  21.3 0.7 fusion.94
  22.3 7.2 %all-to-all-done = bf16[16,73,128]{2,1,0:T(8,128)(2,1)S(1)} async-done(((bf16[16,73,128]{2,1,0:T(8,128)(2,1)}), bf16[16,73,128]{2,1,0:T(8,128)(2,1)S(1)}, u32[]{:S(2)}, u32[]{:S(2)}) %all-to-all-start) | async-done | bytes 299040 | tf_op jit(solution)/shard_map/all_to_all | solution.py:28
  31.0 2.1 %collective-permute-start.6 = (bf16[2,128,72]{2,1,0:T(8,128)(2,1)S(1)}, bf16[2,128,72]{2,1,0:T(8,128)(2,1)S(1)}, u32[]{:S(2)}, u32[]{:S(2)}) collective-permute-start(bf16[2,128,72]{2,1,0:T(8,128)(2,1)S(1)} %get-tuple-element.90), channel_id=1, source_target_pairs={{0,8},{8,0},{1,9},{9,1},{2,10},{10,2},{3,11},{11,3},{4,12},{12,4},... | collective-permute-start | bytes 110600 | tf_op jit(solution)/shard_map/ppermute | solution.py:24
  33.0 0.9 collective-permute-done.6
  34.1 0.7 copy.121
  35.1 8.2 %all-to-all-start.1 = ((bf16[8,32,144]{2,1,0:T(8,128)(2,1)}), bf16[8,32,144]{2,1,0:T(8,128)(2,1)S(1)}, u32[]{:S(2)}, u32[]{:S(2)}) async-start(bf16[8,32,144]{2,1,0:T(8,128)(2,1)} %bitcast.207), calls=%async_computation.1 | async-start | bytes 262144 | tf_op jit(solution)/shard_map/all_to_all | solution.py:28
  43.4 8.3 %all-to-all-done.1.landed_ref = bf16[8,32,144]{2,1,0:T(8,128)(2,1)S(1)} async-done(((bf16[8,32,144]{2,1,0:T(8,128)(2,1)}), bf16[8,32,144]{2,1,0:T(8,128)(2,1)S(1)}, u32[]{:S(2)}, u32[]{:S(2)}) %all-to-all-start.1) | async-done | bytes 73760 | tf_op jit(solution)/shard_map/all_to_all | solution.py:28
  52.3 5.6 %shard_map.192 = bf16[1152,128]{1,0:T(8,128)(2,1)} custom-call(bf16[8,32,144]{2,1,0:T(8,128)(2,1)} %copy-done.1, f32[16,64,1152]{2,1,0:T(8,128)} %state_ref.3), custom_call_target="tpu_custom_call" | custom-call | flops 4718592 | bytes 4718592 | tf_op jit(solution)/shard_map/pallas_call | solution.py:86
  57.9 3.5 %all-to-all-start.2 = ((bf16[8,144,128]{2,1,0:T(8,128)(2,1)}), bf16[8,144,128]{2,1,0:T(8,128)(2,1)S(1)}, u32[]{:S(2)}, u32[]{:S(2)}) async-start(bf16[8,144,128]{2,1,0:T(8,128)(2,1)} %bitcast.205), calls=%async_computation.2 | async-start | bytes 589824 | tf_op jit(solution)/shard_map/all_to_all | solution.py:28
  62.1 1.1 fusion.34
  63.3 0.7 fusion.82
  64.0 1.7 collective-permute-start.24
  65.9 3.5 %constant_dynamic-update-slice_fusion.1 = bf16[2048,1280]{1,0:T(8,128)(2,1)} fusion(bf16[2048,640]{1,0:T(8,128)(2,1)} %param.31), kind=kLoop, calls=%fused_computation.114 | loop fusion | bytes 5242880
  69.4 1.8 constant_dynamic-update-slice_fusion
  72.1 3.0 %collective-permute-start.8 = (f32[72,128]{0,1:T(8,128)S(1)}, f32[72,128]{0,1:T(8,128)S(1)}, u32[]{:S(2)}, u32[]{:S(2)}) collective-permute-start(f32[72,128]{0,1:T(8,128)S(1)} %copy.143), channel_id=1, source_target_pairs={{0,8},{8,0},{1,9},{9,1},{2,10},{10,2},{3,11},{11,3},{4,12},{12,4},... | collective-permute-start | bytes 110600 | tf_op jit(solution)/shard_map/ppermute | solution.py:24
  75.3 0.7 collective-permute-done.8
  76.7 0.8 broadcast_in_dim.59
  77.4 3.7 %all-to-all-start.3 = ((bf16[16,72,128]{2,1,0:T(8,128)(2,1)}), bf16[16,72,128]{2,1,0:T(8,128)(2,1)S(1)}, u32[]{:S(2)}, u32[]{:S(2)}) async-start(bf16[16,72,128]{2,1,0:T(8,128)(2,1)} %broadcast_in_dim.59), calls=%async_computation.3 | async-start | bytes 589824 | tf_op jit(solution)/shard_map/all_to_all | solution.py:28
  81.2 7.7 %all-to-all-done.3 = bf16[16,72,128]{2,1,0:T(8,128)(2,1)S(1)} async-done(((bf16[16,72,128]{2,1,0:T(8,128)(2,1)}), bf16[16,72,128]{2,1,0:T(8,128)(2,1)S(1)}, u32[]{:S(2)}, u32[]{:S(2)}) %all-to-all-start.3) | async-done | bytes 294944 | tf_op jit(solution)/shard_map/all_to_all | solution.py:28
  88.9 5.1 %multiply_reduce_fusion.3 = (f32[72]{0:T(128)S(1)}, f32[72,2048]{1,0:T(8,128)S(1)}) fusion(bf16[2048,2048]{1,0:T(8,128)(2,1)} %all-gather.2.cloned.1.call-done, bf16[16,73,128]{2,1,0:T(8,128)(2,1)S(1)} %all-to-all-done, bf16[16,72,128]{2,1,0:T(8,128)(2,1)S(1)} %all-to-all-done.3), kind=kOutput, calls=%fused_computation.49 | convolution fusion | flops 604569536 | bytes 9568544 | tf_op jit(solution)/shard_map/dot_general | solution.py:266
  94.6 2.4 %collective-permute-start.11 = (bf16[72,1024]{1,0:T(8,128)(2,1)S(1)}, bf16[72,1024]{1,0:T(8,128)(2,1)S(1)}, u32[]{:S(2)}, u32[]{:S(2)}) collective-permute-start(bf16[72,1024]{1,0:T(8,128)(2,1)S(1)} %get-tuple-element.93), channel_id=1, source_target_pairs={{0,7},{1,0},{2,1},{3,2},{4,3},{5,4},{6,5},{7,6},{8,15},{9,8},{10,9... | collective-permute-start | bytes 442376 | tf_op jit(solution)/shard_map/ppermute | solution.py:286
  97.0 2.7 %collective-permute-start.13 = (bf16[72,1024]{1,0:T(8,128)(2,1)S(1)}, bf16[72,1024]{1,0:T(8,128)(2,1)S(1)}, u32[]{:S(2)}, u32[]{:S(2)}) collective-permute-start(bf16[72,1024]{1,0:T(8,128)(2,1)S(1)} %get-tuple-element.94), channel_id=1, source_target_pairs={{0,7},{1,0},{2,1},{3,2},{4,3},{5,4},{6,5},{7,6},{8,15},{9,8},{10,9... | collective-permute-start | bytes 442376 | tf_op jit(solution)/shard_map/ppermute | solution.py:286
  99.7 3.6 %fusion.96 = (f32[72]{0:T(128)S(1)}, f32[72,1280]{1,0:T(8,128)S(1)}) fusion(bf16[72,2048]{1,0:T(8,128)(2,1)S(1)} %multiply_convert_fusion, bf16[2048,1280]{1,0:T(8,128)(2,1)} %constant_dynamic-update-slice_fusion), kind=kOutput, calls=%fused_computation.236 | convolution fusion | flops 377579456 | bytes 5906720 | tf_op jit(solution)/shard_map/dot_general | solution.py:277
  103.4 2.7 %collective-permute-start.15 = (bf16[72,1024]{1,0:T(8,128)(2,1)S(1)}, bf16[72,1024]{1,0:T(8,128)(2,1)S(1)}, u32[]{:S(2)}, u32[]{:S(2)}) collective-permute-start(bf16[72,1024]{1,0:T(8,128)(2,1)S(1)} %collective-permute-done.11), channel_id=1, source_target_pairs={{0,7},{1,0},{2,1},{3,2},{4,3},{5,4},{6,5},{7,6},{8,15},{9,8},{10,9... | collective-permute-start | bytes 442376 | tf_op jit(solution)/shard_map/ppermute | solution.py:286
  106.1 2.7 %collective-permute-start.17 = (bf16[72,1024]{1,0:T(8,128)(2,1)S(1)}, bf16[72,1024]{1,0:T(8,128)(2,1)S(1)}, u32[]{:S(2)}, u32[]{:S(2)}) collective-permute-start(bf16[72,1024]{1,0:T(8,128)(2,1)S(1)} %collective-permute-done.13), channel_id=1, source_target_pairs={{0,7},{1,0},{2,1},{3,2},{4,3},{5,4},{6,5},{7,6},{8,15},{9,8},{10,9... | collective-permute-start | bytes 442376 | tf_op jit(solution)/shard_map/ppermute | solution.py:286
  108.7 3.5 %fusion.99 = (f32[144]{0:T(256)S(1)}, f32[144,1280]{1,0:T(8,128)S(1)}) fusion(bf16[2048,1280]{1,0:T(8,128)(2,1)} %constant_dynamic-update-slice_fusion, bf16[72,1024]{1,0:T(8,128)(2,1)S(1)} %collective-permute-done.13, bf16[72,1024]{1,0:T(8,128)(2,1)S(1)} %collective-permute-done.12, bf16[72,1024]{1,0:T(8,128)(2,1)S(1)} %collective-permute-done.11, ...), kind=kOutput, calls=%fused_computation.239 | convolution fusion | flops 757518208 | bytes 6570560 | tf_op jit(solution)/shard_map/dot_general | solution.py:277
  112.4 2.7 %collective-permute-start.19 = (bf16[72,1024]{1,0:T(8,128)(2,1)S(1)}, bf16[72,1024]{1,0:T(8,128)(2,1)S(1)}, u32[]{:S(2)}, u32[]{:S(2)}) collective-permute-start(bf16[72,1024]{1,0:T(8,128)(2,1)S(1)} %collective-permute-done.15), channel_id=1, source_target_pairs={{0,7},{1,0},{2,1},{3,2},{4,3},{5,4},{6,5},{7,6},{8,15},{9,8},{10,9... | collective-permute-start | bytes 442376 | tf_op jit(solution)/shard_map/ppermute | solution.py:286
  115.1 2.7 %collective-permute-start.21 = (bf16[72,1024]{1,0:T(8,128)(2,1)S(1)}, bf16[72,1024]{1,0:T(8,128)(2,1)S(1)}, u32[]{:S(2)}, u32[]{:S(2)}) collective-permute-start(bf16[72,1024]{1,0:T(8,128)(2,1)S(1)} %collective-permute-done.17), channel_id=1, source_target_pairs={{0,7},{1,0},{2,1},{3,2},{4,3},{5,4},{6,5},{7,6},{8,15},{9,8},{10,9... | collective-permute-start | bytes 442376 | tf_op jit(solution)/shard_map/ppermute | solution.py:286
  117.7 3.5 %fusion.98 = (f32[144]{0:T(256)S(1)}, f32[144,1280]{1,0:T(8,128)S(1)}) fusion(bf16[2048,1280]{1,0:T(8,128)(2,1)} %constant_dynamic-update-slice_fusion, bf16[72,1024]{1,0:T(8,128)(2,1)S(1)} %collective-permute-done.17, bf16[72,1024]{1,0:T(8,128)(2,1)S(1)} %collective-permute-done.16, bf16[72,1024]{1,0:T(8,128)(2,1)S(1)} %collective-permute-done.15, ...), kind=kOutput, calls=%fused_computation.238 | convolution fusion | flops 757518208 | bytes 6570560 | tf_op jit(solution)/shard_map/dot_general | solution.py:277
  121.3 3.5 %fusion.97 = (f32[144]{0:T(256)S(1)}, f32[144,1280]{1,0:T(8,128)S(1)}) fusion(bf16[2048,1280]{1,0:T(8,128)(2,1)} %constant_dynamic-update-slice_fusion, bf16[72,1024]{1,0:T(8,128)(2,1)S(1)} %collective-permute-done.21, bf16[72,1024]{1,0:T(8,128)(2,1)S(1)} %collective-permute-done.20, bf16[72,1024]{1,0:T(8,128)(2,1)S(1)} %collective-permute-done.19, ...), kind=kOutput, calls=%fused_computation.237 | convolution fusion | flops 757518208 | bytes 6570560 | tf_op jit(solution)/shard_map/dot_general | solution.py:277
  124.9 0.9 fusion
  125.9 2.7 %collective-permute-start.23 = (bf16[72,1024]{1,0:T(8,128)(2,1)S(1)}, bf16[72,1024]{1,0:T(8,128)(2,1)S(1)}, u32[]{:S(2)}, u32[]{:S(2)}) collective-permute-start(bf16[72,1024]{1,0:T(8,128)(2,1)S(1)} %collective-permute-done.21), channel_id=1, source_target_pairs={{0,7},{1,0},{2,1},{3,2},{4,3},{5,4},{6,5},{7,6},{8,15},{9,8},{10,9... | collective-permute-start | bytes 442376 | tf_op jit(solution)/shard_map/ppermute | solution.py:286
  128.6 2.5 %collective-permute-done.22 = bf16[72,1024]{1,0:T(8,128)(2,1)S(1)} collective-permute-done((bf16[72,1024]{1,0:T(8,128)(2,1)S(1)}, bf16[72,1024]{1,0:T(8,128)(2,1)S(1)}, u32[]{:S(2)}, u32[]{:S(2)}) %collective-permute-start.22) | collective-permute-done | bytes 147488 | tf_op jit(solution)/shard_map/ppermute | solution.py:286
  131.1 3.6 %fusion.95 = (f32[72]{0:T(128)S(1)}, f32[72,1280]{1,0:T(8,128)S(1)}) fusion(bf16[2048,1280]{1,0:T(8,128)(2,1)} %constant_dynamic-update-slice_fusion, bf16[72,1024]{1,0:T(8,128)(2,1)S(1)} %collective-permute-done.23, bf16[72,1024]{1,0:T(8,128)(2,1)S(1)} %collective-permute-done.22), kind=kOutput, calls=%fused_computation.235 | convolution fusion | flops 378169280 | bytes 5906720 | tf_op jit(solution)/shard_map/dot_general | solution.py:277
  136.2 14.5 %all_to_all.30.sent_ref = f32[8,96,128]{2,1,0:T(8,128)S(1)} all-to-all(f32[8,96,128]{2,1,0:T(8,128)S(1)} %broadcast_in_dim.62), channel_id=1, replica_groups=mesh['row_0'=4,'row_1'=4,'row_2'=2,'col'=8] {'col'}, dimensions={0} | all-to-all | bytes 786432 | tf_op jit(solution)/shard_map/all_to_all | solution.py:28
  151.0 0.7 broadcast_in_dim.64
  151.7 4.0 %all-to-all-start.5 = ((f32[16,4,576]{2,1,0:T(4,128)}), f32[16,4,576]{2,1,0:T(4,128)S(1)}, u32[]{:S(2)}, u32[]{:S(2)}) async-start(f32[16,4,576]{2,1,0:T(4,128)} %broadcast_in_dim.64), calls=%async_computation.5 | async-start | bytes 327680 | tf_op jit(solution)/shard_map/all_to_all | solution.py:28
  155.7 6.0 %shard_map.193 = f32[16,64,1152]{2,1,0:T(8,128)} custom-call(bf16[8,32,144]{2,1,0:T(8,128)(2,1)} %copy-done.1, f32[8,96,128]{2,1,0:T(8,128)} %copy-done, f32[16,64,1152]{2,1,0:T(8,128)} %state_ref.3), custom_call_target="tpu_custom_call" | custom-call | flops 3538944 | bytes 9437184 | tf_op jit(solution)/shard_map/pallas_call | solution.py:139
  161.7 0.8 all-to-all-done.5
  162.7 9.0 %collective-permute-start.25 = (f32[2,576]{1,0:T(2,128)S(1)}, f32[2,576]{1,0:T(2,128)S(1)}, u32[]{:S(2)}, u32[]{:S(2)}) collective-permute-start(f32[2,576]{1,0:T(2,128)S(1)} %pad_maximum_fusion.8), channel_id=1, source_target_pairs={{0,8},{8,0},{1,9},{9,1},{2,10},{10,2},{3,11},{11,3},{4,12},{12,4},... | collective-permute-start | bytes 13832 | tf_op jit(solution)/shard_map/ppermute | solution.py:24
  171.7 0.8 collective-permute-done.25
  172.9 0.7 reshape.163
  (169 shorter events, 11.6 us)
Async XLA Ops:
  7.2 15.0 %copy-start.5 = (bf16[2048,64]{0,1:T(8,128)(2,1)S(1)}, bf16[2048,64]{0,1:T(8,128)(2,1)}, u32[]{:S(2)}) copy-start(bf16[2048,64]{0,1:T(8,128)(2,1)} %param.20) | copy-start | bytes 786436
  7.2 15.0 %copy-start.4 = (bf16[2048,64]{0,1:T(8,128)(2,1)S(1)}, bf16[2048,64]{0,1:T(8,128)(2,1)}, u32[]{:S(2)}) copy-start(bf16[2048,64]{0,1:T(8,128)(2,1)} %param.21) | copy-start | bytes 786436
  7.2 15.0 %copy-start.3 = (bf16[2048,64]{0,1:T(8,128)(2,1)S(1)}, bf16[2048,64]{0,1:T(8,128)(2,1)}, u32[]{:S(2)}) copy-start(bf16[2048,64]{0,1:T(8,128)(2,1)} %param.22) | copy-start | bytes 786436
  7.2 15.0 %copy-start.2 = (bf16[2048,64]{0,1:T(8,128)(2,1)S(1)}, bf16[2048,64]{0,1:T(8,128)(2,1)}, u32[]{:S(2)}) copy-start(bf16[2048,64]{0,1:T(8,128)(2,1)} %param.23) | copy-start | bytes 786436
  7.2 81.7 %all-gather.2.cloned.1.call-start = ((), (), s32[]{:S(2)}) async-start(), calls=%async_computation.6 | async-start | bytes 8650752 | tf_op jit(solution)/shard_map/all_gather | solution.py:194
  7.9 5.5 %collective-permute-start = (bf16[144,64]{0,1:T(8,128)(2,1)}, bf16[144,64]{0,1:T(8,128)(2,1)S(1)}, u32[]{:S(2)}, u32[]{:S(2)}) collective-permute-start(bf16[144,64]{0,1:T(8,128)(2,1)} %param.17), channel_id=1, source_target_pairs={{0,8},{8,0},{1,9},{9,1},{2,10},{10,2},{3,11},{11,3},{4,12},{12,4},... | collective-permute-start | bytes 55304 | tf_op jit(solution)/shard_map/ppermute | solution.py:24
  11.3 1.3 collective-permute-start.1
  15.3 6.7 %collective-permute-start.2 = (bf16[2048,64]{0,1:T(8,128)(2,1)}, bf16[2048,64]{0,1:T(8,128)(2,1)S(1)}, u32[]{:S(2)}, u32[]{:S(2)}) collective-permute-start(bf16[2048,64]{0,1:T(8,128)(2,1)} %param.20), channel_id=1, source_target_pairs={{0,8},{8,0},{1,9},{9,1},{2,10},{10,2},{3,11},{11,3},{4,12},{12,4},... | collective-permute-start | bytes 786440 | tf_op jit(solution)/shard_map/ppermute | solution.py:24
  15.5 6.5 %collective-permute-start.3 = (bf16[2048,64]{0,1:T(8,128)(2,1)}, bf16[2048,64]{0,1:T(8,128)(2,1)S(1)}, u32[]{:S(2)}, u32[]{:S(2)}) collective-permute-start(bf16[2048,64]{0,1:T(8,128)(2,1)} %param.21), channel_id=1, source_target_pairs={{0,8},{8,0},{1,9},{9,1},{2,10},{10,2},{3,11},{11,3},{4,12},{12,4},... | collective-permute-start | bytes 786440 | tf_op jit(solution)/shard_map/ppermute | solution.py:24
  15.8 6.2 %collective-permute-start.4 = (bf16[2048,64]{0,1:T(8,128)(2,1)}, bf16[2048,64]{0,1:T(8,128)(2,1)S(1)}, u32[]{:S(2)}, u32[]{:S(2)}) collective-permute-start(bf16[2048,64]{0,1:T(8,128)(2,1)} %param.22), channel_id=1, source_target_pairs={{0,8},{8,0},{1,9},{9,1},{2,10},{10,2},{3,11},{11,3},{4,12},{12,4},... | collective-permute-start | bytes 786440 | tf_op jit(solution)/shard_map/ppermute | solution.py:24
  16.0 6.0 %collective-permute-start.5 = (bf16[2048,64]{0,1:T(8,128)(2,1)}, bf16[2048,64]{0,1:T(8,128)(2,1)S(1)}, u32[]{:S(2)}, u32[]{:S(2)}) collective-permute-start(bf16[2048,64]{0,1:T(8,128)(2,1)} %param.23), channel_id=1, source_target_pairs={{0,8},{8,0},{1,9},{9,1},{2,10},{10,2},{3,11},{11,3},{4,12},{12,4},... | collective-permute-start | bytes 786440 | tf_op jit(solution)/shard_map/ppermute | solution.py:24
  16.3 13.2 %all-to-all-start = ((bf16[16,73,128]{2,1,0:T(8,128)(2,1)}), bf16[16,73,128]{2,1,0:T(8,128)(2,1)S(1)}, u32[]{:S(2)}, u32[]{:S(2)}) async-start(bf16[16,73,128]{2,1,0:T(8,128)(2,1)} %broadcast_in_dim.57), calls=%async_computation | async-start | bytes 655360 | tf_op jit(solution)/shard_map/all_to_all | solution.py:28
  31.0 3.0 %collective-permute-start.6 = (bf16[2,128,72]{2,1,0:T(8,128)(2,1)S(1)}, bf16[2,128,72]{2,1,0:T(8,128)(2,1)S(1)}, u32[]{:S(2)}, u32[]{:S(2)}) collective-permute-start(bf16[2,128,72]{2,1,0:T(8,128)(2,1)S(1)} %get-tuple-element.90), channel_id=1, source_target_pairs={{0,8},{8,0},{1,9},{9,1},{2,10},{10,2},{3,11},{11,3},{4,12},{12,4},... | collective-permute-start | bytes 110600 | tf_op jit(solution)/shard_map/ppermute | solution.py:24
  34.7 23.1 %collective-permute-start.7 = (bf16[2048,640]{1,0:T(8,128)(2,1)}, bf16[2048,640]{1,0:T(8,128)(2,1)S(1)}, u32[]{:S(2)}, u32[]{:S(2)}) collective-permute-start(bf16[2048,640]{1,0:T(8,128)(2,1)} %param.31), channel_id=1, source_target_pairs={{0,8},{8,0},{1,9},{9,1},{2,10},{10,2},{3,11},{11,3},{4,12},{12,4},... | collective-permute-start | bytes 7864328 | tf_op jit(solution)/shard_map/ppermute | solution.py:24
  35.1 16.6 %all-to-all-start.1 = ((bf16[8,32,144]{2,1,0:T(8,128)(2,1)}), bf16[8,32,144]{2,1,0:T(8,128)(2,1)S(1)}, u32[]{:S(2)}, u32[]{:S(2)}) async-start(bf16[8,32,144]{2,1,0:T(8,128)(2,1)} %bitcast.207), calls=%async_computation.1 | async-start | bytes 262144 | tf_op jit(solution)/shard_map/all_to_all | solution.py:28
  43.3 18.0 %copy-start.8 = (s32[1152]{0:T(1024)S(1)}, s32[1152]{0:T(1024)}, u32[]{:S(2)}) copy-start(s32[1152]{0:T(1024)} %param.32) | copy-start | bytes 13828
  43.3 18.1 %copy-start.11 = (f32[16]{0:T(128)S(1)}, f32[16]{0:T(128)}, u32[]{:S(2)}) copy-start(f32[16]{0:T(128)} %param.26) | copy-start | bytes 196
  43.3 19.9 %copy-start.10 = (f32[16]{0:T(128)S(1)}, f32[16]{0:T(128)}, u32[]{:S(2)}) copy-start(f32[16]{0:T(128)} %param.27) | copy-start | bytes 196
  51.6 0.7 copy-start.1
  57.9 14.0 %all-to-all-start.2 = ((bf16[8,144,128]{2,1,0:T(8,128)(2,1)}), bf16[8,144,128]{2,1,0:T(8,128)(2,1)S(1)}, u32[]{:S(2)}, u32[]{:S(2)}) async-start(bf16[8,144,128]{2,1,0:T(8,128)(2,1)} %bitcast.205), calls=%async_computation.2 | async-start | bytes 589824 | tf_op jit(solution)/shard_map/all_to_all | solution.py:28
  64.0 7.3 %collective-permute-start.24 = (f32[1,72]{1,0:T(1,128)S(1)}, f32[1,72]{1,0:T(1,128)S(1)}, u32[]{:S(2)}, u32[]{:S(2)}) collective-permute-start(f32[1,72]{1,0:T(1,128)S(1)} %fusion.82), channel_id=1, source_target_pairs={{0,8},{8,0},{1,9},{9,1},{2,10},{10,2},{3,11},{11,3},{4,12},{12,4},... | collective-permute-start | bytes 872 | tf_op jit(solution)/shard_map/ppermute | solution.py:24
  69.4 7.1 %copy-start.9 = (f32[128]{0:T(128)S(1)}, f32[128]{0:T(128)}, u32[]{:S(2)}) copy-start(f32[128]{0:T(128)} %param.28) | copy-start | bytes 1540
  72.1 3.9 %collective-permute-start.8 = (f32[72,128]{0,1:T(8,128)S(1)}, f32[72,128]{0,1:T(8,128)S(1)}, u32[]{:S(2)}, u32[]{:S(2)}) collective-permute-start(f32[72,128]{0,1:T(8,128)S(1)} %copy.143), channel_id=1, source_target_pairs={{0,8},{8,0},{1,9},{9,1},{2,10},{10,2},{3,11},{11,3},{4,12},{12,4},... | collective-permute-start | bytes 110600 | tf_op jit(solution)/shard_map/ppermute | solution.py:24
  76.0 5.2 %collective-permute-start.9 = (f32[72,64]{0,1:T(8,128)S(1)}, f32[72,64]{0,1:T(8,128)S(1)}, u32[]{:S(2)}, u32[]{:S(2)}) collective-permute-start(f32[72,64]{0,1:T(8,128)S(1)} %constant_dynamic-slice_fusion.3), channel_id=1, source_target_pairs={{0,8},{8,0},{1,9},{9,1},{2,10},{10,2},{3,11},{11,3},{4,12},{12,4},... | collective-permute-start | bytes 55304 | tf_op jit(solution)/shard_map/ppermute | solution.py:24
  77.4 11.5 %all-to-all-start.3 = ((bf16[16,72,128]{2,1,0:T(8,128)(2,1)}), bf16[16,72,128]{2,1,0:T(8,128)(2,1)S(1)}, u32[]{:S(2)}, u32[]{:S(2)}) async-start(bf16[16,72,128]{2,1,0:T(8,128)(2,1)} %broadcast_in_dim.59), calls=%async_computation.3 | async-start | bytes 589824 | tf_op jit(solution)/shard_map/all_to_all | solution.py:28
  94.2 9.1 %collective-permute-start.10 = (bf16[72,1024]{1,0:T(8,128)(2,1)S(1)}, bf16[72,1024]{1,0:T(8,128)(2,1)S(1)}, u32[]{:S(2)}, u32[]{:S(2)}) collective-permute-start(bf16[72,1024]{1,0:T(8,128)(2,1)S(1)} %get-tuple-element.93), channel_id=1, source_target_pairs={{0,1},{1,2},{2,3},{3,4},{4,5},{5,6},{6,7},{7,0},{8,9},{9,10},{10,1... | collective-permute-start | bytes 442376 | tf_op jit(solution)/shard_map/ppermute | solution.py:286
  94.6 8.8 %collective-permute-start.11 = (bf16[72,1024]{1,0:T(8,128)(2,1)S(1)}, bf16[72,1024]{1,0:T(8,128)(2,1)S(1)}, u32[]{:S(2)}, u32[]{:S(2)}) collective-permute-start(bf16[72,1024]{1,0:T(8,128)(2,1)S(1)} %get-tuple-element.93), channel_id=1, source_target_pairs={{0,7},{1,0},{2,1},{3,2},{4,3},{5,4},{6,5},{7,6},{8,15},{9,8},{10,9... | collective-permute-start | bytes 442376 | tf_op jit(solution)/shard_map/ppermute | solution.py:286
  97.0 9.1 %collective-permute-start.12 = (bf16[72,1024]{1,0:T(8,128)(2,1)S(1)}, bf16[72,1024]{1,0:T(8,128)(2,1)S(1)}, u32[]{:S(2)}, u32[]{:S(2)}) collective-permute-start(bf16[72,1024]{1,0:T(8,128)(2,1)S(1)} %get-tuple-element.94), channel_id=1, source_target_pairs={{0,1},{1,2},{2,3},{3,4},{4,5},{5,6},{6,7},{7,0},{8,9},{9,10},{10,1... | collective-permute-start | bytes 442376 | tf_op jit(solution)/shard_map/ppermute | solution.py:286
  97.0 9.1 %collective-permute-start.13 = (bf16[72,1024]{1,0:T(8,128)(2,1)S(1)}, bf16[72,1024]{1,0:T(8,128)(2,1)S(1)}, u32[]{:S(2)}, u32[]{:S(2)}) collective-permute-start(bf16[72,1024]{1,0:T(8,128)(2,1)S(1)} %get-tuple-element.94), channel_id=1, source_target_pairs={{0,7},{1,0},{2,1},{3,2},{4,3},{5,4},{6,5},{7,6},{8,15},{9,8},{10,9... | collective-permute-start | bytes 442376 | tf_op jit(solution)/shard_map/ppermute | solution.py:286
  103.3 9.0 %collective-permute-start.14 = (bf16[72,1024]{1,0:T(8,128)(2,1)S(1)}, bf16[72,1024]{1,0:T(8,128)(2,1)S(1)}, u32[]{:S(2)}, u32[]{:S(2)}) collective-permute-start(bf16[72,1024]{1,0:T(8,128)(2,1)S(1)} %collective-permute-done.10), channel_id=1, source_target_pairs={{0,1},{1,2},{2,3},{3,4},{4,5},{5,6},{6,7},{7,0},{8,9},{9,10},{10,1... | collective-permute-start | bytes 442376 | tf_op jit(solution)/shard_map/ppermute | solution.py:286
  103.4 9.0 %collective-permute-start.15 = (bf16[72,1024]{1,0:T(8,128)(2,1)S(1)}, bf16[72,1024]{1,0:T(8,128)(2,1)S(1)}, u32[]{:S(2)}, u32[]{:S(2)}) collective-permute-start(bf16[72,1024]{1,0:T(8,128)(2,1)S(1)} %collective-permute-done.11), channel_id=1, source_target_pairs={{0,7},{1,0},{2,1},{3,2},{4,3},{5,4},{6,5},{7,6},{8,15},{9,8},{10,9... | collective-permute-start | bytes 442376 | tf_op jit(solution)/shard_map/ppermute | solution.py:286
  106.1 9.0 %collective-permute-start.16 = (bf16[72,1024]{1,0:T(8,128)(2,1)S(1)}, bf16[72,1024]{1,0:T(8,128)(2,1)S(1)}, u32[]{:S(2)}, u32[]{:S(2)}) collective-permute-start(bf16[72,1024]{1,0:T(8,128)(2,1)S(1)} %collective-permute-done.12), channel_id=1, source_target_pairs={{0,1},{1,2},{2,3},{3,4},{4,5},{5,6},{6,7},{7,0},{8,9},{9,10},{10,1... | collective-permute-start | bytes 442376 | tf_op jit(solution)/shard_map/ppermute | solution.py:286
  106.1 9.0 %collective-permute-start.17 = (bf16[72,1024]{1,0:T(8,128)(2,1)S(1)}, bf16[72,1024]{1,0:T(8,128)(2,1)S(1)}, u32[]{:S(2)}, u32[]{:S(2)}) collective-permute-start(bf16[72,1024]{1,0:T(8,128)(2,1)S(1)} %collective-permute-done.13), channel_id=1, source_target_pairs={{0,7},{1,0},{2,1},{3,2},{4,3},{5,4},{6,5},{7,6},{8,15},{9,8},{10,9... | collective-permute-start | bytes 442376 | tf_op jit(solution)/shard_map/ppermute | solution.py:286
  112.3 9.0 %collective-permute-start.18 = (bf16[72,1024]{1,0:T(8,128)(2,1)S(1)}, bf16[72,1024]{1,0:T(8,128)(2,1)S(1)}, u32[]{:S(2)}, u32[]{:S(2)}) collective-permute-start(bf16[72,1024]{1,0:T(8,128)(2,1)S(1)} %collective-permute-done.14), channel_id=1, source_target_pairs={{0,1},{1,2},{2,3},{3,4},{4,5},{5,6},{6,7},{7,0},{8,9},{9,10},{10,1... | collective-permute-start | bytes 442376 | tf_op jit(solution)/shard_map/ppermute | solution.py:286
  112.4 8.9 %collective-permute-start.19 = (bf16[72,1024]{1,0:T(8,128)(2,1)S(1)}, bf16[72,1024]{1,0:T(8,128)(2,1)S(1)}, u32[]{:S(2)}, u32[]{:S(2)}) collective-permute-start(bf16[72,1024]{1,0:T(8,128)(2,1)S(1)} %collective-permute-done.15), channel_id=1, source_target_pairs={{0,7},{1,0},{2,1},{3,2},{4,3},{5,4},{6,5},{7,6},{8,15},{9,8},{10,9... | collective-permute-start | bytes 442376 | tf_op jit(solution)/shard_map/ppermute | solution.py:286
  115.1 6.3 %collective-permute-start.20 = (bf16[72,1024]{1,0:T(8,128)(2,1)S(1)}, bf16[72,1024]{1,0:T(8,128)(2,1)S(1)}, u32[]{:S(2)}, u32[]{:S(2)}) collective-permute-start(bf16[72,1024]{1,0:T(8,128)(2,1)S(1)} %collective-permute-done.16), channel_id=1, source_target_pairs={{0,1},{1,2},{2,3},{3,4},{4,5},{5,6},{6,7},{7,0},{8,9},{9,10},{10,1... | collective-permute-start | bytes 442376 | tf_op jit(solution)/shard_map/ppermute | solution.py:286
  115.1 6.3 %collective-permute-start.21 = (bf16[72,1024]{1,0:T(8,128)(2,1)S(1)}, bf16[72,1024]{1,0:T(8,128)(2,1)S(1)}, u32[]{:S(2)}, u32[]{:S(2)}) collective-permute-start(bf16[72,1024]{1,0:T(8,128)(2,1)S(1)} %collective-permute-done.17), channel_id=1, source_target_pairs={{0,7},{1,0},{2,1},{3,2},{4,3},{5,4},{6,5},{7,6},{8,15},{9,8},{10,9... | collective-permute-start | bytes 442376 | tf_op jit(solution)/shard_map/ppermute | solution.py:286
  125.8 5.3 %collective-permute-start.22 = (bf16[72,1024]{1,0:T(8,128)(2,1)S(1)}, bf16[72,1024]{1,0:T(8,128)(2,1)S(1)}, u32[]{:S(2)}, u32[]{:S(2)}) collective-permute-start(bf16[72,1024]{1,0:T(8,128)(2,1)S(1)} %collective-permute-done.18), channel_id=1, source_target_pairs={{0,1},{1,2},{2,3},{3,4},{4,5},{5,6},{6,7},{7,0},{8,9},{9,10},{10,1... | collective-permute-start | bytes 442376 | tf_op jit(solution)/shard_map/ppermute | solution.py:286
  125.9 5.2 %collective-permute-start.23 = (bf16[72,1024]{1,0:T(8,128)(2,1)S(1)}, bf16[72,1024]{1,0:T(8,128)(2,1)S(1)}, u32[]{:S(2)}, u32[]{:S(2)}) collective-permute-start(bf16[72,1024]{1,0:T(8,128)(2,1)S(1)} %collective-permute-done.21), channel_id=1, source_target_pairs={{0,7},{1,0},{2,1},{3,2},{4,3},{5,4},{6,5},{7,6},{8,15},{9,8},{10,9... | collective-permute-start | bytes 442376 | tf_op jit(solution)/shard_map/ppermute | solution.py:286
  150.7 5.0 %copy-start = (f32[8,96,128]{2,1,0:T(8,128)}, f32[8,96,128]{2,1,0:T(8,128)S(1)}, u32[]{:S(2)}) copy-start(f32[8,96,128]{2,1,0:T(8,128)S(1)} %all_to_all.30.sent_ref) | copy-start | bytes 1179652
  151.7 10.8 %all-to-all-start.5 = ((f32[16,4,576]{2,1,0:T(4,128)}), f32[16,4,576]{2,1,0:T(4,128)S(1)}, u32[]{:S(2)}, u32[]{:S(2)}) async-start(f32[16,4,576]{2,1,0:T(4,128)} %broadcast_in_dim.64), calls=%async_computation.5 | async-start | bytes 327680 | tf_op jit(solution)/shard_map/all_to_all | solution.py:28
  155.7 17.9 %copy-start.7 = (f32[1152]{0:T(1024)S(1)}, f32[1152]{0:T(1024)}, u32[]{:S(2)}) copy-start(f32[1152]{0:T(1024)} %param.33) | copy-start | bytes 13828
  162.7 9.8 %collective-permute-start.25 = (f32[2,576]{1,0:T(2,128)S(1)}, f32[2,576]{1,0:T(2,128)S(1)}, u32[]{:S(2)}, u32[]{:S(2)}) collective-permute-start(f32[2,576]{1,0:T(2,128)S(1)} %pad_maximum_fusion.8), channel_id=1, source_target_pairs={{0,8},{8,0},{1,9},{9,1},{2,10},{10,2},{3,11},{11,3},{4,12},{12,4},... | collective-permute-start | bytes 13832 | tf_op jit(solution)/shard_map/ppermute | solution.py:24
  172.8 1.4 copy-start.6
Sparse Core Ops, SparseCore 0:
  10.6 62.1 all-gather.1

commit v7 on v6

--- a/solution.py
+++ b/solution.py
@@ -1,3 +1,5 @@
+import functools
+
 import jax
 import jax.numpy as jnp
 from jax import lax
@@ -50,61 +52,68 @@
     )
 
 
-def state_sums_kernel(landed_ref, state_ref, out_ref, qk_ref, held_ref, sems):
+def state_sums_kernel(landed_ref, state_ref, out_ref, qk_ref, sums_ref):
     pieces, both, width = landed_ref.shape
-    chunks, key_rows, half, lanes = held_ref.shape
-    ahead = 3
-    copies = [
-        pltpu.make_async_copy(
-            state_ref.at[:, :, pl.ds(c * lanes, lanes)], held_ref.at[c], sems.at[c]
-        )
-        for c in range(chunks)
-    ]
-    for c in range(ahead):
-        copies[c].start()
-    for k in range(pieces):
-        qk_ref[:, k * width : (k + 1) * width] = landed_ref[k].astype(jnp.float32)
-    for c in range(chunks):
-        copies[c].wait()
-        if c + ahead < chunks:
-            copies[c + ahead].start()
-        for at in range(0, lanes, 128):
-            chunk = qk_ref[:, c * lanes + at : c * lanes + at + 128]
-            answer = jnp.zeros((half, 128), jnp.float32)
-            recall = jnp.zeros((half, 128), jnp.float32)
-            for k in range(key_rows):
-                tile = held_ref[c, k, :, at : at + 128]
-                answer += tile * chunk[k : k + 1]
-                recall += tile * chunk[key_rows + k : key_rows + k + 1]
-            pair = jnp.concatenate([recall, answer], axis=0).T
-            out_ref[c * lanes + at : c * lanes + at + 128, :] = pair.astype(jnp.bfloat16)
+    slab, half, batch = state_ref.shape
+    key_rows = both // 2
+    step = pl.program_id(0)
+
+    @pl.when(step == 0)
+    def _():
+        for k in range(pieces):
+            qk_ref[:, k * width : (k + 1) * width] = landed_ref[k].astype(jnp.float32)
+        sums_ref[...] = jnp.zeros_like(sums_ref)
+
+    def add(first):
+        for at in range(0, batch, 128):
+            chunk = qk_ref[:, at : at + 128]
+            recall = sums_ref[:half, at : at + 128]
+            answer = sums_ref[half:, at : at + 128]
+            for k in range(slab):
+                tile = state_ref[k, :, at : at + 128]
+                answer += tile * chunk[first + k : first + k + 1]
+                recall += tile * chunk[key_rows + first + k : key_rows + first + k + 1]
+            sums_ref[:half, at : at + 128] = recall
+            sums_ref[half:, at : at + 128] = answer
+
+    for part in range(key_rows // slab):
+        pl.when(step == part)(functools.partial(add, part * slab))
+
+    @pl.when(step == pl.num_programs(0) - 1)
+    def _():
+        for at in range(0, batch, 128):
+            out_ref[at : at + 128, :] = sums_ref[:, at : at + 128].T.astype(jnp.bfloat16)
 
 
 def state_sums(landed, state):
     key_rows, half, batch = state.shape
-    chunks = batch // 128
+    slab = 4
     return pl.pallas_call(
         state_sums_kernel,
-        in_specs=[pl.BlockSpec(memory_space=pltpu.VMEM), pl.BlockSpec(memory_space=pl.ANY)],
-        out_specs=pl.BlockSpec(memory_space=pltpu.VMEM),
+        grid=(key_rows // slab,),
+        in_specs=[
+            pl.BlockSpec(landed.shape, lambda i: (0, 0, 0)),
+            pl.BlockSpec((slab, half, batch), lambda i: (i, 0, 0)),
+        ],
+        out_specs=pl.BlockSpec((batch, 2 * half), lambda i: (0, 0)),
         out_shape=jax.ShapeDtypeStruct((batch, 2 * half), jnp.bfloat16),
         scratch_shapes=[
             pltpu.VMEM((2 * key_rows, batch), jnp.float32),
-            pltpu.VMEM((chunks, key_rows, half, batch // chunks), jnp.float32),
-            pltpu.SemaphoreType.DMA((chunks,)),
+            pltpu.VMEM((2 * half, batch), jnp.float32),
         ],
-        compiler_params=pltpu.CompilerParams(vmem_limit_bytes=60 * 1024 * 1024),
+        compiler_params=pltpu.CompilerParams(vmem_limit_bytes=12 * 1024 * 1024),
         cost_estimate=pl.CostEstimate(
             flops=4 * state.size, bytes_accessed=4 * state.size, transcendentals=0
         ),
-    )(landed, state)
+    )(landed, pltpu.with_memory_space_constraint(state, pltpu.HBM))
 
 
 def state_update_kernel(landed_ref, sent_ref, state_ref, out_ref, key_ref, write_ref, decay_ref):
     pieces, both, width = landed_ref.shape
-    key_rows, half, lanes = state_ref.shape
+    slab, half, batch = state_ref.shape
+    key_rows = both // 2
     rows = width // 2
-    at_decay = both_rows(rows, pieces)
+    at_decay = rows + 4 * pieces * rows // 128
     step = pl.program_id(0)
 
     @pl.when(step == 0)
@@ -117,28 +126,25 @@
                 write_ref[:, at : at + rows] = turned[c * half : (c + 1) * half]
                 decay_ref[:, at : at + rows] = sent_ref[k, at_decay + c : at_decay + c + 1, :rows]
 
-    for at in range(0, lanes, 128):
-        here = pl.ds(pl.multiple_of(step * lanes + at, 128), 128)
-        write = write_ref[:, here]
-        decay = decay_ref[:, here]
-        key = key_ref[:, here]
-        for k in range(key_rows):
-            tile = state_ref[k, :, at : at + 128]
-            row = key[key_rows + k : key_rows + k + 1]
-            out_ref[k, :, at : at + 128] = decay * tile + row * write
-
-
-def both_rows(rows, pieces):
-    return rows + 4 * pieces * rows // 128
+    def update(first):
+        for at in range(0, batch, 128):
+            write = write_ref[:, at : at + 128]
+            decay = decay_ref[:, at : at + 128]
+            for k in range(slab):
+                row = key_ref[key_rows + first + k : key_rows + first + k + 1, at : at + 128]
+                out_ref[k, :, at : at + 128] = decay * state_ref[k, :, at : at + 128] + row * write
+
+    for part in range(key_rows // slab):
+        pl.when(step == part)(functools.partial(update, part * slab))
 
 
 def state_update(landed, sent, state):
     key_rows, half, batch = state.shape
-    lanes = 384
-    block = pl.BlockSpec((key_rows, half, lanes), lambda i: (0, 0, i))
+    slab = 4
+    block = pl.BlockSpec((slab, half, batch), lambda i: (i, 0, 0))
     return pl.pallas_call(
         state_update_kernel,
-        grid=(batch // lanes,),
+        grid=(key_rows // slab,),
         in_specs=[
             pl.BlockSpec(landed.shape, lambda i: (0, 0, 0)),
             pl.BlockSpec(sent.shape, lambda i: (0, 0, 0)),
@@ -151,11 +157,11 @@
             pltpu.VMEM((half, batch), jnp.float32),
             pltpu.VMEM((1, batch), jnp.float32),
         ],
-        compiler_params=pltpu.CompilerParams(vmem_limit_bytes=60 * 1024 * 1024),
+        compiler_params=pltpu.CompilerParams(vmem_limit_bytes=12 * 1024 * 1024),
         cost_estimate=pl.CostEstimate(
             flops=3 * state.size, bytes_accessed=8 * state.size, transcendentals=0
         ),
-    )(landed, sent, state)
+    )(landed, sent, pltpu.with_memory_space_constraint(state, pltpu.HBM))
 
 
 def per_device(
@@ -287,7 +293,6 @@
 
     middle = n_z // 2
     by_distance = [None] * n_z
-    by_distance[0] = statistics(final, ids[:, :1])
     up = down = (final[:, : D // 2], final[:, D // 2 :])
     for step in range(1, middle):
         pairs = [(along_z(u, 1), along_z(d, -1)) for u, d in zip(up, down)]
@@ -299,7 +304,10 @@
         )
         by_distance[back], by_distance[step] = two[:, :rows], two[:, rows:]
     block = jnp.concatenate([along_z(up[0], 1), along_z(down[1], -1)], axis=1)
-    by_distance[middle] = statistics(block, ids[:, middle : middle + 1])
+    two = statistics(
+        jnp.concatenate([final, block]), jnp.concatenate([ids[:, :1], ids[:, middle : middle + 1]])
+    )
+    by_distance[0], by_distance[middle] = two[:, :rows], two[:, rows:]
     stats = jnp.stack(by_distance)
     stats = lax.dynamic_slice_in_dim(jnp.concatenate([stats, stats]), n_z - zed, n_z, 0)
     stats = jnp.moveaxis(stats, 1, 0).reshape(4, n_z * rows)

time: 182 us -> 178 us (0.978)
  waiting for transfers between devices: 31.3 us -> 37.4 us
  starting transfers between devices: 64.4 us -> 58.6 us
  matrix products: 25 us -> 20.3 us
  other arithmetic: 7.01 us -> 9.86 us
  Pallas kernels: 11.6 us -> 9.68 us
    all_to_all x5, waiting for transfers between devices: 24.6 us -> 29 us  [exchange(): return lax.all_to_all(blocks, axes, split_axis=0, concat_axis=0, tiled=True)]
    dot_general x5 -> x4, matrix products: 17.9 us -> 14.1 us  [statistics(): logits = jnp.dot(block, lm_both, preferred_element_type=jnp.float32)]
    ppermute x14, starting transfers between devices: 19 us -> 15.3 us  [along_z(): return lax.ppermute(block, Z, [(k, (k + step) % n_z) for k in range(n_z)])]
    ppermute x12, starting transfers between devices: 21 us -> 18.8 us  [swapped(): return lax.ppermute(array, CORE, [(0, 1), (1, 0)])]
    ppermute x14, waiting for transfers between devices: 2.53 us -> 4.49 us  [along_z(): return lax.ppermute(block, Z, [(k, (k + step) % n_z) for k in range(n_z)])]
    pallas_call x2, Pallas kernels: 11.6 us -> 9.68 us  [the longest x1 5.44 us: state_update(): pl.pallas_call(state_update_kernel, grid=(key_rows // slab,), in_specs=[p...]
    unnamed x39 -> x20, local copies, waits for them, and re-layouts: 5.02 us -> 3.95 us
  transfers between devices with their start and end apart: 32 -> 32, of which waited for: 10 -> 13; matrix products, arithmetic and copies ran while one was open for 14% -> 19% of each run, Pallas kernels for 6% -> 5%
where the time goes in v7:
time: 178 us; the launch traced here: 176 us
  starting transfers between devices  58.6 us (33%)
  waiting for transfers between devices  37.4 us (21%)
  matrix products  20.3 us (11%)
  between operations  14.7 us (8%)
  blocking collectives  14.2 us (8%)
  local copies, waits for them, and re-layouts  11.7 us (7%)
  other arithmetic  9.86 us (6%)
  Pallas kernels  9.68 us (5%)
    all_to_all x5, waiting for transfers between devices, exchange(): return lax.all_to_all(blocks, axes, split_axis=0, concat_axis=0, tiled=True)  29 us
    all_to_all x5, starting transfers between devices, exchange(): return lax.all_to_all(blocks, axes, split_axis=0, concat_axis=0, tiled=True)  24.4 us
    ppermute x12, starting transfers between devices, swapped(): return lax.ppermute(array, CORE, [(0, 1), (1, 0)])  18.8 us
    ppermute x14, starting transfers between devices, along_z(): return lax.ppermute(block, Z, [(k, (k + step) % n_z) for k in range(n_z)])  15.3 us
    all_to_all x1, blocking collectives, exchange(): return lax.all_to_all(blocks, axes, split_axis=0, concat_axis=0, tiled=True)  14.2 us
    dot_general x4, matrix products, statistics(): logits = jnp.dot(block, lm_both, preferred_element_type=jnp.float32)  14.1 us
    pallas_call x1, Pallas kernels, state_update(): pl.pallas_call(state_update_kernel, grid=(key_rows // slab,), in_specs=[p...  5.44 us
    dot_general x1, matrix products, per_device(): jnp.dot(mixed_full, out_full, preferred_element_type=jnp.float32)  5.08 us
  transfers between devices with their start and end apart: 32, of which 13 were waited for; matrix products, arithmetic and copies ran while one was open for 19% of the time, Pallas kernels for 5%

profile of v7, /device:TPU:1, one launch (start us, length us, event | category | flops | bytes accessed | tf_op | source)
XLA Modules:
  0.0 176.5 jit_solution(15649428105693190365)
XLA Ops:
  7.2 0.7 all-gather.2.cloned.1.call-update
  7.9 3.3 %collective-permute-start.1 = (bf16[64]{0:T(256)(128)(2,1)}, bf16[64]{0:T(256)(128)(2,1)S(1)}, u32[]{:S(2)}, u32[]{:S(2)}) collective-permute-start(bf16[64]{0:T(256)(128)(2,1)} %param.30), channel_id=1, source_target_pairs={{0,8},{8,0},{1,9},{9,1},{2,10},{10,2},{3,11},{11,3},{4,12},{12,4},... | collective-permute-start | bytes 392 | tf_op jit(solution)/shard_map/ppermute | solution.py:26
  11.3 0.9 collective-permute-done.1
  13.1 0.8 broadcast_select_fusion.4
  14.2 0.8 broadcast_in_dim.52
  16.0 5.0 %all-to-all-start = ((bf16[16,73,128]{2,1,0:T(8,128)(2,1)}), bf16[16,73,128]{2,1,0:T(8,128)(2,1)S(1)}, u32[]{:S(2)}, u32[]{:S(2)}) async-start(bf16[16,73,128]{2,1,0:T(8,128)(2,1)} %broadcast_in_dim.52), calls=%async_computation | async-start | bytes 655360 | tf_op jit(solution)/shard_map/all_to_all | solution.py:30
  21.0 0.7 fusion.100
  21.7 1.3 pad_maximum_fusion
  23.0 1.0 pad_maximum_fusion.1
  24.0 5.0 %all-to-all-done = bf16[16,73,128]{2,1,0:T(8,128)(2,1)S(1)} async-done(((bf16[16,73,128]{2,1,0:T(8,128)(2,1)}), bf16[16,73,128]{2,1,0:T(8,128)(2,1)S(1)}, u32[]{:S(2)}, u32[]{:S(2)}) %all-to-all-start) | async-done | bytes 299040 | tf_op jit(solution)/shard_map/all_to_all | solution.py:30
  30.5 2.2 %collective-permute-start.6 = (bf16[2,128,72]{2,1,0:T(8,128)(2,1)S(1)}, bf16[2,128,72]{2,1,0:T(8,128)(2,1)S(1)}, u32[]{:S(2)}, u32[]{:S(2)}) collective-permute-start(bf16[2,128,72]{2,1,0:T(8,128)(2,1)S(1)} %get-tuple-element.87), channel_id=1, source_target_pairs={{0,8},{8,0},{1,9},{9,1},{2,10},{10,2},{3,11},{11,3},{4,12},{12,4},... | collective-permute-start | bytes 110600 | tf_op jit(solution)/shard_map/ppermute | solution.py:26
  32.7 0.9 collective-permute-done.6
  34.7 8.3 %all-to-all-start.1 = ((bf16[8,32,144]{2,1,0:T(8,128)(2,1)}), bf16[8,32,144]{2,1,0:T(8,128)(2,1)S(1)}, u32[]{:S(2)}, u32[]{:S(2)}) async-start(bf16[8,32,144]{2,1,0:T(8,128)(2,1)} %bitcast.169), calls=%async_computation.1 | async-start | bytes 262144 | tf_op jit(solution)/shard_map/all_to_all | solution.py:30
  43.1 8.3 %all-to-all-done.1.landed_ref = bf16[8,32,144]{2,1,0:T(8,128)(2,1)S(1)} async-done(((bf16[8,32,144]{2,1,0:T(8,128)(2,1)}), bf16[8,32,144]{2,1,0:T(8,128)(2,1)S(1)}, u32[]{:S(2)}, u32[]{:S(2)}) %all-to-all-start.1) | async-done | bytes 73760 | tf_op jit(solution)/shard_map/all_to_all | solution.py:30
  51.4 4.2 %shard_map.192 = bf16[1152,128]{1,0:T(8,128)(2,1)} custom-call(bf16[8,32,144]{2,1,0:T(8,128)(2,1)S(1)} %all-to-all-done.1.landed_ref, f32[16,64,1152]{2,1,0:T(8,128)} %state_ref.3), custom_call_target="tpu_custom_call" | custom-call | flops 4718592 | bytes 4718592 | tf_op jit(solution)/shard_map/pallas_call | solution.py:91
  56.6 0.7 fusion.83
  57.3 1.7 collective-permute-start.24
  59.0 4.1 %all-to-all-start.2 = ((bf16[8,144,128]{2,1,0:T(8,128)(2,1)}), bf16[8,144,128]{2,1,0:T(8,128)(2,1)}, u32[]{:S(2)}, u32[]{:S(2)}) async-start(bf16[8,144,128]{2,1,0:T(8,128)(2,1)} %bitcast.17), calls=%async_computation.2 | async-start | bytes 589824 | tf_op jit(solution)/shard_map/all_to_all | solution.py:30
  63.4 3.7 %constant_dynamic-update-slice_fusion.1 = bf16[2048,1280]{1,0:T(8,128)(2,1)} fusion(bf16[2048,640]{1,0:T(8,128)(2,1)} %param.31), kind=kLoop, calls=%fused_computation.146 | loop fusion | bytes 5242880
  67.1 1.8 %constant_dynamic-update-slice_fusion = bf16[2048,1280]{1,0:T(8,128)(2,1)} fusion(bf16[2048,1280]{1,0:T(8,128)(2,1)} %constant_dynamic-update-slice_fusion.1, bf16[2048,640]{1,0:T(8,128)(2,1)S(1)} %collective-permute-done.7), kind=kLoop, calls=%fused_computation.145 | loop fusion | bytes 5242880 | tf_op jit(solution)/shard_map/concatenate | solution.py:242
  68.9 7.3 %all-to-all-done.2 = bf16[8,144,128]{2,1,0:T(8,128)(2,1)} async-done(((bf16[8,144,128]{2,1,0:T(8,128)(2,1)}), bf16[8,144,128]{2,1,0:T(8,128)(2,1)}, u32[]{:S(2)}, u32[]{:S(2)}) %all-to-all-start.2) | async-done | bytes 294944 | tf_op jit(solution)/shard_map/all_to_all | solution.py:30
  76.2 1.0 convert_reduce_fusion
  79.0 0.8 broadcast_in_dim.54
  79.8 3.5 %all-to-all-start.3 = ((bf16[16,72,128]{2,1,0:T(8,128)(2,1)}), bf16[16,72,128]{2,1,0:T(8,128)(2,1)S(1)}, u32[]{:S(2)}, u32[]{:S(2)}) async-start(bf16[16,72,128]{2,1,0:T(8,128)(2,1)} %broadcast_in_dim.54), calls=%async_computation.3 | async-start | bytes 589824 | tf_op jit(solution)/shard_map/all_to_all | solution.py:30
  84.1 7.2 %all-to-all-done.3 = bf16[16,72,128]{2,1,0:T(8,128)(2,1)S(1)} async-done(((bf16[16,72,128]{2,1,0:T(8,128)(2,1)}), bf16[16,72,128]{2,1,0:T(8,128)(2,1)S(1)}, u32[]{:S(2)}, u32[]{:S(2)}) %all-to-all-start.3) | async-done | bytes 294944 | tf_op jit(solution)/shard_map/all_to_all | solution.py:30
  91.2 5.1 %multiply_reduce_fusion.4 = (f32[72]{0:T(128)S(1)}, f32[72,2048]{1,0:T(8,128)S(1)}) fusion(bf16[2048,2048]{1,0:T(8,128)(2,1)} %all-gather.2.cloned.1.call-done, bf16[16,73,128]{2,1,0:T(8,128)(2,1)S(1)} %all-to-all-done, bf16[16,72,128]{2,1,0:T(8,128)(2,1)S(1)} %all-to-all-done.3), kind=kOutput, calls=%fused_computation.59 | convolution fusion | flops 604569536 | bytes 9568544 | tf_op jit(solution)/shard_map/dot_general | solution.py:272
  96.6 1.5 collective-permute-start.19
  98.1 1.3 collective-permute-start.18
  99.5 1.0 collective-permute-done.14
  100.6 1.6 collective-permute-start.15
  102.3 0.9 collective-permute-done.18
  103.3 2.1 %collective-permute-start.20 = (bf16[72,1024]{1,0:T(8,128)(2,1)S(1)}, bf16[72,1024]{1,0:T(8,128)(2,1)S(1)}, u32[]{:S(2)}, u32[]{:S(2)}) collective-permute-start(bf16[72,1024]{1,0:T(8,128)(2,1)S(1)} %collective-permute-done.18), channel_id=1, source_target_pairs={{0,7},{1,0},{2,1},{3,2},{4,3},{5,4},{6,5},{7,6},{8,15},{9,8},{10,9... | collective-permute-start | bytes 442376 | tf_op jit(solution)/shard_map/ppermute | solution.py:292
  105.8 3.5 %fusion.102 = (f32[144]{0:T(256)S(1)}, f32[144,1280]{1,0:T(8,128)S(1)}) fusion(bf16[2048,1280]{1,0:T(8,128)(2,1)} %constant_dynamic-update-slice_fusion, bf16[72,1024]{1,0:T(8,128)(2,1)S(1)} %collective-permute-done.14, bf16[72,1024]{1,0:T(8,128)(2,1)S(1)} %collective-permute-done.19, bf16[72,1024]{1,0:T(8,128)(2,1)S(1)} %collective-permute-done.18, ...), kind=kOutput, calls=%fused_computation.215 | convolution fusion | flops 757518208 | bytes 6570560 | tf_op jit(solution)/shard_map/dot_general | solution.py:283
  109.3 2.8 %collective-permute-start.16 = (bf16[72,1024]{1,0:T(8,128)(2,1)S(1)}, bf16[72,1024]{1,0:T(8,128)(2,1)S(1)}, u32[]{:S(2)}, u32[]{:S(2)}) collective-permute-start(bf16[72,1024]{1,0:T(8,128)(2,1)S(1)} %collective-permute-done.15), channel_id=1, source_target_pairs={{0,7},{1,0},{2,1},{3,2},{4,3},{5,4},{6,5},{7,6},{8,15},{9,8},{10,9... | collective-permute-start | bytes 442376 | tf_op jit(solution)/shard_map/ppermute | solution.py:292
  112.1 2.7 %collective-permute-start.22 = (bf16[72,1024]{1,0:T(8,128)(2,1)S(1)}, bf16[72,1024]{1,0:T(8,128)(2,1)S(1)}, u32[]{:S(2)}, u32[]{:S(2)}) collective-permute-start(bf16[72,1024]{1,0:T(8,128)(2,1)S(1)} %collective-permute-done.20), channel_id=1, source_target_pairs={{0,7},{1,0},{2,1},{3,2},{4,3},{5,4},{6,5},{7,6},{8,15},{9,8},{10,9... | collective-permute-start | bytes 442376 | tf_op jit(solution)/shard_map/ppermute | solution.py:292
  114.7 3.5 %fusion.103 = (f32[144]{0:T(256)S(1)}, f32[144,1280]{1,0:T(8,128)S(1)}) fusion(bf16[2048,1280]{1,0:T(8,128)(2,1)} %constant_dynamic-update-slice_fusion, bf16[72,1024]{1,0:T(8,128)(2,1)S(1)} %collective-permute-done.15, bf16[72,1024]{1,0:T(8,128)(2,1)S(1)} %collective-permute-done.21, bf16[72,1024]{1,0:T(8,128)(2,1)S(1)} %collective-permute-done.20, ...), kind=kOutput, calls=%fused_computation.216 | convolution fusion | flops 757518208 | bytes 6570560 | tf_op jit(solution)/shard_map/dot_general | solution.py:283
  118.3 3.0 %collective-permute-start.17 = (bf16[72,1024]{1,0:T(8,128)(2,1)S(1)}, bf16[72,1024]{1,0:T(8,128)(2,1)S(1)}, u32[]{:S(2)}, u32[]{:S(2)}) collective-permute-start(bf16[72,1024]{1,0:T(8,128)(2,1)S(1)} %collective-permute-done.16), channel_id=1, source_target_pairs={{0,7},{1,0},{2,1},{3,2},{4,3},{5,4},{6,5},{7,6},{8,15},{9,8},{10,9... | collective-permute-start | bytes 442376 | tf_op jit(solution)/shard_map/ppermute | solution.py:292
  121.3 3.5 %fusion.101 = (f32[144]{0:T(256)S(1)}, f32[144,1280]{1,0:T(8,128)S(1)}) fusion(bf16[2048,1280]{1,0:T(8,128)(2,1)} %constant_dynamic-update-slice_fusion, bf16[72,1024]{1,0:T(8,128)(2,1)S(1)} %collective-permute-done.16, bf16[72,1024]{1,0:T(8,128)(2,1)S(1)} %collective-permute-done.23, bf16[72,1024]{1,0:T(8,128)(2,1)S(1)} %collective-permute-done.22, ...), kind=kOutput, calls=%fused_computation.214 | convolution fusion | flops 757518208 | bytes 6570560 | tf_op jit(solution)/shard_map/dot_general | solution.py:283
  124.8 2.1 %collective-permute-done.13 = bf16[72,1024]{1,0:T(8,128)(2,1)S(1)} collective-permute-done((bf16[72,1024]{1,0:T(8,128)(2,1)S(1)}, bf16[72,1024]{1,0:T(8,128)(2,1)S(1)}, u32[]{:S(2)}, u32[]{:S(2)}) %collective-permute-start.13) | collective-permute-done | bytes 147488 | tf_op jit(solution)/shard_map/ppermute | solution.py:292
  127.0 3.5 %fusion.104 = (f32[144]{0:T(256)S(1)}, f32[144,1280]{1,0:T(8,128)S(1)}) fusion(bf16[2048,1280]{1,0:T(8,128)(2,1)} %constant_dynamic-update-slice_fusion, bf16[72,1024]{1,0:T(8,128)(2,1)S(1)} %collective-permute-done.17, bf16[72,1024]{1,0:T(8,128)(2,1)S(1)} %collective-permute-done.13, bf16[72,2048]{1,0:T(8,128)(2,1)S(1)} %multiply_convert_fusion), kind=kOutput, calls=%fused_computation.217 | convolution fusion | flops 756928384 | bytes 6570560 | tf_op jit(solution)/shard_map/dot_general | solution.py:283
  130.5 1.2 fusion
  132.5 14.2 %all_to_all.30.sent_ref = f32[8,96,128]{2,1,0:T(8,128)S(1)} all-to-all(f32[8,96,128]{2,1,0:T(8,128)S(1)} %broadcast_in_dim.57), channel_id=1, replica_groups=mesh['row_0'=4,'row_1'=4,'row_2'=2,'col'=8] {'col'}, dimensions={0} | all-to-all | bytes 786432 | tf_op jit(solution)/shard_map/all_to_all | solution.py:30
  147.7 3.5 %all-to-all-start.5 = ((f32[16,4,576]{2,1,0:T(4,128)}), f32[16,4,576]{2,1,0:T(4,128)S(1)}, u32[]{:S(2)}, u32[]{:S(2)}) async-start(f32[16,4,576]{2,1,0:T(4,128)} %broadcast_in_dim.59), calls=%async_computation.5 | async-start | bytes 327680 | tf_op jit(solution)/shard_map/all_to_all | solution.py:30
  151.3 5.4 %shard_map.193 = f32[16,64,1152]{2,1,0:T(8,128)} custom-call(bf16[8,32,144]{2,1,0:T(8,128)(2,1)S(1)} %all-to-all-done.1.landed_ref, f32[8,96,128]{2,1,0:T(8,128)S(1)} %all_to_all.30.sent_ref, f32[16,64,1152]{2,1,0:T(8,128)} %state_ref.3), custom_call_target="tpu_custom_call" | custom-call | flops 3538944 | bytes 9437184 | tf_op jit(solution)/shard_map/pallas_call | solution.py:145
  156.7 1.3 all-to-all-done.5
  158.2 8.9 %collective-permute-start.25 = (f32[2,576]{1,0:T(2,128)S(1)}, f32[2,576]{1,0:T(2,128)S(1)}, u32[]{:S(2)}, u32[]{:S(2)}) collective-permute-start(f32[2,576]{1,0:T(2,128)S(1)} %pad_maximum_fusion.8), channel_id=1, source_target_pairs={{0,8},{8,0},{1,9},{9,1},{2,10},{10,2},{3,11},{11,3},{4,12},{12,4},... | collective-permute-start | bytes 13832 | tf_op jit(solution)/shard_map/ppermute | solution.py:26
  167.1 0.8 collective-permute-done.25
  168.3 0.7 reshape.162
  (148 shorter events, 12.7 us)
Async XLA Ops:
  7.2 84.1 %all-gather.2.cloned.1.call-start = ((), (), s32[]{:S(2)}) async-start(), calls=%async_computation.6 | async-start | bytes 8650752 | tf_op jit(solution)/shard_map/all_gather | solution.py:200
  7.9 4.3 %collective-permute-start.1 = (bf16[64]{0:T(256)(128)(2,1)}, bf16[64]{0:T(256)(128)(2,1)S(1)}, u32[]{:S(2)}, u32[]{:S(2)}) collective-permute-start(bf16[64]{0:T(256)(128)(2,1)} %param.30), channel_id=1, source_target_pairs={{0,8},{8,0},{1,9},{9,1},{2,10},{10,2},{3,11},{11,3},{4,12},{12,4},... | collective-permute-start | bytes 392 | tf_op jit(solution)/shard_map/ppermute | solution.py:26
  11.2 1.8 %collective-permute-start = (bf16[144,64]{0,1:T(8,128)(2,1)}, bf16[144,64]{0,1:T(8,128)(2,1)S(1)}, u32[]{:S(2)}, u32[]{:S(2)}) collective-permute-start(bf16[144,64]{0,1:T(8,128)(2,1)} %param.17), channel_id=1, source_target_pairs={{0,8},{8,0},{1,9},{9,1},{2,10},{10,2},{3,11},{11,3},{4,12},{12,4},... | collective-permute-start | bytes 55304 | tf_op jit(solution)/shard_map/ppermute | solution.py:26
  14.9 6.7 %collective-permute-start.2 = (bf16[2048,64]{0,1:T(8,128)(2,1)}, bf16[2048,64]{0,1:T(8,128)(2,1)S(1)}, u32[]{:S(2)}, u32[]{:S(2)}) collective-permute-start(bf16[2048,64]{0,1:T(8,128)(2,1)} %param.20), channel_id=1, source_target_pairs={{0,8},{8,0},{1,9},{9,1},{2,10},{10,2},{3,11},{11,3},{4,12},{12,4},... | collective-permute-start | bytes 786440 | tf_op jit(solution)/shard_map/ppermute | solution.py:26
  15.2 6.4 %collective-permute-start.3 = (bf16[2048,64]{0,1:T(8,128)(2,1)}, bf16[2048,64]{0,1:T(8,128)(2,1)S(1)}, u32[]{:S(2)}, u32[]{:S(2)}) collective-permute-start(bf16[2048,64]{0,1:T(8,128)(2,1)} %param.21), channel_id=1, source_target_pairs={{0,8},{8,0},{1,9},{9,1},{2,10},{10,2},{3,11},{11,3},{4,12},{12,4},... | collective-permute-start | bytes 786440 | tf_op jit(solution)/shard_map/ppermute | solution.py:26
  15.5 6.2 %collective-permute-start.4 = (bf16[2048,64]{0,1:T(8,128)(2,1)}, bf16[2048,64]{0,1:T(8,128)(2,1)S(1)}, u32[]{:S(2)}, u32[]{:S(2)}) collective-permute-start(bf16[2048,64]{0,1:T(8,128)(2,1)} %param.22), channel_id=1, source_target_pairs={{0,8},{8,0},{1,9},{9,1},{2,10},{10,2},{3,11},{11,3},{4,12},{12,4},... | collective-permute-start | bytes 786440 | tf_op jit(solution)/shard_map/ppermute | solution.py:26
  15.8 5.9 %collective-permute-start.5 = (bf16[2048,64]{0,1:T(8,128)(2,1)}, bf16[2048,64]{0,1:T(8,128)(2,1)}, u32[]{:S(2)}, u32[]{:S(2)}) collective-permute-start(bf16[2048,64]{0,1:T(8,128)(2,1)} %param.23), channel_id=1, source_target_pairs={{0,8},{8,0},{1,9},{9,1},{2,10},{10,2},{3,11},{11,3},{4,12},{12,4},... | collective-permute-start | bytes 786440 | tf_op jit(solution)/shard_map/ppermute | solution.py:26
  16.0 13.0 %all-to-all-start = ((bf16[16,73,128]{2,1,0:T(8,128)(2,1)}), bf16[16,73,128]{2,1,0:T(8,128)(2,1)S(1)}, u32[]{:S(2)}, u32[]{:S(2)}) async-start(bf16[16,73,128]{2,1,0:T(8,128)(2,1)} %broadcast_in_dim.52), calls=%async_computation | async-start | bytes 655360 | tf_op jit(solution)/shard_map/all_to_all | solution.py:30
  30.5 3.1 %collective-permute-start.6 = (bf16[2,128,72]{2,1,0:T(8,128)(2,1)S(1)}, bf16[2,128,72]{2,1,0:T(8,128)(2,1)S(1)}, u32[]{:S(2)}, u32[]{:S(2)}) collective-permute-start(bf16[2,128,72]{2,1,0:T(8,128)(2,1)S(1)} %get-tuple-element.87), channel_id=1, source_target_pairs={{0,8},{8,0},{1,9},{9,1},{2,10},{10,2},{3,11},{11,3},{4,12},{12,4},... | collective-permute-start | bytes 110600 | tf_op jit(solution)/shard_map/ppermute | solution.py:26
  34.4 21.2 %collective-permute-start.7 = (bf16[2048,640]{1,0:T(8,128)(2,1)}, bf16[2048,640]{1,0:T(8,128)(2,1)S(1)}, u32[]{:S(2)}, u32[]{:S(2)}) collective-permute-start(bf16[2048,640]{1,0:T(8,128)(2,1)} %param.31), channel_id=1, source_target_pairs={{0,8},{8,0},{1,9},{9,1},{2,10},{10,2},{3,11},{11,3},{4,12},{12,4},... | collective-permute-start | bytes 7864328 | tf_op jit(solution)/shard_map/ppermute | solution.py:26
  34.7 16.6 %all-to-all-start.1 = ((bf16[8,32,144]{2,1,0:T(8,128)(2,1)}), bf16[8,32,144]{2,1,0:T(8,128)(2,1)S(1)}, u32[]{:S(2)}, u32[]{:S(2)}) async-start(bf16[8,32,144]{2,1,0:T(8,128)(2,1)} %bitcast.169), calls=%async_computation.1 | async-start | bytes 262144 | tf_op jit(solution)/shard_map/all_to_all | solution.py:30
  43.1 12.6 %copy-start.7 = (f32[16]{0:T(128)S(1)}, f32[16]{0:T(128)}, u32[]{:S(2)}) copy-start(f32[16]{0:T(128)} %param.26) | copy-start | bytes 196
  43.1 13.2 %copy-start.5 = (bf16[2048,16]{0,1:T(8,128)(2,1)S(1)}, bf16[2048,16]{0,1:T(8,128)(2,1)}, u32[]{:S(2)}) copy-start(bf16[2048,16]{0,1:T(8,128)(2,1)} %param.25) | copy-start | bytes 196612
  43.1 13.4 %copy-start.4 = (f32[16]{0:T(128)S(1)}, f32[16]{0:T(128)}, u32[]{:S(2)}) copy-start(f32[16]{0:T(128)} %param.27) | copy-start | bytes 196
  43.1 20.0 %copy-start.2 = (s32[1152]{0:T(1024)S(1)}, s32[1152]{0:T(1024)}, u32[]{:S(2)}) copy-start(s32[1152]{0:T(1024)} %param.32) | copy-start | bytes 13828
  51.4 4.9 %copy-start.6 = (bf16[2048,16]{0,1:T(8,128)(2,1)S(1)}, bf16[2048,16]{0,1:T(8,128)(2,1)}, u32[]{:S(2)}) copy-start(bf16[2048,16]{0,1:T(8,128)(2,1)} %param.24) | copy-start | bytes 196612
  57.3 26.0 %collective-permute-start.24 = (f32[1,72]{1,0:T(1,128)S(1)}, f32[1,72]{1,0:T(1,128)S(1)}, u32[]{:S(2)}, u32[]{:S(2)}) collective-permute-start(f32[1,72]{1,0:T(1,128)S(1)} %fusion.83), channel_id=1, source_target_pairs={{0,8},{8,0},{1,9},{9,1},{2,10},{10,2},{3,11},{11,3},{4,12},{12,4},... | collective-permute-start | bytes 872 | tf_op jit(solution)/shard_map/ppermute | solution.py:26
  59.0 17.1 %all-to-all-start.2 = ((bf16[8,144,128]{2,1,0:T(8,128)(2,1)}), bf16[8,144,128]{2,1,0:T(8,128)(2,1)}, u32[]{:S(2)}, u32[]{:S(2)}) async-start(bf16[8,144,128]{2,1,0:T(8,128)(2,1)} %bitcast.17), calls=%async_computation.2 | async-start | bytes 589824 | tf_op jit(solution)/shard_map/all_to_all | solution.py:30
  67.1 11.7 %copy-start.3 = (f32[128]{0:T(128)S(1)}, f32[128]{0:T(128)}, u32[]{:S(2)}) copy-start(f32[128]{0:T(128)} %param.28) | copy-start | bytes 1540
  77.3 1.4 collective-permute-start.8
  79.8 11.5 %all-to-all-start.3 = ((bf16[16,72,128]{2,1,0:T(8,128)(2,1)}), bf16[16,72,128]{2,1,0:T(8,128)(2,1)S(1)}, u32[]{:S(2)}, u32[]{:S(2)}) async-start(bf16[16,72,128]{2,1,0:T(8,128)(2,1)} %broadcast_in_dim.54), calls=%async_computation.3 | async-start | bytes 589824 | tf_op jit(solution)/shard_map/all_to_all | solution.py:30
  83.4 16.1 %collective-permute-start.9 = (f32[72,64]{0,1:T(8,128)S(1)}, f32[72,64]{0,1:T(8,128)S(1)}, u32[]{:S(2)}, u32[]{:S(2)}) collective-permute-start(f32[72,64]{0,1:T(8,128)S(1)} %constant_dynamic-slice_fusion.3), channel_id=1, source_target_pairs={{0,8},{8,0},{1,9},{9,1},{2,10},{10,2},{3,11},{11,3},{4,12},{12,4},... | collective-permute-start | bytes 55304 | tf_op jit(solution)/shard_map/ppermute | solution.py:26
  96.5 4.1 %collective-permute-start.14 = (bf16[72,1024]{1,0:T(8,128)(2,1)S(1)}, bf16[72,1024]{1,0:T(8,128)(2,1)S(1)}, u32[]{:S(2)}, u32[]{:S(2)}) collective-permute-start(bf16[72,1024]{1,0:T(8,128)(2,1)S(1)} %get-tuple-element.91), channel_id=1, source_target_pairs={{0,7},{1,0},{2,1},{3,2},{4,3},{5,4},{6,5},{7,6},{8,15},{9,8},{10,9... | collective-permute-start | bytes 442376 | tf_op jit(solution)/shard_map/ppermute | solution.py:292
  96.6 5.5 %collective-permute-start.19 = (bf16[72,1024]{1,0:T(8,128)(2,1)S(1)}, bf16[72,1024]{1,0:T(8,128)(2,1)S(1)}, u32[]{:S(2)}, u32[]{:S(2)}) collective-permute-start(bf16[72,1024]{1,0:T(8,128)(2,1)S(1)} %get-tuple-element.91), channel_id=1, source_target_pairs={{0,1},{1,2},{2,3},{3,4},{4,5},{5,6},{6,7},{7,0},{8,9},{9,10},{10,1... | collective-permute-start | bytes 442376 | tf_op jit(solution)/shard_map/ppermute | solution.py:292
  98.1 5.2 %collective-permute-start.18 = (bf16[72,1024]{1,0:T(8,128)(2,1)S(1)}, bf16[72,1024]{1,0:T(8,128)(2,1)S(1)}, u32[]{:S(2)}, u32[]{:S(2)}) collective-permute-start(bf16[72,1024]{1,0:T(8,128)(2,1)S(1)} %get-tuple-element.90), channel_id=1, source_target_pairs={{0,7},{1,0},{2,1},{3,2},{4,3},{5,4},{6,5},{7,6},{8,15},{9,8},{10,9... | collective-permute-start | bytes 442376 | tf_op jit(solution)/shard_map/ppermute | solution.py:292
  99.4 6.4 %collective-permute-start.10 = (bf16[72,1024]{1,0:T(8,128)(2,1)S(1)}, bf16[72,1024]{1,0:T(8,128)(2,1)S(1)}, u32[]{:S(2)}, u32[]{:S(2)}) collective-permute-start(bf16[72,1024]{1,0:T(8,128)(2,1)S(1)} %get-tuple-element.90), channel_id=1, source_target_pairs={{0,1},{1,2},{2,3},{3,4},{4,5},{5,6},{6,7},{7,0},{8,9},{9,10},{10,1... | collective-permute-start | bytes 442376 | tf_op jit(solution)/shard_map/ppermute | solution.py:292
  100.6 8.7 %collective-permute-start.15 = (bf16[72,1024]{1,0:T(8,128)(2,1)S(1)}, bf16[72,1024]{1,0:T(8,128)(2,1)S(1)}, u32[]{:S(2)}, u32[]{:S(2)}) collective-permute-start(bf16[72,1024]{1,0:T(8,128)(2,1)S(1)} %collective-permute-done.14), channel_id=1, source_target_pairs={{0,7},{1,0},{2,1},{3,2},{4,3},{5,4},{6,5},{7,6},{8,15},{9,8},{10,9... | collective-permute-start | bytes 442376 | tf_op jit(solution)/shard_map/ppermute | solution.py:292
  102.1 9.9 %collective-permute-start.21 = (bf16[72,1024]{1,0:T(8,128)(2,1)S(1)}, bf16[72,1024]{1,0:T(8,128)(2,1)S(1)}, u32[]{:S(2)}, u32[]{:S(2)}) collective-permute-start(bf16[72,1024]{1,0:T(8,128)(2,1)S(1)} %collective-permute-done.19), channel_id=1, source_target_pairs={{0,1},{1,2},{2,3},{3,4},{4,5},{5,6},{6,7},{7,0},{8,9},{9,10},{10,1... | collective-permute-start | bytes 442376 | tf_op jit(solution)/shard_map/ppermute | solution.py:292
  103.3 8.8 %collective-permute-start.20 = (bf16[72,1024]{1,0:T(8,128)(2,1)S(1)}, bf16[72,1024]{1,0:T(8,128)(2,1)S(1)}, u32[]{:S(2)}, u32[]{:S(2)}) collective-permute-start(bf16[72,1024]{1,0:T(8,128)(2,1)S(1)} %collective-permute-done.18), channel_id=1, source_target_pairs={{0,7},{1,0},{2,1},{3,2},{4,3},{5,4},{6,5},{7,6},{8,15},{9,8},{10,9... | collective-permute-start | bytes 442376 | tf_op jit(solution)/shard_map/ppermute | solution.py:292
  105.7 9.0 %collective-permute-start.11 = (bf16[72,1024]{1,0:T(8,128)(2,1)S(1)}, bf16[72,1024]{1,0:T(8,128)(2,1)S(1)}, u32[]{:S(2)}, u32[]{:S(2)}) collective-permute-start(bf16[72,1024]{1,0:T(8,128)(2,1)S(1)} %collective-permute-done.10), channel_id=1, source_target_pairs={{0,1},{1,2},{2,3},{3,4},{4,5},{5,6},{6,7},{7,0},{8,9},{9,10},{10,1... | collective-permute-start | bytes 442376 | tf_op jit(solution)/shard_map/ppermute | solution.py:292
  109.3 9.0 %collective-permute-start.16 = (bf16[72,1024]{1,0:T(8,128)(2,1)S(1)}, bf16[72,1024]{1,0:T(8,128)(2,1)S(1)}, u32[]{:S(2)}, u32[]{:S(2)}) collective-permute-start(bf16[72,1024]{1,0:T(8,128)(2,1)S(1)} %collective-permute-done.15), channel_id=1, source_target_pairs={{0,7},{1,0},{2,1},{3,2},{4,3},{5,4},{6,5},{7,6},{8,15},{9,8},{10,9... | collective-permute-start | bytes 442376 | tf_op jit(solution)/shard_map/ppermute | solution.py:292
  112.0 9.2 %collective-permute-start.23 = (bf16[72,1024]{1,0:T(8,128)(2,1)S(1)}, bf16[72,1024]{1,0:T(8,128)(2,1)S(1)}, u32[]{:S(2)}, u32[]{:S(2)}) collective-permute-start(bf16[72,1024]{1,0:T(8,128)(2,1)S(1)} %collective-permute-done.21), channel_id=1, source_target_pairs={{0,1},{1,2},{2,3},{3,4},{4,5},{5,6},{6,7},{7,0},{8,9},{9,10},{10,1... | collective-permute-start | bytes 442376 | tf_op jit(solution)/shard_map/ppermute | solution.py:292
  112.1 9.2 %collective-permute-start.22 = (bf16[72,1024]{1,0:T(8,128)(2,1)S(1)}, bf16[72,1024]{1,0:T(8,128)(2,1)S(1)}, u32[]{:S(2)}, u32[]{:S(2)}) collective-permute-start(bf16[72,1024]{1,0:T(8,128)(2,1)S(1)} %collective-permute-done.20), channel_id=1, source_target_pairs={{0,7},{1,0},{2,1},{3,2},{4,3},{5,4},{6,5},{7,6},{8,15},{9,8},{10,9... | collective-permute-start | bytes 442376 | tf_op jit(solution)/shard_map/ppermute | solution.py:292
  114.7 6.5 %collective-permute-start.12 = (bf16[72,1024]{1,0:T(8,128)(2,1)S(1)}, bf16[72,1024]{1,0:T(8,128)(2,1)S(1)}, u32[]{:S(2)}, u32[]{:S(2)}) collective-permute-start(bf16[72,1024]{1,0:T(8,128)(2,1)S(1)} %collective-permute-done.11), channel_id=1, source_target_pairs={{0,1},{1,2},{2,3},{3,4},{4,5},{5,6},{6,7},{7,0},{8,9},{9,10},{10,1... | collective-permute-start | bytes 442376 | tf_op jit(solution)/shard_map/ppermute | solution.py:292
  118.3 6.5 %collective-permute-start.17 = (bf16[72,1024]{1,0:T(8,128)(2,1)S(1)}, bf16[72,1024]{1,0:T(8,128)(2,1)S(1)}, u32[]{:S(2)}, u32[]{:S(2)}) collective-permute-start(bf16[72,1024]{1,0:T(8,128)(2,1)S(1)} %collective-permute-done.16), channel_id=1, source_target_pairs={{0,7},{1,0},{2,1},{3,2},{4,3},{5,4},{6,5},{7,6},{8,15},{9,8},{10,9... | collective-permute-start | bytes 442376 | tf_op jit(solution)/shard_map/ppermute | solution.py:292
  121.3 5.7 %collective-permute-start.13 = (bf16[72,1024]{1,0:T(8,128)(2,1)S(1)}, bf16[72,1024]{1,0:T(8,128)(2,1)S(1)}, u32[]{:S(2)}, u32[]{:S(2)}) collective-permute-start(bf16[72,1024]{1,0:T(8,128)(2,1)S(1)} %collective-permute-done.12), channel_id=1, source_target_pairs={{0,1},{1,2},{2,3},{3,4},{4,5},{5,6},{6,7},{7,0},{8,9},{9,10},{10,1... | collective-permute-start | bytes 442376 | tf_op jit(solution)/shard_map/ppermute | solution.py:292
  147.7 10.3 %all-to-all-start.5 = ((f32[16,4,576]{2,1,0:T(4,128)}), f32[16,4,576]{2,1,0:T(4,128)S(1)}, u32[]{:S(2)}, u32[]{:S(2)}) async-start(f32[16,4,576]{2,1,0:T(4,128)} %broadcast_in_dim.59), calls=%async_computation.5 | async-start | bytes 327680 | tf_op jit(solution)/shard_map/all_to_all | solution.py:30
  151.2 17.8 %copy-start.1 = (f32[1152]{0:T(1024)S(1)}, f32[1152]{0:T(1024)}, u32[]{:S(2)}) copy-start(f32[1152]{0:T(1024)} %param.33) | copy-start | bytes 13828
  158.2 9.7 %collective-permute-start.25 = (f32[2,576]{1,0:T(2,128)S(1)}, f32[2,576]{1,0:T(2,128)S(1)}, u32[]{:S(2)}, u32[]{:S(2)}) collective-permute-start(f32[2,576]{1,0:T(2,128)S(1)} %pad_maximum_fusion.8), channel_id=1, source_target_pairs={{0,8},{8,0},{1,9},{9,1},{2,10},{10,2},{3,11},{11,3},{4,12},{12,4},... | collective-permute-start | bytes 13832 | tf_op jit(solution)/shard_map/ppermute | solution.py:26
  168.2 1.4 copy-start
Sparse Core Ops, SparseCore 0:
  10.6 62.1 all-gather.1

commit v8 on v7

--- a/solution.py
+++ b/solution.py
@@ -52,60 +52,72 @@
     )
 
 
-def state_sums_kernel(landed_ref, state_ref, out_ref, qk_ref, sums_ref):
+def held_kernel(count, chunks, *refs):
+    sources, out_ref, sems = refs[:count], refs[-2], refs[-1]
+    copies = []
+    at = 0
+    for n, source in enumerate(sources):
+        width = source.shape[-1]
+        size = source.shape[0] // chunks
+        for c in range(chunks):
+            here = pl.ds(c * size, size)
+            if count == 1:
+                target = out_ref.at[here]
+            else:
+                target = out_ref.at[here, pl.ds(at, width)]
+            copies.append(pltpu.make_async_copy(source.at[here], target, sems.at[n, c]))
+            copies[-1].start()
+        at += width
+    for copy in copies:
+        copy.wait()
+
+
+def held(arrays, after):
+    count, chunks = len(arrays), 4
+    shape = (*arrays[0].shape[:-1], sum(a.shape[-1] for a in arrays))
+    size = sum(a.size * a.dtype.itemsize for a in arrays)
+    arrays = [pltpu.with_memory_space_constraint(a, pltpu.HBM) for a in arrays]
+    return pl.pallas_call(
+        functools.partial(held_kernel, count, chunks),
+        in_specs=[pl.BlockSpec(memory_space=pl.ANY)] * (count + 1),
+        out_specs=pl.BlockSpec(memory_space=pltpu.VMEM),
+        out_shape=pltpu.VMEM(shape, arrays[0].dtype),
+        scratch_shapes=[pltpu.SemaphoreType.DMA((count, chunks))],
+        compiler_params=pltpu.CompilerParams(vmem_limit_bytes=12 * 1024 * 1024),
+        cost_estimate=pl.CostEstimate(flops=0, bytes_accessed=2 * size, transcendentals=0),
+    )(*arrays, after)
+
+
+def state_sums_kernel(landed_ref, state_ref, out_ref, qk_ref):
     pieces, both, width = landed_ref.shape
-    slab, half, batch = state_ref.shape
-    key_rows = both // 2
-    step = pl.program_id(0)
-
-    @pl.when(step == 0)
-    def _():
-        for k in range(pieces):
-            qk_ref[:, k * width : (k + 1) * width] = landed_ref[k].astype(jnp.float32)
-        sums_ref[...] = jnp.zeros_like(sums_ref)
-
-    def add(first):
-        for at in range(0, batch, 128):
-            chunk = qk_ref[:, at : at + 128]
-            recall = sums_ref[:half, at : at + 128]
-            answer = sums_ref[half:, at : at + 128]
-            for k in range(slab):
-                tile = state_ref[k, :, at : at + 128]
-                answer += tile * chunk[first + k : first + k + 1]
-                recall += tile * chunk[key_rows + first + k : key_rows + first + k + 1]
-            sums_ref[:half, at : at + 128] = recall
-            sums_ref[half:, at : at + 128] = answer
-
-    for part in range(key_rows // slab):
-        pl.when(step == part)(functools.partial(add, part * slab))
-
-    @pl.when(step == pl.num_programs(0) - 1)
-    def _():
-        for at in range(0, batch, 128):
-            out_ref[at : at + 128, :] = sums_ref[:, at : at + 128].T.astype(jnp.bfloat16)
+    key_rows, half, batch = state_ref.shape
+    for k in range(pieces):
+        qk_ref[:, k * width : (k + 1) * width] = landed_ref[k].astype(jnp.float32)
+    for at in range(0, batch, 128):
+        chunk = qk_ref[:, at : at + 128]
+        answer = jnp.zeros((half, 128), jnp.float32)
+        recall = jnp.zeros((half, 128), jnp.float32)
+        for k in range(key_rows):
+            tile = state_ref[k, :, at : at + 128]
+            answer += tile * chunk[k : k + 1]
+            recall += tile * chunk[key_rows + k : key_rows + k + 1]
+        pair = jnp.concatenate([recall, answer], axis=0).T
+        out_ref[at : at + 128, :] = pair.astype(jnp.bfloat16)
 
 
 def state_sums(landed, state):
     key_rows, half, batch = state.shape
-    slab = 4
     return pl.pallas_call(
         state_sums_kernel,
-        grid=(key_rows // slab,),
-        in_specs=[
-            pl.BlockSpec(landed.shape, lambda i: (0, 0, 0)),
-            pl.BlockSpec((slab, half, batch), lambda i: (i, 0, 0)),
-        ],
-        out_specs=pl.BlockSpec((batch, 2 * half), lambda i: (0, 0)),
+        in_specs=[pl.BlockSpec(memory_space=pltpu.VMEM)] * 2,
+        out_specs=pl.BlockSpec(memory_space=pltpu.VMEM),
         out_shape=jax.ShapeDtypeStruct((batch, 2 * half), jnp.bfloat16),
-        scratch_shapes=[
-            pltpu.VMEM((2 * key_rows, batch), jnp.float32),
-            pltpu.VMEM((2 * half, batch), jnp.float32),
-        ],
+        scratch_shapes=[pltpu.VMEM((2 * key_rows, batch), jnp.float32)],
         compiler_params=pltpu.CompilerParams(vmem_limit_bytes=12 * 1024 * 1024),
         cost_estimate=pl.CostEstimate(
             flops=4 * state.size, bytes_accessed=4 * state.size, transcendentals=0
         ),
-    )(landed, pltpu.with_memory_space_constraint(state, pltpu.HBM))
+    )(landed, state)
 
 
 def state_update_kernel(landed_ref, sent_ref, state_ref, out_ref, key_ref, write_ref, decay_ref):
@@ -229,17 +241,18 @@
     unit_pair = in_core_order(core, unit, swapped(unit), 2)
     parts = jnp.moveaxis(unit_pair.reshape(2, n_z, key_rows, 2 * rows), 1, 0)
     parts = parts.reshape(n_z, 2 * key_rows, 2 * rows)
-    parts, lm_weight = lax.optimization_barrier((parts, lm_weight))
+    parts, lm_weight, after = lax.optimization_barrier((parts, lm_weight, head_gain))
+    state_held = held([state], after)
     lm_other = swapped(lm_weight)
     landed = exchange(parts, Z)
 
-    both = state_sums(landed, state)
+    both = state_sums(landed, state_held)
     small_in = (w_decay, w_beta, decay_log, decay_bias, token_ids, pieces, head_gain)
     both, lm_weight, lm_other, small_in = lax.optimization_barrier(
         (both, lm_weight, lm_other, small_in)
     )
     w_decay, w_beta, decay_log, decay_bias, token_ids, pieces, head_gain = small_in
-    lm_both = jnp.concatenate([lm_weight, lm_other], axis=1)
+    lm_both = held([lm_weight, lm_other], head_gain)
     gain_full = pieces[:, rows].reshape(D).astype(jnp.float32)
     both = exchange(both.reshape(n_z, 2 * rows, 2 * half), Z)
     both = jnp.sum(both.astype(jnp.float32), axis=0)
@@ -268,8 +281,11 @@
         readout * lax.rsqrt(power + 1e-05) * head_gain[None, :] * jax.nn.silu(gate)
     ).astype(jnp.bfloat16)
 
-    mixed_full = jnp.moveaxis(to_all(mixed, XY), 0, 1).reshape(rows, D)
-    hidden = x_full + jnp.dot(mixed_full, out_full, preferred_element_type=jnp.float32)
+    copies = jnp.broadcast_to(mixed, (lax.axis_size(XY), *mixed.shape))
+    copies, after = lax.optimization_barrier((copies, head_gain))
+    out_held = held([out_full], after)
+    mixed_full = jnp.moveaxis(exchange(copies, XY), 0, 1).reshape(rows, D)
+    hidden = x_full + jnp.dot(mixed_full, out_held, preferred_element_type=jnp.float32)
     energy = jnp.mean(hidden * hidden, axis=1, keepdims=True)
     final = (hidden * lax.rsqrt(energy + 1e-06) * gain_full[None, :]).astype(jnp.bfloat16)
 

time: 178 us -> 174 us (0.978)
  waiting for transfers between devices: 37.4 us -> 24.4 us
  Pallas kernels: 9.68 us -> 15.8 us
  local copies, waits for them, and re-layouts: 11.7 us -> 16.5 us
  starting transfers between devices: 58.6 us -> 62.9 us
  matrix products: 20.3 us -> 16.3 us
  other arithmetic: 9.86 us -> 7.81 us
    all_to_all x5, waiting for transfers between devices: 29 us -> 13.2 us  [exchange(): return lax.all_to_all(blocks, axes, split_axis=0, concat_axis=0, tiled=True)]
    unnamed x20 -> x39, local copies, waits for them, and re-layouts: 3.95 us -> 10.5 us
    pallas_call x1 -> x4, Pallas kernels: 4.25 us -> 10.3 us  [the longest x3 8.63 us: held(): pl.pallas_call(functools.partial(held_kernel, count, chunks), in_specs=[p...]
    dot_general x4, matrix products: 14.1 us -> 9.22 us  [statistics(): logits = jnp.dot(block, lm_both, preferred_element_type=jnp.float32)]
    all_to_all x5, starting transfers between devices: 24.4 us -> 28.3 us  [exchange(): return lax.all_to_all(blocks, axes, split_axis=0, concat_axis=0, tiled=True)]
    ppermute x14, waiting for transfers between devices: 4.49 us -> 6.89 us  [along_z(): return lax.ppermute(block, Z, [(k, (k + step) % n_z) for k in range(n_z)])]
    concatenate x1 -> x0, local copies, waits for them, and re-layouts: 1.78 us -> none  [per_device(): lm_both = jnp.concatenate([lm_weight, lm_other], axis=1)]
  transfers between devices with their start and end apart: 32 -> 32, of which waited for: 13 -> 12; matrix products, arithmetic and copies ran while one was open for 19% -> 14% of each run, Pallas kernels for 5% -> 9%
where the time goes in v8:
time: 174 us; the launch traced here: 173 us
  starting transfers between devices  62.9 us (36%)
  waiting for transfers between devices  24.4 us (14%)
  local copies, waits for them, and re-layouts  16.5 us (9%)
  matrix products  16.3 us (9%)
  Pallas kernels  15.8 us (9%)
  between operations  14.8 us (9%)
  blocking collectives  14.7 us (8%)
  other arithmetic  7.81 us (4%)
    all_to_all x5, starting transfers between devices, exchange(): return lax.all_to_all(blocks, axes, split_axis=0, concat_axis=0, tiled=True)  28.3 us
    ppermute x12, starting transfers between devices, swapped(): return lax.ppermute(array, CORE, [(0, 1), (1, 0)])  19.8 us
    ppermute x14, starting transfers between devices, along_z(): return lax.ppermute(block, Z, [(k, (k + step) % n_z) for k in range(n_z)])  14.8 us
    all_to_all x1, blocking collectives, exchange(): return lax.all_to_all(blocks, axes, split_axis=0, concat_axis=0, tiled=True)  14.7 us
    all_to_all x5, waiting for transfers between devices, exchange(): return lax.all_to_all(blocks, axes, split_axis=0, concat_axis=0, tiled=True)  13.2 us
    unnamed x39, local copies, waits for them, and re-layouts  10.5 us
    dot_general x4, matrix products, statistics(): logits = jnp.dot(block, lm_both, preferred_element_type=jnp.float32)  9.22 us
    pallas_call x3, Pallas kernels, held(): pl.pallas_call(functools.partial(held_kernel, count, chunks), in_specs=[p...  8.63 us
  transfers between devices with their start and end apart: 32, of which 12 were waited for; matrix products, arithmetic and copies ran while one was open for 14% of the time, Pallas kernels for 9%

profile of v8, /device:TPU:1, one launch (start us, length us, event | category | flops | bytes accessed | tf_op | source)
XLA Modules:
  0.0 173.1 jit_solution(4434944707231854643)
XLA Ops:
  7.9 3.3 %collective-permute-start = (bf16[144,64]{0,1:T(8,128)(2,1)}, bf16[144,64]{0,1:T(8,128)(2,1)S(1)}, u32[]{:S(2)}, u32[]{:S(2)}) collective-permute-start(bf16[144,64]{0,1:T(8,128)(2,1)} %param.17), channel_id=1, source_target_pairs={{0,8},{8,0},{1,9},{9,1},{2,10},{10,2},{3,11},{11,3},{4,12},{12,4},... | collective-permute-start | bytes 55304 | tf_op jit(solution)/shard_map/ppermute | solution.py:26
  11.4 1.2 collective-permute-done.1
  13.4 0.8 broadcast_select_fusion.4
  14.5 0.8 broadcast_in_dim.52
  16.3 5.0 %all-to-all-start = ((bf16[16,73,128]{2,1,0:T(8,128)(2,1)}), bf16[16,73,128]{2,1,0:T(8,128)(2,1)S(1)}, u32[]{:S(2)}, u32[]{:S(2)}) async-start(bf16[16,73,128]{2,1,0:T(8,128)(2,1)} %broadcast_in_dim.52), calls=%async_computation | async-start | bytes 655360 | tf_op jit(solution)/shard_map/all_to_all | solution.py:30
  22.4 7.0 %all-to-all-done = bf16[16,73,128]{2,1,0:T(8,128)(2,1)S(1)} async-done(((bf16[16,73,128]{2,1,0:T(8,128)(2,1)}), bf16[16,73,128]{2,1,0:T(8,128)(2,1)S(1)}, u32[]{:S(2)}, u32[]{:S(2)}) %all-to-all-start) | async-done | bytes 299040 | tf_op jit(solution)/shard_map/all_to_all | solution.py:30
  30.9 2.1 %collective-permute-start.6 = (bf16[2,128,72]{2,1,0:T(8,128)(2,1)S(1)}, bf16[2,128,72]{2,1,0:T(8,128)(2,1)S(1)}, u32[]{:S(2)}, u32[]{:S(2)}) collective-permute-start(bf16[2,128,72]{2,1,0:T(8,128)(2,1)S(1)} %get-tuple-element.93), channel_id=1, source_target_pairs={{0,8},{8,0},{1,9},{9,1},{2,10},{10,2},{3,11},{11,3},{4,12},{12,4},... | collective-permute-start | bytes 110600 | tf_op jit(solution)/shard_map/ppermute | solution.py:26
  33.0 0.9 collective-permute-done.6
  35.1 8.2 %all-to-all-start.1 = ((bf16[8,32,144]{2,1,0:T(8,128)(2,1)}), bf16[8,32,144]{2,1,0:T(8,128)(2,1)S(1)}, u32[]{:S(2)}, u32[]{:S(2)}) async-start(bf16[8,32,144]{2,1,0:T(8,128)(2,1)} %bitcast.171), calls=%async_computation.1 | async-start | bytes 262144 | tf_op jit(solution)/shard_map/all_to_all | solution.py:30
  43.3 2.4 %shard_map.192.state_ref = f32[16,64,1152]{2,1,0:T(8,128)S(1)} custom-call(f32[16,64,1152]{2,1,0:T(8,128)} %state_ref.1, f32[128]{0:T(128)S(1)} %copy-done.4), custom_call_target="tpu_custom_call" | custom-call | bytes 9437184 | tf_op jit(solution)/shard_map/pallas_call | solution.py:80
  45.7 2.2 %copy-done.1 = f32[16,64,1152]{2,1,0:T(8,128)} copy-done((f32[16,64,1152]{2,1,0:T(8,128)}, f32[16,64,1152]{2,1,0:T(8,128)S(1)}, u32[]{:S(2)}) %copy-start.1) | copy-done | bytes 4718616
  47.9 3.7 %all-to-all-done.1.landed_ref = bf16[8,32,144]{2,1,0:T(8,128)(2,1)S(1)} async-done(((bf16[8,32,144]{2,1,0:T(8,128)(2,1)}), bf16[8,32,144]{2,1,0:T(8,128)(2,1)S(1)}, u32[]{:S(2)}, u32[]{:S(2)}) %all-to-all-start.1) | async-done | bytes 73760 | tf_op jit(solution)/shard_map/all_to_all | solution.py:30
  51.6 2.3 %copy-done.2 = f32[16,64,1152]{2,1,0:T(8,128)S(1)} copy-done((f32[16,64,1152]{2,1,0:T(8,128)S(1)}, f32[16,64,1152]{2,1,0:T(8,128)}, u32[]{:S(2)}) %copy-start.2) | copy-done | bytes 4718616
  54.0 1.7 shard_map.193
  55.7 4.1 %all-to-all-start.2 = ((bf16[8,144,128]{2,1,0:T(8,128)(2,1)}), bf16[8,144,128]{2,1,0:T(8,128)(2,1)}, u32[]{:S(2)}, u32[]{:S(2)}) async-start(bf16[8,144,128]{2,1,0:T(8,128)(2,1)} %bitcast.17), calls=%async_computation.2 | async-start | bytes 589824 | tf_op jit(solution)/shard_map/all_to_all | solution.py:30
  60.5 1.1 fusion.39
  62.4 1.8 %collective-permute-start.24 = (f32[1,72]{1,0:T(1,128)S(1)}, f32[1,72]{1,0:T(1,128)S(1)}, u32[]{:S(2)}, u32[]{:S(2)}) collective-permute-start(f32[1,72]{1,0:T(1,128)S(1)} %fusion.83), channel_id=1, source_target_pairs={{0,8},{8,0},{1,9},{9,1},{2,10},{10,2},{3,11},{11,3},{4,12},{12,4},... | collective-permute-start | bytes 872 | tf_op jit(solution)/shard_map/ppermute | solution.py:26
  64.2 2.8 %shard_map.195 = bf16[2048,1280]{1,0:T(8,128)(2,1)S(1)} custom-call(bf16[2048,640]{1,0:T(8,128)(2,1)} %refs_0_.2, bf16[2048,640]{1,0:T(8,128)(2,1)} %copy-done.5, f32[128]{0:T(128)S(1)} %copy-done.4), custom_call_target="tpu_custom_call" | custom-call | bytes 10485760 | tf_op jit(solution)/shard_map/pallas_call | solution.py:80
  66.9 2.4 %copy-done.3 = bf16[2048,1280]{1,0:T(8,128)(2,1)} copy-done((bf16[2048,1280]{1,0:T(8,128)(2,1)}, bf16[2048,1280]{1,0:T(8,128)(2,1)S(1)}, u32[]{:S(2)}) %copy-start.3) | copy-done | bytes 5242904
  69.6 0.8 all-to-all-done.2
  70.3 1.0 convert_reduce_fusion
  71.5 3.0 %collective-permute-start.8 = (f32[72,128]{0,1:T(8,128)S(1)}, f32[72,128]{0,1:T(8,128)S(1)}, u32[]{:S(2)}, u32[]{:S(2)}) collective-permute-start(f32[72,128]{0,1:T(8,128)S(1)} %copy.185), channel_id=1, source_target_pairs={{0,8},{8,0},{1,9},{9,1},{2,10},{10,2},{3,11},{11,3},{4,12},{12,4},... | collective-permute-start | bytes 110600 | tf_op jit(solution)/shard_map/ppermute | solution.py:26
  75.7 0.8 broadcast_in_dim.54
  76.4 3.5 %all-to-all-start.3 = ((bf16[16,72,128]{2,1,0:T(8,128)(2,1)}), bf16[16,72,128]{2,1,0:T(8,128)(2,1)S(1)}, u32[]{:S(2)}, u32[]{:S(2)}) async-start(bf16[16,72,128]{2,1,0:T(8,128)(2,1)} %broadcast_in_dim.54), calls=%async_computation.3 | async-start | bytes 589824 | tf_op jit(solution)/shard_map/all_to_all | solution.py:30
  80.8 3.5 %shard_map.194 = bf16[2048,2048]{1,0:T(8,128)(2,1)S(1)} custom-call(bf16[2048,2048]{1,0:T(8,128)(2,1)} %all-gather.2.cloned.1.call-done.refs_0_, f32[128]{0:T(128)S(1)} %copy-done.4), custom_call_target="tpu_custom_call" | custom-call | bytes 16777216 | tf_op jit(solution)/shard_map/pallas_call | solution.py:80
  84.3 3.2 %copy-done = bf16[2048,2048]{1,0:T(8,128)(2,1)} copy-done((bf16[2048,2048]{1,0:T(8,128)(2,1)}, bf16[2048,2048]{1,0:T(8,128)(2,1)S(1)}, u32[]{:S(2)}) %copy-start) | copy-done | bytes 8388632
  87.8 5.1 %multiply_reduce_fusion.4 = (f32[72]{0:T(128)S(1)}, f32[72,2048]{1,0:T(8,128)S(1)}) fusion(bf16[2048,2048]{1,0:T(8,128)(2,1)} %copy-done, bf16[16,73,128]{2,1,0:T(8,128)(2,1)S(1)} %all-to-all-done, bf16[16,72,128]{2,1,0:T(8,128)(2,1)S(1)} %all-to-all-done.3), kind=kOutput, calls=%fused_computation.59 | convolution fusion | flops 604569536 | bytes 9568544 | tf_op jit(solution)/shard_map/dot_general | solution.py:288
  93.5 2.4 %collective-permute-start.18 = (bf16[72,1024]{1,0:T(8,128)(2,1)S(1)}, bf16[72,1024]{1,0:T(8,128)(2,1)S(1)}, u32[]{:S(2)}, u32[]{:S(2)}) collective-permute-start(bf16[72,1024]{1,0:T(8,128)(2,1)S(1)} %get-tuple-element.96), channel_id=1, source_target_pairs={{0,7},{1,0},{2,1},{3,2},{4,3},{5,4},{6,5},{7,6},{8,15},{9,8},{10,9... | collective-permute-start | bytes 442376 | tf_op jit(solution)/shard_map/ppermute | solution.py:308
  95.9 1.4 collective-permute-start.19
  97.4 1.0 collective-permute-done.10
  98.4 3.1 %collective-permute-done.14 = bf16[72,1024]{1,0:T(8,128)(2,1)S(1)} collective-permute-done((bf16[72,1024]{1,0:T(8,128)(2,1)S(1)}, bf16[72,1024]{1,0:T(8,128)(2,1)S(1)}, u32[]{:S(2)}, u32[]{:S(2)}) %collective-permute-start.14) | collective-permute-done | bytes 147488 | tf_op jit(solution)/shard_map/ppermute | solution.py:308
  101.5 1.9 %collective-permute-start.15 = (bf16[72,1024]{1,0:T(8,128)(2,1)S(1)}, bf16[72,1024]{1,0:T(8,128)(2,1)S(1)}, u32[]{:S(2)}, u32[]{:S(2)}) collective-permute-start(bf16[72,1024]{1,0:T(8,128)(2,1)S(1)} %collective-permute-done.14), channel_id=1, source_target_pairs={{0,7},{1,0},{2,1},{3,2},{4,3},{5,4},{6,5},{7,6},{8,15},{9,8},{10,9... | collective-permute-start | bytes 442376 | tf_op jit(solution)/shard_map/ppermute | solution.py:308
  103.5 1.4 collective-permute-start.21
  104.9 3.5 %fusion.102 = (f32[144]{0:T(256)S(1)}, f32[144,1280]{1,0:T(8,128)S(1)}) fusion(bf16[2048,1280]{1,0:T(8,128)(2,1)} %copy-done.3, bf16[72,1024]{1,0:T(8,128)(2,1)S(1)} %collective-permute-done.14, bf16[72,1024]{1,0:T(8,128)(2,1)S(1)} %collective-permute-done.19, bf16[72,1024]{1,0:T(8,128)(2,1)S(1)} %collective-permute-done.18, ...), kind=kOutput, calls=%fused_computation.213 | convolution fusion | flops 757518208 | bytes 6570560 | tf_op jit(solution)/shard_map/dot_general | solution.py:299
  108.6 2.7 %collective-permute-start.16 = (bf16[72,1024]{1,0:T(8,128)(2,1)S(1)}, bf16[72,1024]{1,0:T(8,128)(2,1)S(1)}, u32[]{:S(2)}, u32[]{:S(2)}) collective-permute-start(bf16[72,1024]{1,0:T(8,128)(2,1)S(1)} %collective-permute-done.15), channel_id=1, source_target_pairs={{0,7},{1,0},{2,1},{3,2},{4,3},{5,4},{6,5},{7,6},{8,15},{9,8},{10,9... | collective-permute-start | bytes 442376 | tf_op jit(solution)/shard_map/ppermute | solution.py:308
  111.3 1.4 collective-permute-start.23
  112.7 3.5 %fusion.103 = (f32[144]{0:T(256)S(1)}, f32[144,1280]{1,0:T(8,128)S(1)}) fusion(bf16[2048,1280]{1,0:T(8,128)(2,1)} %copy-done.3, bf16[72,1024]{1,0:T(8,128)(2,1)S(1)} %collective-permute-done.15, bf16[72,1024]{1,0:T(8,128)(2,1)S(1)} %collective-permute-done.21, bf16[72,1024]{1,0:T(8,128)(2,1)S(1)} %collective-permute-done.20, ...), kind=kOutput, calls=%fused_computation.214 | convolution fusion | flops 757518208 | bytes 6570560 | tf_op jit(solution)/shard_map/dot_general | solution.py:299
  116.6 2.7 %collective-permute-start.17 = (bf16[72,1024]{1,0:T(8,128)(2,1)S(1)}, bf16[72,1024]{1,0:T(8,128)(2,1)S(1)}, u32[]{:S(2)}, u32[]{:S(2)}) collective-permute-start(bf16[72,1024]{1,0:T(8,128)(2,1)S(1)} %collective-permute-done.16), channel_id=1, source_target_pairs={{0,7},{1,0},{2,1},{3,2},{4,3},{5,4},{6,5},{7,6},{8,15},{9,8},{10,9... | collective-permute-start | bytes 442376 | tf_op jit(solution)/shard_map/ppermute | solution.py:308
  119.3 1.1 fusion.101
  120.3 2.7 %collective-permute-done.13 = bf16[72,1024]{1,0:T(8,128)(2,1)S(1)} collective-permute-done((bf16[72,1024]{1,0:T(8,128)(2,1)S(1)}, bf16[72,1024]{1,0:T(8,128)(2,1)S(1)}, u32[]{:S(2)}, u32[]{:S(2)}) %collective-permute-start.13) | collective-permute-done | bytes 147488 | tf_op jit(solution)/shard_map/ppermute | solution.py:308
  123.1 1.1 fusion.104
  124.1 1.2 fusion
  126.2 14.7 %all_to_all.30.sent_ref = f32[8,96,128]{2,1,0:T(8,128)S(1)} all-to-all(f32[8,96,128]{2,1,0:T(8,128)S(1)} %broadcast_in_dim.57), channel_id=1, replica_groups=mesh['row_0'=4,'row_1'=4,'row_2'=2,'col'=8] {'col'}, dimensions={0} | all-to-all | bytes 786432 | tf_op jit(solution)/shard_map/all_to_all | solution.py:30
  141.9 7.5 %all-to-all-start.5 = ((f32[16,4,576]{2,1,0:T(4,128)}), f32[16,4,576]{2,1,0:T(4,128)S(1)}, u32[]{:S(2)}, u32[]{:S(2)}) async-start(f32[16,4,576]{2,1,0:T(4,128)} %broadcast_in_dim.59), calls=%async_computation.5 | async-start | bytes 327680 | tf_op jit(solution)/shard_map/all_to_all | solution.py:30
  149.4 5.4 %shard_map.196 = f32[16,64,1152]{2,1,0:T(8,128)} custom-call(bf16[8,32,144]{2,1,0:T(8,128)(2,1)S(1)} %all-to-all-done.1.landed_ref, f32[8,96,128]{2,1,0:T(8,128)S(1)} %all_to_all.30.sent_ref, f32[16,64,1152]{2,1,0:T(8,128)} %state_ref.1), custom_call_target="tpu_custom_call" | custom-call | flops 3538944 | bytes 9437184 | tf_op jit(solution)/shard_map/pallas_call | solution.py:157
  154.8 1.3 all-to-all-done.5
  156.4 7.3 %collective-permute-start.25 = (f32[2,576]{1,0:T(2,128)S(1)}, f32[2,576]{1,0:T(2,128)S(1)}, u32[]{:S(2)}, u32[]{:S(2)}) collective-permute-start(f32[2,576]{1,0:T(2,128)S(1)} %pad_maximum_fusion.8), channel_id=1, source_target_pairs={{0,8},{8,0},{1,9},{9,1},{2,10},{10,2},{3,11},{11,3},{4,12},{12,4},... | collective-permute-start | bytes 13832 | tf_op jit(solution)/shard_map/ppermute | solution.py:26
  163.7 0.8 collective-permute-done.25
  (170 shorter events, 15.4 us)
Async XLA Ops:
  7.2 15.0 %copy-start.8 = (bf16[2048,64]{0,1:T(8,128)(2,1)S(1)}, bf16[2048,64]{0,1:T(8,128)(2,1)}, u32[]{:S(2)}) copy-start(bf16[2048,64]{0,1:T(8,128)(2,1)} %param.21) | copy-start | bytes 786436
  7.2 15.0 %copy-start.7 = (bf16[2048,64]{0,1:T(8,128)(2,1)S(1)}, bf16[2048,64]{0,1:T(8,128)(2,1)}, u32[]{:S(2)}) copy-start(bf16[2048,64]{0,1:T(8,128)(2,1)} %param.22) | copy-start | bytes 786436
  7.2 15.0 %copy-start.6 = (bf16[2048,64]{0,1:T(8,128)(2,1)S(1)}, bf16[2048,64]{0,1:T(8,128)(2,1)}, u32[]{:S(2)}) copy-start(bf16[2048,64]{0,1:T(8,128)(2,1)} %param.23) | copy-start | bytes 786436
  7.2 73.6 %all-gather.2.cloned.1.call-start = ((), (), s32[]{:S(2)}) async-start(), calls=%async_computation.6 | async-start | bytes 8650752 | tf_op jit(solution)/shard_map/all_gather | solution.py:212
  7.9 5.5 %collective-permute-start = (bf16[144,64]{0,1:T(8,128)(2,1)}, bf16[144,64]{0,1:T(8,128)(2,1)S(1)}, u32[]{:S(2)}, u32[]{:S(2)}) collective-permute-start(bf16[144,64]{0,1:T(8,128)(2,1)} %param.17), channel_id=1, source_target_pairs={{0,8},{8,0},{1,9},{9,1},{2,10},{10,2},{3,11},{11,3},{4,12},{12,4},... | collective-permute-start | bytes 55304 | tf_op jit(solution)/shard_map/ppermute | solution.py:26
  11.3 1.3 collective-permute-start.1
  15.3 6.8 %collective-permute-start.2 = (bf16[2048,64]{0,1:T(8,128)(2,1)}, bf16[2048,64]{0,1:T(8,128)(2,1)S(1)}, u32[]{:S(2)}, u32[]{:S(2)}) collective-permute-start(bf16[2048,64]{0,1:T(8,128)(2,1)} %param.20), channel_id=1, source_target_pairs={{0,8},{8,0},{1,9},{9,1},{2,10},{10,2},{3,11},{11,3},{4,12},{12,4},... | collective-permute-start | bytes 786440 | tf_op jit(solution)/shard_map/ppermute | solution.py:26
  15.5 6.6 %collective-permute-start.3 = (bf16[2048,64]{0,1:T(8,128)(2,1)}, bf16[2048,64]{0,1:T(8,128)(2,1)S(1)}, u32[]{:S(2)}, u32[]{:S(2)}) collective-permute-start(bf16[2048,64]{0,1:T(8,128)(2,1)} %param.21), channel_id=1, source_target_pairs={{0,8},{8,0},{1,9},{9,1},{2,10},{10,2},{3,11},{11,3},{4,12},{12,4},... | collective-permute-start | bytes 786440 | tf_op jit(solution)/shard_map/ppermute | solution.py:26
  15.8 6.3 %collective-permute-start.4 = (bf16[2048,64]{0,1:T(8,128)(2,1)}, bf16[2048,64]{0,1:T(8,128)(2,1)S(1)}, u32[]{:S(2)}, u32[]{:S(2)}) collective-permute-start(bf16[2048,64]{0,1:T(8,128)(2,1)} %param.22), channel_id=1, source_target_pairs={{0,8},{8,0},{1,9},{9,1},{2,10},{10,2},{3,11},{11,3},{4,12},{12,4},... | collective-permute-start | bytes 786440 | tf_op jit(solution)/shard_map/ppermute | solution.py:26
  16.0 6.1 %collective-permute-start.5 = (bf16[2048,64]{0,1:T(8,128)(2,1)}, bf16[2048,64]{0,1:T(8,128)(2,1)S(1)}, u32[]{:S(2)}, u32[]{:S(2)}) collective-permute-start(bf16[2048,64]{0,1:T(8,128)(2,1)} %param.23), channel_id=1, source_target_pairs={{0,8},{8,0},{1,9},{9,1},{2,10},{10,2},{3,11},{11,3},{4,12},{12,4},... | collective-permute-start | bytes 786440 | tf_op jit(solution)/shard_map/ppermute | solution.py:26
  16.3 13.2 %all-to-all-start = ((bf16[16,73,128]{2,1,0:T(8,128)(2,1)}), bf16[16,73,128]{2,1,0:T(8,128)(2,1)S(1)}, u32[]{:S(2)}, u32[]{:S(2)}) async-start(bf16[16,73,128]{2,1,0:T(8,128)(2,1)} %broadcast_in_dim.52), calls=%async_computation | async-start | bytes 655360 | tf_op jit(solution)/shard_map/all_to_all | solution.py:30
  30.4 12.9 %copy-start.4 = (f32[128]{0:T(128)S(1)}, f32[128]{0:T(128)}, u32[]{:S(2)}) copy-start(f32[128]{0:T(128)} %refs_2_) | copy-start | bytes 1540
  30.9 3.0 %collective-permute-start.6 = (bf16[2,128,72]{2,1,0:T(8,128)(2,1)S(1)}, bf16[2,128,72]{2,1,0:T(8,128)(2,1)S(1)}, u32[]{:S(2)}, u32[]{:S(2)}) collective-permute-start(bf16[2,128,72]{2,1,0:T(8,128)(2,1)S(1)} %get-tuple-element.93), channel_id=1, source_target_pairs={{0,8},{8,0},{1,9},{9,1},{2,10},{10,2},{3,11},{11,3},{4,12},{12,4},... | collective-permute-start | bytes 110600 | tf_op jit(solution)/shard_map/ppermute | solution.py:26
  34.7 21.0 %collective-permute-start.7 = (bf16[2048,640]{1,0:T(8,128)(2,1)}, bf16[2048,640]{1,0:T(8,128)(2,1)S(1)}, u32[]{:S(2)}, u32[]{:S(2)}) collective-permute-start(bf16[2048,640]{1,0:T(8,128)(2,1)} %refs_0_.2), channel_id=1, source_target_pairs={{0,8},{8,0},{1,9},{9,1},{2,10},{10,2},{3,11},{11,3},{4,12},{12,4},... | collective-permute-start | bytes 7864328 | tf_op jit(solution)/shard_map/ppermute | solution.py:26
  35.1 16.6 %all-to-all-start.1 = ((bf16[8,32,144]{2,1,0:T(8,128)(2,1)}), bf16[8,32,144]{2,1,0:T(8,128)(2,1)S(1)}, u32[]{:S(2)}, u32[]{:S(2)}) async-start(bf16[8,32,144]{2,1,0:T(8,128)(2,1)} %bitcast.171), calls=%async_computation.1 | async-start | bytes 262144 | tf_op jit(solution)/shard_map/all_to_all | solution.py:30
  45.7 2.2 %copy-start.1 = (f32[16,64,1152]{2,1,0:T(8,128)}, f32[16,64,1152]{2,1,0:T(8,128)S(1)}, u32[]{:S(2)}) copy-start(f32[16,64,1152]{2,1,0:T(8,128)S(1)} %shard_map.192.state_ref) | copy-start | bytes 14155780
  51.6 2.3 %copy-start.2 = (f32[16,64,1152]{2,1,0:T(8,128)S(1)}, f32[16,64,1152]{2,1,0:T(8,128)}, u32[]{:S(2)}) copy-start(f32[16,64,1152]{2,1,0:T(8,128)} %copy-done.1) | copy-start | bytes 14155780
  54.0 5.8 %copy-start.12 = (s32[1152]{0:T(1024)S(1)}, s32[1152]{0:T(1024)}, u32[]{:S(2)}) copy-start(s32[1152]{0:T(1024)} %param.32) | copy-start | bytes 13828
  54.0 5.9 %copy-start.15 = (f32[16]{0:T(128)S(1)}, f32[16]{0:T(128)}, u32[]{:S(2)}) copy-start(f32[16]{0:T(128)} %param.26) | copy-start | bytes 196
  54.0 6.5 %copy-start.14 = (bf16[2048,16]{0,1:T(8,128)(2,1)S(1)}, bf16[2048,16]{0,1:T(8,128)(2,1)}, u32[]{:S(2)}) copy-start(bf16[2048,16]{0,1:T(8,128)(2,1)} %param.25) | copy-start | bytes 196612
  54.0 7.6 %copy-start.13 = (f32[16]{0:T(128)S(1)}, f32[16]{0:T(128)}, u32[]{:S(2)}) copy-start(f32[16]{0:T(128)} %param.27) | copy-start | bytes 196
  55.7 8.4 %copy-start.5 = (bf16[2048,640]{1,0:T(8,128)(2,1)}, bf16[2048,640]{1,0:T(8,128)(2,1)S(1)}, u32[]{:S(2)}) copy-start(bf16[2048,640]{1,0:T(8,128)(2,1)S(1)} %collective-permute-done.7.refs_1_) | copy-start | bytes 7864324
  55.7 14.6 %all-to-all-start.2 = ((bf16[8,144,128]{2,1,0:T(8,128)(2,1)}), bf16[8,144,128]{2,1,0:T(8,128)(2,1)}, u32[]{:S(2)}, u32[]{:S(2)}) async-start(bf16[8,144,128]{2,1,0:T(8,128)(2,1)} %bitcast.17), calls=%async_computation.2 | async-start | bytes 589824 | tf_op jit(solution)/shard_map/all_to_all | solution.py:30
  62.4 17.6 %collective-permute-start.24 = (f32[1,72]{1,0:T(1,128)S(1)}, f32[1,72]{1,0:T(1,128)S(1)}, u32[]{:S(2)}, u32[]{:S(2)}) collective-permute-start(f32[1,72]{1,0:T(1,128)S(1)} %fusion.83), channel_id=1, source_target_pairs={{0,8},{8,0},{1,9},{9,1},{2,10},{10,2},{3,11},{11,3},{4,12},{12,4},... | collective-permute-start | bytes 872 | tf_op jit(solution)/shard_map/ppermute | solution.py:26
  66.9 2.4 %copy-start.3 = (bf16[2048,1280]{1,0:T(8,128)(2,1)}, bf16[2048,1280]{1,0:T(8,128)(2,1)S(1)}, u32[]{:S(2)}) copy-start(bf16[2048,1280]{1,0:T(8,128)(2,1)S(1)} %shard_map.195) | copy-start | bytes 15728644
  71.5 3.9 %collective-permute-start.8 = (f32[72,128]{0,1:T(8,128)S(1)}, f32[72,128]{0,1:T(8,128)S(1)}, u32[]{:S(2)}, u32[]{:S(2)}) collective-permute-start(f32[72,128]{0,1:T(8,128)S(1)} %copy.185), channel_id=1, source_target_pairs={{0,8},{8,0},{1,9},{9,1},{2,10},{10,2},{3,11},{11,3},{4,12},{12,4},... | collective-permute-start | bytes 110600 | tf_op jit(solution)/shard_map/ppermute | solution.py:26
  76.4 11.4 %all-to-all-start.3 = ((bf16[16,72,128]{2,1,0:T(8,128)(2,1)}), bf16[16,72,128]{2,1,0:T(8,128)(2,1)S(1)}, u32[]{:S(2)}, u32[]{:S(2)}) async-start(bf16[16,72,128]{2,1,0:T(8,128)(2,1)} %broadcast_in_dim.54), calls=%async_computation.3 | async-start | bytes 589824 | tf_op jit(solution)/shard_map/all_to_all | solution.py:30
  80.1 17.3 %collective-permute-start.9 = (f32[72,64]{0,1:T(8,128)S(1)}, f32[72,64]{0,1:T(8,128)S(1)}, u32[]{:S(2)}, u32[]{:S(2)}) collective-permute-start(f32[72,64]{0,1:T(8,128)S(1)} %constant_dynamic-slice_fusion.3), channel_id=1, source_target_pairs={{0,8},{8,0},{1,9},{9,1},{2,10},{10,2},{3,11},{11,3},{4,12},{12,4},... | collective-permute-start | bytes 55304 | tf_op jit(solution)/shard_map/ppermute | solution.py:26
  84.3 3.2 %copy-start = (bf16[2048,2048]{1,0:T(8,128)(2,1)}, bf16[2048,2048]{1,0:T(8,128)(2,1)S(1)}, u32[]{:S(2)}) copy-start(bf16[2048,2048]{1,0:T(8,128)(2,1)S(1)} %shard_map.194) | copy-start | bytes 25165828
  93.1 26.1 %slice-start = ((s8[5242880]{0:T(1024)(128)(4,1)}), s8[4194304]{0:T(1024)(128)(4,1)S(1)}, s32[]{:S(2)}) async-start(s8[5242880]{0:T(1024)(128)(4,1)} %bitcast.166), calls=%async_computation.7 | async-start | bytes 8388608
  93.1 5.3 %collective-permute-start.10 = (bf16[72,1024]{1,0:T(8,128)(2,1)S(1)}, bf16[72,1024]{1,0:T(8,128)(2,1)S(1)}, u32[]{:S(2)}, u32[]{:S(2)}) collective-permute-start(bf16[72,1024]{1,0:T(8,128)(2,1)S(1)} %get-tuple-element.96), channel_id=1, source_target_pairs={{0,1},{1,2},{2,3},{3,4},{4,5},{5,6},{6,7},{7,0},{8,9},{9,10},{10,1... | collective-permute-start | bytes 442376 | tf_op jit(solution)/shard_map/ppermute | solution.py:308
  93.5 9.9 %collective-permute-start.18 = (bf16[72,1024]{1,0:T(8,128)(2,1)S(1)}, bf16[72,1024]{1,0:T(8,128)(2,1)S(1)}, u32[]{:S(2)}, u32[]{:S(2)}) collective-permute-start(bf16[72,1024]{1,0:T(8,128)(2,1)S(1)} %get-tuple-element.96), channel_id=1, source_target_pairs={{0,7},{1,0},{2,1},{3,2},{4,3},{5,4},{6,5},{7,6},{8,15},{9,8},{10,9... | collective-permute-start | bytes 442376 | tf_op jit(solution)/shard_map/ppermute | solution.py:308
  95.9 5.6 %collective-permute-start.14 = (bf16[72,1024]{1,0:T(8,128)(2,1)S(1)}, bf16[72,1024]{1,0:T(8,128)(2,1)S(1)}, u32[]{:S(2)}, u32[]{:S(2)}) collective-permute-start(bf16[72,1024]{1,0:T(8,128)(2,1)S(1)} %get-tuple-element.97), channel_id=1, source_target_pairs={{0,7},{1,0},{2,1},{3,2},{4,3},{5,4},{6,5},{7,6},{8,15},{9,8},{10,9... | collective-permute-start | bytes 442376 | tf_op jit(solution)/shard_map/ppermute | solution.py:308
  95.9 7.5 %collective-permute-start.19 = (bf16[72,1024]{1,0:T(8,128)(2,1)S(1)}, bf16[72,1024]{1,0:T(8,128)(2,1)S(1)}, u32[]{:S(2)}, u32[]{:S(2)}) collective-permute-start(bf16[72,1024]{1,0:T(8,128)(2,1)S(1)} %get-tuple-element.97), channel_id=1, source_target_pairs={{0,1},{1,2},{2,3},{3,4},{4,5},{5,6},{6,7},{7,0},{8,9},{9,10},{10,1... | collective-permute-start | bytes 442376 | tf_op jit(solution)/shard_map/ppermute | solution.py:308
  97.4 21.9 %slice-start.1 = ((s8[5242880]{0:T(1024)(128)(4,1)}), s8[1048576]{0:T(1024)(128)(4,1)S(1)}, s32[]{:S(2)}) async-start(s8[5242880]{0:T(1024)(128)(4,1)} %bitcast.166), calls=%async_computation.8 | async-start | bytes 2097152
  98.4 10.0 %collective-permute-start.11 = (bf16[72,1024]{1,0:T(8,128)(2,1)S(1)}, bf16[72,1024]{1,0:T(8,128)(2,1)S(1)}, u32[]{:S(2)}, u32[]{:S(2)}) collective-permute-start(bf16[72,1024]{1,0:T(8,128)(2,1)S(1)} %collective-permute-done.10), channel_id=1, source_target_pairs={{0,1},{1,2},{2,3},{3,4},{4,5},{5,6},{6,7},{7,0},{8,9},{9,10},{10,1... | collective-permute-start | bytes 442376 | tf_op jit(solution)/shard_map/ppermute | solution.py:308
  101.5 7.1 %collective-permute-start.15 = (bf16[72,1024]{1,0:T(8,128)(2,1)S(1)}, bf16[72,1024]{1,0:T(8,128)(2,1)S(1)}, u32[]{:S(2)}, u32[]{:S(2)}) collective-permute-start(bf16[72,1024]{1,0:T(8,128)(2,1)S(1)} %collective-permute-done.14), channel_id=1, source_target_pairs={{0,7},{1,0},{2,1},{3,2},{4,3},{5,4},{6,5},{7,6},{8,15},{9,8},{10,9... | collective-permute-start | bytes 442376 | tf_op jit(solution)/shard_map/ppermute | solution.py:308
  103.4 7.8 %collective-permute-start.20 = (bf16[72,1024]{1,0:T(8,128)(2,1)S(1)}, bf16[72,1024]{1,0:T(8,128)(2,1)S(1)}, u32[]{:S(2)}, u32[]{:S(2)}) collective-permute-start(bf16[72,1024]{1,0:T(8,128)(2,1)S(1)} %collective-permute-done.18), channel_id=1, source_target_pairs={{0,7},{1,0},{2,1},{3,2},{4,3},{5,4},{6,5},{7,6},{8,15},{9,8},{10,9... | collective-permute-start | bytes 442376 | tf_op jit(solution)/shard_map/ppermute | solution.py:308
  103.5 7.8 %collective-permute-start.21 = (bf16[72,1024]{1,0:T(8,128)(2,1)S(1)}, bf16[72,1024]{1,0:T(8,128)(2,1)S(1)}, u32[]{:S(2)}, u32[]{:S(2)}) collective-permute-start(bf16[72,1024]{1,0:T(8,128)(2,1)S(1)} %collective-permute-done.19), channel_id=1, source_target_pairs={{0,1},{1,2},{2,3},{3,4},{4,5},{5,6},{6,7},{7,0},{8,9},{9,10},{10,1... | collective-permute-start | bytes 442376 | tf_op jit(solution)/shard_map/ppermute | solution.py:308
  108.5 7.8 %collective-permute-start.12 = (bf16[72,1024]{1,0:T(8,128)(2,1)S(1)}, bf16[72,1024]{1,0:T(8,128)(2,1)S(1)}, u32[]{:S(2)}, u32[]{:S(2)}) collective-permute-start(bf16[72,1024]{1,0:T(8,128)(2,1)S(1)} %collective-permute-done.11), channel_id=1, source_target_pairs={{0,1},{1,2},{2,3},{3,4},{4,5},{5,6},{6,7},{7,0},{8,9},{9,10},{10,1... | collective-permute-start | bytes 442376 | tf_op jit(solution)/shard_map/ppermute | solution.py:308
  108.6 8.0 %collective-permute-start.16 = (bf16[72,1024]{1,0:T(8,128)(2,1)S(1)}, bf16[72,1024]{1,0:T(8,128)(2,1)S(1)}, u32[]{:S(2)}, u32[]{:S(2)}) collective-permute-start(bf16[72,1024]{1,0:T(8,128)(2,1)S(1)} %collective-permute-done.15), channel_id=1, source_target_pairs={{0,7},{1,0},{2,1},{3,2},{4,3},{5,4},{6,5},{7,6},{8,15},{9,8},{10,9... | collective-permute-start | bytes 442376 | tf_op jit(solution)/shard_map/ppermute | solution.py:308
  111.2 8.0 %collective-permute-start.22 = (bf16[72,1024]{1,0:T(8,128)(2,1)S(1)}, bf16[72,1024]{1,0:T(8,128)(2,1)S(1)}, u32[]{:S(2)}, u32[]{:S(2)}) collective-permute-start(bf16[72,1024]{1,0:T(8,128)(2,1)S(1)} %collective-permute-done.20), channel_id=1, source_target_pairs={{0,7},{1,0},{2,1},{3,2},{4,3},{5,4},{6,5},{7,6},{8,15},{9,8},{10,9... | collective-permute-start | bytes 442376 | tf_op jit(solution)/shard_map/ppermute | solution.py:308
  111.3 7.9 %collective-permute-start.23 = (bf16[72,1024]{1,0:T(8,128)(2,1)S(1)}, bf16[72,1024]{1,0:T(8,128)(2,1)S(1)}, u32[]{:S(2)}, u32[]{:S(2)}) collective-permute-start(bf16[72,1024]{1,0:T(8,128)(2,1)S(1)} %collective-permute-done.21), channel_id=1, source_target_pairs={{0,1},{1,2},{2,3},{3,4},{4,5},{5,6},{6,7},{7,0},{8,9},{9,10},{10,1... | collective-permute-start | bytes 442376 | tf_op jit(solution)/shard_map/ppermute | solution.py:308
  116.2 6.8 %collective-permute-start.13 = (bf16[72,1024]{1,0:T(8,128)(2,1)S(1)}, bf16[72,1024]{1,0:T(8,128)(2,1)S(1)}, u32[]{:S(2)}, u32[]{:S(2)}) collective-permute-start(bf16[72,1024]{1,0:T(8,128)(2,1)S(1)} %collective-permute-done.12), channel_id=1, source_target_pairs={{0,1},{1,2},{2,3},{3,4},{4,5},{5,6},{6,7},{7,0},{8,9},{9,10},{10,1... | collective-permute-start | bytes 442376 | tf_op jit(solution)/shard_map/ppermute | solution.py:308
  116.6 6.5 %collective-permute-start.17 = (bf16[72,1024]{1,0:T(8,128)(2,1)S(1)}, bf16[72,1024]{1,0:T(8,128)(2,1)S(1)}, u32[]{:S(2)}, u32[]{:S(2)}) collective-permute-start(bf16[72,1024]{1,0:T(8,128)(2,1)S(1)} %collective-permute-done.16), channel_id=1, source_target_pairs={{0,7},{1,0},{2,1},{3,2},{4,3},{5,4},{6,5},{7,6},{8,15},{9,8},{10,9... | collective-permute-start | bytes 442376 | tf_op jit(solution)/shard_map/ppermute | solution.py:308
  141.9 14.3 %all-to-all-start.5 = ((f32[16,4,576]{2,1,0:T(4,128)}), f32[16,4,576]{2,1,0:T(4,128)S(1)}, u32[]{:S(2)}, u32[]{:S(2)}) async-start(f32[16,4,576]{2,1,0:T(4,128)} %broadcast_in_dim.59), calls=%async_computation.5 | async-start | bytes 327680 | tf_op jit(solution)/shard_map/all_to_all | solution.py:30
  149.3 16.3 %copy-start.11 = (f32[1152]{0:T(1024)S(1)}, f32[1152]{0:T(1024)}, u32[]{:S(2)}) copy-start(f32[1152]{0:T(1024)} %param.33) | copy-start | bytes 13828
  156.4 8.2 %collective-permute-start.25 = (f32[2,576]{1,0:T(2,128)S(1)}, f32[2,576]{1,0:T(2,128)S(1)}, u32[]{:S(2)}, u32[]{:S(2)}) collective-permute-start(f32[2,576]{1,0:T(2,128)S(1)} %pad_maximum_fusion.8), channel_id=1, source_target_pairs={{0,8},{8,0},{1,9},{9,1},{2,10},{10,2},{3,11},{11,3},{4,12},{12,4},... | collective-permute-start | bytes 13832 | tf_op jit(solution)/shard_map/ppermute | solution.py:26
  (2 other events, 2.4 us)
Sparse Core Ops, SparseCore 0:
  10.6 62.1 all-gather.1

commit v9 on v8

--- a/solution.py
+++ b/solution.py
@@ -117,7 +117,7 @@
         cost_estimate=pl.CostEstimate(
             flops=4 * state.size, bytes_accessed=4 * state.size, transcendentals=0
         ),
-    )(landed, state)
+    )(landed, pltpu.with_memory_space_constraint(state, pltpu.VMEM))
 
 
 def state_update_kernel(landed_ref, sent_ref, state_ref, out_ref, key_ref, write_ref, decay_ref):
@@ -281,11 +281,8 @@
         readout * lax.rsqrt(power + 1e-05) * head_gain[None, :] * jax.nn.silu(gate)
     ).astype(jnp.bfloat16)
 
-    copies = jnp.broadcast_to(mixed, (lax.axis_size(XY), *mixed.shape))
-    copies, after = lax.optimization_barrier((copies, head_gain))
-    out_held = held([out_full], after)
-    mixed_full = jnp.moveaxis(exchange(copies, XY), 0, 1).reshape(rows, D)
-    hidden = x_full + jnp.dot(mixed_full, out_held, preferred_element_type=jnp.float32)
+    mixed_full = jnp.moveaxis(to_all(mixed, XY), 0, 1).reshape(rows, D)
+    hidden = x_full + jnp.dot(mixed_full, out_full, preferred_element_type=jnp.float32)
     energy = jnp.mean(hidden * hidden, axis=1, keepdims=True)
     final = (hidden * lax.rsqrt(energy + 1e-06) * gain_full[None, :]).astype(jnp.bfloat16)
 

time: 174 us -> 172 us (0.989)
  waiting for transfers between devices: 24.4 us -> 31.1 us
  Pallas kernels: 15.8 us -> 12.3 us
  local copies, waits for them, and re-layouts: 16.5 us -> 13.3 us
  starting transfers between devices: 62.9 us -> 60.3 us
    all_to_all x5, waiting for transfers between devices: 13.2 us -> 20 us  [exchange(): return lax.all_to_all(blocks, axes, split_axis=0, concat_axis=0, tiled=True)]
    all_to_all x5, starting transfers between devices: 28.3 us -> 24.8 us  [exchange(): return lax.all_to_all(blocks, axes, split_axis=0, concat_axis=0, tiled=True)]
    pallas_call x3 -> x2, Pallas kernels: 8.63 us -> 5.13 us  [held(): pl.pallas_call(functools.partial(held_kernel, count, chunks), in_specs=[p...]
    unnamed x39 -> x37, local copies, waits for them, and re-layouts: 10.5 us -> 7.25 us
  transfers between devices with their start and end apart: 32 -> 32, of which waited for: 12 -> 12; matrix products, arithmetic and copies ran while one was open for 14% -> 14% of each run, Pallas kernels for 9% -> 7%
where the time goes in v9:
time: 172 us; the launch traced here: 171 us
  starting transfers between devices  60.3 us (35%)
  waiting for transfers between devices  31.1 us (18%)
  matrix products  16.3 us (9%)
  between operations  14.8 us (9%)
  blocking collectives  14.7 us (9%)
  local copies, waits for them, and re-layouts  13.3 us (8%)
  Pallas kernels  12.3 us (7%)
  other arithmetic  7.81 us (5%)
    all_to_all x5, starting transfers between devices, exchange(): return lax.all_to_all(blocks, axes, split_axis=0, concat_axis=0, tiled=True)  24.8 us
    ppermute x12, starting transfers between devices, swapped(): return lax.ppermute(array, CORE, [(0, 1), (1, 0)])  20.7 us
    all_to_all x5, waiting for transfers between devices, exchange(): return lax.all_to_all(blocks, axes, split_axis=0, concat_axis=0, tiled=True)  20 us
    ppermute x14, starting transfers between devices, along_z(): return lax.ppermute(block, Z, [(k, (k + step) % n_z) for k in range(n_z)])  14.8 us
    all_to_all x1, blocking collectives, exchange(): return lax.all_to_all(blocks, axes, split_axis=0, concat_axis=0, tiled=True)  14.7 us
    dot_general x4, matrix products, statistics(): logits = jnp.dot(block, lm_both, preferred_element_type=jnp.float32)  9.21 us
    unnamed x37, local copies, waits for them, and re-layouts  7.25 us
    ppermute x14, waiting for transfers between devices, along_z(): return lax.ppermute(block, Z, [(k, (k + step) % n_z) for k in range(n_z)])  6.87 us
  transfers between devices with their start and end apart: 32, of which 12 were waited for; matrix products, arithmetic and copies ran while one was open for 14% of the time, Pallas kernels for 7%

profile of v9, /device:TPU:1, one launch (start us, length us, event | category | flops | bytes accessed | tf_op | source)
XLA Modules:
  0.0 170.5 jit_solution(13095003426257984684)
XLA Ops:
  7.9 3.3 %collective-permute-start = (bf16[144,64]{0,1:T(8,128)(2,1)}, bf16[144,64]{0,1:T(8,128)(2,1)S(1)}, u32[]{:S(2)}, u32[]{:S(2)}) collective-permute-start(bf16[144,64]{0,1:T(8,128)(2,1)} %param.17), channel_id=1, source_target_pairs={{0,8},{8,0},{1,9},{9,1},{2,10},{10,2},{3,11},{11,3},{4,12},{12,4},... | collective-permute-start | bytes 55304 | tf_op jit(solution)/shard_map/ppermute | solution.py:26
  11.4 1.2 collective-permute-done.1
  13.4 0.8 broadcast_select_fusion.4
  14.5 0.8 broadcast_in_dim.52
  16.3 5.0 %all-to-all-start = ((bf16[16,73,128]{2,1,0:T(8,128)(2,1)}), bf16[16,73,128]{2,1,0:T(8,128)(2,1)S(1)}, u32[]{:S(2)}, u32[]{:S(2)}) async-start(bf16[16,73,128]{2,1,0:T(8,128)(2,1)} %broadcast_in_dim.52), calls=%async_computation | async-start | bytes 655360 | tf_op jit(solution)/shard_map/all_to_all | solution.py:30
  21.3 0.7 fusion.100
  22.4 7.0 %all-to-all-done = bf16[16,73,128]{2,1,0:T(8,128)(2,1)S(1)} async-done(((bf16[16,73,128]{2,1,0:T(8,128)(2,1)}), bf16[16,73,128]{2,1,0:T(8,128)(2,1)S(1)}, u32[]{:S(2)}, u32[]{:S(2)}) %all-to-all-start) | async-done | bytes 299040 | tf_op jit(solution)/shard_map/all_to_all | solution.py:30
  30.9 2.1 %collective-permute-start.6 = (bf16[2,128,72]{2,1,0:T(8,128)(2,1)S(1)}, bf16[2,128,72]{2,1,0:T(8,128)(2,1)S(1)}, u32[]{:S(2)}, u32[]{:S(2)}) collective-permute-start(bf16[2,128,72]{2,1,0:T(8,128)(2,1)S(1)} %get-tuple-element.89), channel_id=1, source_target_pairs={{0,8},{8,0},{1,9},{9,1},{2,10},{10,2},{3,11},{11,3},{4,12},{12,4},... | collective-permute-start | bytes 110600 | tf_op jit(solution)/shard_map/ppermute | solution.py:26
  33.0 0.9 collective-permute-done.6
  35.1 8.2 %all-to-all-start.1 = ((bf16[8,32,144]{2,1,0:T(8,128)(2,1)}), bf16[8,32,144]{2,1,0:T(8,128)(2,1)S(1)}, u32[]{:S(2)}, u32[]{:S(2)}) async-start(bf16[8,32,144]{2,1,0:T(8,128)(2,1)} %bitcast.171), calls=%async_computation.1 | async-start | bytes 262144 | tf_op jit(solution)/shard_map/all_to_all | solution.py:30
  43.3 2.4 %shard_map.192.state_ref = f32[16,64,1152]{2,1,0:T(8,128)S(1)} custom-call(f32[16,64,1152]{2,1,0:T(8,128)} %state_ref.1, f32[128]{0:T(128)S(1)} %copy-done.3), custom_call_target="tpu_custom_call" | custom-call | bytes 9437184 | tf_op jit(solution)/shard_map/pallas_call | solution.py:80
  45.7 2.2 %copy-done = f32[16,64,1152]{2,1,0:T(8,128)} copy-done((f32[16,64,1152]{2,1,0:T(8,128)}, f32[16,64,1152]{2,1,0:T(8,128)S(1)}, u32[]{:S(2)}) %copy-start) | copy-done | bytes 4718616
  47.9 3.7 %all-to-all-done.1.landed_ref = bf16[8,32,144]{2,1,0:T(8,128)(2,1)S(1)} async-done(((bf16[8,32,144]{2,1,0:T(8,128)(2,1)}), bf16[8,32,144]{2,1,0:T(8,128)(2,1)S(1)}, u32[]{:S(2)}, u32[]{:S(2)}) %all-to-all-start.1) | async-done | bytes 73760 | tf_op jit(solution)/shard_map/all_to_all | solution.py:30
  51.7 2.3 %copy-done.1 = f32[16,64,1152]{2,1,0:T(8,128)S(1)} copy-done((f32[16,64,1152]{2,1,0:T(8,128)S(1)}, f32[16,64,1152]{2,1,0:T(8,128)}, u32[]{:S(2)}) %copy-start.1) | copy-done | bytes 4718616
  54.0 1.7 %shard_map.193 = bf16[1152,128]{1,0:T(8,128)(2,1)} custom-call(bf16[8,32,144]{2,1,0:T(8,128)(2,1)S(1)} %all-to-all-done.1.landed_ref, f32[16,64,1152]{2,1,0:T(8,128)S(1)} %copy-done.1), custom_call_target="tpu_custom_call" | custom-call | flops 4718592 | bytes 4718592 | tf_op jit(solution)/shard_map/pallas_call | solution.py:110
  55.7 4.1 %all-to-all-start.2 = ((bf16[8,144,128]{2,1,0:T(8,128)(2,1)}), bf16[8,144,128]{2,1,0:T(8,128)(2,1)}, u32[]{:S(2)}, u32[]{:S(2)}) async-start(bf16[8,144,128]{2,1,0:T(8,128)(2,1)} %bitcast.17), calls=%async_computation.2 | async-start | bytes 589824 | tf_op jit(solution)/shard_map/all_to_all | solution.py:30
  60.5 1.1 fusion.39
  62.4 1.8 %collective-permute-start.24 = (f32[1,72]{1,0:T(1,128)S(1)}, f32[1,72]{1,0:T(1,128)S(1)}, u32[]{:S(2)}, u32[]{:S(2)}) collective-permute-start(f32[1,72]{1,0:T(1,128)S(1)} %fusion.83), channel_id=1, source_target_pairs={{0,8},{8,0},{1,9},{9,1},{2,10},{10,2},{3,11},{11,3},{4,12},{12,4},... | collective-permute-start | bytes 872 | tf_op jit(solution)/shard_map/ppermute | solution.py:26
  64.2 2.8 %shard_map.194 = bf16[2048,1280]{1,0:T(8,128)(2,1)S(1)} custom-call(bf16[2048,640]{1,0:T(8,128)(2,1)} %refs_0_.2, bf16[2048,640]{1,0:T(8,128)(2,1)} %copy-done.4, f32[128]{0:T(128)S(1)} %copy-done.3), custom_call_target="tpu_custom_call" | custom-call | bytes 10485760 | tf_op jit(solution)/shard_map/pallas_call | solution.py:80
  66.9 2.4 %copy-done.2 = bf16[2048,1280]{1,0:T(8,128)(2,1)} copy-done((bf16[2048,1280]{1,0:T(8,128)(2,1)}, bf16[2048,1280]{1,0:T(8,128)(2,1)S(1)}, u32[]{:S(2)}) %copy-start.2) | copy-done | bytes 5242904
  69.5 0.8 all-to-all-done.2
  70.4 1.0 convert_reduce_fusion
  71.5 3.0 %collective-permute-start.8 = (f32[72,128]{0,1:T(8,128)S(1)}, f32[72,128]{0,1:T(8,128)S(1)}, u32[]{:S(2)}, u32[]{:S(2)}) collective-permute-start(f32[72,128]{0,1:T(8,128)S(1)} %copy.185), channel_id=1, source_target_pairs={{0,8},{8,0},{1,9},{9,1},{2,10},{10,2},{3,11},{11,3},{4,12},{12,4},... | collective-permute-start | bytes 110600 | tf_op jit(solution)/shard_map/ppermute | solution.py:26
  75.7 0.8 broadcast_in_dim.54
  76.5 3.5 %all-to-all-start.3 = ((bf16[16,72,128]{2,1,0:T(8,128)(2,1)}), bf16[16,72,128]{2,1,0:T(8,128)(2,1)S(1)}, u32[]{:S(2)}, u32[]{:S(2)}) async-start(bf16[16,72,128]{2,1,0:T(8,128)(2,1)} %broadcast_in_dim.54), calls=%async_computation.3 | async-start | bytes 589824 | tf_op jit(solution)/shard_map/all_to_all | solution.py:30
  80.8 7.0 %all-to-all-done.3 = bf16[16,72,128]{2,1,0:T(8,128)(2,1)S(1)} async-done(((bf16[16,72,128]{2,1,0:T(8,128)(2,1)}), bf16[16,72,128]{2,1,0:T(8,128)(2,1)S(1)}, u32[]{:S(2)}, u32[]{:S(2)}) %all-to-all-start.3) | async-done | bytes 294944 | tf_op jit(solution)/shard_map/all_to_all | solution.py:30
  87.9 5.1 %multiply_reduce_fusion.4 = (f32[72]{0:T(128)S(1)}, f32[72,2048]{1,0:T(8,128)S(1)}) fusion(bf16[2048,2048]{1,0:T(8,128)(2,1)} %all-gather.2.cloned.1.call-done, bf16[16,73,128]{2,1,0:T(8,128)(2,1)S(1)} %all-to-all-done, bf16[16,72,128]{2,1,0:T(8,128)(2,1)S(1)} %all-to-all-done.3), kind=kOutput, calls=%fused_computation.59 | convolution fusion | flops 604569536 | bytes 9568544 | tf_op jit(solution)/shard_map/dot_general | solution.py:285
  93.5 2.4 %collective-permute-start.18 = (bf16[72,1024]{1,0:T(8,128)(2,1)S(1)}, bf16[72,1024]{1,0:T(8,128)(2,1)S(1)}, u32[]{:S(2)}, u32[]{:S(2)}) collective-permute-start(bf16[72,1024]{1,0:T(8,128)(2,1)S(1)} %get-tuple-element.92), channel_id=1, source_target_pairs={{0,7},{1,0},{2,1},{3,2},{4,3},{5,4},{6,5},{7,6},{8,15},{9,8},{10,9... | collective-permute-start | bytes 442376 | tf_op jit(solution)/shard_map/ppermute | solution.py:305
  95.9 1.4 collective-permute-start.19
  97.4 1.0 collective-permute-done.10
  98.4 3.1 %collective-permute-done.14 = bf16[72,1024]{1,0:T(8,128)(2,1)S(1)} collective-permute-done((bf16[72,1024]{1,0:T(8,128)(2,1)S(1)}, bf16[72,1024]{1,0:T(8,128)(2,1)S(1)}, u32[]{:S(2)}, u32[]{:S(2)}) %collective-permute-start.14) | collective-permute-done | bytes 147488 | tf_op jit(solution)/shard_map/ppermute | solution.py:305
  101.5 1.9 %collective-permute-start.15 = (bf16[72,1024]{1,0:T(8,128)(2,1)S(1)}, bf16[72,1024]{1,0:T(8,128)(2,1)S(1)}, u32[]{:S(2)}, u32[]{:S(2)}) collective-permute-start(bf16[72,1024]{1,0:T(8,128)(2,1)S(1)} %collective-permute-done.14), channel_id=1, source_target_pairs={{0,7},{1,0},{2,1},{3,2},{4,3},{5,4},{6,5},{7,6},{8,15},{9,8},{10,9... | collective-permute-start | bytes 442376 | tf_op jit(solution)/shard_map/ppermute | solution.py:305
  103.5 1.4 collective-permute-start.21
  104.9 3.5 %fusion.102 = (f32[144]{0:T(256)S(1)}, f32[144,1280]{1,0:T(8,128)S(1)}) fusion(bf16[2048,1280]{1,0:T(8,128)(2,1)} %copy-done.2, bf16[72,1024]{1,0:T(8,128)(2,1)S(1)} %collective-permute-done.14, bf16[72,1024]{1,0:T(8,128)(2,1)S(1)} %collective-permute-done.19, bf16[72,1024]{1,0:T(8,128)(2,1)S(1)} %collective-permute-done.18, ...), kind=kOutput, calls=%fused_computation.213 | convolution fusion | flops 757518208 | bytes 6570560 | tf_op jit(solution)/shard_map/dot_general | solution.py:296
  108.6 2.7 %collective-permute-start.16 = (bf16[72,1024]{1,0:T(8,128)(2,1)S(1)}, bf16[72,1024]{1,0:T(8,128)(2,1)S(1)}, u32[]{:S(2)}, u32[]{:S(2)}) collective-permute-start(bf16[72,1024]{1,0:T(8,128)(2,1)S(1)} %collective-permute-done.15), channel_id=1, source_target_pairs={{0,7},{1,0},{2,1},{3,2},{4,3},{5,4},{6,5},{7,6},{8,15},{9,8},{10,9... | collective-permute-start | bytes 442376 | tf_op jit(solution)/shard_map/ppermute | solution.py:305
  111.3 1.4 collective-permute-start.23
  112.7 3.5 %fusion.103 = (f32[144]{0:T(256)S(1)}, f32[144,1280]{1,0:T(8,128)S(1)}) fusion(bf16[2048,1280]{1,0:T(8,128)(2,1)} %copy-done.2, bf16[72,1024]{1,0:T(8,128)(2,1)S(1)} %collective-permute-done.15, bf16[72,1024]{1,0:T(8,128)(2,1)S(1)} %collective-permute-done.21, bf16[72,1024]{1,0:T(8,128)(2,1)S(1)} %collective-permute-done.20, ...), kind=kOutput, calls=%fused_computation.214 | convolution fusion | flops 757518208 | bytes 6570560 | tf_op jit(solution)/shard_map/dot_general | solution.py:296
  116.6 2.7 %collective-permute-start.17 = (bf16[72,1024]{1,0:T(8,128)(2,1)S(1)}, bf16[72,1024]{1,0:T(8,128)(2,1)S(1)}, u32[]{:S(2)}, u32[]{:S(2)}) collective-permute-start(bf16[72,1024]{1,0:T(8,128)(2,1)S(1)} %collective-permute-done.16), channel_id=1, source_target_pairs={{0,7},{1,0},{2,1},{3,2},{4,3},{5,4},{6,5},{7,6},{8,15},{9,8},{10,9... | collective-permute-start | bytes 442376 | tf_op jit(solution)/shard_map/ppermute | solution.py:305
  119.3 1.1 fusion.101
  120.3 2.7 %collective-permute-done.13 = bf16[72,1024]{1,0:T(8,128)(2,1)S(1)} collective-permute-done((bf16[72,1024]{1,0:T(8,128)(2,1)S(1)}, bf16[72,1024]{1,0:T(8,128)(2,1)S(1)}, u32[]{:S(2)}, u32[]{:S(2)}) %collective-permute-start.13) | collective-permute-done | bytes 147488 | tf_op jit(solution)/shard_map/ppermute | solution.py:305
  123.1 1.1 fusion.104
  124.1 1.2 fusion
  126.2 14.7 %all_to_all.30.sent_ref = f32[8,96,128]{2,1,0:T(8,128)S(1)} all-to-all(f32[8,96,128]{2,1,0:T(8,128)S(1)} %broadcast_in_dim.57), channel_id=1, replica_groups=mesh['row_0'=4,'row_1'=4,'row_2'=2,'col'=8] {'col'}, dimensions={0} | all-to-all | bytes 786432 | tf_op jit(solution)/shard_map/all_to_all | solution.py:30
  141.9 4.0 %all-to-all-start.5 = ((f32[16,4,576]{2,1,0:T(4,128)}), f32[16,4,576]{2,1,0:T(4,128)S(1)}, u32[]{:S(2)}, u32[]{:S(2)}) async-start(f32[16,4,576]{2,1,0:T(4,128)} %broadcast_in_dim.59), calls=%async_computation.5 | async-start | bytes 327680 | tf_op jit(solution)/shard_map/all_to_all | solution.py:30
  145.8 5.4 %shard_map.195 = f32[16,64,1152]{2,1,0:T(8,128)} custom-call(bf16[8,32,144]{2,1,0:T(8,128)(2,1)S(1)} %all-to-all-done.1.landed_ref, f32[8,96,128]{2,1,0:T(8,128)S(1)} %all_to_all.30.sent_ref, f32[16,64,1152]{2,1,0:T(8,128)} %state_ref.1), custom_call_target="tpu_custom_call" | custom-call | flops 3538944 | bytes 9437184 | tf_op jit(solution)/shard_map/pallas_call | solution.py:157
  151.3 1.3 all-to-all-done.5
  152.9 8.3 %collective-permute-start.25 = (f32[2,576]{1,0:T(2,128)S(1)}, f32[2,576]{1,0:T(2,128)S(1)}, u32[]{:S(2)}, u32[]{:S(2)}) collective-permute-start(f32[2,576]{1,0:T(2,128)S(1)} %pad_maximum_fusion.8), channel_id=1, source_target_pairs={{0,8},{8,0},{1,9},{9,1},{2,10},{10,2},{3,11},{11,3},{4,12},{12,4},... | collective-permute-start | bytes 13832 | tf_op jit(solution)/shard_map/ppermute | solution.py:26
  161.2 0.8 collective-permute-done.25
  (167 shorter events, 14.4 us)
Async XLA Ops:
  7.2 15.0 %copy-start.7 = (bf16[2048,64]{0,1:T(8,128)(2,1)S(1)}, bf16[2048,64]{0,1:T(8,128)(2,1)}, u32[]{:S(2)}) copy-start(bf16[2048,64]{0,1:T(8,128)(2,1)} %param.21) | copy-start | bytes 786436
  7.2 15.0 %copy-start.6 = (bf16[2048,64]{0,1:T(8,128)(2,1)S(1)}, bf16[2048,64]{0,1:T(8,128)(2,1)}, u32[]{:S(2)}) copy-start(bf16[2048,64]{0,1:T(8,128)(2,1)} %param.22) | copy-start | bytes 786436
  7.2 15.0 %copy-start.5 = (bf16[2048,64]{0,1:T(8,128)(2,1)S(1)}, bf16[2048,64]{0,1:T(8,128)(2,1)}, u32[]{:S(2)}) copy-start(bf16[2048,64]{0,1:T(8,128)(2,1)} %param.23) | copy-start | bytes 786436
  7.2 80.7 %all-gather.2.cloned.1.call-start = ((), (), s32[]{:S(2)}) async-start(), calls=%async_computation.6 | async-start | bytes 8650752 | tf_op jit(solution)/shard_map/all_gather | solution.py:212
  7.9 5.5 %collective-permute-start = (bf16[144,64]{0,1:T(8,128)(2,1)}, bf16[144,64]{0,1:T(8,128)(2,1)S(1)}, u32[]{:S(2)}, u32[]{:S(2)}) collective-permute-start(bf16[144,64]{0,1:T(8,128)(2,1)} %param.17), channel_id=1, source_target_pairs={{0,8},{8,0},{1,9},{9,1},{2,10},{10,2},{3,11},{11,3},{4,12},{12,4},... | collective-permute-start | bytes 55304 | tf_op jit(solution)/shard_map/ppermute | solution.py:26
  11.3 1.3 collective-permute-start.1
  15.3 6.8 %collective-permute-start.2 = (bf16[2048,64]{0,1:T(8,128)(2,1)}, bf16[2048,64]{0,1:T(8,128)(2,1)S(1)}, u32[]{:S(2)}, u32[]{:S(2)}) collective-permute-start(bf16[2048,64]{0,1:T(8,128)(2,1)} %param.20), channel_id=1, source_target_pairs={{0,8},{8,0},{1,9},{9,1},{2,10},{10,2},{3,11},{11,3},{4,12},{12,4},... | collective-permute-start | bytes 786440 | tf_op jit(solution)/shard_map/ppermute | solution.py:26
  15.5 6.6 %collective-permute-start.3 = (bf16[2048,64]{0,1:T(8,128)(2,1)}, bf16[2048,64]{0,1:T(8,128)(2,1)S(1)}, u32[]{:S(2)}, u32[]{:S(2)}) collective-permute-start(bf16[2048,64]{0,1:T(8,128)(2,1)} %param.21), channel_id=1, source_target_pairs={{0,8},{8,0},{1,9},{9,1},{2,10},{10,2},{3,11},{11,3},{4,12},{12,4},... | collective-permute-start | bytes 786440 | tf_op jit(solution)/shard_map/ppermute | solution.py:26
  15.8 6.3 %collective-permute-start.4 = (bf16[2048,64]{0,1:T(8,128)(2,1)}, bf16[2048,64]{0,1:T(8,128)(2,1)S(1)}, u32[]{:S(2)}, u32[]{:S(2)}) collective-permute-start(bf16[2048,64]{0,1:T(8,128)(2,1)} %param.22), channel_id=1, source_target_pairs={{0,8},{8,0},{1,9},{9,1},{2,10},{10,2},{3,11},{11,3},{4,12},{12,4},... | collective-permute-start | bytes 786440 | tf_op jit(solution)/shard_map/ppermute | solution.py:26
  16.0 6.1 %collective-permute-start.5 = (bf16[2048,64]{0,1:T(8,128)(2,1)}, bf16[2048,64]{0,1:T(8,128)(2,1)S(1)}, u32[]{:S(2)}, u32[]{:S(2)}) collective-permute-start(bf16[2048,64]{0,1:T(8,128)(2,1)} %param.23), channel_id=1, source_target_pairs={{0,8},{8,0},{1,9},{9,1},{2,10},{10,2},{3,11},{11,3},{4,12},{12,4},... | collective-permute-start | bytes 786440 | tf_op jit(solution)/shard_map/ppermute | solution.py:26
  16.3 13.2 %all-to-all-start = ((bf16[16,73,128]{2,1,0:T(8,128)(2,1)}), bf16[16,73,128]{2,1,0:T(8,128)(2,1)S(1)}, u32[]{:S(2)}, u32[]{:S(2)}) async-start(bf16[16,73,128]{2,1,0:T(8,128)(2,1)} %broadcast_in_dim.52), calls=%async_computation | async-start | bytes 655360 | tf_op jit(solution)/shard_map/all_to_all | solution.py:30
  30.4 12.9 %copy-start.3 = (f32[128]{0:T(128)S(1)}, f32[128]{0:T(128)}, u32[]{:S(2)}) copy-start(f32[128]{0:T(128)} %refs_2_) | copy-start | bytes 1540
  30.9 3.0 %collective-permute-start.6 = (bf16[2,128,72]{2,1,0:T(8,128)(2,1)S(1)}, bf16[2,128,72]{2,1,0:T(8,128)(2,1)S(1)}, u32[]{:S(2)}, u32[]{:S(2)}) collective-permute-start(bf16[2,128,72]{2,1,0:T(8,128)(2,1)S(1)} %get-tuple-element.89), channel_id=1, source_target_pairs={{0,8},{8,0},{1,9},{9,1},{2,10},{10,2},{3,11},{11,3},{4,12},{12,4},... | collective-permute-start | bytes 110600 | tf_op jit(solution)/shard_map/ppermute | solution.py:26
  34.7 21.0 %collective-permute-start.7 = (bf16[2048,640]{1,0:T(8,128)(2,1)}, bf16[2048,640]{1,0:T(8,128)(2,1)S(1)}, u32[]{:S(2)}, u32[]{:S(2)}) collective-permute-start(bf16[2048,640]{1,0:T(8,128)(2,1)} %refs_0_.2), channel_id=1, source_target_pairs={{0,8},{8,0},{1,9},{9,1},{2,10},{10,2},{3,11},{11,3},{4,12},{12,4},... | collective-permute-start | bytes 7864328 | tf_op jit(solution)/shard_map/ppermute | solution.py:26
  35.1 16.6 %all-to-all-start.1 = ((bf16[8,32,144]{2,1,0:T(8,128)(2,1)}), bf16[8,32,144]{2,1,0:T(8,128)(2,1)S(1)}, u32[]{:S(2)}, u32[]{:S(2)}) async-start(bf16[8,32,144]{2,1,0:T(8,128)(2,1)} %bitcast.171), calls=%async_computation.1 | async-start | bytes 262144 | tf_op jit(solution)/shard_map/all_to_all | solution.py:30
  45.7 2.2 %copy-start = (f32[16,64,1152]{2,1,0:T(8,128)}, f32[16,64,1152]{2,1,0:T(8,128)S(1)}, u32[]{:S(2)}) copy-start(f32[16,64,1152]{2,1,0:T(8,128)S(1)} %shard_map.192.state_ref) | copy-start | bytes 14155780
  51.7 2.3 %copy-start.1 = (f32[16,64,1152]{2,1,0:T(8,128)S(1)}, f32[16,64,1152]{2,1,0:T(8,128)}, u32[]{:S(2)}) copy-start(f32[16,64,1152]{2,1,0:T(8,128)} %copy-done) | copy-start | bytes 14155780
  54.0 5.8 %copy-start.11 = (s32[1152]{0:T(1024)S(1)}, s32[1152]{0:T(1024)}, u32[]{:S(2)}) copy-start(s32[1152]{0:T(1024)} %param.32) | copy-start | bytes 13828
  54.0 5.9 %copy-start.14 = (f32[16]{0:T(128)S(1)}, f32[16]{0:T(128)}, u32[]{:S(2)}) copy-start(f32[16]{0:T(128)} %param.26) | copy-start | bytes 196
  54.0 6.5 %copy-start.13 = (bf16[2048,16]{0,1:T(8,128)(2,1)S(1)}, bf16[2048,16]{0,1:T(8,128)(2,1)}, u32[]{:S(2)}) copy-start(bf16[2048,16]{0,1:T(8,128)(2,1)} %param.25) | copy-start | bytes 196612
  54.0 7.6 %copy-start.12 = (f32[16]{0:T(128)S(1)}, f32[16]{0:T(128)}, u32[]{:S(2)}) copy-start(f32[16]{0:T(128)} %param.27) | copy-start | bytes 196
  55.7 8.4 %copy-start.4 = (bf16[2048,640]{1,0:T(8,128)(2,1)}, bf16[2048,640]{1,0:T(8,128)(2,1)S(1)}, u32[]{:S(2)}) copy-start(bf16[2048,640]{1,0:T(8,128)(2,1)S(1)} %collective-permute-done.7.refs_1_) | copy-start | bytes 7864324
  55.7 14.6 %all-to-all-start.2 = ((bf16[8,144,128]{2,1,0:T(8,128)(2,1)}), bf16[8,144,128]{2,1,0:T(8,128)(2,1)}, u32[]{:S(2)}, u32[]{:S(2)}) async-start(bf16[8,144,128]{2,1,0:T(8,128)(2,1)} %bitcast.17), calls=%async_computation.2 | async-start | bytes 589824 | tf_op jit(solution)/shard_map/all_to_all | solution.py:30
  62.4 17.6 %collective-permute-start.24 = (f32[1,72]{1,0:T(1,128)S(1)}, f32[1,72]{1,0:T(1,128)S(1)}, u32[]{:S(2)}, u32[]{:S(2)}) collective-permute-start(f32[1,72]{1,0:T(1,128)S(1)} %fusion.83), channel_id=1, source_target_pairs={{0,8},{8,0},{1,9},{9,1},{2,10},{10,2},{3,11},{11,3},{4,12},{12,4},... | collective-permute-start | bytes 872 | tf_op jit(solution)/shard_map/ppermute | solution.py:26
  66.9 2.4 %copy-start.2 = (bf16[2048,1280]{1,0:T(8,128)(2,1)}, bf16[2048,1280]{1,0:T(8,128)(2,1)S(1)}, u32[]{:S(2)}) copy-start(bf16[2048,1280]{1,0:T(8,128)(2,1)S(1)} %shard_map.194) | copy-start | bytes 15728644
  71.5 4.0 %collective-permute-start.8 = (f32[72,128]{0,1:T(8,128)S(1)}, f32[72,128]{0,1:T(8,128)S(1)}, u32[]{:S(2)}, u32[]{:S(2)}) collective-permute-start(f32[72,128]{0,1:T(8,128)S(1)} %copy.185), channel_id=1, source_target_pairs={{0,8},{8,0},{1,9},{9,1},{2,10},{10,2},{3,11},{11,3},{4,12},{12,4},... | collective-permute-start | bytes 110600 | tf_op jit(solution)/shard_map/ppermute | solution.py:26
  76.5 11.4 %all-to-all-start.3 = ((bf16[16,72,128]{2,1,0:T(8,128)(2,1)}), bf16[16,72,128]{2,1,0:T(8,128)(2,1)S(1)}, u32[]{:S(2)}, u32[]{:S(2)}) async-start(bf16[16,72,128]{2,1,0:T(8,128)(2,1)} %broadcast_in_dim.54), calls=%async_computation.3 | async-start | bytes 589824 | tf_op jit(solution)/shard_map/all_to_all | solution.py:30
  80.1 17.3 %collective-permute-start.9 = (f32[72,64]{0,1:T(8,128)S(1)}, f32[72,64]{0,1:T(8,128)S(1)}, u32[]{:S(2)}, u32[]{:S(2)}) collective-permute-start(f32[72,64]{0,1:T(8,128)S(1)} %constant_dynamic-slice_fusion.3), channel_id=1, source_target_pairs={{0,8},{8,0},{1,9},{9,1},{2,10},{10,2},{3,11},{11,3},{4,12},{12,4},... | collective-permute-start | bytes 55304 | tf_op jit(solution)/shard_map/ppermute | solution.py:26
  93.1 26.1 %slice-start = ((s8[5242880]{0:T(1024)(128)(4,1)}), s8[4194304]{0:T(1024)(128)(4,1)S(1)}, s32[]{:S(2)}) async-start(s8[5242880]{0:T(1024)(128)(4,1)} %bitcast.166), calls=%async_computation.7 | async-start | bytes 8388608
  93.1 5.3 %collective-permute-start.10 = (bf16[72,1024]{1,0:T(8,128)(2,1)S(1)}, bf16[72,1024]{1,0:T(8,128)(2,1)S(1)}, u32[]{:S(2)}, u32[]{:S(2)}) collective-permute-start(bf16[72,1024]{1,0:T(8,128)(2,1)S(1)} %get-tuple-element.92), channel_id=1, source_target_pairs={{0,1},{1,2},{2,3},{3,4},{4,5},{5,6},{6,7},{7,0},{8,9},{9,10},{10,1... | collective-permute-start | bytes 442376 | tf_op jit(solution)/shard_map/ppermute | solution.py:305
  93.5 9.9 %collective-permute-start.18 = (bf16[72,1024]{1,0:T(8,128)(2,1)S(1)}, bf16[72,1024]{1,0:T(8,128)(2,1)S(1)}, u32[]{:S(2)}, u32[]{:S(2)}) collective-permute-start(bf16[72,1024]{1,0:T(8,128)(2,1)S(1)} %get-tuple-element.92), channel_id=1, source_target_pairs={{0,7},{1,0},{2,1},{3,2},{4,3},{5,4},{6,5},{7,6},{8,15},{9,8},{10,9... | collective-permute-start | bytes 442376 | tf_op jit(solution)/shard_map/ppermute | solution.py:305
  95.9 5.6 %collective-permute-start.14 = (bf16[72,1024]{1,0:T(8,128)(2,1)S(1)}, bf16[72,1024]{1,0:T(8,128)(2,1)S(1)}, u32[]{:S(2)}, u32[]{:S(2)}) collective-permute-start(bf16[72,1024]{1,0:T(8,128)(2,1)S(1)} %get-tuple-element.93), channel_id=1, source_target_pairs={{0,7},{1,0},{2,1},{3,2},{4,3},{5,4},{6,5},{7,6},{8,15},{9,8},{10,9... | collective-permute-start | bytes 442376 | tf_op jit(solution)/shard_map/ppermute | solution.py:305
  95.9 7.5 %collective-permute-start.19 = (bf16[72,1024]{1,0:T(8,128)(2,1)S(1)}, bf16[72,1024]{1,0:T(8,128)(2,1)S(1)}, u32[]{:S(2)}, u32[]{:S(2)}) collective-permute-start(bf16[72,1024]{1,0:T(8,128)(2,1)S(1)} %get-tuple-element.93), channel_id=1, source_target_pairs={{0,1},{1,2},{2,3},{3,4},{4,5},{5,6},{6,7},{7,0},{8,9},{9,10},{10,1... | collective-permute-start | bytes 442376 | tf_op jit(solution)/shard_map/ppermute | solution.py:305
  97.4 21.9 %slice-start.1 = ((s8[5242880]{0:T(1024)(128)(4,1)}), s8[1048576]{0:T(1024)(128)(4,1)S(1)}, s32[]{:S(2)}) async-start(s8[5242880]{0:T(1024)(128)(4,1)} %bitcast.166), calls=%async_computation.8 | async-start | bytes 2097152
  98.4 10.0 %collective-permute-start.11 = (bf16[72,1024]{1,0:T(8,128)(2,1)S(1)}, bf16[72,1024]{1,0:T(8,128)(2,1)S(1)}, u32[]{:S(2)}, u32[]{:S(2)}) collective-permute-start(bf16[72,1024]{1,0:T(8,128)(2,1)S(1)} %collective-permute-done.10), channel_id=1, source_target_pairs={{0,1},{1,2},{2,3},{3,4},{4,5},{5,6},{6,7},{7,0},{8,9},{9,10},{10,1... | collective-permute-start | bytes 442376 | tf_op jit(solution)/shard_map/ppermute | solution.py:305
  101.5 7.0 %collective-permute-start.15 = (bf16[72,1024]{1,0:T(8,128)(2,1)S(1)}, bf16[72,1024]{1,0:T(8,128)(2,1)S(1)}, u32[]{:S(2)}, u32[]{:S(2)}) collective-permute-start(bf16[72,1024]{1,0:T(8,128)(2,1)S(1)} %collective-permute-done.14), channel_id=1, source_target_pairs={{0,7},{1,0},{2,1},{3,2},{4,3},{5,4},{6,5},{7,6},{8,15},{9,8},{10,9... | collective-permute-start | bytes 442376 | tf_op jit(solution)/shard_map/ppermute | solution.py:305
  103.5 7.8 %collective-permute-start.20 = (bf16[72,1024]{1,0:T(8,128)(2,1)S(1)}, bf16[72,1024]{1,0:T(8,128)(2,1)S(1)}, u32[]{:S(2)}, u32[]{:S(2)}) collective-permute-start(bf16[72,1024]{1,0:T(8,128)(2,1)S(1)} %collective-permute-done.18), channel_id=1, source_target_pairs={{0,7},{1,0},{2,1},{3,2},{4,3},{5,4},{6,5},{7,6},{8,15},{9,8},{10,9... | collective-permute-start | bytes 442376 | tf_op jit(solution)/shard_map/ppermute | solution.py:305
  103.5 7.8 %collective-permute-start.21 = (bf16[72,1024]{1,0:T(8,128)(2,1)S(1)}, bf16[72,1024]{1,0:T(8,128)(2,1)S(1)}, u32[]{:S(2)}, u32[]{:S(2)}) collective-permute-start(bf16[72,1024]{1,0:T(8,128)(2,1)S(1)} %collective-permute-done.19), channel_id=1, source_target_pairs={{0,1},{1,2},{2,3},{3,4},{4,5},{5,6},{6,7},{7,0},{8,9},{9,10},{10,1... | collective-permute-start | bytes 442376 | tf_op jit(solution)/shard_map/ppermute | solution.py:305
  108.5 7.8 %collective-permute-start.12 = (bf16[72,1024]{1,0:T(8,128)(2,1)S(1)}, bf16[72,1024]{1,0:T(8,128)(2,1)S(1)}, u32[]{:S(2)}, u32[]{:S(2)}) collective-permute-start(bf16[72,1024]{1,0:T(8,128)(2,1)S(1)} %collective-permute-done.11), channel_id=1, source_target_pairs={{0,1},{1,2},{2,3},{3,4},{4,5},{5,6},{6,7},{7,0},{8,9},{9,10},{10,1... | collective-permute-start | bytes 442376 | tf_op jit(solution)/shard_map/ppermute | solution.py:305
  108.6 8.0 %collective-permute-start.16 = (bf16[72,1024]{1,0:T(8,128)(2,1)S(1)}, bf16[72,1024]{1,0:T(8,128)(2,1)S(1)}, u32[]{:S(2)}, u32[]{:S(2)}) collective-permute-start(bf16[72,1024]{1,0:T(8,128)(2,1)S(1)} %collective-permute-done.15), channel_id=1, source_target_pairs={{0,7},{1,0},{2,1},{3,2},{4,3},{5,4},{6,5},{7,6},{8,15},{9,8},{10,9... | collective-permute-start | bytes 442376 | tf_op jit(solution)/shard_map/ppermute | solution.py:305
  111.2 8.0 %collective-permute-start.22 = (bf16[72,1024]{1,0:T(8,128)(2,1)S(1)}, bf16[72,1024]{1,0:T(8,128)(2,1)S(1)}, u32[]{:S(2)}, u32[]{:S(2)}) collective-permute-start(bf16[72,1024]{1,0:T(8,128)(2,1)S(1)} %collective-permute-done.20), channel_id=1, source_target_pairs={{0,7},{1,0},{2,1},{3,2},{4,3},{5,4},{6,5},{7,6},{8,15},{9,8},{10,9... | collective-permute-start | bytes 442376 | tf_op jit(solution)/shard_map/ppermute | solution.py:305
  111.3 7.9 %collective-permute-start.23 = (bf16[72,1024]{1,0:T(8,128)(2,1)S(1)}, bf16[72,1024]{1,0:T(8,128)(2,1)S(1)}, u32[]{:S(2)}, u32[]{:S(2)}) collective-permute-start(bf16[72,1024]{1,0:T(8,128)(2,1)S(1)} %collective-permute-done.21), channel_id=1, source_target_pairs={{0,1},{1,2},{2,3},{3,4},{4,5},{5,6},{6,7},{7,0},{8,9},{9,10},{10,1... | collective-permute-start | bytes 442376 | tf_op jit(solution)/shard_map/ppermute | solution.py:305
  116.3 6.8 %collective-permute-start.13 = (bf16[72,1024]{1,0:T(8,128)(2,1)S(1)}, bf16[72,1024]{1,0:T(8,128)(2,1)S(1)}, u32[]{:S(2)}, u32[]{:S(2)}) collective-permute-start(bf16[72,1024]{1,0:T(8,128)(2,1)S(1)} %collective-permute-done.12), channel_id=1, source_target_pairs={{0,1},{1,2},{2,3},{3,4},{4,5},{5,6},{6,7},{7,0},{8,9},{9,10},{10,1... | collective-permute-start | bytes 442376 | tf_op jit(solution)/shard_map/ppermute | solution.py:305
  116.6 6.5 %collective-permute-start.17 = (bf16[72,1024]{1,0:T(8,128)(2,1)S(1)}, bf16[72,1024]{1,0:T(8,128)(2,1)S(1)}, u32[]{:S(2)}, u32[]{:S(2)}) collective-permute-start(bf16[72,1024]{1,0:T(8,128)(2,1)S(1)} %collective-permute-done.16), channel_id=1, source_target_pairs={{0,7},{1,0},{2,1},{3,2},{4,3},{5,4},{6,5},{7,6},{8,15},{9,8},{10,9... | collective-permute-start | bytes 442376 | tf_op jit(solution)/shard_map/ppermute | solution.py:305
  141.9 10.8 %all-to-all-start.5 = ((f32[16,4,576]{2,1,0:T(4,128)}), f32[16,4,576]{2,1,0:T(4,128)S(1)}, u32[]{:S(2)}, u32[]{:S(2)}) async-start(f32[16,4,576]{2,1,0:T(4,128)} %broadcast_in_dim.59), calls=%async_computation.5 | async-start | bytes 327680 | tf_op jit(solution)/shard_map/all_to_all | solution.py:30
  145.8 17.2 %copy-start.10 = (f32[1152]{0:T(1024)S(1)}, f32[1152]{0:T(1024)}, u32[]{:S(2)}) copy-start(f32[1152]{0:T(1024)} %param.33) | copy-start | bytes 13828
  152.9 9.1 %collective-permute-start.25 = (f32[2,576]{1,0:T(2,128)S(1)}, f32[2,576]{1,0:T(2,128)S(1)}, u32[]{:S(2)}, u32[]{:S(2)}) collective-permute-start(f32[2,576]{1,0:T(2,128)S(1)} %pad_maximum_fusion.8), channel_id=1, source_target_pairs={{0,8},{8,0},{1,9},{9,1},{2,10},{10,2},{3,11},{11,3},{4,12},{12,4},... | collective-permute-start | bytes 13832 | tf_op jit(solution)/shard_map/ppermute | solution.py:26
  162.2 1.4 copy-start.9
  (1 other events, 1.0 us)
Sparse Core Ops, SparseCore 0:
  10.6 62.1 all-gather.1
